TPU v7x, 32 devices: a whole 2x2x4 slice. The times are simulated.
32 devices in a mesh: sect: 4 (over x, core), grp: 4 (over z), span: 2 (over y).
Axes of the slice: x: 2, y: 2, z: 4, core: 2. Of those that a mesh axis runs over, the one named last changes fastest.
Arguments:
- grad_out: bfloat16 [320, 8192], P('grp', 'span'), may hold values from -6 to 6
- destination: int32 [320], P('grp'), may hold values from 0 to 319, as said below
- w_down: bfloat16 [5120, 8192], P('sect', 'span'), may hold values from -0.078125 to 0.078125
- pre_act: bfloat16 [320, 5120], P('grp', ('sect', 'span')), may hold values from -6 to 6
- w_up: bfloat16 [5120, 5120], P(None, ('sect', 'span')), may hold values from -0.078125 to 0.078125
- queries: bfloat16 [1280, 1280], P('grp', ('sect', 'span')), may hold values from -16 to 16
- key_states: bfloat16 [1280, 1280], P('grp', ('sect', 'span')), may hold values from -16 to 16
- value_states: bfloat16 [1280, 1280], P('grp', ('sect', 'span')), may hold values from -6 to 6
- lengths: int32 [12], replicated, may hold values from 1 to 80, 320 in all
Outputs:
- grad_queries: bfloat16 [1280, 1280], P('grp', ('sect', 'span'))
- grad_keys: bfloat16 [1280, 1280], P('grp', ('sect', 'span'))
- grad_values: bfloat16 [1280, 1280], P('grp', ('sect', 'span'))
Inputs may be any that keep to these rules, and one draw needn't show every extreme that they name: `destination`: a permutation of the merged tokens; the merged tokens on one index of grp go to exactly 4 indices of grp, exactly 20 to each. `lengths`: an image has 4 patches for each merged token; images lie one after another along the merged tokens.
All inputs are finite; a program needn't handle non-finite values.
Results may differ from a plain program's by a relative error of at most 0.015.
Values may be sent and summed in bfloat16 or wider, within the bound.
No kernel may reach another device: no remote copies, remote signals or barrier semaphores. Data moves between devices by JAX's collectives and lax.ppermute only.
A program may use at most 64 MiB of HBM per device.

v0:
```python
import functools

import jax
import jax.numpy as jnp
from jax import lax
from jax.experimental import pallas as pl
from jax.experimental.pallas import tpu as pltpu
from jax.sharding import PartitionSpec as P

HEAD_DIM = 80
SCALE = HEAD_DIM**-0.5
MIB = 1024 * 1024
VMEM = pltpu.MemorySpace.VMEM
NT = (((1,), (1,)), ((), ()))
NN = (((1,), (0,)), ((), ()))
TN = (((0,), (0,)), ((), ()))


def dot(a, b, dims):
    return lax.dot_general(a, b, dims, preferred_element_type=jnp.float32)


def iota(shape, dim):
    return lax.broadcasted_iota(jnp.int32, shape, dim)


def params(mib):
    return pltpu.CompilerParams(vmem_limit_bytes=mib * MIB)


def in_vmem(count):
    return [pl.BlockSpec(memory_space=VMEM) for _ in range(count)]


def in_hbm(count):
    return [pl.BlockSpec(memory_space=pltpu.MemorySpace.HBM) for _ in range(count)]


def fetched(pairs, sems):
    copies = [pltpu.make_async_copy(a, b, sems.at[i]) for i, (a, b) in enumerate(pairs)]
    for copy in copies:
        copy.start()
    return copies


def padded_slots(row_count, groups):
    offsets = min(groups, row_count // 2)
    capacity = row_count // offsets
    return capacity, -(-(capacity + 1) // 8) * 8


def one_product(count, slots, hidden):
    return count * slots <= hidden


def down_kernel(groups, spans, capacity, slots, steps, dest_hbm, rows_hbm, weight_ref, out_ref,
                dest_ref, rows_ref, held, sems):
    row_count = rows_ref.shape[0]
    hidden = weight_ref.shape[0] // spans
    pairs = [(dest_hbm, dest_ref), (rows_hbm, rows_ref)]
    at = 0
    for step in steps:
        pairs.append((weight_ref.at[pl.ds(at, step)], held.at[pl.ds(at, step)]))
        at += step
    copies = fetched(pairs, sems)
    copies[0].wait()
    across = jnp.broadcast_to(dest_ref[...].astype(jnp.float32), (row_count, row_count))
    down = across.T
    group_across = jnp.floor((across + 0.5) * (1.0 / row_count))
    group_down = jnp.floor((down + 0.5) * (1.0 / row_count))
    slot_down = down - group_down * row_count
    same = group_across == group_down
    earlier = iota((row_count, row_count), 0) < iota((row_count, row_count), 1)
    later = iota((row_count, row_count), 1) < iota((row_count, row_count), 0)
    rank_across = jnp.sum(jnp.where(same & earlier, 1.0, 0.0), 0, keepdims=True)
    rank_down = jnp.sum(jnp.where(same & later, 1.0, 0.0), 1, keepdims=True)
    row_of = group_across[:1] * slots + rank_across
    places = iota((groups * slots, row_count), 0).astype(jnp.float32)
    pick = jnp.where(places == row_of, 1.0, 0.0).astype(jnp.bfloat16)
    lane = iota((row_count, hidden), 1).astype(jnp.float32)
    shift = 0.0
    if one_product(groups * spans, slots, hidden):
        device = lax.axis_index("grp") * spans + lax.axis_index("span")
        shift = (device * slots).astype(jnp.float32)
    at_rank = lane == rank_down + shift
    label_row = iota((slots, hidden), 0) == capacity
    labels = []
    for g in range(groups):
        hit = at_rank & (group_down[:, :1] == g)
        labels.append(jnp.sum(jnp.where(hit, slot_down[:, :1] + 1.0, 0.0), 0, keepdims=True) - 1.0)
    copies[1].wait()
    at, n = 0, 0
    for s in range(spans):
        total = []
        while at < (s + 1) * hidden:
            copies[2 + n].wait()
            product = dot(held[at : at + steps[n]], rows_ref[...], NT)
            total.append(product.astype(jnp.bfloat16))
            at, n = at + steps[n], n + 1
        moved = dot(pick, jnp.concatenate(total, 0), NT)
        for g in range(groups):
            piece = jnp.where(label_row, labels[g], moved[g * slots : (g + 1) * slots])
            out_ref[g * spans + s] = piece.astype(jnp.bfloat16)


def down_pieces(dest, rows, weight, groups, spans):
    row_count = rows.shape[0]
    capacity, slots = padded_slots(row_count, groups)
    hidden = weight.shape[0] // spans
    steps = [128, hidden - 128]
    if hidden > 512:
        steps = [128, 256, hidden - 384]
    steps += [hidden // 2, hidden - hidden // 2] * (spans - 1)
    return pl.pallas_call(
        functools.partial(down_kernel, groups, spans, capacity, slots, steps),
        out_shape=jax.ShapeDtypeStruct((groups * spans, slots, hidden), jnp.bfloat16),
        in_specs=in_hbm(3),
        out_specs=pl.BlockSpec(memory_space=VMEM),
        scratch_shapes=[
            pltpu.VMEM((1, row_count), jnp.int32),
            pltpu.VMEM(rows.shape, jnp.bfloat16),
            pltpu.VMEM(weight.shape, jnp.bfloat16),
            pltpu.SemaphoreType.DMA((2 + len(steps),)),
        ],
        compiler_params=params(60),
        name="down_product",
    )(dest.reshape(1, row_count), rows, weight)


def up_kernel(heads, capacity, pieces_ref, pre_ref, weight_ref, out_ref, held, sems):
    row_count, hidden = pre_ref.shape
    count, slots, _ = pieces_ref.shape
    width = weight_ref.shape[0] // (4 * heads)
    copies = []
    for h in range(heads):
        for j in range(4):
            copy = pltpu.make_async_copy(
                weight_ref.at[pl.ds((j * heads + h) * width, width)],
                held.at[h, pl.ds(j * width, width)],
                sems.at[h * 4 + j],
            )
            copy.start()
            copies.append(copy)
    label_at = slice(capacity, capacity + 1)
    if one_product(count, slots, hidden):
        pieces = [pieces_ref[p].astype(jnp.float32) for p in range(count)]
        labels = functools.reduce(jnp.maximum, [x[label_at, : count * slots] for x in pieces])
        row = iota((row_count, count * slots), 0).astype(jnp.float32)
        put = jnp.where(row == labels, 1.0, 0.0).astype(jnp.bfloat16)
        total = dot(put, jnp.concatenate(pieces, 0).astype(jnp.bfloat16), NN)
    else:
        row = iota((row_count, slots), 0).astype(jnp.float32)

        def placed(p, total):
            piece = pieces_ref[p]
            labels = piece.astype(jnp.float32)[label_at, :slots]
            put = jnp.where(row == labels, 1.0, 0.0).astype(jnp.bfloat16)
            return total + dot(put, piece, NN)

        total = lax.fori_loop(0, count, placed, jnp.zeros((row_count, hidden), jnp.float32))
    pre = pre_ref[...].astype(jnp.float32)
    cdf = 0.5 * (1.0 + lax.erf(pre * 0.7071067811865476))
    slope = cdf + pre * jnp.exp(-0.5 * pre * pre) * 0.3989422804014327
    grad_pre = (total * slope).astype(jnp.bfloat16)
    for h in range(heads):
        for j in range(4):
            copies[h * 4 + j].wait()
        out_ref[h] = dot(held[h], grad_pre, NT).T.astype(jnp.bfloat16)


def up_pieces(pieces, pre, weight, heads, capacity):
    width = weight.shape[0] // heads
    return pl.pallas_call(
        functools.partial(up_kernel, heads, capacity),
        out_shape=jax.ShapeDtypeStruct((heads, pre.shape[0], width), jnp.bfloat16),
        in_specs=in_vmem(2) + in_hbm(1),
        out_specs=pl.BlockSpec(memory_space=VMEM),
        scratch_shapes=[
            pltpu.VMEM((heads, width, weight.shape[1]), jnp.bfloat16),
            pltpu.SemaphoreType.DMA((heads * 4,)),
        ],
        compiler_params=params(52),
        cost_estimate=pl.CostEstimate(
            flops=8 * pre.shape[0] * weight.size, bytes_accessed=8 * weight.size, transcendentals=0
        ),
        name="up_product",
    )(pieces, pre, weight)


class Rows:
    def __init__(self, columns, patches):
        heads = columns // HEAD_DIM
        self.lanes = -(-3 * patches // 128) * 128
        self.side_lanes = -(-2 * patches // 128) * 128
        self.columns, self.patches = columns, patches
        self.values, self.keys, self.queries, self.attended = [i * columns for i in range(4)]
        self.probs_at = 4 * columns
        self.side_at = self.probs_at + heads * patches
        self.total = self.side_at + heads * patches

    def head(self, start, h):
        return slice(start + h * HEAD_DIM, start + (h + 1) * HEAD_DIM)

    def kind(self, start, count=1):
        return slice(start, start + count * self.columns)

    def probs(self, h):
        return slice(self.probs_at + h * self.patches, self.probs_at + (h + 1) * self.patches)

    def side_probs(self, h):
        return slice(self.side_at + h * self.patches, self.side_at + (h + 1) * self.patches)


def softmax_kernel(lengths_ref, first_ref, own_ref, before_ref, after_ref, out_hbm, done_ref, held,
                   sems):
    columns, patches = own_ref.shape[0] // 3, own_ref.shape[1]
    heads = columns // HEAD_DIM
    rows = Rows(columns, patches)
    blocks = (own_ref, before_ref, after_ref)
    first = first_ref[0, 0]

    def image_of(shape, dim, block):
        token = iota(shape, dim) // 4 + (first + block * (patches // 4))

        def step(i, state):
            image, bound = state
            bound = bound + lengths_ref[0, i]
            return image + jnp.where(token >= bound, 1, 0), bound

        start = (jnp.where(token < 0, -1, 0), jnp.int32(0))
        return lax.fori_loop(0, lengths_ref.shape[1], step, start)[0]

    down = [image_of((patches, 1), 0, b) for b in (0, -1, 1)]
    across = [image_of((1, patches), 1, b) for b in (0, -1, 1)]
    all_keys = jnp.concatenate(across, 1)
    same_own = down[0] == all_keys
    copies = []

    def send(part, lanes):
        at = (pl.ds(part.start, part.stop - part.start), pl.ds(0, lanes))
        copy = pltpu.make_async_copy(held.at[at], out_hbm.at[at], sems.at[len(copies)])
        copy.start()
        copies.append(copy)

    def kind(block, t, h=None):
        start = t * columns + (0 if h is None else h * HEAD_DIM)
        return blocks[block][start : start + (columns if h is None else HEAD_DIM)]

    def wide(t, which):
        return jnp.concatenate([kind(b, t).astype(jnp.float32) for b in which], 1).astype(jnp.bfloat16)

    held[rows.kind(rows.values), : 3 * patches] = wide(2, (0, 1, 2))
    held[rows.kind(rows.keys), : 3 * patches] = wide(1, (0, 1, 2))
    held[rows.kind(rows.queries), : 2 * patches] = wide(0, (1, 2))
    send(rows.kind(rows.values, 2), rows.lanes)
    send(rows.kind(rows.queries), rows.side_lanes)
    for h in range(heads):
        keys = held[rows.head(rows.keys, h), : 3 * patches]
        scores = dot(kind(0, 0, h), keys, TN) * SCALE
        scores = jnp.where(same_own, scores, -jnp.inf)
        weights = jnp.exp(scores - jnp.max(scores, 1, keepdims=True))
        over = 1.0 / jnp.sum(weights, 1, keepdims=True)
        held[rows.probs(h), : 3 * patches] = (weights * over).astype(jnp.bfloat16)
        send(rows.probs(h), rows.lanes)
    for h in range(heads):
        own_keys = kind(0, 1, h).astype(jnp.float32).T.astype(jnp.bfloat16)
        side, attended = [], []
        for b in (1, 2):
            queries = kind(b, 0, h)
            keys = kind(b, 1, h).astype(jnp.float32).T.astype(jnp.bfloat16)
            scores = []
            for n, k in ((0, own_keys), (b, keys)):
                scores.append(jnp.where(down[n] == across[b], dot(k, queries, NN) * SCALE, -jnp.inf))
            top = functools.reduce(jnp.maximum, [jnp.max(x, 0, keepdims=True) for x in scores])
            weights = [jnp.exp(x - top) for x in scores]
            over = 1.0 / sum([jnp.sum(w, 0, keepdims=True) for w in weights])
            probs = [(w * over).astype(jnp.bfloat16) for w in weights]
            attended.append(dot(kind(0, 2, h), probs[0], NN) + dot(kind(b, 2, h), probs[1], NN))
            side.append(probs[0].astype(jnp.float32))
        held[rows.side_probs(h), : 2 * patches] = jnp.concatenate(side, 1).astype(jnp.bfloat16)
        send(rows.side_probs(h), rows.side_lanes)
        attended = jnp.concatenate(attended, 1).astype(jnp.bfloat16)
        held[rows.head(rows.attended, h), : 2 * patches] = attended
    send(rows.kind(rows.attended), rows.side_lanes)
    for copy in copies:
        copy.wait()
    done_ref[...] = jnp.zeros(done_ref.shape, jnp.float32)


def softmax_parts(lengths, first, own, before, after):
    columns, patches = own.shape[0] // 3, own.shape[1]
    heads = columns // HEAD_DIM
    rows = Rows(columns, patches)
    smem = pl.BlockSpec(memory_space=pltpu.MemorySpace.SMEM)
    work = heads * patches * patches
    return pl.pallas_call(
        softmax_kernel,
        out_shape=(
            jax.ShapeDtypeStruct((rows.total, rows.lanes), jnp.bfloat16),
            jax.ShapeDtypeStruct((8, 128), jnp.float32),
        ),
        in_specs=[smem, smem] + in_vmem(3),
        out_specs=tuple(in_hbm(1) + in_vmem(1)),
        scratch_shapes=[
            pltpu.VMEM((rows.total, rows.lanes), jnp.bfloat16),
            pltpu.SemaphoreType.DMA((3 + 2 * heads,)),
        ],
        compiler_params=params(52),
        cost_estimate=pl.CostEstimate(
            flops=100_000 * work, bytes_accessed=500 * work, transcendentals=9 * work
        ),
        name="softmax_parts",
    )(lengths.reshape(1, -1), first.reshape(1, 1), own, before, after)


def gather_kernel(pieces_ref, _, out_ref):
    count, row_count, width = pieces_ref.shape
    total = pieces_ref[0].astype(jnp.float32)
    for p in range(1, count):
        total = total + pieces_ref[p].astype(jnp.float32)
    total = total.astype(jnp.bfloat16)
    columns = width // 4
    patch = iota((row_count, 4 * row_count), 1)
    token = iota((row_count, 4 * row_count), 0)
    result = jnp.zeros((columns, 4 * row_count), jnp.float32)
    for j in range(4):
        put = jnp.where(patch == 4 * token + j, 1.0, 0.0).astype(jnp.bfloat16)
        result = result + dot(total[:, j * columns : (j + 1) * columns], put, TN)
    out_ref[...] = result.astype(jnp.bfloat16)


def gathered(pieces, later):
    _, row_count, width = pieces.shape
    return pl.pallas_call(
        gather_kernel,
        out_shape=jax.ShapeDtypeStruct((width // 4, 4 * row_count), jnp.bfloat16),
        in_specs=in_vmem(2),
        out_specs=pl.BlockSpec(memory_space=VMEM),
        compiler_params=params(16),
        cost_estimate=pl.CostEstimate(
            flops=20_000 * pieces.size, bytes_accessed=400 * pieces.size, transcendentals=0
        ),
        name="gather_sum",
    )(pieces, later)


def own_kernel(grad_ref, own_ref, held_ref, query_ref, key_ref, value_ref):
    columns, patches = grad_ref.shape
    rows = Rows(columns, patches)
    for h in range(columns // HEAD_DIM):
        cols = slice(h * HEAD_DIM, (h + 1) * HEAD_DIM)
        grad = grad_ref[cols]
        slope = dot(grad, held_ref[rows.head(rows.values, h), : 3 * patches], TN)
        probs = held_ref[rows.probs(h), : 3 * patches]
        wide = probs.astype(jnp.float32)
        delta = jnp.sum(wide * slope, 1, keepdims=True)
        scores = (wide * (slope - delta)).astype(jnp.bfloat16)
        query = dot(scores, held_ref[rows.head(rows.keys, h), : 3 * patches], NT) * SCALE
        query_ref[cols] = query.T.astype(jnp.bfloat16)
        key_ref[cols] = dot(own_ref[cols], scores[:, :patches], NN)
        value_ref[cols] = dot(grad, probs[:, :patches], NN)


def own_terms(grad, own, held):
    return pl.pallas_call(
        own_kernel,
        out_shape=(
            jax.ShapeDtypeStruct(grad.shape, jnp.bfloat16),
            jax.ShapeDtypeStruct(grad.shape, jnp.float32),
            jax.ShapeDtypeStruct(grad.shape, jnp.float32),
        ),
        in_specs=in_vmem(3),
        out_specs=tuple(in_vmem(3)),
        compiler_params=params(24),
        name="own_terms",
    )(grad, own, held)


def side_kernel(left_ref, right_ref, key_part_ref, value_part_ref, held_ref, key_ref, value_ref):
    columns, patches = left_ref.shape
    rows = Rows(columns, patches)
    lanes = slice(0, 2 * patches)
    for h in range(columns // HEAD_DIM):
        cols = slice(h * HEAD_DIM, (h + 1) * HEAD_DIM)
        wide = jnp.concatenate([x[cols].astype(jnp.float32) for x in (left_ref, right_ref)], 1)
        grad = wide.astype(jnp.bfloat16)
        slope = dot(held_ref[rows.head(rows.values, h), :patches], grad, TN)
        attended = held_ref[rows.head(rows.attended, h), lanes].astype(jnp.float32)
        delta = jnp.sum(wide * attended, 0, keepdims=True)
        probs = held_ref[rows.side_probs(h), lanes]
        value = dot(probs, grad, NT)
        scores = (probs.astype(jnp.float32) * (slope - delta)).astype(jnp.bfloat16)
        key = dot(scores, held_ref[rows.head(rows.queries, h), lanes], NT)
        key_ref[cols] = ((key_part_ref[cols] + key.T) * SCALE).astype(jnp.bfloat16)
        value_ref[cols] = (value_part_ref[cols] + value.T).astype(jnp.bfloat16)


def side_terms(left, right, key_part, value_part, held):
    shape = jax.ShapeDtypeStruct(left.shape, jnp.bfloat16)
    return pl.pallas_call(
        side_kernel,
        out_shape=(shape, shape),
        in_specs=in_vmem(5),
        out_specs=tuple(in_vmem(2)),
        compiler_params=params(24),
        name="side_terms",
    )(left, right, key_part, value_part, held)


def from_both_sides(x, axis):
    size = lax.axis_size(axis)
    up = [(i, i + 1) for i in range(size - 1)]
    return (
        lax.ppermute(x, axis, up),
        lax.ppermute(x, axis, [(j, i) for i, j in up]),
    )


def on_device(
    grad_out, destination, w_down, pre_act, w_up, queries, key_states, value_states, lengths
):
    groups = lax.axis_size("grp")
    spans = lax.axis_size("span")
    heads = lax.axis_size(("sect", "span"))
    row_count = grad_out.shape[0]
    capacity, _ = padded_slots(row_count, groups)
    pieces = down_pieces(destination, grad_out, w_down, groups, spans)
    pieces, queries, key_states, value_states = lax.optimization_barrier(
        (pieces, queries, key_states, value_states)
    )
    arrived = lax.all_to_all(pieces, ("grp", "span"), split_axis=0, concat_axis=0, tiled=True)
    own = jnp.concatenate([queries.T, key_states.T, value_states.T], 0)
    before, after = from_both_sides(own, "grp")
    first = lax.axis_index("grp") * row_count
    held, held_done = softmax_parts(lengths, first, own, before, after)
    shares = up_pieces(arrived, pre_act, w_up, heads, capacity)
    shares = lax.all_to_all(shares, ("sect", "span"), split_axis=0, concat_axis=0, tiled=True)
    grad = gathered(shares, held_done)
    left, right = from_both_sides(grad, "grp")
    grad_query, key_part, value_part = own_terms(grad, queries.T, held)
    grad_key, grad_value = side_terms(left, right, key_part, value_part, held)
    return grad_query.T, grad_key.T, grad_value.T


def solution(mesh):
    split = P("grp", ("sect", "span"))
    placed = (
        P("grp", "span"),
        P("grp"),
        P("sect", "span"),
        split,
        P(None, ("sect", "span")),
        split,
        split,
        split,
        P(),
    )
    return jax.shard_map(
        on_device,
        mesh=mesh,
        in_specs=placed,
        out_specs=(split, split, split),
        check_vma=False,
    )
```

profile of v0, /device:TPU:0, one launch (start us, length us, event | category | flops | bytes accessed | tf_op | source)
XLA Modules:
  0.0 59.4 jit_solution(14241107994828603607)
XLA Ops:
  0.6 0.0 copy-start.1
  0.6 0.0 copy-start.5
  0.7 0.0 copy-start.4
  0.7 0.0 copy-start.2
  0.7 8.4 %down_product.1 = bf16[8,24,640]{2,1,0:T(8,128)(2,1)} custom-call(s32[1,80]{1,0:T(1,128)} %bitcast.14, bf16[80,4096]{1,0:T(8,128)(2,1)} %rows_hbm.1, bf16[1280,4096]{1,0:T(8,128)(2,1)} %weight_ref.2), custom_call_target="tpu_custom_call" | custom-call | tf_op jit(solution)/shard_map/down_product/pallas_call | solution.py:114
  9.1 0.0 copy-start.3
  9.1 7.3 %all-to-all-start = ((bf16[8,24,640]{2,1,0:T(8,128)(2,1)}), bf16[8,24,640]{2,1,0:T(8,128)(2,1)S(1)}, u32[]{:S(2)}, u32[]{:S(2)}) async-start(bf16[8,24,640]{2,1,0:T(8,128)(2,1)} %down_product.1), calls=%async_computation | async-start | bytes 491520 | tf_op jit(solution)/shard_map/all_to_all | solution.py:431
  16.4 0.0 copy-done.1
  16.4 0.0 copy-done.5
  16.4 0.0 copy-done.4
  16.5 3.9 %collective-permute-start = (bf16[480,320]{1,0:T(8,128)(2,1)S(1)}, bf16[480,320]{1,0:T(8,128)(2,1)S(1)}, u32[]{:S(2)}, u32[]{:S(2)}) collective-permute-start(bf16[480,320]{1,0:T(8,128)(2,1)S(1)} %pad_maximum_fusion.own_ref), channel_id=1, source_target_pairs={{0,2},{2,4},{4,6},{1,3},{3,5},{5,7},{8,10},{10,12},{12,14},{9,11},... | collective-permute-start | bytes 921608 | tf_op jit(solution)/shard_map/ppermute | solution.py:414
  20.4 1.3 %collective-permute-start.1 = (bf16[480,320]{1,0:T(8,128)(2,1)S(1)}, bf16[480,320]{1,0:T(8,128)(2,1)S(1)}, u32[]{:S(2)}, u32[]{:S(2)}) collective-permute-start(bf16[480,320]{1,0:T(8,128)(2,1)S(1)} %pad_maximum_fusion.own_ref), channel_id=1, source_target_pairs={{2,0},{4,2},{6,4},{3,1},{5,3},{7,5},{10,8},{12,10},{14,12},{11,9},... | collective-permute-start | bytes 921608 | tf_op jit(solution)/shard_map/ppermute | solution.py:415
  21.7 3.4 %all-to-all-done.pieces_ref = bf16[8,24,640]{2,1,0:T(8,128)(2,1)S(1)} async-done(((bf16[8,24,640]{2,1,0:T(8,128)(2,1)}), bf16[8,24,640]{2,1,0:T(8,128)(2,1)S(1)}, u32[]{:S(2)}, u32[]{:S(2)}) %all-to-all-start) | async-done | bytes 245792 | tf_op jit(solution)/shard_map/all_to_all | solution.py:431
  25.1 0.0 copy-done.2
  25.1 6.7 %up_product.1 = bf16[8,80,640]{2,1,0:T(8,128)(2,1)} custom-call(bf16[8,24,640]{2,1,0:T(8,128)(2,1)S(1)} %all-to-all-done.pieces_ref, bf16[80,640]{1,0:T(8,128)(2,1)S(1)} %copy-done.2, bf16[5120,640]{1,0:T(8,128)(2,1)} %weight_ref.3), custom_call_target="tpu_custom_call" | custom-call | flops 2097152000 | bytes 26214400 | tf_op jit(solution)/shard_map/up_product/pallas_call | solution.py:173
  31.9 3.6 %all-to-all-start.1 = ((bf16[8,80,640]{2,1,0:T(8,128)(2,1)}), bf16[8,80,640]{2,1,0:T(8,128)(2,1)S(1)}, u32[]{:S(2)}, u32[]{:S(2)}) async-start(bf16[8,80,640]{2,1,0:T(8,128)(2,1)} %up_product.1), calls=%async_computation.1 | async-start | bytes 1638400 | tf_op jit(solution)/shard_map/all_to_all | solution.py:437
  35.4 0.0 collective-permute-done.before_ref
  35.4 0.0 collective-permute-done.1.after_ref
  35.5 0.0 copy-done.3
  35.5 6.6 %softmax_parts.1 = (bf16[1920,1024]{1,0:T(8,128)(2,1)}, f32[8,128]{1,0:T(8,128)S(1)}) custom-call(s32[1,12]{1,0:T(1,128)S(1)} %bitcast.11, s32[1,1]{1,0:T(1,128)} %bitcast.2.first_ref, bf16[480,320]{1,0:T(8,128)(2,1)S(1)} %pad_maximum_fusion.own_ref, bf16[480,320]{1,0:T(8,128)(2,1)S(1)} %collective-permute-done.before_ref, ...), custom_call_target="tpu_custom_call" | custom-call | flops 20480000000 | bytes 102400000 | tf_op jit(solution)/shard_map/softmax_parts/pallas_call | solution.py:296
  42.1 5.4 %all-to-all-done.1.pieces_ref = bf16[8,80,640]{2,1,0:T(8,128)(2,1)S(1)} async-done(((bf16[8,80,640]{2,1,0:T(8,128)(2,1)}), bf16[8,80,640]{2,1,0:T(8,128)(2,1)S(1)}, u32[]{:S(2)}, u32[]{:S(2)}) %all-to-all-start.1) | async-done | bytes 819232 | tf_op jit(solution)/shard_map/all_to_all | solution.py:437
  47.5 0.0 copy-start
  47.5 0.5 gather_sum.1.grad_ref
  48.0 2.9 %collective-permute-start.2 = (bf16[160,320]{1,0:T(8,128)(2,1)S(1)}, bf16[160,320]{1,0:T(8,128)(2,1)S(1)}, u32[]{:S(2)}, u32[]{:S(2)}) collective-permute-start(bf16[160,320]{1,0:T(8,128)(2,1)S(1)} %gather_sum.1.grad_ref), channel_id=1, source_target_pairs={{0,2},{2,4},{4,6},{1,3},{3,5},{5,7},{8,10},{10,12},{12,14},{9,11},... | collective-permute-start | bytes 307208 | tf_op jit(solution)/shard_map/ppermute | solution.py:414
  50.9 1.3 %collective-permute-start.3 = (bf16[160,320]{1,0:T(8,128)(2,1)S(1)}, bf16[160,320]{1,0:T(8,128)(2,1)S(1)}, u32[]{:S(2)}, u32[]{:S(2)}) collective-permute-start(bf16[160,320]{1,0:T(8,128)(2,1)S(1)} %gather_sum.1.grad_ref), channel_id=1, source_target_pairs={{2,0},{4,2},{6,4},{3,1},{5,3},{7,5},{10,8},{12,10},{14,12},{11,9},... | collective-permute-start | bytes 307208 | tf_op jit(solution)/shard_map/ppermute | solution.py:415
  52.2 0.0 copy-done
  52.2 2.4 %own_terms.1 = (bf16[160,320]{1,0:T(8,128)(2,1)}, f32[160,320]{1,0:T(8,128)S(1)}, f32[160,320]{1,0:T(8,128)S(1)}) custom-call(bf16[160,320]{1,0:T(8,128)(2,1)S(1)} %gather_sum.1.grad_ref, bf16[160,320]{1,0:T(8,128)(2,1)S(1)} %bitcast.10, bf16[1920,1024]{1,0:T(8,128)(2,1)S(1)} %copy-done), custom_call_target="tpu_custom_call" | custom-call | tf_op jit(solution)/shard_map/own_terms/pallas_call | solution.py:365
  54.6 0.0 collective-permute-done.2.left_ref
  54.6 3.2 %collective-permute-done.3.right_ref = bf16[160,320]{1,0:T(8,128)(2,1)S(1)} collective-permute-done((bf16[160,320]{1,0:T(8,128)(2,1)S(1)}, bf16[160,320]{1,0:T(8,128)(2,1)S(1)}, u32[]{:S(2)}, u32[]{:S(2)}) %collective-permute-start.3) | collective-permute-done | bytes 102432 | tf_op jit(solution)/shard_map/ppermute | solution.py:415
  57.8 1.7 %side_terms.1 = (bf16[160,320]{1,0:T(8,128)(2,1)}, bf16[160,320]{1,0:T(8,128)(2,1)}) custom-call(bf16[160,320]{1,0:T(8,128)(2,1)S(1)} %collective-permute-done.2.left_ref, bf16[160,320]{1,0:T(8,128)(2,1)S(1)} %collective-permute-done.3.right_ref, f32[160,320]{1,0:T(8,128)S(1)} %get-tuple-element.21.key_part_ref, ...), custom_call_target="tpu_custom_call" | custom-call | tf_op jit(solution)/shard_map/side_terms/pallas_call | solution.py:400
  (1 shorter events, 0.0 us)
Async XLA Ops:
  0.6 15.8 %copy-start.1 = (bf16[320,160]{0,1:T(8,128)(2,1)S(1)}, bf16[320,160]{0,1:T(8,128)(2,1)}, u32[]{:S(2)}) copy-start(bf16[320,160]{0,1:T(8,128)(2,1)} %param.14) | copy-start | bytes 307204
  0.6 15.8 %copy-start.5 = (bf16[320,160]{0,1:T(8,128)(2,1)S(1)}, bf16[320,160]{0,1:T(8,128)(2,1)}, u32[]{:S(2)}) copy-start(bf16[320,160]{0,1:T(8,128)(2,1)} %param.15) | copy-start | bytes 307204
  0.7 15.8 %copy-start.4 = (bf16[320,160]{0,1:T(8,128)(2,1)S(1)}, bf16[320,160]{0,1:T(8,128)(2,1)}, u32[]{:S(2)}) copy-start(bf16[320,160]{0,1:T(8,128)(2,1)} %param.16) | copy-start | bytes 307204
  0.7 24.5 %copy-start.2 = (bf16[80,640]{1,0:T(8,128)(2,1)S(1)}, bf16[80,640]{1,0:T(8,128)(2,1)}, u32[]{:S(2)}) copy-start(bf16[80,640]{1,0:T(8,128)(2,1)} %pre_ref.1) | copy-start | bytes 307204
  9.1 26.3 %copy-start.3 = (s32[12]{0:T(128)S(1)}, s32[12]{0:T(128)}, u32[]{:S(2)}) copy-start(s32[12]{0:T(128)} %param.17) | copy-start | bytes 148
  9.1 16.0 %all-to-all-start = ((bf16[8,24,640]{2,1,0:T(8,128)(2,1)}), bf16[8,24,640]{2,1,0:T(8,128)(2,1)S(1)}, u32[]{:S(2)}, u32[]{:S(2)}) async-start(bf16[8,24,640]{2,1,0:T(8,128)(2,1)} %down_product.1), calls=%async_computation | async-start | bytes 491520 | tf_op jit(solution)/shard_map/all_to_all | solution.py:431
  16.5 18.9 %collective-permute-start = (bf16[480,320]{1,0:T(8,128)(2,1)S(1)}, bf16[480,320]{1,0:T(8,128)(2,1)S(1)}, u32[]{:S(2)}, u32[]{:S(2)}) collective-permute-start(bf16[480,320]{1,0:T(8,128)(2,1)S(1)} %pad_maximum_fusion.own_ref), channel_id=1, source_target_pairs={{0,2},{2,4},{4,6},{1,3},{3,5},{5,7},{8,10},{10,12},{12,14},{9,11},... | collective-permute-start | bytes 921608 | tf_op jit(solution)/shard_map/ppermute | solution.py:414
  20.4 15.0 %collective-permute-start.1 = (bf16[480,320]{1,0:T(8,128)(2,1)S(1)}, bf16[480,320]{1,0:T(8,128)(2,1)S(1)}, u32[]{:S(2)}, u32[]{:S(2)}) collective-permute-start(bf16[480,320]{1,0:T(8,128)(2,1)S(1)} %pad_maximum_fusion.own_ref), channel_id=1, source_target_pairs={{2,0},{4,2},{6,4},{3,1},{5,3},{7,5},{10,8},{12,10},{14,12},{11,9},... | collective-permute-start | bytes 921608 | tf_op jit(solution)/shard_map/ppermute | solution.py:415
  31.9 15.6 %all-to-all-start.1 = ((bf16[8,80,640]{2,1,0:T(8,128)(2,1)}), bf16[8,80,640]{2,1,0:T(8,128)(2,1)S(1)}, u32[]{:S(2)}, u32[]{:S(2)}) async-start(bf16[8,80,640]{2,1,0:T(8,128)(2,1)} %up_product.1), calls=%async_computation.1 | async-start | bytes 1638400 | tf_op jit(solution)/shard_map/all_to_all | solution.py:437
  47.5 4.7 %copy-start = (bf16[1920,1024]{1,0:T(8,128)(2,1)S(1)}, bf16[1920,1024]{1,0:T(8,128)(2,1)}, u32[]{:S(2)}) copy-start(bf16[1920,1024]{1,0:T(8,128)(2,1)} %get-tuple-element.19.held_ref) | copy-start | bytes 11796484
  48.0 6.6 %collective-permute-start.2 = (bf16[160,320]{1,0:T(8,128)(2,1)S(1)}, bf16[160,320]{1,0:T(8,128)(2,1)S(1)}, u32[]{:S(2)}, u32[]{:S(2)}) collective-permute-start(bf16[160,320]{1,0:T(8,128)(2,1)S(1)} %gather_sum.1.grad_ref), channel_id=1, source_target_pairs={{0,2},{2,4},{4,6},{1,3},{3,5},{5,7},{8,10},{10,12},{12,14},{9,11},... | collective-permute-start | bytes 307208 | tf_op jit(solution)/shard_map/ppermute | solution.py:414
  50.9 6.8 %collective-permute-start.3 = (bf16[160,320]{1,0:T(8,128)(2,1)S(1)}, bf16[160,320]{1,0:T(8,128)(2,1)S(1)}, u32[]{:S(2)}, u32[]{:S(2)}) collective-permute-start(bf16[160,320]{1,0:T(8,128)(2,1)S(1)} %gather_sum.1.grad_ref), channel_id=1, source_target_pairs={{2,0},{4,2},{6,4},{3,1},{5,3},{7,5},{10,8},{12,10},{14,12},{11,9},... | collective-permute-start | bytes 307208 | tf_op jit(solution)/shard_map/ppermute | solution.py:415
where the time goes:
time: 59.8 us; the launch traced here: 59.4 us
  Pallas kernels  26.3 us (44%)
  starting transfers between devices  20.3 us (34%)
  waiting for transfers between devices  11.9 us (20%)
  between operations  0.81 us (1%)
    pallas_call x1, Pallas kernels, down_pieces(): pl.pallas_call(functools.partial(down_kernel, groups, spans, capacity, sl...  8.44 us
    all_to_all x1, starting transfers between devices, on_device(): lax.all_to_all(pieces, ('grp', 'span'), split_axis=0, concat_axis=0, tile...  7.29 us
    ppermute x2, starting transfers between devices, from_both_sides(): lax.ppermute(x, axis, up)  6.87 us
    pallas_call x1, Pallas kernels, up_pieces(): pl.pallas_call(functools.partial(up_kernel, heads, capacity), out_shape=j...  6.73 us
    pallas_call x1, Pallas kernels, softmax_parts(): pl.pallas_call(softmax_kernel, out_shape=(jax.ShapeDtypeStruct((rows.tota...  6.65 us
    all_to_all x1, waiting for transfers between devices, on_device(): lax.all_to_all(shares, ('sect', 'span'), split_axis=0, concat_axis=0, til...  5.39 us
    all_to_all x1, starting transfers between devices, on_device(): lax.all_to_all(shares, ('sect', 'span'), split_axis=0, concat_axis=0, til...  3.56 us
    all_to_all x1, waiting for transfers between devices, on_device(): lax.all_to_all(pieces, ('grp', 'span'), split_axis=0, concat_axis=0, tile...  3.37 us
  transfers between devices with their start and end apart: 6, of which 3 were waited for; matrix products, arithmetic and copies ran while one was open for 0% of the time, Pallas kernels for 26%

commit v1 on v0

--- a/solution.py
+++ b/solution.py
@@ -54,7 +54,7 @@
 
 
 def down_kernel(groups, spans, capacity, slots, steps, dest_hbm, rows_hbm, weight_ref, out_ref,
-                dest_ref, rows_ref, held, sems):
+                dest_ref, rows_ref, turned, held, sems):
     row_count = rows_ref.shape[0]
     hidden = weight_ref.shape[0] // spans
     pairs = [(dest_hbm, dest_ref), (rows_hbm, rows_ref)]
@@ -89,12 +89,14 @@
         hit = at_rank & (group_down[:, :1] == g)
         labels.append(jnp.sum(jnp.where(hit, slot_down[:, :1] + 1.0, 0.0), 0, keepdims=True) - 1.0)
     copies[1].wait()
+    for c in range(0, rows_ref.shape[1], 512):
+        turned[c : c + 512] = rows_ref[:, c : c + 512].astype(jnp.float32).T.astype(jnp.bfloat16)
     at, n = 0, 0
     for s in range(spans):
         total = []
         while at < (s + 1) * hidden:
             copies[2 + n].wait()
-            product = dot(held[at : at + steps[n]], rows_ref[...], NT)
+            product = dot(held[at : at + steps[n]], turned[...], NN)
             total.append(product.astype(jnp.bfloat16))
             at, n = at + steps[n], n + 1
         moved = dot(pick, jnp.concatenate(total, 0), NT)
@@ -119,6 +121,7 @@
         scratch_shapes=[
             pltpu.VMEM((1, row_count), jnp.int32),
             pltpu.VMEM(rows.shape, jnp.bfloat16),
+            pltpu.VMEM(rows.shape[::-1], jnp.bfloat16),
             pltpu.VMEM(weight.shape, jnp.bfloat16),
             pltpu.SemaphoreType.DMA((2 + len(steps),)),
         ],
@@ -161,11 +164,11 @@
     pre = pre_ref[...].astype(jnp.float32)
     cdf = 0.5 * (1.0 + lax.erf(pre * 0.7071067811865476))
     slope = cdf + pre * jnp.exp(-0.5 * pre * pre) * 0.3989422804014327
-    grad_pre = (total * slope).astype(jnp.bfloat16)
+    grad_pre = (total * slope).T.astype(jnp.bfloat16)
     for h in range(heads):
         for j in range(4):
             copies[h * 4 + j].wait()
-        out_ref[h] = dot(held[h], grad_pre, NT).T.astype(jnp.bfloat16)
+        out_ref[h] = dot(held[h], grad_pre, NN).T.astype(jnp.bfloat16)
 
 
 def up_pieces(pieces, pre, weight, heads, capacity):

time: 59.8 us -> 59.2 us (0.990)
  Pallas kernels: 26.3 us -> 25.7 us
    pallas_call x1, Pallas kernels: 8.44 us -> 7.58 us  [down_pieces(): pl.pallas_call(functools.partial(down_kernel, groups, spans, capacity, sl...]
  transfers between devices with their start and end apart: 6 -> 6, of which waited for: 3 -> 3; matrix products, arithmetic and copies ran while one was open for 0% -> 0% of each run, Pallas kernels for 26% -> 27%
where the time goes in v1:
time: 59.2 us; the launch traced here: 58.8 us
  Pallas kernels  25.7 us (43%)
  starting transfers between devices  20.3 us (34%)
  waiting for transfers between devices  11.9 us (20%)
  between operations  0.81 us (1%)
    pallas_call x1, Pallas kernels, down_pieces(): pl.pallas_call(functools.partial(down_kernel, groups, spans, capacity, sl...  7.58 us
    all_to_all x1, starting transfers between devices, on_device(): lax.all_to_all(pieces, ('grp', 'span'), split_axis=0, concat_axis=0, tile...  7.29 us
    pallas_call x1, Pallas kernels, up_pieces(): pl.pallas_call(functools.partial(up_kernel, heads, capacity), out_shape=j...  6.99 us
    ppermute x2, starting transfers between devices, from_both_sides(): lax.ppermute(x, axis, up)  6.86 us
    pallas_call x1, Pallas kernels, softmax_parts(): pl.pallas_call(softmax_kernel, out_shape=(jax.ShapeDtypeStruct((rows.tota...  6.65 us
    all_to_all x1, waiting for transfers between devices, on_device(): lax.all_to_all(shares, ('sect', 'span'), split_axis=0, concat_axis=0, til...  5.39 us
    all_to_all x1, starting transfers between devices, on_device(): lax.all_to_all(shares, ('sect', 'span'), split_axis=0, concat_axis=0, til...  3.56 us
    all_to_all x1, waiting for transfers between devices, on_device(): lax.all_to_all(pieces, ('grp', 'span'), split_axis=0, concat_axis=0, tile...  3.37 us
  transfers between devices with their start and end apart: 6, of which 3 were waited for; matrix products, arithmetic and copies ran while one was open for 0% of the time, Pallas kernels for 27%

profile of v1, /device:TPU:0, one launch (start us, length us, event | category | flops | bytes accessed | tf_op | source)
XLA Modules:
  0.0 58.8 jit_solution(12782162848487507161)
XLA Ops:
  0.6 0.0 copy-start.1
  0.6 0.0 copy-start.5
  0.7 0.0 copy-start.4
  0.7 0.0 copy-start.2
  0.7 7.6 %down_product.1 = bf16[8,24,640]{2,1,0:T(8,128)(2,1)} custom-call(s32[1,80]{1,0:T(1,128)} %bitcast.14, bf16[80,4096]{1,0:T(8,128)(2,1)} %rows_hbm.1, bf16[1280,4096]{1,0:T(8,128)(2,1)} %weight_ref.2), custom_call_target="tpu_custom_call" | custom-call | tf_op jit(solution)/shard_map/down_product/pallas_call | solution.py:116
  8.3 0.0 copy-start.3
  8.3 7.3 %all-to-all-start = ((bf16[8,24,640]{2,1,0:T(8,128)(2,1)}), bf16[8,24,640]{2,1,0:T(8,128)(2,1)S(1)}, u32[]{:S(2)}, u32[]{:S(2)}) async-start(bf16[8,24,640]{2,1,0:T(8,128)(2,1)} %down_product.1), calls=%async_computation | async-start | bytes 491520 | tf_op jit(solution)/shard_map/all_to_all | solution.py:434
  15.6 0.0 copy-done.1
  15.6 0.0 copy-done.5
  15.6 0.0 copy-done.4
  15.6 3.9 %collective-permute-start = (bf16[480,320]{1,0:T(8,128)(2,1)S(1)}, bf16[480,320]{1,0:T(8,128)(2,1)S(1)}, u32[]{:S(2)}, u32[]{:S(2)}) collective-permute-start(bf16[480,320]{1,0:T(8,128)(2,1)S(1)} %pad_maximum_fusion.own_ref), channel_id=1, source_target_pairs={{0,2},{2,4},{4,6},{1,3},{3,5},{5,7},{8,10},{10,12},{12,14},{9,11},... | collective-permute-start | bytes 921608 | tf_op jit(solution)/shard_map/ppermute | solution.py:417
  19.6 1.3 %collective-permute-start.1 = (bf16[480,320]{1,0:T(8,128)(2,1)S(1)}, bf16[480,320]{1,0:T(8,128)(2,1)S(1)}, u32[]{:S(2)}, u32[]{:S(2)}) collective-permute-start(bf16[480,320]{1,0:T(8,128)(2,1)S(1)} %pad_maximum_fusion.own_ref), channel_id=1, source_target_pairs={{2,0},{4,2},{6,4},{3,1},{5,3},{7,5},{10,8},{12,10},{14,12},{11,9},... | collective-permute-start | bytes 921608 | tf_op jit(solution)/shard_map/ppermute | solution.py:418
  20.9 3.4 %all-to-all-done.pieces_ref = bf16[8,24,640]{2,1,0:T(8,128)(2,1)S(1)} async-done(((bf16[8,24,640]{2,1,0:T(8,128)(2,1)}), bf16[8,24,640]{2,1,0:T(8,128)(2,1)S(1)}, u32[]{:S(2)}, u32[]{:S(2)}) %all-to-all-start) | async-done | bytes 245792 | tf_op jit(solution)/shard_map/all_to_all | solution.py:434
  24.3 0.0 copy-done.2
  24.3 7.0 %up_product.1 = bf16[8,80,640]{2,1,0:T(8,128)(2,1)} custom-call(bf16[8,24,640]{2,1,0:T(8,128)(2,1)S(1)} %all-to-all-done.pieces_ref, bf16[80,640]{1,0:T(8,128)(2,1)S(1)} %copy-done.2, bf16[5120,640]{1,0:T(8,128)(2,1)} %weight_ref.3), custom_call_target="tpu_custom_call" | custom-call | flops 2097152000 | bytes 26214400 | tf_op jit(solution)/shard_map/up_product/pallas_call | solution.py:176
  31.3 3.6 %all-to-all-start.1 = ((bf16[8,80,640]{2,1,0:T(8,128)(2,1)}), bf16[8,80,640]{2,1,0:T(8,128)(2,1)S(1)}, u32[]{:S(2)}, u32[]{:S(2)}) async-start(bf16[8,80,640]{2,1,0:T(8,128)(2,1)} %up_product.1), calls=%async_computation.1 | async-start | bytes 1638400 | tf_op jit(solution)/shard_map/all_to_all | solution.py:440
  34.8 0.0 collective-permute-done.before_ref
  34.8 0.0 collective-permute-done.1.after_ref
  34.9 0.0 copy-done.3
  34.9 6.6 %softmax_parts.1 = (bf16[1920,1024]{1,0:T(8,128)(2,1)}, f32[8,128]{1,0:T(8,128)S(1)}) custom-call(s32[1,12]{1,0:T(1,128)S(1)} %bitcast.11, s32[1,1]{1,0:T(1,128)} %bitcast.2.first_ref, bf16[480,320]{1,0:T(8,128)(2,1)S(1)} %pad_maximum_fusion.own_ref, bf16[480,320]{1,0:T(8,128)(2,1)S(1)} %collective-permute-done.before_ref, ...), custom_call_target="tpu_custom_call" | custom-call | flops 20480000000 | bytes 102400000 | tf_op jit(solution)/shard_map/softmax_parts/pallas_call | solution.py:299
  41.5 5.4 %all-to-all-done.1.pieces_ref = bf16[8,80,640]{2,1,0:T(8,128)(2,1)S(1)} async-done(((bf16[8,80,640]{2,1,0:T(8,128)(2,1)}), bf16[8,80,640]{2,1,0:T(8,128)(2,1)S(1)}, u32[]{:S(2)}, u32[]{:S(2)}) %all-to-all-start.1) | async-done | bytes 819232 | tf_op jit(solution)/shard_map/all_to_all | solution.py:440
  46.9 0.0 copy-start
  46.9 0.5 gather_sum.1.grad_ref
  47.4 2.9 %collective-permute-start.2 = (bf16[160,320]{1,0:T(8,128)(2,1)S(1)}, bf16[160,320]{1,0:T(8,128)(2,1)S(1)}, u32[]{:S(2)}, u32[]{:S(2)}) collective-permute-start(bf16[160,320]{1,0:T(8,128)(2,1)S(1)} %gather_sum.1.grad_ref), channel_id=1, source_target_pairs={{0,2},{2,4},{4,6},{1,3},{3,5},{5,7},{8,10},{10,12},{12,14},{9,11},... | collective-permute-start | bytes 307208 | tf_op jit(solution)/shard_map/ppermute | solution.py:417
  50.3 1.3 %collective-permute-start.3 = (bf16[160,320]{1,0:T(8,128)(2,1)S(1)}, bf16[160,320]{1,0:T(8,128)(2,1)S(1)}, u32[]{:S(2)}, u32[]{:S(2)}) collective-permute-start(bf16[160,320]{1,0:T(8,128)(2,1)S(1)} %gather_sum.1.grad_ref), channel_id=1, source_target_pairs={{2,0},{4,2},{6,4},{3,1},{5,3},{7,5},{10,8},{12,10},{14,12},{11,9},... | collective-permute-start | bytes 307208 | tf_op jit(solution)/shard_map/ppermute | solution.py:418
  51.6 0.0 copy-done
  51.6 2.4 %own_terms.1 = (bf16[160,320]{1,0:T(8,128)(2,1)}, f32[160,320]{1,0:T(8,128)S(1)}, f32[160,320]{1,0:T(8,128)S(1)}) custom-call(bf16[160,320]{1,0:T(8,128)(2,1)S(1)} %gather_sum.1.grad_ref, bf16[160,320]{1,0:T(8,128)(2,1)S(1)} %bitcast.10, bf16[1920,1024]{1,0:T(8,128)(2,1)S(1)} %copy-done), custom_call_target="tpu_custom_call" | custom-call | tf_op jit(solution)/shard_map/own_terms/pallas_call | solution.py:368
  54.0 0.0 collective-permute-done.2.left_ref
  54.0 3.2 %collective-permute-done.3.right_ref = bf16[160,320]{1,0:T(8,128)(2,1)S(1)} collective-permute-done((bf16[160,320]{1,0:T(8,128)(2,1)S(1)}, bf16[160,320]{1,0:T(8,128)(2,1)S(1)}, u32[]{:S(2)}, u32[]{:S(2)}) %collective-permute-start.3) | collective-permute-done | bytes 102432 | tf_op jit(solution)/shard_map/ppermute | solution.py:418
  57.2 1.7 %side_terms.1 = (bf16[160,320]{1,0:T(8,128)(2,1)}, bf16[160,320]{1,0:T(8,128)(2,1)}) custom-call(bf16[160,320]{1,0:T(8,128)(2,1)S(1)} %collective-permute-done.2.left_ref, bf16[160,320]{1,0:T(8,128)(2,1)S(1)} %collective-permute-done.3.right_ref, f32[160,320]{1,0:T(8,128)S(1)} %get-tuple-element.21.key_part_ref, ...), custom_call_target="tpu_custom_call" | custom-call | tf_op jit(solution)/shard_map/side_terms/pallas_call | solution.py:403
  (1 shorter events, 0.0 us)
Async XLA Ops:
  0.6 14.9 %copy-start.1 = (bf16[320,160]{0,1:T(8,128)(2,1)S(1)}, bf16[320,160]{0,1:T(8,128)(2,1)}, u32[]{:S(2)}) copy-start(bf16[320,160]{0,1:T(8,128)(2,1)} %param.14) | copy-start | bytes 307204
  0.6 14.9 %copy-start.5 = (bf16[320,160]{0,1:T(8,128)(2,1)S(1)}, bf16[320,160]{0,1:T(8,128)(2,1)}, u32[]{:S(2)}) copy-start(bf16[320,160]{0,1:T(8,128)(2,1)} %param.15) | copy-start | bytes 307204
  0.7 14.9 %copy-start.4 = (bf16[320,160]{0,1:T(8,128)(2,1)S(1)}, bf16[320,160]{0,1:T(8,128)(2,1)}, u32[]{:S(2)}) copy-start(bf16[320,160]{0,1:T(8,128)(2,1)} %param.16) | copy-start | bytes 307204
  0.7 23.6 %copy-start.2 = (bf16[80,640]{1,0:T(8,128)(2,1)S(1)}, bf16[80,640]{1,0:T(8,128)(2,1)}, u32[]{:S(2)}) copy-start(bf16[80,640]{1,0:T(8,128)(2,1)} %pre_ref.1) | copy-start | bytes 307204
  8.3 26.6 %copy-start.3 = (s32[12]{0:T(128)S(1)}, s32[12]{0:T(128)}, u32[]{:S(2)}) copy-start(s32[12]{0:T(128)} %param.17) | copy-start | bytes 148
  8.3 16.0 %all-to-all-start = ((bf16[8,24,640]{2,1,0:T(8,128)(2,1)}), bf16[8,24,640]{2,1,0:T(8,128)(2,1)S(1)}, u32[]{:S(2)}, u32[]{:S(2)}) async-start(bf16[8,24,640]{2,1,0:T(8,128)(2,1)} %down_product.1), calls=%async_computation | async-start | bytes 491520 | tf_op jit(solution)/shard_map/all_to_all | solution.py:434
  15.6 19.2 %collective-permute-start = (bf16[480,320]{1,0:T(8,128)(2,1)S(1)}, bf16[480,320]{1,0:T(8,128)(2,1)S(1)}, u32[]{:S(2)}, u32[]{:S(2)}) collective-permute-start(bf16[480,320]{1,0:T(8,128)(2,1)S(1)} %pad_maximum_fusion.own_ref), channel_id=1, source_target_pairs={{0,2},{2,4},{4,6},{1,3},{3,5},{5,7},{8,10},{10,12},{12,14},{9,11},... | collective-permute-start | bytes 921608 | tf_op jit(solution)/shard_map/ppermute | solution.py:417
  19.6 15.3 %collective-permute-start.1 = (bf16[480,320]{1,0:T(8,128)(2,1)S(1)}, bf16[480,320]{1,0:T(8,128)(2,1)S(1)}, u32[]{:S(2)}, u32[]{:S(2)}) collective-permute-start(bf16[480,320]{1,0:T(8,128)(2,1)S(1)} %pad_maximum_fusion.own_ref), channel_id=1, source_target_pairs={{2,0},{4,2},{6,4},{3,1},{5,3},{7,5},{10,8},{12,10},{14,12},{11,9},... | collective-permute-start | bytes 921608 | tf_op jit(solution)/shard_map/ppermute | solution.py:418
  31.3 15.6 %all-to-all-start.1 = ((bf16[8,80,640]{2,1,0:T(8,128)(2,1)}), bf16[8,80,640]{2,1,0:T(8,128)(2,1)S(1)}, u32[]{:S(2)}, u32[]{:S(2)}) async-start(bf16[8,80,640]{2,1,0:T(8,128)(2,1)} %up_product.1), calls=%async_computation.1 | async-start | bytes 1638400 | tf_op jit(solution)/shard_map/all_to_all | solution.py:440
  46.9 4.7 %copy-start = (bf16[1920,1024]{1,0:T(8,128)(2,1)S(1)}, bf16[1920,1024]{1,0:T(8,128)(2,1)}, u32[]{:S(2)}) copy-start(bf16[1920,1024]{1,0:T(8,128)(2,1)} %get-tuple-element.19.held_ref) | copy-start | bytes 11796484
  47.4 6.6 %collective-permute-start.2 = (bf16[160,320]{1,0:T(8,128)(2,1)S(1)}, bf16[160,320]{1,0:T(8,128)(2,1)S(1)}, u32[]{:S(2)}, u32[]{:S(2)}) collective-permute-start(bf16[160,320]{1,0:T(8,128)(2,1)S(1)} %gather_sum.1.grad_ref), channel_id=1, source_target_pairs={{0,2},{2,4},{4,6},{1,3},{3,5},{5,7},{8,10},{10,12},{12,14},{9,11},... | collective-permute-start | bytes 307208 | tf_op jit(solution)/shard_map/ppermute | solution.py:417
  50.3 6.8 %collective-permute-start.3 = (bf16[160,320]{1,0:T(8,128)(2,1)S(1)}, bf16[160,320]{1,0:T(8,128)(2,1)S(1)}, u32[]{:S(2)}, u32[]{:S(2)}) collective-permute-start(bf16[160,320]{1,0:T(8,128)(2,1)S(1)} %gather_sum.1.grad_ref), channel_id=1, source_target_pairs={{2,0},{4,2},{6,4},{3,1},{5,3},{7,5},{10,8},{12,10},{14,12},{11,9},... | collective-permute-start | bytes 307208 | tf_op jit(solution)/shard_map/ppermute | solution.py:418

commit v2 on v0

--- a/solution.py
+++ b/solution.py
@@ -54,14 +54,14 @@
 
 
 def down_kernel(groups, spans, capacity, slots, steps, dest_hbm, rows_hbm, weight_ref, out_ref,
-                dest_ref, rows_ref, held, sems):
+                dest_ref, rows_ref, held, total_ref, sems):
     row_count = rows_ref.shape[0]
     hidden = weight_ref.shape[0] // spans
+    everything = pl.ds(0, weight_ref.shape[0])
     pairs = [(dest_hbm, dest_ref), (rows_hbm, rows_ref)]
-    at = 0
-    for step in steps:
-        pairs.append((weight_ref.at[pl.ds(at, step)], held.at[pl.ds(at, step)]))
-        at += step
+    for at, step in steps:
+        part = (everything, pl.ds(at, step))
+        pairs.append((weight_ref.at[part], held.at[part]))
     copies = fetched(pairs, sems)
     copies[0].wait()
     across = jnp.broadcast_to(dest_ref[...].astype(jnp.float32), (row_count, row_count))
@@ -89,15 +89,14 @@
         hit = at_rank & (group_down[:, :1] == g)
         labels.append(jnp.sum(jnp.where(hit, slot_down[:, :1] + 1.0, 0.0), 0, keepdims=True) - 1.0)
     copies[1].wait()
-    at, n = 0, 0
+    for n, (at, step) in enumerate(steps):
+        turned = rows_ref[:, at : at + step].astype(jnp.float32).T.astype(jnp.bfloat16)
+        copies[2 + n].wait()
+        product = dot(held[:, at : at + step], turned, NN)
+        total_ref[...] = product if n == 0 else total_ref[...] + product
     for s in range(spans):
-        total = []
-        while at < (s + 1) * hidden:
-            copies[2 + n].wait()
-            product = dot(held[at : at + steps[n]], rows_ref[...], NT)
-            total.append(product.astype(jnp.bfloat16))
-            at, n = at + steps[n], n + 1
-        moved = dot(pick, jnp.concatenate(total, 0), NT)
+        part = total_ref[s * hidden : (s + 1) * hidden].astype(jnp.bfloat16)
+        moved = dot(pick, part, NT)
         for g in range(groups):
             piece = jnp.where(label_row, labels[g], moved[g * slots : (g + 1) * slots])
             out_ref[g * spans + s] = piece.astype(jnp.bfloat16)
@@ -107,10 +106,9 @@
     row_count = rows.shape[0]
     capacity, slots = padded_slots(row_count, groups)
     hidden = weight.shape[0] // spans
-    steps = [128, hidden - 128]
-    if hidden > 512:
-        steps = [128, 256, hidden - 384]
-    steps += [hidden // 2, hidden - hidden // 2] * (spans - 1)
+    depth = weight.shape[1]
+    edges = [0, depth // 8, 3 * depth // 8, 5 * depth // 8, depth]
+    steps = [(i, j - i) for i, j in zip(edges, edges[1:])]
     return pl.pallas_call(
         functools.partial(down_kernel, groups, spans, capacity, slots, steps),
         out_shape=jax.ShapeDtypeStruct((groups * spans, slots, hidden), jnp.bfloat16),
@@ -120,6 +118,7 @@
             pltpu.VMEM((1, row_count), jnp.int32),
             pltpu.VMEM(rows.shape, jnp.bfloat16),
             pltpu.VMEM(weight.shape, jnp.bfloat16),
+            pltpu.VMEM((weight.shape[0], row_count), jnp.float32),
             pltpu.SemaphoreType.DMA((2 + len(steps),)),
         ],
         compiler_params=params(60),
@@ -161,11 +160,20 @@
     pre = pre_ref[...].astype(jnp.float32)
     cdf = 0.5 * (1.0 + lax.erf(pre * 0.7071067811865476))
     slope = cdf + pre * jnp.exp(-0.5 * pre * pre) * 0.3989422804014327
-    grad_pre = (total * slope).astype(jnp.bfloat16)
-    for h in range(heads):
-        for j in range(4):
-            copies[h * 4 + j].wait()
-        out_ref[h] = dot(held[h], grad_pre, NT).T.astype(jnp.bfloat16)
+    grad_pre = (total * slope).T.astype(jnp.bfloat16)
+    width = 4 * width
+    waiting = None
+    for h in range(0, heads, 2):
+        for copy in copies[h * 4 : h * 4 + 8]:
+            copy.wait()
+        product = dot(held[h : h + 2].reshape(2 * width, hidden), grad_pre, NN)
+        if waiting is not None:
+            for i in range(2):
+                part = waiting[i * width : (i + 1) * width]
+                out_ref[h - 2 + i] = part.T.astype(jnp.bfloat16)
+        waiting = product
+    for i in range(2):
+        out_ref[heads - 2 + i] = waiting[i * width : (i + 1) * width].T.astype(jnp.bfloat16)
 
 
 def up_pieces(pieces, pre, weight, heads, capacity):

time: 59.8 us -> 57.4 us (0.960)
  Pallas kernels: 26.3 us -> 24 us
    pallas_call x1, Pallas kernels: 8.44 us -> 6.57 us  [down_pieces(): pl.pallas_call(functools.partial(down_kernel, groups, spans, capacity, sl...]
  transfers between devices with their start and end apart: 6 -> 6, of which waited for: 3 -> 3; matrix products, arithmetic and copies ran while one was open for 0% -> 0% of each run, Pallas kernels for 26% -> 27%
where the time goes in v2:
time: 57.4 us; the launch traced here: 57.1 us
  Pallas kernels  24 us (42%)
  starting transfers between devices  20.3 us (35%)
  waiting for transfers between devices  11.9 us (21%)
  between operations  0.81 us (1%)
    all_to_all x1, starting transfers between devices, on_device(): lax.all_to_all(pieces, ('grp', 'span'), split_axis=0, concat_axis=0, tile...  7.29 us
    ppermute x2, starting transfers between devices, from_both_sides(): lax.ppermute(x, axis, up)  6.87 us
    pallas_call x1, Pallas kernels, softmax_parts(): pl.pallas_call(softmax_kernel, out_shape=(jax.ShapeDtypeStruct((rows.tota...  6.65 us
    pallas_call x1, Pallas kernels, down_pieces(): pl.pallas_call(functools.partial(down_kernel, groups, spans, capacity, sl...  6.57 us
    pallas_call x1, Pallas kernels, up_pieces(): pl.pallas_call(functools.partial(up_kernel, heads, capacity), out_shape=j...  6.24 us
    all_to_all x1, waiting for transfers between devices, on_device(): lax.all_to_all(shares, ('sect', 'span'), split_axis=0, concat_axis=0, til...  5.39 us
    all_to_all x1, starting transfers between devices, on_device(): lax.all_to_all(shares, ('sect', 'span'), split_axis=0, concat_axis=0, til...  3.56 us
    all_to_all x1, waiting for transfers between devices, on_device(): lax.all_to_all(pieces, ('grp', 'span'), split_axis=0, concat_axis=0, tile...  3.37 us
  transfers between devices with their start and end apart: 6, of which 3 were waited for; matrix products, arithmetic and copies ran while one was open for 0% of the time, Pallas kernels for 27%

profile of v2, /device:TPU:0, one launch (start us, length us, event | category | flops | bytes accessed | tf_op | source)
XLA Modules:
  0.0 57.1 jit_solution(10275610137938426770)
XLA Ops:
  0.6 0.0 copy-start.1
  0.6 0.0 copy-start.5
  0.7 0.0 copy-start.4
  0.7 0.0 copy-start.2
  0.7 6.6 %down_product.1 = bf16[8,24,640]{2,1,0:T(8,128)(2,1)} custom-call(s32[1,80]{1,0:T(1,128)} %bitcast.14, bf16[80,4096]{1,0:T(8,128)(2,1)} %rows_hbm.1, bf16[1280,4096]{1,0:T(8,128)(2,1)} %weight_ref.2), custom_call_target="tpu_custom_call" | custom-call | tf_op jit(solution)/shard_map/down_product/pallas_call | solution.py:112
  7.3 0.0 copy-start.3
  7.3 7.3 %all-to-all-start = ((bf16[8,24,640]{2,1,0:T(8,128)(2,1)}), bf16[8,24,640]{2,1,0:T(8,128)(2,1)S(1)}, u32[]{:S(2)}, u32[]{:S(2)}) async-start(bf16[8,24,640]{2,1,0:T(8,128)(2,1)} %down_product.1), calls=%async_computation | async-start | bytes 491520 | tf_op jit(solution)/shard_map/all_to_all | solution.py:439
  14.6 0.0 copy-done.1
  14.6 0.0 copy-done.5
  14.6 0.0 copy-done.4
  14.6 3.9 %collective-permute-start = (bf16[480,320]{1,0:T(8,128)(2,1)S(1)}, bf16[480,320]{1,0:T(8,128)(2,1)S(1)}, u32[]{:S(2)}, u32[]{:S(2)}) collective-permute-start(bf16[480,320]{1,0:T(8,128)(2,1)S(1)} %pad_maximum_fusion.own_ref), channel_id=1, source_target_pairs={{0,2},{2,4},{4,6},{1,3},{3,5},{5,7},{8,10},{10,12},{12,14},{9,11},... | collective-permute-start | bytes 921608 | tf_op jit(solution)/shard_map/ppermute | solution.py:422
  18.6 1.3 %collective-permute-start.1 = (bf16[480,320]{1,0:T(8,128)(2,1)S(1)}, bf16[480,320]{1,0:T(8,128)(2,1)S(1)}, u32[]{:S(2)}, u32[]{:S(2)}) collective-permute-start(bf16[480,320]{1,0:T(8,128)(2,1)S(1)} %pad_maximum_fusion.own_ref), channel_id=1, source_target_pairs={{2,0},{4,2},{6,4},{3,1},{5,3},{7,5},{10,8},{12,10},{14,12},{11,9},... | collective-permute-start | bytes 921608 | tf_op jit(solution)/shard_map/ppermute | solution.py:423
  19.9 3.4 %all-to-all-done.pieces_ref = bf16[8,24,640]{2,1,0:T(8,128)(2,1)S(1)} async-done(((bf16[8,24,640]{2,1,0:T(8,128)(2,1)}), bf16[8,24,640]{2,1,0:T(8,128)(2,1)S(1)}, u32[]{:S(2)}, u32[]{:S(2)}) %all-to-all-start) | async-done | bytes 245792 | tf_op jit(solution)/shard_map/all_to_all | solution.py:439
  23.3 0.0 copy-done.2
  23.3 6.2 %up_product.1 = bf16[8,80,640]{2,1,0:T(8,128)(2,1)} custom-call(bf16[8,24,640]{2,1,0:T(8,128)(2,1)S(1)} %all-to-all-done.pieces_ref, bf16[80,640]{1,0:T(8,128)(2,1)S(1)} %copy-done.2, bf16[5120,640]{1,0:T(8,128)(2,1)} %weight_ref.3), custom_call_target="tpu_custom_call" | custom-call | flops 2097152000 | bytes 26214400 | tf_op jit(solution)/shard_map/up_product/pallas_call | solution.py:181
  29.5 3.6 %all-to-all-start.1 = ((bf16[8,80,640]{2,1,0:T(8,128)(2,1)}), bf16[8,80,640]{2,1,0:T(8,128)(2,1)S(1)}, u32[]{:S(2)}, u32[]{:S(2)}) async-start(bf16[8,80,640]{2,1,0:T(8,128)(2,1)} %up_product.1), calls=%async_computation.1 | async-start | bytes 1638400 | tf_op jit(solution)/shard_map/all_to_all | solution.py:445
  33.1 0.0 collective-permute-done.before_ref
  33.1 0.0 collective-permute-done.1.after_ref
  33.1 0.0 copy-done.3
  33.1 6.6 %softmax_parts.1 = (bf16[1920,1024]{1,0:T(8,128)(2,1)}, f32[8,128]{1,0:T(8,128)S(1)}) custom-call(s32[1,12]{1,0:T(1,128)S(1)} %bitcast.11, s32[1,1]{1,0:T(1,128)} %bitcast.2.first_ref, bf16[480,320]{1,0:T(8,128)(2,1)S(1)} %pad_maximum_fusion.own_ref, bf16[480,320]{1,0:T(8,128)(2,1)S(1)} %collective-permute-done.before_ref, ...), custom_call_target="tpu_custom_call" | custom-call | flops 20480000000 | bytes 102400000 | tf_op jit(solution)/shard_map/softmax_parts/pallas_call | solution.py:304
  39.8 5.4 %all-to-all-done.1.pieces_ref = bf16[8,80,640]{2,1,0:T(8,128)(2,1)S(1)} async-done(((bf16[8,80,640]{2,1,0:T(8,128)(2,1)}), bf16[8,80,640]{2,1,0:T(8,128)(2,1)S(1)}, u32[]{:S(2)}, u32[]{:S(2)}) %all-to-all-start.1) | async-done | bytes 819232 | tf_op jit(solution)/shard_map/all_to_all | solution.py:445
  45.2 0.0 copy-start
  45.2 0.5 gather_sum.1.grad_ref
  45.6 2.9 %collective-permute-start.2 = (bf16[160,320]{1,0:T(8,128)(2,1)S(1)}, bf16[160,320]{1,0:T(8,128)(2,1)S(1)}, u32[]{:S(2)}, u32[]{:S(2)}) collective-permute-start(bf16[160,320]{1,0:T(8,128)(2,1)S(1)} %gather_sum.1.grad_ref), channel_id=1, source_target_pairs={{0,2},{2,4},{4,6},{1,3},{3,5},{5,7},{8,10},{10,12},{12,14},{9,11},... | collective-permute-start | bytes 307208 | tf_op jit(solution)/shard_map/ppermute | solution.py:422
  48.6 1.3 %collective-permute-start.3 = (bf16[160,320]{1,0:T(8,128)(2,1)S(1)}, bf16[160,320]{1,0:T(8,128)(2,1)S(1)}, u32[]{:S(2)}, u32[]{:S(2)}) collective-permute-start(bf16[160,320]{1,0:T(8,128)(2,1)S(1)} %gather_sum.1.grad_ref), channel_id=1, source_target_pairs={{2,0},{4,2},{6,4},{3,1},{5,3},{7,5},{10,8},{12,10},{14,12},{11,9},... | collective-permute-start | bytes 307208 | tf_op jit(solution)/shard_map/ppermute | solution.py:423
  49.9 0.0 copy-done
  49.9 2.4 %own_terms.1 = (bf16[160,320]{1,0:T(8,128)(2,1)}, f32[160,320]{1,0:T(8,128)S(1)}, f32[160,320]{1,0:T(8,128)S(1)}) custom-call(bf16[160,320]{1,0:T(8,128)(2,1)S(1)} %gather_sum.1.grad_ref, bf16[160,320]{1,0:T(8,128)(2,1)S(1)} %bitcast.10, bf16[1920,1024]{1,0:T(8,128)(2,1)S(1)} %copy-done), custom_call_target="tpu_custom_call" | custom-call | tf_op jit(solution)/shard_map/own_terms/pallas_call | solution.py:373
  52.2 0.0 collective-permute-done.2.left_ref
  52.2 3.2 %collective-permute-done.3.right_ref = bf16[160,320]{1,0:T(8,128)(2,1)S(1)} collective-permute-done((bf16[160,320]{1,0:T(8,128)(2,1)S(1)}, bf16[160,320]{1,0:T(8,128)(2,1)S(1)}, u32[]{:S(2)}, u32[]{:S(2)}) %collective-permute-start.3) | collective-permute-done | bytes 102432 | tf_op jit(solution)/shard_map/ppermute | solution.py:423
  55.4 1.7 %side_terms.1 = (bf16[160,320]{1,0:T(8,128)(2,1)}, bf16[160,320]{1,0:T(8,128)(2,1)}) custom-call(bf16[160,320]{1,0:T(8,128)(2,1)S(1)} %collective-permute-done.2.left_ref, bf16[160,320]{1,0:T(8,128)(2,1)S(1)} %collective-permute-done.3.right_ref, f32[160,320]{1,0:T(8,128)S(1)} %get-tuple-element.21.key_part_ref, ...), custom_call_target="tpu_custom_call" | custom-call | tf_op jit(solution)/shard_map/side_terms/pallas_call | solution.py:408
  (1 shorter events, 0.0 us)
Async XLA Ops:
  0.6 13.9 %copy-start.1 = (bf16[320,160]{0,1:T(8,128)(2,1)S(1)}, bf16[320,160]{0,1:T(8,128)(2,1)}, u32[]{:S(2)}) copy-start(bf16[320,160]{0,1:T(8,128)(2,1)} %param.14) | copy-start | bytes 307204
  0.6 13.9 %copy-start.5 = (bf16[320,160]{0,1:T(8,128)(2,1)S(1)}, bf16[320,160]{0,1:T(8,128)(2,1)}, u32[]{:S(2)}) copy-start(bf16[320,160]{0,1:T(8,128)(2,1)} %param.15) | copy-start | bytes 307204
  0.7 13.9 %copy-start.4 = (bf16[320,160]{0,1:T(8,128)(2,1)S(1)}, bf16[320,160]{0,1:T(8,128)(2,1)}, u32[]{:S(2)}) copy-start(bf16[320,160]{0,1:T(8,128)(2,1)} %param.16) | copy-start | bytes 307204
  0.7 22.6 %copy-start.2 = (bf16[80,640]{1,0:T(8,128)(2,1)S(1)}, bf16[80,640]{1,0:T(8,128)(2,1)}, u32[]{:S(2)}) copy-start(bf16[80,640]{1,0:T(8,128)(2,1)} %pre_ref.1) | copy-start | bytes 307204
  7.3 25.8 %copy-start.3 = (s32[12]{0:T(128)S(1)}, s32[12]{0:T(128)}, u32[]{:S(2)}) copy-start(s32[12]{0:T(128)} %param.17) | copy-start | bytes 148
  7.3 16.0 %all-to-all-start = ((bf16[8,24,640]{2,1,0:T(8,128)(2,1)}), bf16[8,24,640]{2,1,0:T(8,128)(2,1)S(1)}, u32[]{:S(2)}, u32[]{:S(2)}) async-start(bf16[8,24,640]{2,1,0:T(8,128)(2,1)} %down_product.1), calls=%async_computation | async-start | bytes 491520 | tf_op jit(solution)/shard_map/all_to_all | solution.py:439
  14.6 18.4 %collective-permute-start = (bf16[480,320]{1,0:T(8,128)(2,1)S(1)}, bf16[480,320]{1,0:T(8,128)(2,1)S(1)}, u32[]{:S(2)}, u32[]{:S(2)}) collective-permute-start(bf16[480,320]{1,0:T(8,128)(2,1)S(1)} %pad_maximum_fusion.own_ref), channel_id=1, source_target_pairs={{0,2},{2,4},{4,6},{1,3},{3,5},{5,7},{8,10},{10,12},{12,14},{9,11},... | collective-permute-start | bytes 921608 | tf_op jit(solution)/shard_map/ppermute | solution.py:422
  18.6 14.5 %collective-permute-start.1 = (bf16[480,320]{1,0:T(8,128)(2,1)S(1)}, bf16[480,320]{1,0:T(8,128)(2,1)S(1)}, u32[]{:S(2)}, u32[]{:S(2)}) collective-permute-start(bf16[480,320]{1,0:T(8,128)(2,1)S(1)} %pad_maximum_fusion.own_ref), channel_id=1, source_target_pairs={{2,0},{4,2},{6,4},{3,1},{5,3},{7,5},{10,8},{12,10},{14,12},{11,9},... | collective-permute-start | bytes 921608 | tf_op jit(solution)/shard_map/ppermute | solution.py:423
  29.5 15.6 %all-to-all-start.1 = ((bf16[8,80,640]{2,1,0:T(8,128)(2,1)}), bf16[8,80,640]{2,1,0:T(8,128)(2,1)S(1)}, u32[]{:S(2)}, u32[]{:S(2)}) async-start(bf16[8,80,640]{2,1,0:T(8,128)(2,1)} %up_product.1), calls=%async_computation.1 | async-start | bytes 1638400 | tf_op jit(solution)/shard_map/all_to_all | solution.py:445
  45.2 4.7 %copy-start = (bf16[1920,1024]{1,0:T(8,128)(2,1)S(1)}, bf16[1920,1024]{1,0:T(8,128)(2,1)}, u32[]{:S(2)}) copy-start(bf16[1920,1024]{1,0:T(8,128)(2,1)} %get-tuple-element.19.held_ref) | copy-start | bytes 11796484
  45.6 6.6 %collective-permute-start.2 = (bf16[160,320]{1,0:T(8,128)(2,1)S(1)}, bf16[160,320]{1,0:T(8,128)(2,1)S(1)}, u32[]{:S(2)}, u32[]{:S(2)}) collective-permute-start(bf16[160,320]{1,0:T(8,128)(2,1)S(1)} %gather_sum.1.grad_ref), channel_id=1, source_target_pairs={{0,2},{2,4},{4,6},{1,3},{3,5},{5,7},{8,10},{10,12},{12,14},{9,11},... | collective-permute-start | bytes 307208 | tf_op jit(solution)/shard_map/ppermute | solution.py:422
  48.6 6.8 %collective-permute-start.3 = (bf16[160,320]{1,0:T(8,128)(2,1)S(1)}, bf16[160,320]{1,0:T(8,128)(2,1)S(1)}, u32[]{:S(2)}, u32[]{:S(2)}) collective-permute-start(bf16[160,320]{1,0:T(8,128)(2,1)S(1)} %gather_sum.1.grad_ref), channel_id=1, source_target_pairs={{2,0},{4,2},{6,4},{3,1},{5,3},{7,5},{10,8},{12,10},{14,12},{11,9},... | collective-permute-start | bytes 307208 | tf_op jit(solution)/shard_map/ppermute | solution.py:423

commit v3 on v2

--- a/solution.py
+++ b/solution.py
@@ -36,9 +36,9 @@
     return [pl.BlockSpec(memory_space=pltpu.MemorySpace.HBM) for _ in range(count)]
 
 
-def fetched(pairs, sems):
+def fetched(pairs, sems, at_first=None):
     copies = [pltpu.make_async_copy(a, b, sems.at[i]) for i, (a, b) in enumerate(pairs)]
-    for copy in copies:
+    for copy in copies[:at_first]:
         copy.start()
     return copies
 
@@ -62,7 +62,8 @@
     for at, step in steps:
         part = (everything, pl.ds(at, step))
         pairs.append((weight_ref.at[part], held.at[part]))
-    copies = fetched(pairs, sems)
+    ahead = 3
+    copies = fetched(pairs, sems, 2 + ahead)
     copies[0].wait()
     across = jnp.broadcast_to(dest_ref[...].astype(jnp.float32), (row_count, row_count))
     down = across.T
@@ -92,6 +93,8 @@
     for n, (at, step) in enumerate(steps):
         turned = rows_ref[:, at : at + step].astype(jnp.float32).T.astype(jnp.bfloat16)
         copies[2 + n].wait()
+        for copy in copies[2 + n + ahead : 3 + n + ahead]:
+            copy.start()
         product = dot(held[:, at : at + step], turned, NN)
         total_ref[...] = product if n == 0 else total_ref[...] + product
     for s in range(spans):
@@ -107,7 +110,7 @@
     capacity, slots = padded_slots(row_count, groups)
     hidden = weight.shape[0] // spans
     depth = weight.shape[1]
-    edges = [0, depth // 8, 3 * depth // 8, 5 * depth // 8, depth]
+    edges = [depth * i // 16 for i in (0, 2, 5, 8, 11, 14, 16)]
     steps = [(i, j - i) for i, j in zip(edges, edges[1:])]
     return pl.pallas_call(
         functools.partial(down_kernel, groups, spans, capacity, slots, steps),
@@ -130,16 +133,13 @@
     row_count, hidden = pre_ref.shape
     count, slots, _ = pieces_ref.shape
     width = weight_ref.shape[0] // (4 * heads)
-    copies = []
+    pairs = []
     for h in range(heads):
         for j in range(4):
-            copy = pltpu.make_async_copy(
-                weight_ref.at[pl.ds((j * heads + h) * width, width)],
-                held.at[h, pl.ds(j * width, width)],
-                sems.at[h * 4 + j],
-            )
-            copy.start()
-            copies.append(copy)
+            source = weight_ref.at[pl.ds((j * heads + h) * width, width)]
+            pairs.append((source, held.at[h, pl.ds(j * width, width)]))
+    ahead = 16
+    copies = fetched(pairs, sems, ahead)
     label_at = slice(capacity, capacity + 1)
     if one_product(count, slots, hidden):
         pieces = [pieces_ref[p].astype(jnp.float32) for p in range(count)]
@@ -162,18 +162,41 @@
     slope = cdf + pre * jnp.exp(-0.5 * pre * pre) * 0.3989422804014327
     grad_pre = (total * slope).T.astype(jnp.bfloat16)
     width = 4 * width
+    deep = hidden - hidden % 256
+    if hidden - deep == 128 and row_count <= 128:
+        tail = jnp.concatenate([grad_pre[deep:], jnp.zeros((128, 128 - row_count), jnp.bfloat16)], 1)
+        zero = jnp.zeros_like(tail)
+        twice = jnp.concatenate(
+            [jnp.concatenate([tail, zero], 1), jnp.concatenate([zero, tail], 1)], 0
+        )
+
+        def products(h):
+            main = dot(held[h : h + 2].reshape(2 * width, hidden)[:, :deep], grad_pre[:deep], NN)
+            both = dot(jnp.concatenate([held[h, :, deep:], held[h + 1, :, deep:]], 1), twice, NN)
+            return (
+                main[:width] + both[:, :row_count],
+                main[width:] + both[:, 128 : 128 + row_count],
+            )
+
+    else:
+
+        def products(h):
+            both = dot(held[h : h + 2].reshape(2 * width, hidden), grad_pre, NN)
+            return both[:width], both[width:]
+
     waiting = None
     for h in range(0, heads, 2):
         for copy in copies[h * 4 : h * 4 + 8]:
             copy.wait()
-        product = dot(held[h : h + 2].reshape(2 * width, hidden), grad_pre, NN)
+        for copy in copies[h * 4 + ahead : h * 4 + 8 + ahead]:
+            copy.start()
+        product = products(h)
         if waiting is not None:
             for i in range(2):
-                part = waiting[i * width : (i + 1) * width]
-                out_ref[h - 2 + i] = part.T.astype(jnp.bfloat16)
+                out_ref[h - 2 + i] = waiting[i].T.astype(jnp.bfloat16)
         waiting = product
     for i in range(2):
-        out_ref[heads - 2 + i] = waiting[i * width : (i + 1) * width].T.astype(jnp.bfloat16)
+        out_ref[heads - 2 + i] = waiting[i].T.astype(jnp.bfloat16)
 
 
 def up_pieces(pieces, pre, weight, heads, capacity):

time: 57.4 us -> 58.1 us (1.012)
  Pallas kernels: 24 us -> 24.7 us
    pallas_call x1, Pallas kernels: 6.57 us -> 7.27 us  [down_pieces(): pl.pallas_call(functools.partial(down_kernel, groups, spans, capacity, sl...]
  transfers between devices with their start and end apart: 6 -> 6, of which waited for: 3 -> 3; matrix products, arithmetic and copies ran while one was open for 0% -> 0% of each run, Pallas kernels for 27% -> 26%
where the time goes in v3:
time: 58.1 us; the launch traced here: 57.8 us
  Pallas kernels  24.7 us (43%)
  starting transfers between devices  20.3 us (35%)
  waiting for transfers between devices  11.9 us (20%)
  between operations  0.81 us (1%)
    all_to_all x1, starting transfers between devices, on_device(): lax.all_to_all(pieces, ('grp', 'span'), split_axis=0, concat_axis=0, tile...  7.29 us
    pallas_call x1, Pallas kernels, down_pieces(): pl.pallas_call(functools.partial(down_kernel, groups, spans, capacity, sl...  7.27 us
    ppermute x2, starting transfers between devices, from_both_sides(): lax.ppermute(x, axis, up)  6.87 us
    pallas_call x1, Pallas kernels, softmax_parts(): pl.pallas_call(softmax_kernel, out_shape=(jax.ShapeDtypeStruct((rows.tota...  6.65 us
    pallas_call x1, Pallas kernels, up_pieces(): pl.pallas_call(functools.partial(up_kernel, heads, capacity), out_shape=j...  6.24 us
    all_to_all x1, waiting for transfers between devices, on_device(): lax.all_to_all(shares, ('sect', 'span'), split_axis=0, concat_axis=0, til...  5.38 us
    all_to_all x1, starting transfers between devices, on_device(): lax.all_to_all(shares, ('sect', 'span'), split_axis=0, concat_axis=0, til...  3.56 us
    all_to_all x1, waiting for transfers between devices, on_device(): lax.all_to_all(pieces, ('grp', 'span'), split_axis=0, concat_axis=0, tile...  3.37 us
  transfers between devices with their start and end apart: 6, of which 3 were waited for; matrix products, arithmetic and copies ran while one was open for 0% of the time, Pallas kernels for 26%

profile of v3, /device:TPU:0, one launch (start us, length us, event | category | flops | bytes accessed | tf_op | source)
XLA Modules:
  0.0 57.8 jit_solution(14005644971488737989)
XLA Ops:
  0.6 0.0 copy-start.1
  0.6 0.0 copy-start.5
  0.7 0.0 copy-start.4
  0.7 0.0 copy-start.2
  0.7 7.3 %down_product.1 = bf16[8,24,640]{2,1,0:T(8,128)(2,1)} custom-call(s32[1,80]{1,0:T(1,128)} %bitcast.14, bf16[80,4096]{1,0:T(8,128)(2,1)} %rows_hbm.1, bf16[1280,4096]{1,0:T(8,128)(2,1)} %weight_ref.2), custom_call_target="tpu_custom_call" | custom-call | tf_op jit(solution)/shard_map/down_product/pallas_call | solution.py:115
  7.9 0.0 copy-start.3
  8.0 7.3 %all-to-all-start = ((bf16[8,24,640]{2,1,0:T(8,128)(2,1)}), bf16[8,24,640]{2,1,0:T(8,128)(2,1)S(1)}, u32[]{:S(2)}, u32[]{:S(2)}) async-start(bf16[8,24,640]{2,1,0:T(8,128)(2,1)} %down_product.1), calls=%async_computation | async-start | bytes 491520 | tf_op jit(solution)/shard_map/all_to_all | solution.py:462
  15.2 0.0 copy-done.1
  15.2 0.0 copy-done.5
  15.3 0.0 copy-done.4
  15.3 3.9 %collective-permute-start = (bf16[480,320]{1,0:T(8,128)(2,1)S(1)}, bf16[480,320]{1,0:T(8,128)(2,1)S(1)}, u32[]{:S(2)}, u32[]{:S(2)}) collective-permute-start(bf16[480,320]{1,0:T(8,128)(2,1)S(1)} %pad_maximum_fusion.own_ref), channel_id=1, source_target_pairs={{0,2},{2,4},{4,6},{1,3},{3,5},{5,7},{8,10},{10,12},{12,14},{9,11},... | collective-permute-start | bytes 921608 | tf_op jit(solution)/shard_map/ppermute | solution.py:445
  19.3 1.3 %collective-permute-start.1 = (bf16[480,320]{1,0:T(8,128)(2,1)S(1)}, bf16[480,320]{1,0:T(8,128)(2,1)S(1)}, u32[]{:S(2)}, u32[]{:S(2)}) collective-permute-start(bf16[480,320]{1,0:T(8,128)(2,1)S(1)} %pad_maximum_fusion.own_ref), channel_id=1, source_target_pairs={{2,0},{4,2},{6,4},{3,1},{5,3},{7,5},{10,8},{12,10},{14,12},{11,9},... | collective-permute-start | bytes 921608 | tf_op jit(solution)/shard_map/ppermute | solution.py:446
  20.6 3.4 %all-to-all-done.pieces_ref = bf16[8,24,640]{2,1,0:T(8,128)(2,1)S(1)} async-done(((bf16[8,24,640]{2,1,0:T(8,128)(2,1)}), bf16[8,24,640]{2,1,0:T(8,128)(2,1)S(1)}, u32[]{:S(2)}, u32[]{:S(2)}) %all-to-all-start) | async-done | bytes 245792 | tf_op jit(solution)/shard_map/all_to_all | solution.py:462
  23.9 0.0 copy-done.2
  24.0 6.2 %up_product.1 = bf16[8,80,640]{2,1,0:T(8,128)(2,1)} custom-call(bf16[8,24,640]{2,1,0:T(8,128)(2,1)S(1)} %all-to-all-done.pieces_ref, bf16[80,640]{1,0:T(8,128)(2,1)S(1)} %copy-done.2, bf16[5120,640]{1,0:T(8,128)(2,1)} %weight_ref.3), custom_call_target="tpu_custom_call" | custom-call | flops 2097152000 | bytes 26214400 | tf_op jit(solution)/shard_map/up_product/pallas_call | solution.py:204
  30.2 3.6 %all-to-all-start.1 = ((bf16[8,80,640]{2,1,0:T(8,128)(2,1)}), bf16[8,80,640]{2,1,0:T(8,128)(2,1)S(1)}, u32[]{:S(2)}, u32[]{:S(2)}) async-start(bf16[8,80,640]{2,1,0:T(8,128)(2,1)} %up_product.1), calls=%async_computation.1 | async-start | bytes 1638400 | tf_op jit(solution)/shard_map/all_to_all | solution.py:468
  33.8 0.0 collective-permute-done.before_ref
  33.8 0.0 collective-permute-done.1.after_ref
  33.8 0.0 copy-done.3
  33.8 6.7 %softmax_parts.1 = (bf16[1920,1024]{1,0:T(8,128)(2,1)}, f32[8,128]{1,0:T(8,128)S(1)}) custom-call(s32[1,12]{1,0:T(1,128)S(1)} %bitcast.11, s32[1,1]{1,0:T(1,128)} %bitcast.2.first_ref, bf16[480,320]{1,0:T(8,128)(2,1)S(1)} %pad_maximum_fusion.own_ref, bf16[480,320]{1,0:T(8,128)(2,1)S(1)} %collective-permute-done.before_ref, ...), custom_call_target="tpu_custom_call" | custom-call | flops 20480000000 | bytes 102400000 | tf_op jit(solution)/shard_map/softmax_parts/pallas_call | solution.py:327
  40.5 5.4 %all-to-all-done.1.pieces_ref = bf16[8,80,640]{2,1,0:T(8,128)(2,1)S(1)} async-done(((bf16[8,80,640]{2,1,0:T(8,128)(2,1)}), bf16[8,80,640]{2,1,0:T(8,128)(2,1)S(1)}, u32[]{:S(2)}, u32[]{:S(2)}) %all-to-all-start.1) | async-done | bytes 819232 | tf_op jit(solution)/shard_map/all_to_all | solution.py:468
  45.8 0.0 copy-start
  45.8 0.5 gather_sum.1.grad_ref
  46.3 2.9 %collective-permute-start.2 = (bf16[160,320]{1,0:T(8,128)(2,1)S(1)}, bf16[160,320]{1,0:T(8,128)(2,1)S(1)}, u32[]{:S(2)}, u32[]{:S(2)}) collective-permute-start(bf16[160,320]{1,0:T(8,128)(2,1)S(1)} %gather_sum.1.grad_ref), channel_id=1, source_target_pairs={{0,2},{2,4},{4,6},{1,3},{3,5},{5,7},{8,10},{10,12},{12,14},{9,11},... | collective-permute-start | bytes 307208 | tf_op jit(solution)/shard_map/ppermute | solution.py:445
  49.3 1.3 %collective-permute-start.3 = (bf16[160,320]{1,0:T(8,128)(2,1)S(1)}, bf16[160,320]{1,0:T(8,128)(2,1)S(1)}, u32[]{:S(2)}, u32[]{:S(2)}) collective-permute-start(bf16[160,320]{1,0:T(8,128)(2,1)S(1)} %gather_sum.1.grad_ref), channel_id=1, source_target_pairs={{2,0},{4,2},{6,4},{3,1},{5,3},{7,5},{10,8},{12,10},{14,12},{11,9},... | collective-permute-start | bytes 307208 | tf_op jit(solution)/shard_map/ppermute | solution.py:446
  50.6 0.0 copy-done
  50.6 2.4 %own_terms.1 = (bf16[160,320]{1,0:T(8,128)(2,1)}, f32[160,320]{1,0:T(8,128)S(1)}, f32[160,320]{1,0:T(8,128)S(1)}) custom-call(bf16[160,320]{1,0:T(8,128)(2,1)S(1)} %gather_sum.1.grad_ref, bf16[160,320]{1,0:T(8,128)(2,1)S(1)} %bitcast.10, bf16[1920,1024]{1,0:T(8,128)(2,1)S(1)} %copy-done), custom_call_target="tpu_custom_call" | custom-call | tf_op jit(solution)/shard_map/own_terms/pallas_call | solution.py:396
  52.9 0.0 collective-permute-done.2.left_ref
  52.9 3.2 %collective-permute-done.3.right_ref = bf16[160,320]{1,0:T(8,128)(2,1)S(1)} collective-permute-done((bf16[160,320]{1,0:T(8,128)(2,1)S(1)}, bf16[160,320]{1,0:T(8,128)(2,1)S(1)}, u32[]{:S(2)}, u32[]{:S(2)}) %collective-permute-start.3) | collective-permute-done | bytes 102432 | tf_op jit(solution)/shard_map/ppermute | solution.py:446
  56.1 1.7 %side_terms.1 = (bf16[160,320]{1,0:T(8,128)(2,1)}, bf16[160,320]{1,0:T(8,128)(2,1)}) custom-call(bf16[160,320]{1,0:T(8,128)(2,1)S(1)} %collective-permute-done.2.left_ref, bf16[160,320]{1,0:T(8,128)(2,1)S(1)} %collective-permute-done.3.right_ref, f32[160,320]{1,0:T(8,128)S(1)} %get-tuple-element.21.key_part_ref, ...), custom_call_target="tpu_custom_call" | custom-call | tf_op jit(solution)/shard_map/side_terms/pallas_call | solution.py:431
  (1 shorter events, 0.0 us)
Async XLA Ops:
  0.6 14.6 %copy-start.1 = (bf16[320,160]{0,1:T(8,128)(2,1)S(1)}, bf16[320,160]{0,1:T(8,128)(2,1)}, u32[]{:S(2)}) copy-start(bf16[320,160]{0,1:T(8,128)(2,1)} %param.14) | copy-start | bytes 307204
  0.6 14.6 %copy-start.5 = (bf16[320,160]{0,1:T(8,128)(2,1)S(1)}, bf16[320,160]{0,1:T(8,128)(2,1)}, u32[]{:S(2)}) copy-start(bf16[320,160]{0,1:T(8,128)(2,1)} %param.15) | copy-start | bytes 307204
  0.7 14.6 %copy-start.4 = (bf16[320,160]{0,1:T(8,128)(2,1)S(1)}, bf16[320,160]{0,1:T(8,128)(2,1)}, u32[]{:S(2)}) copy-start(bf16[320,160]{0,1:T(8,128)(2,1)} %param.16) | copy-start | bytes 307204
  0.7 23.3 %copy-start.2 = (bf16[80,640]{1,0:T(8,128)(2,1)S(1)}, bf16[80,640]{1,0:T(8,128)(2,1)}, u32[]{:S(2)}) copy-start(bf16[80,640]{1,0:T(8,128)(2,1)} %pre_ref.1) | copy-start | bytes 307204
  7.9 25.8 %copy-start.3 = (s32[12]{0:T(128)S(1)}, s32[12]{0:T(128)}, u32[]{:S(2)}) copy-start(s32[12]{0:T(128)} %param.17) | copy-start | bytes 148
  8.0 16.0 %all-to-all-start = ((bf16[8,24,640]{2,1,0:T(8,128)(2,1)}), bf16[8,24,640]{2,1,0:T(8,128)(2,1)S(1)}, u32[]{:S(2)}, u32[]{:S(2)}) async-start(bf16[8,24,640]{2,1,0:T(8,128)(2,1)} %down_product.1), calls=%async_computation | async-start | bytes 491520 | tf_op jit(solution)/shard_map/all_to_all | solution.py:462
  15.3 18.5 %collective-permute-start = (bf16[480,320]{1,0:T(8,128)(2,1)S(1)}, bf16[480,320]{1,0:T(8,128)(2,1)S(1)}, u32[]{:S(2)}, u32[]{:S(2)}) collective-permute-start(bf16[480,320]{1,0:T(8,128)(2,1)S(1)} %pad_maximum_fusion.own_ref), channel_id=1, source_target_pairs={{0,2},{2,4},{4,6},{1,3},{3,5},{5,7},{8,10},{10,12},{12,14},{9,11},... | collective-permute-start | bytes 921608 | tf_op jit(solution)/shard_map/ppermute | solution.py:445
  19.3 14.5 %collective-permute-start.1 = (bf16[480,320]{1,0:T(8,128)(2,1)S(1)}, bf16[480,320]{1,0:T(8,128)(2,1)S(1)}, u32[]{:S(2)}, u32[]{:S(2)}) collective-permute-start(bf16[480,320]{1,0:T(8,128)(2,1)S(1)} %pad_maximum_fusion.own_ref), channel_id=1, source_target_pairs={{2,0},{4,2},{6,4},{3,1},{5,3},{7,5},{10,8},{12,10},{14,12},{11,9},... | collective-permute-start | bytes 921608 | tf_op jit(solution)/shard_map/ppermute | solution.py:446
  30.2 15.6 %all-to-all-start.1 = ((bf16[8,80,640]{2,1,0:T(8,128)(2,1)}), bf16[8,80,640]{2,1,0:T(8,128)(2,1)S(1)}, u32[]{:S(2)}, u32[]{:S(2)}) async-start(bf16[8,80,640]{2,1,0:T(8,128)(2,1)} %up_product.1), calls=%async_computation.1 | async-start | bytes 1638400 | tf_op jit(solution)/shard_map/all_to_all | solution.py:468
  45.8 4.7 %copy-start = (bf16[1920,1024]{1,0:T(8,128)(2,1)S(1)}, bf16[1920,1024]{1,0:T(8,128)(2,1)}, u32[]{:S(2)}) copy-start(bf16[1920,1024]{1,0:T(8,128)(2,1)} %get-tuple-element.19.held_ref) | copy-start | bytes 11796484
  46.3 6.6 %collective-permute-start.2 = (bf16[160,320]{1,0:T(8,128)(2,1)S(1)}, bf16[160,320]{1,0:T(8,128)(2,1)S(1)}, u32[]{:S(2)}, u32[]{:S(2)}) collective-permute-start(bf16[160,320]{1,0:T(8,128)(2,1)S(1)} %gather_sum.1.grad_ref), channel_id=1, source_target_pairs={{0,2},{2,4},{4,6},{1,3},{3,5},{5,7},{8,10},{10,12},{12,14},{9,11},... | collective-permute-start | bytes 307208 | tf_op jit(solution)/shard_map/ppermute | solution.py:445
  49.3 6.8 %collective-permute-start.3 = (bf16[160,320]{1,0:T(8,128)(2,1)S(1)}, bf16[160,320]{1,0:T(8,128)(2,1)S(1)}, u32[]{:S(2)}, u32[]{:S(2)}) collective-permute-start(bf16[160,320]{1,0:T(8,128)(2,1)S(1)} %gather_sum.1.grad_ref), channel_id=1, source_target_pairs={{2,0},{4,2},{6,4},{3,1},{5,3},{7,5},{10,8},{12,10},{14,12},{11,9},... | collective-permute-start | bytes 307208 | tf_op jit(solution)/shard_map/ppermute | solution.py:446

commit v4 on v2

--- a/solution.py
+++ b/solution.py
@@ -53,8 +53,8 @@
     return count * slots <= hidden
 
 
-def down_kernel(groups, spans, capacity, slots, steps, dest_hbm, rows_hbm, weight_ref, out_ref,
-                dest_ref, rows_ref, held, total_ref, sems):
+def down_kernel(groups, spans, capacity, slots, steps, dest_hbm, rows_hbm, weight_ref, out_hbm,
+                dest_ref, rows_ref, held, total_ref, pieces_ref, sems, out_sems):
     row_count = rows_ref.shape[0]
     hidden = weight_ref.shape[0] // spans
     everything = pl.ds(0, weight_ref.shape[0])
@@ -94,12 +94,18 @@
         copies[2 + n].wait()
         product = dot(held[:, at : at + step], turned, NN)
         total_ref[...] = product if n == 0 else total_ref[...] + product
+    outgoing = []
     for s in range(spans):
         part = total_ref[s * hidden : (s + 1) * hidden].astype(jnp.bfloat16)
         moved = dot(pick, part, NT)
         for g in range(groups):
             piece = jnp.where(label_row, labels[g], moved[g * slots : (g + 1) * slots])
-            out_ref[g * spans + s] = piece.astype(jnp.bfloat16)
+            pieces_ref[s, g] = piece.astype(jnp.bfloat16)
+        copy = pltpu.make_async_copy(pieces_ref.at[s], out_hbm.at[:, s], out_sems.at[s])
+        copy.start()
+        outgoing.append(copy)
+    for copy in outgoing:
+        copy.wait()
 
 
 def down_pieces(dest, rows, weight, groups, spans):
@@ -107,26 +113,30 @@
     capacity, slots = padded_slots(row_count, groups)
     hidden = weight.shape[0] // spans
     depth = weight.shape[1]
-    edges = [0, depth // 8, 3 * depth // 8, 5 * depth // 8, depth]
+    edges = [depth * i // 8 for i in (0, 2, 5, 7, 8)]
     steps = [(i, j - i) for i, j in zip(edges, edges[1:])]
-    return pl.pallas_call(
+    pieces = pl.pallas_call(
         functools.partial(down_kernel, groups, spans, capacity, slots, steps),
-        out_shape=jax.ShapeDtypeStruct((groups * spans, slots, hidden), jnp.bfloat16),
+        out_shape=jax.ShapeDtypeStruct((groups, spans, slots, hidden), jnp.bfloat16),
         in_specs=in_hbm(3),
-        out_specs=pl.BlockSpec(memory_space=VMEM),
+        out_specs=in_hbm(1)[0],
         scratch_shapes=[
             pltpu.VMEM((1, row_count), jnp.int32),
             pltpu.VMEM(rows.shape, jnp.bfloat16),
             pltpu.VMEM(weight.shape, jnp.bfloat16),
             pltpu.VMEM((weight.shape[0], row_count), jnp.float32),
+            pltpu.VMEM((spans, groups, slots, hidden), jnp.bfloat16),
             pltpu.SemaphoreType.DMA((2 + len(steps),)),
+            pltpu.SemaphoreType.DMA((spans,)),
         ],
         compiler_params=params(60),
         name="down_product",
     )(dest.reshape(1, row_count), rows, weight)
-
-
-def up_kernel(heads, capacity, pieces_ref, pre_ref, weight_ref, out_ref, held, sems):
+    return pieces.reshape(groups * spans, slots, hidden)
+
+
+def up_kernel(heads, capacity, pieces_ref, pre_ref, weight_ref, out_hbm, held, out_ref, sems,
+              out_sems):
     row_count, hidden = pre_ref.shape
     count, slots, _ = pieces_ref.shape
     width = weight_ref.shape[0] // (4 * heads)
@@ -162,18 +172,27 @@
     slope = cdf + pre * jnp.exp(-0.5 * pre * pre) * 0.3989422804014327
     grad_pre = (total * slope).T.astype(jnp.bfloat16)
     width = 4 * width
+    outgoing = []
+
+    def send(h, products):
+        for i in range(2):
+            part = products[i * width : (i + 1) * width]
+            out_ref[h + i] = part.T.astype(jnp.bfloat16)
+        at = pl.ds(h, 2)
+        outgoing.append(pltpu.make_async_copy(out_ref.at[at], out_hbm.at[at], out_sems.at[h // 2]))
+        outgoing[-1].start()
+
     waiting = None
     for h in range(0, heads, 2):
         for copy in copies[h * 4 : h * 4 + 8]:
             copy.wait()
         product = dot(held[h : h + 2].reshape(2 * width, hidden), grad_pre, NN)
         if waiting is not None:
-            for i in range(2):
-                part = waiting[i * width : (i + 1) * width]
-                out_ref[h - 2 + i] = part.T.astype(jnp.bfloat16)
+            send(h - 2, waiting)
         waiting = product
-    for i in range(2):
-        out_ref[heads - 2 + i] = waiting[i * width : (i + 1) * width].T.astype(jnp.bfloat16)
+    send(heads - 2, waiting)
+    for copy in outgoing:
+        copy.wait()
 
 
 def up_pieces(pieces, pre, weight, heads, capacity):
@@ -182,10 +201,12 @@
         functools.partial(up_kernel, heads, capacity),
         out_shape=jax.ShapeDtypeStruct((heads, pre.shape[0], width), jnp.bfloat16),
         in_specs=in_vmem(2) + in_hbm(1),
-        out_specs=pl.BlockSpec(memory_space=VMEM),
+        out_specs=in_hbm(1)[0],
         scratch_shapes=[
             pltpu.VMEM((heads, width, weight.shape[1]), jnp.bfloat16),
+            pltpu.VMEM((heads, pre.shape[0], width), jnp.bfloat16),
             pltpu.SemaphoreType.DMA((heads * 4,)),
+            pltpu.SemaphoreType.DMA((heads // 2,)),
         ],
         compiler_params=params(52),
         cost_estimate=pl.CostEstimate(
@@ -384,13 +405,16 @@
     )(grad, own, held)
 
 
-def side_kernel(left_ref, right_ref, key_part_ref, value_part_ref, held_ref, key_ref, value_ref):
-    columns, patches = left_ref.shape
+def side_kernel(even_ref, odd_ref, key_part_ref, value_part_ref, held_ref, key_ref, value_ref):
+    columns, patches = even_ref.shape
+    is_even = lax.rem(lax.axis_index("grp"), 2) == 0
     rows = Rows(columns, patches)
     lanes = slice(0, 2 * patches)
     for h in range(columns // HEAD_DIM):
         cols = slice(h * HEAD_DIM, (h + 1) * HEAD_DIM)
-        wide = jnp.concatenate([x[cols].astype(jnp.float32) for x in (left_ref, right_ref)], 1)
+        even, odd = even_ref[cols].astype(jnp.float32), odd_ref[cols].astype(jnp.float32)
+        left, right = jnp.where(is_even, odd, even), jnp.where(is_even, even, odd)
+        wide = jnp.concatenate([left, right], 1)
         grad = wide.astype(jnp.bfloat16)
         slope = dot(held_ref[rows.head(rows.values, h), :patches], grad, TN)
         attended = held_ref[rows.head(rows.attended, h), lanes].astype(jnp.float32)
@@ -403,8 +427,8 @@
         value_ref[cols] = (value_part_ref[cols] + value.T).astype(jnp.bfloat16)
 
 
-def side_terms(left, right, key_part, value_part, held):
-    shape = jax.ShapeDtypeStruct(left.shape, jnp.bfloat16)
+def side_terms(even, odd, key_part, value_part, held):
+    shape = jax.ShapeDtypeStruct(even.shape, jnp.bfloat16)
     return pl.pallas_call(
         side_kernel,
         out_shape=(shape, shape),
@@ -412,7 +436,7 @@
         out_specs=tuple(in_vmem(2)),
         compiler_params=params(24),
         name="side_terms",
-    )(left, right, key_part, value_part, held)
+    )(even, odd, key_part, value_part, held)
 
 
 def from_both_sides(x, axis):
@@ -422,6 +446,16 @@
         lax.ppermute(x, axis, up),
         lax.ppermute(x, axis, [(j, i) for i, j in up]),
     )
+
+
+def from_pairs(x, axis):
+    size = lax.axis_size(axis)
+
+    def swapped(first):
+        low = range(first, size - 1, 2)
+        return lax.ppermute(x, axis, [(i, i + 1) for i in low] + [(i + 1, i) for i in low])
+
+    return swapped(0), swapped(1)
 
 
 def on_device(
@@ -444,9 +478,9 @@
     shares = up_pieces(arrived, pre_act, w_up, heads, capacity)
     shares = lax.all_to_all(shares, ("sect", "span"), split_axis=0, concat_axis=0, tiled=True)
     grad = gathered(shares, held_done)
-    left, right = from_both_sides(grad, "grp")
+    even, odd = from_pairs(grad, "grp")
     grad_query, key_part, value_part = own_terms(grad, queries.T, held)
-    grad_key, grad_value = side_terms(left, right, key_part, value_part, held)
+    grad_key, grad_value = side_terms(even, odd, key_part, value_part, held)
     return grad_query.T, grad_key.T, grad_value.T
 
 

time: 57.4 us -> 54.5 us (0.949); the launches traced: 57.1 us -> 53.6 us
  starting transfers between devices: 20.3 us -> 17.7 us
  waiting for transfers between devices: 11.9 us -> 10.1 us
  Pallas kernels: 24 us -> 24.9 us
    ppermute x2 -> x1, waiting for transfers between devices: 3.18 us -> 0.01 us  [from_both_sides(): lax.ppermute(x, axis, [(j, i) for i, j in up])]
    ppermute x2 -> x1, starting transfers between devices: 6.87 us -> 3.94 us  [from_both_sides(): lax.ppermute(x, axis, up)]
    ppermute x0 -> x2, starting transfers between devices: none -> 1.61 us  [swapped(): lax.ppermute(x, axis, [(i, i + 1) for i in low] + [(i + 1, i) for i in low])]
    ppermute x0 -> x2, waiting for transfers between devices: none -> 1.34 us  [swapped(): lax.ppermute(x, axis, [(i, i + 1) for i in low] + [(i + 1, i) for i in low])]
    ppermute x2 -> x1, starting transfers between devices: 2.58 us -> 1.29 us  [from_both_sides(): lax.ppermute(x, axis, [(j, i) for i, j in up])]
    pallas_call x1, Pallas kernels: 6.57 us -> 7.66 us  [down_pieces(): pl.pallas_call(functools.partial(down_kernel, groups, spans, capacity, sl...]
  transfers between devices with their start and end apart: 6 -> 6, of which waited for: 3 -> 3; matrix products, arithmetic and copies ran while one was open for 0% -> 0% of each run, Pallas kernels for 27% -> 28%
where the time goes in v4:
time: 54.5 us; the launch traced here: 53.6 us
  Pallas kernels  24.9 us (46%)
  starting transfers between devices  17.7 us (32%)
  waiting for transfers between devices  10.1 us (19%)
  between operations  0.8 us (1%)
    pallas_call x1, Pallas kernels, down_pieces(): pl.pallas_call(functools.partial(down_kernel, groups, spans, capacity, sl...  7.66 us
    all_to_all x1, starting transfers between devices, on_device(): lax.all_to_all(pieces, ('grp', 'span'), split_axis=0, concat_axis=0, tile...  7.28 us
    pallas_call x1, Pallas kernels, softmax_parts(): pl.pallas_call(softmax_kernel, out_shape=(jax.ShapeDtypeStruct((rows.tota...  6.65 us
    pallas_call x1, Pallas kernels, up_pieces(): pl.pallas_call(functools.partial(up_kernel, heads, capacity), out_shape=j...  6.05 us
    all_to_all x1, waiting for transfers between devices, on_device(): lax.all_to_all(shares, ('sect', 'span'), split_axis=0, concat_axis=0, til...  5.38 us
    ppermute x1, starting transfers between devices, from_both_sides(): lax.ppermute(x, axis, up)  3.94 us
    all_to_all x1, starting transfers between devices, on_device(): lax.all_to_all(shares, ('sect', 'span'), split_axis=0, concat_axis=0, til...  3.56 us
    all_to_all x1, waiting for transfers between devices, on_device(): lax.all_to_all(pieces, ('grp', 'span'), split_axis=0, concat_axis=0, tile...  3.38 us
  transfers between devices with their start and end apart: 6, of which 3 were waited for; matrix products, arithmetic and copies ran while one was open for 0% of the time, Pallas kernels for 28%

profile of v4, /device:TPU:0, one launch (start us, length us, event | category | flops | bytes accessed | tf_op | source)
XLA Modules:
  0.0 53.6 jit_solution(18229649762373355714)
XLA Ops:
  0.6 0.0 copy-start.1
  0.6 0.0 copy-start.5
  0.7 0.0 copy-start.4
  0.7 0.0 copy-start.2
  0.7 7.7 %down_product.1 = bf16[4,2,24,640]{3,2,1,0:T(8,128)(2,1)} custom-call(s32[1,80]{1,0:T(1,128)} %bitcast.16, bf16[80,4096]{1,0:T(8,128)(2,1)} %rows_hbm.1, bf16[1280,4096]{1,0:T(8,128)(2,1)} %weight_ref.2), custom_call_target="tpu_custom_call" | custom-call | tf_op jit(solution)/shard_map/down_product/pallas_call | solution.py:118
  8.3 0.0 copy-start.3
  8.4 7.3 %all-to-all-start = ((bf16[8,24,640]{2,1,0:T(8,128)(2,1)}), bf16[8,24,640]{2,1,0:T(8,128)(2,1)S(1)}, u32[]{:S(2)}, u32[]{:S(2)}) async-start(bf16[8,24,640]{2,1,0:T(8,128)(2,1)} %bitcast.13), calls=%async_computation | async-start | bytes 491520 | tf_op jit(solution)/shard_map/all_to_all | solution.py:473
  15.6 0.0 copy-done.1
  15.6 0.0 copy-done.5
  15.7 0.0 copy-done.4
  15.7 3.9 %collective-permute-start = (bf16[480,320]{1,0:T(8,128)(2,1)S(1)}, bf16[480,320]{1,0:T(8,128)(2,1)S(1)}, u32[]{:S(2)}, u32[]{:S(2)}) collective-permute-start(bf16[480,320]{1,0:T(8,128)(2,1)S(1)} %pad_maximum_fusion.own_ref), channel_id=1, source_target_pairs={{0,2},{2,4},{4,6},{1,3},{3,5},{5,7},{8,10},{10,12},{12,14},{9,11},... | collective-permute-start | bytes 921608 | tf_op jit(solution)/shard_map/ppermute | solution.py:446
  19.7 1.3 %collective-permute-start.1 = (bf16[480,320]{1,0:T(8,128)(2,1)S(1)}, bf16[480,320]{1,0:T(8,128)(2,1)S(1)}, u32[]{:S(2)}, u32[]{:S(2)}) collective-permute-start(bf16[480,320]{1,0:T(8,128)(2,1)S(1)} %pad_maximum_fusion.own_ref), channel_id=1, source_target_pairs={{2,0},{4,2},{6,4},{3,1},{5,3},{7,5},{10,8},{12,10},{14,12},{11,9},... | collective-permute-start | bytes 921608 | tf_op jit(solution)/shard_map/ppermute | solution.py:447
  21.0 3.4 %all-to-all-done.pieces_ref = bf16[8,24,640]{2,1,0:T(8,128)(2,1)S(1)} async-done(((bf16[8,24,640]{2,1,0:T(8,128)(2,1)}), bf16[8,24,640]{2,1,0:T(8,128)(2,1)S(1)}, u32[]{:S(2)}, u32[]{:S(2)}) %all-to-all-start) | async-done | bytes 245792 | tf_op jit(solution)/shard_map/all_to_all | solution.py:473
  24.3 0.0 copy-done.2
  24.4 6.1 %up_product.1 = bf16[8,80,640]{2,1,0:T(8,128)(2,1)} custom-call(bf16[8,24,640]{2,1,0:T(8,128)(2,1)S(1)} %all-to-all-done.pieces_ref, bf16[80,640]{1,0:T(8,128)(2,1)S(1)} %copy-done.2, bf16[5120,640]{1,0:T(8,128)(2,1)} %weight_ref.3), custom_call_target="tpu_custom_call" | custom-call | flops 2097152000 | bytes 26214400 | tf_op jit(solution)/shard_map/up_product/pallas_call | solution.py:200
  30.4 3.6 %all-to-all-start.1 = ((bf16[8,80,640]{2,1,0:T(8,128)(2,1)}), bf16[8,80,640]{2,1,0:T(8,128)(2,1)S(1)}, u32[]{:S(2)}, u32[]{:S(2)}) async-start(bf16[8,80,640]{2,1,0:T(8,128)(2,1)} %up_product.1), calls=%async_computation.1 | async-start | bytes 1638400 | tf_op jit(solution)/shard_map/all_to_all | solution.py:479
  34.0 0.0 collective-permute-done.before_ref
  34.0 0.0 collective-permute-done.1.after_ref
  34.0 0.0 copy-done.3
  34.0 6.6 %softmax_parts.1 = (bf16[1920,1024]{1,0:T(8,128)(2,1)}, f32[8,128]{1,0:T(8,128)S(1)}) custom-call(s32[1,12]{1,0:T(1,128)S(1)} %bitcast.12, s32[1,1]{1,0:T(1,128)} %bitcast.3.first_ref, bf16[480,320]{1,0:T(8,128)(2,1)S(1)} %pad_maximum_fusion.own_ref, bf16[480,320]{1,0:T(8,128)(2,1)S(1)} %collective-permute-done.before_ref, ...), custom_call_target="tpu_custom_call" | custom-call | flops 20480000000 | bytes 102400000 | tf_op jit(solution)/shard_map/softmax_parts/pallas_call | solution.py:325
  40.7 5.4 %all-to-all-done.1.pieces_ref = bf16[8,80,640]{2,1,0:T(8,128)(2,1)S(1)} async-done(((bf16[8,80,640]{2,1,0:T(8,128)(2,1)}), bf16[8,80,640]{2,1,0:T(8,128)(2,1)S(1)}, u32[]{:S(2)}, u32[]{:S(2)}) %all-to-all-start.1) | async-done | bytes 819232 | tf_op jit(solution)/shard_map/all_to_all | solution.py:479
  46.1 0.0 copy-start
  46.1 0.5 gather_sum.1.grad_ref
  46.5 1.0 %collective-permute-start.2 = (bf16[160,320]{1,0:T(8,128)(2,1)S(1)}, bf16[160,320]{1,0:T(8,128)(2,1)S(1)}, u32[]{:S(2)}, u32[]{:S(2)}) collective-permute-start(bf16[160,320]{1,0:T(8,128)(2,1)S(1)} %gather_sum.1.grad_ref), channel_id=1, source_target_pairs={{0,2},{4,6},{2,0},{6,4},{1,3},{5,7},{3,1},{7,5},{8,10},{12,14},{10... | collective-permute-start | bytes 307208 | tf_op jit(solution)/shard_map/ppermute | solution.py:456
  47.5 0.7 %collective-permute-start.3 = (bf16[160,320]{1,0:T(8,128)(2,1)S(1)}, bf16[160,320]{1,0:T(8,128)(2,1)S(1)}, u32[]{:S(2)}, u32[]{:S(2)}) collective-permute-start(bf16[160,320]{1,0:T(8,128)(2,1)S(1)} %gather_sum.1.grad_ref), channel_id=1, source_target_pairs={{2,4},{4,2},{3,5},{5,3},{10,12},{12,10},{11,13},{13,11},{18,20},{2... | collective-permute-start | bytes 307208 | tf_op jit(solution)/shard_map/ppermute | solution.py:456
  48.2 0.0 copy-done
  48.2 2.4 %own_terms.1 = (bf16[160,320]{1,0:T(8,128)(2,1)}, f32[160,320]{1,0:T(8,128)S(1)}, f32[160,320]{1,0:T(8,128)S(1)}) custom-call(bf16[160,320]{1,0:T(8,128)(2,1)S(1)} %gather_sum.1.grad_ref, bf16[160,320]{1,0:T(8,128)(2,1)S(1)} %bitcast.11, bf16[1920,1024]{1,0:T(8,128)(2,1)S(1)} %copy-done), custom_call_target="tpu_custom_call" | custom-call | tf_op jit(solution)/shard_map/own_terms/pallas_call | solution.py:394
  50.5 1.3 %collective-permute-done.2.even_ref = bf16[160,320]{1,0:T(8,128)(2,1)S(1)} collective-permute-done((bf16[160,320]{1,0:T(8,128)(2,1)S(1)}, bf16[160,320]{1,0:T(8,128)(2,1)S(1)}, u32[]{:S(2)}, u32[]{:S(2)}) %collective-permute-start.2) | collective-permute-done | bytes 102432 | tf_op jit(solution)/shard_map/ppermute | solution.py:456
  51.9 0.0 collective-permute-done.3.odd_ref
  51.9 1.7 %side_terms.1 = (bf16[160,320]{1,0:T(8,128)(2,1)}, bf16[160,320]{1,0:T(8,128)(2,1)}) custom-call(bf16[160,320]{1,0:T(8,128)(2,1)S(1)} %collective-permute-done.2.even_ref, bf16[160,320]{1,0:T(8,128)(2,1)S(1)} %collective-permute-done.3.odd_ref, f32[160,320]{1,0:T(8,128)S(1)} %get-tuple-element.21.key_part_ref, ...), custom_call_target="tpu_custom_call" | custom-call | tf_op jit(solution)/shard_map/side_terms/pallas_call | solution.py:432
  (1 shorter events, 0.0 us)
Async XLA Ops:
  0.6 15.0 %copy-start.1 = (bf16[320,160]{0,1:T(8,128)(2,1)S(1)}, bf16[320,160]{0,1:T(8,128)(2,1)}, u32[]{:S(2)}) copy-start(bf16[320,160]{0,1:T(8,128)(2,1)} %param.14) | copy-start | bytes 307204
  0.6 15.0 %copy-start.5 = (bf16[320,160]{0,1:T(8,128)(2,1)S(1)}, bf16[320,160]{0,1:T(8,128)(2,1)}, u32[]{:S(2)}) copy-start(bf16[320,160]{0,1:T(8,128)(2,1)} %param.15) | copy-start | bytes 307204
  0.7 15.0 %copy-start.4 = (bf16[320,160]{0,1:T(8,128)(2,1)S(1)}, bf16[320,160]{0,1:T(8,128)(2,1)}, u32[]{:S(2)}) copy-start(bf16[320,160]{0,1:T(8,128)(2,1)} %param.16) | copy-start | bytes 307204
  0.7 23.7 %copy-start.2 = (bf16[80,640]{1,0:T(8,128)(2,1)S(1)}, bf16[80,640]{1,0:T(8,128)(2,1)}, u32[]{:S(2)}) copy-start(bf16[80,640]{1,0:T(8,128)(2,1)} %pre_ref.1) | copy-start | bytes 307204
  8.3 25.7 %copy-start.3 = (s32[12]{0:T(128)S(1)}, s32[12]{0:T(128)}, u32[]{:S(2)}) copy-start(s32[12]{0:T(128)} %param.17) | copy-start | bytes 148
  8.4 16.0 %all-to-all-start = ((bf16[8,24,640]{2,1,0:T(8,128)(2,1)}), bf16[8,24,640]{2,1,0:T(8,128)(2,1)S(1)}, u32[]{:S(2)}, u32[]{:S(2)}) async-start(bf16[8,24,640]{2,1,0:T(8,128)(2,1)} %bitcast.13), calls=%async_computation | async-start | bytes 491520 | tf_op jit(solution)/shard_map/all_to_all | solution.py:473
  15.7 18.3 %collective-permute-start = (bf16[480,320]{1,0:T(8,128)(2,1)S(1)}, bf16[480,320]{1,0:T(8,128)(2,1)S(1)}, u32[]{:S(2)}, u32[]{:S(2)}) collective-permute-start(bf16[480,320]{1,0:T(8,128)(2,1)S(1)} %pad_maximum_fusion.own_ref), channel_id=1, source_target_pairs={{0,2},{2,4},{4,6},{1,3},{3,5},{5,7},{8,10},{10,12},{12,14},{9,11},... | collective-permute-start | bytes 921608 | tf_op jit(solution)/shard_map/ppermute | solution.py:446
  19.7 14.3 %collective-permute-start.1 = (bf16[480,320]{1,0:T(8,128)(2,1)S(1)}, bf16[480,320]{1,0:T(8,128)(2,1)S(1)}, u32[]{:S(2)}, u32[]{:S(2)}) collective-permute-start(bf16[480,320]{1,0:T(8,128)(2,1)S(1)} %pad_maximum_fusion.own_ref), channel_id=1, source_target_pairs={{2,0},{4,2},{6,4},{3,1},{5,3},{7,5},{10,8},{12,10},{14,12},{11,9},... | collective-permute-start | bytes 921608 | tf_op jit(solution)/shard_map/ppermute | solution.py:447
  30.4 15.6 %all-to-all-start.1 = ((bf16[8,80,640]{2,1,0:T(8,128)(2,1)}), bf16[8,80,640]{2,1,0:T(8,128)(2,1)S(1)}, u32[]{:S(2)}, u32[]{:S(2)}) async-start(bf16[8,80,640]{2,1,0:T(8,128)(2,1)} %up_product.1), calls=%async_computation.1 | async-start | bytes 1638400 | tf_op jit(solution)/shard_map/all_to_all | solution.py:479
  46.1 2.1 %copy-start = (bf16[1920,1024]{1,0:T(8,128)(2,1)S(1)}, bf16[1920,1024]{1,0:T(8,128)(2,1)}, u32[]{:S(2)}) copy-start(bf16[1920,1024]{1,0:T(8,128)(2,1)} %get-tuple-element.19.held_ref) | copy-start | bytes 11796484
  46.5 5.3 %collective-permute-start.2 = (bf16[160,320]{1,0:T(8,128)(2,1)S(1)}, bf16[160,320]{1,0:T(8,128)(2,1)S(1)}, u32[]{:S(2)}, u32[]{:S(2)}) collective-permute-start(bf16[160,320]{1,0:T(8,128)(2,1)S(1)} %gather_sum.1.grad_ref), channel_id=1, source_target_pairs={{0,2},{4,6},{2,0},{6,4},{1,3},{5,7},{3,1},{7,5},{8,10},{12,14},{10... | collective-permute-start | bytes 307208 | tf_op jit(solution)/shard_map/ppermute | solution.py:456
  47.5 4.4 %collective-permute-start.3 = (bf16[160,320]{1,0:T(8,128)(2,1)S(1)}, bf16[160,320]{1,0:T(8,128)(2,1)S(1)}, u32[]{:S(2)}, u32[]{:S(2)}) collective-permute-start(bf16[160,320]{1,0:T(8,128)(2,1)S(1)} %gather_sum.1.grad_ref), channel_id=1, source_target_pairs={{2,4},{4,2},{3,5},{5,3},{10,12},{12,10},{11,13},{13,11},{18,20},{2... | collective-permute-start | bytes 307208 | tf_op jit(solution)/shard_map/ppermute | solution.py:456

commit v5 on v4

--- a/solution.py
+++ b/solution.py
@@ -113,7 +113,7 @@
     capacity, slots = padded_slots(row_count, groups)
     hidden = weight.shape[0] // spans
     depth = weight.shape[1]
-    edges = [depth * i // 8 for i in (0, 2, 5, 7, 8)]
+    edges = [depth * i // 8 for i in (0, 1, 3, 5, 8)]
     steps = [(i, j - i) for i, j in zip(edges, edges[1:])]
     pieces = pl.pallas_call(
         functools.partial(down_kernel, groups, spans, capacity, slots, steps),
@@ -135,16 +135,25 @@
     return pieces.reshape(groups * spans, slots, hidden)
 
 
-def up_kernel(heads, capacity, pieces_ref, pre_ref, weight_ref, out_hbm, held, out_ref, sems,
-              out_sems):
+def up_kernel(heads, capacity, pieces_ref, pre_ref, weight_ref, send_hbm, keep_hbm, held, out_ref,
+              sems, out_sems):
     row_count, hidden = pre_ref.shape
     count, slots, _ = pieces_ref.shape
     width = weight_ref.shape[0] // (4 * heads)
+    spans = lax.axis_size("span")
+    core = lax.axis_index("core")
+    half = heads // 2
+
+    def head_of(n):
+        chip, span = (n % half) // spans, n % spans
+        return (chip * 2 + (1 - core if n < half else core)) * spans + span
+
     copies = []
     for h in range(heads):
         for j in range(4):
+            start = pl.multiple_of((j * heads + head_of(h)) * width, width)
             copy = pltpu.make_async_copy(
-                weight_ref.at[pl.ds((j * heads + h) * width, width)],
+                weight_ref.at[pl.ds(start, width)],
                 held.at[h, pl.ds(j * width, width)],
                 sems.at[h * 4 + j],
             )
@@ -178,8 +187,11 @@
         for i in range(2):
             part = products[i * width : (i + 1) * width]
             out_ref[h + i] = part.T.astype(jnp.bfloat16)
-        at = pl.ds(h, 2)
-        outgoing.append(pltpu.make_async_copy(out_ref.at[at], out_hbm.at[at], out_sems.at[h // 2]))
+        out_hbm = send_hbm if h < half else keep_hbm
+        copy = pltpu.make_async_copy(
+            out_ref.at[pl.ds(h, 2)], out_hbm.at[pl.ds(h % half, 2)], out_sems.at[h // 2]
+        )
+        outgoing.append(copy)
         outgoing[-1].start()
 
     waiting = None
@@ -199,9 +211,9 @@
     width = weight.shape[0] // heads
     return pl.pallas_call(
         functools.partial(up_kernel, heads, capacity),
-        out_shape=jax.ShapeDtypeStruct((heads, pre.shape[0], width), jnp.bfloat16),
+        out_shape=[jax.ShapeDtypeStruct((heads // 2, pre.shape[0], width), jnp.bfloat16)] * 2,
         in_specs=in_vmem(2) + in_hbm(1),
-        out_specs=in_hbm(1)[0],
+        out_specs=in_hbm(2),
         scratch_shapes=[
             pltpu.VMEM((heads, width, weight.shape[1]), jnp.bfloat16),
             pltpu.VMEM((heads, pre.shape[0], width), jnp.bfloat16),
@@ -453,7 +465,9 @@
 
     def swapped(first):
         low = range(first, size - 1, 2)
-        return lax.ppermute(x, axis, [(i, i + 1) for i in low] + [(i + 1, i) for i in low])
+        pairs = [(i, i + 1) for i in low] + [(i + 1, i) for i in low]
+        alone = set(range(size)) - {i for i, _ in pairs}
+        return lax.ppermute(x, axis, pairs + [(i, i) for i in sorted(alone)])
 
     return swapped(0), swapped(1)
 
@@ -463,7 +477,7 @@
 ):
     groups = lax.axis_size("grp")
     spans = lax.axis_size("span")
-    heads = lax.axis_size(("sect", "span"))
+    heads = lax.axis_size(("chip", "core", "span"))
     row_count = grad_out.shape[0]
     capacity, _ = padded_slots(row_count, groups)
     pieces = down_pieces(destination, grad_out, w_down, groups, spans)
@@ -474,9 +488,12 @@
     own = jnp.concatenate([queries.T, key_states.T, value_states.T], 0)
     before, after = from_both_sides(own, "grp")
     first = lax.axis_index("grp") * row_count
+    other, shares = up_pieces(arrived, pre_act, w_up, heads, capacity)
+    other = lax.ppermute(other, "core", [(0, 1), (1, 0)])
+    shares = (other.astype(jnp.float32) + shares.astype(jnp.float32)).astype(jnp.bfloat16)
+    shares, own = lax.optimization_barrier((shares, own))
     held, held_done = softmax_parts(lengths, first, own, before, after)
-    shares = up_pieces(arrived, pre_act, w_up, heads, capacity)
-    shares = lax.all_to_all(shares, ("sect", "span"), split_axis=0, concat_axis=0, tiled=True)
+    shares = lax.all_to_all(shares, ("chip", "span"), split_axis=0, concat_axis=0, tiled=True)
     grad = gathered(shares, held_done)
     even, odd = from_pairs(grad, "grp")
     grad_query, key_part, value_part = own_terms(grad, queries.T, held)
@@ -485,13 +502,17 @@
 
 
 def solution(mesh):
-    split = P("grp", ("sect", "span"))
+    sect, grp, span = (mesh.shape[name] for name in ("sect", "grp", "span"))
+    finer = jax.sharding.Mesh(
+        mesh.devices.reshape(sect // 2, 2, grp, span), ("chip", "core", "grp", "span")
+    )
+    split = P("grp", ("chip", "core", "span"))
     placed = (
         P("grp", "span"),
         P("grp"),
-        P("sect", "span"),
+        P(("chip", "core"), "span"),
         split,
-        P(None, ("sect", "span")),
+        P(None, ("chip", "core", "span")),
         split,
         split,
         split,
@@ -499,7 +520,7 @@
     )
     return jax.shard_map(
         on_device,
-        mesh=mesh,
+        mesh=finer,
         in_specs=placed,
         out_specs=(split, split, split),
         check_vma=False,

time: 54.5 us -> 61.8 us (1.13); the launches traced: 53.6 us -> 61.5 us
  blocking collectives: 0 us -> 16.1 us
  waiting for transfers between devices: 10.1 us -> 4.31 us
  starting transfers between devices: 17.7 us -> 15.2 us
  other arithmetic: 0.04 us -> 0.9 us
  Pallas kernels: 24.9 us -> 24.2 us
    all_to_all x0 -> x1, blocking collectives: none -> 16.1 us  [on_device(): lax.all_to_all(pieces, ('grp', 'span'), split_axis=0, concat_axis=0, tile...]
    all_to_all x2 -> x1, waiting for transfers between devices: 8.76 us -> 0.01 us  [on_device(): lax.all_to_all(shares, ('chip', 'span'), split_axis=0, concat_axis=0, til...]
    all_to_all x2 -> x1, starting transfers between devices: 10.8 us -> 3.5 us  [on_device(): lax.all_to_all(shares, ('chip', 'span'), split_axis=0, concat_axis=0, til...]
    ppermute x2 -> x3, starting transfers between devices: 1.61 us -> 5.81 us  [the longest x2 5.74 us: swapped(): return lax.ppermute(x, axis, pairs + [(i, i) for i in sorted(alone)])]
    ppermute x1, waiting for transfers between devices: 0.01 us -> 2.6 us  [from_both_sides(): lax.ppermute(x, axis, [(j, i) for i, j in up])]
    ppermute x1, waiting for transfers between devices: 0.01 us -> 1.18 us  [from_both_sides(): lax.ppermute(x, axis, up)]
    pallas_call x1, Pallas kernels: 7.66 us -> 6.54 us  [down_pieces(): pl.pallas_call(functools.partial(down_kernel, groups, spans, capacity, sl...]
    convert_element_type x0 -> x1, other arithmetic: none -> 0.86 us  [on_device(): (other.astype(jnp.float32) + shares.astype(jnp.float32)).astype(jnp.bfloa...]
  transfers between devices with their start and end apart: 6 -> 6, of which waited for: 3 -> 3; matrix products, arithmetic and copies ran while one was open for 0% -> 1% of each run, Pallas kernels for 28% -> 15%
where the time goes in v5:
time: 61.8 us; the launch traced here: 61.5 us
  Pallas kernels  24.2 us (39%)
  blocking collectives  16.1 us (26%)
  starting transfers between devices  15.2 us (25%)
  waiting for transfers between devices  4.31 us (7%)
  other arithmetic  0.9 us (1%)
  between operations  0.8 us (1%)
    all_to_all x1, blocking collectives, on_device(): lax.all_to_all(pieces, ('grp', 'span'), split_axis=0, concat_axis=0, tile...  16.1 us
    pallas_call x1, Pallas kernels, softmax_parts(): pl.pallas_call(softmax_kernel, out_shape=(jax.ShapeDtypeStruct((rows.tota...  6.66 us
    pallas_call x1, Pallas kernels, down_pieces(): pl.pallas_call(functools.partial(down_kernel, groups, spans, capacity, sl...  6.54 us
    pallas_call x1, Pallas kernels, up_pieces(): pl.pallas_call(functools.partial(up_kernel, heads, capacity), out_shape=[...  6.51 us
    ppermute x2, starting transfers between devices, swapped(): return lax.ppermute(x, axis, pairs + [(i, i) for i in sorted(alone)])  5.74 us
    ppermute x1, starting transfers between devices, from_both_sides(): lax.ppermute(x, axis, up)  4.57 us
    all_to_all x1, starting transfers between devices, on_device(): lax.all_to_all(shares, ('chip', 'span'), split_axis=0, concat_axis=0, til...  3.5 us
    ppermute x1, waiting for transfers between devices, from_both_sides(): lax.ppermute(x, axis, [(j, i) for i, j in up])  2.6 us
  transfers between devices with their start and end apart: 6, of which 3 were waited for; matrix products, arithmetic and copies ran while one was open for 1% of the time, Pallas kernels for 15%

profile of v5, /device:TPU:0, one launch (start us, length us, event | category | flops | bytes accessed | tf_op | source)
XLA Modules:
  0.0 61.5 jit_solution(15910177192246879279)
XLA Ops:
  0.6 0.0 copy-start.2
  0.6 6.5 %down_product.1 = bf16[4,2,24,640]{3,2,1,0:T(8,128)(2,1)} custom-call(s32[1,80]{1,0:T(1,128)} %bitcast.16, bf16[80,4096]{1,0:T(8,128)(2,1)} %rows_hbm.1, bf16[1280,4096]{1,0:T(8,128)(2,1)} %weight_ref.2), custom_call_target="tpu_custom_call" | custom-call | tf_op jit(solution)/shard_map/down_product/pallas_call | solution.py:118
  7.2 0.0 copy-start.1
  7.2 0.0 copy-start.4
  7.2 0.0 copy-start.5
  7.2 0.0 copy-start.3
  7.2 16.1 %all_to_all.10.pieces_ref = bf16[8,24,640]{2,1,0:T(8,128)(2,1)S(1)} all-to-all(bf16[8,24,640]{2,1,0:T(8,128)(2,1)} %bitcast.13), channel_id=1, replica_groups=mesh['chip'=2,'core'=2,'grp'=4,'span'=2] {'grp','span'}, dimensions={0} | all-to-all | bytes 491520 | tf_op jit(solution)/shard_map/all_to_all | solution.py:487
  23.3 0.0 copy-done.2
  23.3 6.5 %up_product.1 = (bf16[4,80,640]{2,1,0:T(8,128)(2,1)S(1)}, bf16[4,80,640]{2,1,0:T(8,128)(2,1)S(1)}) custom-call(bf16[8,24,640]{2,1,0:T(8,128)(2,1)S(1)} %all_to_all.10.pieces_ref, bf16[80,640]{1,0:T(8,128)(2,1)S(1)} %copy-done.2, bf16[5120,640]{1,0:T(8,128)(2,1)} %weight_ref.3), custom_call_target="tpu_custom_call" | custom-call | flops 2097152000 | bytes 26214400 | tf_op jit(solution)/shard_map/up_product/pallas_call | solution.py:212
  29.8 0.1 collective-permute-start
  29.9 0.0 copy-done.1
  29.9 0.0 copy-done.4
  29.9 0.0 copy-done.5
  30.0 1.3 %collective-permute-start.2 = (bf16[480,320]{1,0:T(8,128)(2,1)S(1)}, bf16[480,320]{1,0:T(8,128)(2,1)S(1)}, u32[]{:S(2)}, u32[]{:S(2)}) collective-permute-start(bf16[480,320]{1,0:T(8,128)(2,1)S(1)} %pad_maximum_fusion.own_ref), channel_id=1, source_target_pairs={{2,0},{4,2},{6,4},{3,1},{5,3},{7,5},{10,8},{12,10},{14,12},{11,9},... | collective-permute-start | bytes 921608 | tf_op jit(solution)/shard_map/ppermute | solution.py:459
  31.3 4.6 %collective-permute-start.1 = (bf16[480,320]{1,0:T(8,128)(2,1)S(1)}, bf16[480,320]{1,0:T(8,128)(2,1)S(1)}, u32[]{:S(2)}, u32[]{:S(2)}) collective-permute-start(bf16[480,320]{1,0:T(8,128)(2,1)S(1)} %pad_maximum_fusion.own_ref), channel_id=1, source_target_pairs={{0,2},{2,4},{4,6},{1,3},{3,5},{5,7},{8,10},{10,12},{12,14},{9,11},... | collective-permute-start | bytes 921608 | tf_op jit(solution)/shard_map/ppermute | solution.py:458
  35.9 0.0 collective-permute-done
  35.9 0.9 %add_convert_fusion = bf16[4,80,640]{2,1,0:T(8,128)(2,1)} fusion(bf16[4,80,640]{2,1,0:T(8,128)(2,1)S(1)} %get-tuple-element.20, bf16[4,80,640]{2,1,0:T(8,128)(2,1)S(1)} %collective-permute-done), kind=kLoop, calls=%fused_computation | loop fusion | flops 819200 | bytes 1228800 | tf_op jit(solution)/shard_map/convert_element_type | solution.py:493
  36.8 3.5 %all-to-all-start.1 = ((bf16[4,80,640]{2,1,0:T(8,128)(2,1)}), bf16[4,80,640]{2,1,0:T(8,128)(2,1)S(1)}, u32[]{:S(2)}, u32[]{:S(2)}) async-start(bf16[4,80,640]{2,1,0:T(8,128)(2,1)} %add_convert_fusion), calls=%async_computation.1 | async-start | bytes 819200 | tf_op jit(solution)/shard_map/all_to_all | solution.py:496
  40.3 2.6 %collective-permute-done.2.after_ref = bf16[480,320]{1,0:T(8,128)(2,1)S(1)} collective-permute-done((bf16[480,320]{1,0:T(8,128)(2,1)S(1)}, bf16[480,320]{1,0:T(8,128)(2,1)S(1)}, u32[]{:S(2)}, u32[]{:S(2)}) %collective-permute-start.2) | collective-permute-done | bytes 307232 | tf_op jit(solution)/shard_map/ppermute | solution.py:459
  42.9 1.2 %collective-permute-done.1.before_ref = bf16[480,320]{1,0:T(8,128)(2,1)S(1)} collective-permute-done((bf16[480,320]{1,0:T(8,128)(2,1)S(1)}, bf16[480,320]{1,0:T(8,128)(2,1)S(1)}, u32[]{:S(2)}, u32[]{:S(2)}) %collective-permute-start.1) | collective-permute-done | bytes 307232 | tf_op jit(solution)/shard_map/ppermute | solution.py:458
  44.0 0.0 copy-done.3
  44.1 6.7 %softmax_parts.1 = (bf16[1920,1024]{1,0:T(8,128)(2,1)}, f32[8,128]{1,0:T(8,128)S(1)}) custom-call(s32[1,12]{1,0:T(1,128)S(1)} %bitcast.12, s32[1,1]{1,0:T(1,128)} %bitcast.6.first_ref, bf16[480,320]{1,0:T(8,128)(2,1)S(1)} %pad_maximum_fusion.own_ref, bf16[480,320]{1,0:T(8,128)(2,1)S(1)} %collective-permute-done.1.before_ref, ...), custom_call_target="tpu_custom_call" | custom-call | flops 20480000000 | bytes 102400000 | tf_op jit(solution)/shard_map/softmax_parts/pallas_call | solution.py:337
  50.7 0.0 all-to-all-done.1.pieces_ref
  50.7 0.0 copy-start
  50.7 0.5 gather_sum.1.grad_ref
  51.2 1.0 %collective-permute-start.4 = (bf16[160,320]{1,0:T(8,128)(2,1)S(1)}, bf16[160,320]{1,0:T(8,128)(2,1)S(1)}, u32[]{:S(2)}, u32[]{:S(2)}) collective-permute-start(bf16[160,320]{1,0:T(8,128)(2,1)S(1)} %gather_sum.1.grad_ref), channel_id=1, source_target_pairs={{2,4},{4,2},{0,0},{6,6},{3,5},{5,3},{1,1},{7,7},{10,12},{12,10},{8... | collective-permute-start | bytes 307208 | tf_op jit(solution)/shard_map/ppermute | solution.py:470
  52.2 4.8 %collective-permute-start.3 = (bf16[160,320]{1,0:T(8,128)(2,1)S(1)}, bf16[160,320]{1,0:T(8,128)(2,1)S(1)}, u32[]{:S(2)}, u32[]{:S(2)}) collective-permute-start(bf16[160,320]{1,0:T(8,128)(2,1)S(1)} %gather_sum.1.grad_ref), channel_id=1, source_target_pairs={{0,2},{4,6},{2,0},{6,4},{1,3},{5,7},{3,1},{7,5},{8,10},{12,14},{10... | collective-permute-start | bytes 307208 | tf_op jit(solution)/shard_map/ppermute | solution.py:470
  57.0 0.0 copy-done
  57.0 2.3 %own_terms.1 = (bf16[160,320]{1,0:T(8,128)(2,1)}, f32[160,320]{1,0:T(8,128)S(1)}, f32[160,320]{1,0:T(8,128)S(1)}) custom-call(bf16[160,320]{1,0:T(8,128)(2,1)S(1)} %gather_sum.1.grad_ref, bf16[160,320]{1,0:T(8,128)(2,1)S(1)} %bitcast.11, bf16[1920,1024]{1,0:T(8,128)(2,1)S(1)} %copy-done), custom_call_target="tpu_custom_call" | custom-call | tf_op jit(solution)/shard_map/own_terms/pallas_call | solution.py:406
  59.3 0.0 collective-permute-done.4.odd_ref
  59.3 0.5 collective-permute-done.3.even_ref
  59.8 1.7 %side_terms.1 = (bf16[160,320]{1,0:T(8,128)(2,1)}, bf16[160,320]{1,0:T(8,128)(2,1)}) custom-call(bf16[160,320]{1,0:T(8,128)(2,1)S(1)} %collective-permute-done.3.even_ref, bf16[160,320]{1,0:T(8,128)(2,1)S(1)} %collective-permute-done.4.odd_ref, f32[160,320]{1,0:T(8,128)S(1)} %get-tuple-element.29.key_part_ref, ...), custom_call_target="tpu_custom_call" | custom-call | tf_op jit(solution)/shard_map/side_terms/pallas_call | solution.py:444
  (1 shorter events, 0.0 us)
Async XLA Ops:
  0.6 22.7 %copy-start.2 = (bf16[80,640]{1,0:T(8,128)(2,1)S(1)}, bf16[80,640]{1,0:T(8,128)(2,1)}, u32[]{:S(2)}) copy-start(bf16[80,640]{1,0:T(8,128)(2,1)} %pre_ref.1) | copy-start | bytes 307204
  7.2 22.7 %copy-start.1 = (bf16[320,160]{0,1:T(8,128)(2,1)S(1)}, bf16[320,160]{0,1:T(8,128)(2,1)}, u32[]{:S(2)}) copy-start(bf16[320,160]{0,1:T(8,128)(2,1)} %param.14) | copy-start | bytes 307204
  7.2 22.7 %copy-start.4 = (bf16[320,160]{0,1:T(8,128)(2,1)S(1)}, bf16[320,160]{0,1:T(8,128)(2,1)}, u32[]{:S(2)}) copy-start(bf16[320,160]{0,1:T(8,128)(2,1)} %param.16) | copy-start | bytes 307204
  7.2 22.7 %copy-start.5 = (bf16[320,160]{0,1:T(8,128)(2,1)S(1)}, bf16[320,160]{0,1:T(8,128)(2,1)}, u32[]{:S(2)}) copy-start(bf16[320,160]{0,1:T(8,128)(2,1)} %param.15) | copy-start | bytes 307204
  7.2 36.8 %copy-start.3 = (s32[12]{0:T(128)S(1)}, s32[12]{0:T(128)}, u32[]{:S(2)}) copy-start(s32[12]{0:T(128)} %param.17) | copy-start | bytes 148
  29.8 6.0 %collective-permute-start = (bf16[4,80,640]{2,1,0:T(8,128)(2,1)S(1)}, bf16[4,80,640]{2,1,0:T(8,128)(2,1)S(1)}, u32[]{:S(2)}, u32[]{:S(2)}) collective-permute-start(bf16[4,80,640]{2,1,0:T(8,128)(2,1)S(1)} %get-tuple-element.19), channel_id=1, source_target_pairs={{0,8},{8,0},{1,9},{9,1},{2,10},{10,2},{3,11},{11,3},{4,12},{12,4},... | collective-permute-start | bytes 1228808 | tf_op jit(solution)/shard_map/ppermute | solution.py:492
  30.0 12.9 %collective-permute-start.2 = (bf16[480,320]{1,0:T(8,128)(2,1)S(1)}, bf16[480,320]{1,0:T(8,128)(2,1)S(1)}, u32[]{:S(2)}, u32[]{:S(2)}) collective-permute-start(bf16[480,320]{1,0:T(8,128)(2,1)S(1)} %pad_maximum_fusion.own_ref), channel_id=1, source_target_pairs={{2,0},{4,2},{6,4},{3,1},{5,3},{7,5},{10,8},{12,10},{14,12},{11,9},... | collective-permute-start | bytes 921608 | tf_op jit(solution)/shard_map/ppermute | solution.py:459
  31.3 12.7 %collective-permute-start.1 = (bf16[480,320]{1,0:T(8,128)(2,1)S(1)}, bf16[480,320]{1,0:T(8,128)(2,1)S(1)}, u32[]{:S(2)}, u32[]{:S(2)}) collective-permute-start(bf16[480,320]{1,0:T(8,128)(2,1)S(1)} %pad_maximum_fusion.own_ref), channel_id=1, source_target_pairs={{0,2},{2,4},{4,6},{1,3},{3,5},{5,7},{8,10},{10,12},{12,14},{9,11},... | collective-permute-start | bytes 921608 | tf_op jit(solution)/shard_map/ppermute | solution.py:458
  36.8 14.0 %all-to-all-start.1 = ((bf16[4,80,640]{2,1,0:T(8,128)(2,1)}), bf16[4,80,640]{2,1,0:T(8,128)(2,1)S(1)}, u32[]{:S(2)}, u32[]{:S(2)}) async-start(bf16[4,80,640]{2,1,0:T(8,128)(2,1)} %add_convert_fusion), calls=%async_computation.1 | async-start | bytes 819200 | tf_op jit(solution)/shard_map/all_to_all | solution.py:496
  50.7 6.2 %copy-start = (bf16[1920,1024]{1,0:T(8,128)(2,1)S(1)}, bf16[1920,1024]{1,0:T(8,128)(2,1)}, u32[]{:S(2)}) copy-start(bf16[1920,1024]{1,0:T(8,128)(2,1)} %get-tuple-element.27.held_ref) | copy-start | bytes 11796484
  51.2 8.1 %collective-permute-start.4 = (bf16[160,320]{1,0:T(8,128)(2,1)S(1)}, bf16[160,320]{1,0:T(8,128)(2,1)S(1)}, u32[]{:S(2)}, u32[]{:S(2)}) collective-permute-start(bf16[160,320]{1,0:T(8,128)(2,1)S(1)} %gather_sum.1.grad_ref), channel_id=1, source_target_pairs={{2,4},{4,2},{0,0},{6,6},{3,5},{5,3},{1,1},{7,7},{10,12},{12,10},{8... | collective-permute-start | bytes 307208 | tf_op jit(solution)/shard_map/ppermute | solution.py:470
  52.2 7.6 %collective-permute-start.3 = (bf16[160,320]{1,0:T(8,128)(2,1)S(1)}, bf16[160,320]{1,0:T(8,128)(2,1)S(1)}, u32[]{:S(2)}, u32[]{:S(2)}) collective-permute-start(bf16[160,320]{1,0:T(8,128)(2,1)S(1)} %gather_sum.1.grad_ref), channel_id=1, source_target_pairs={{0,2},{4,6},{2,0},{6,4},{1,3},{5,7},{3,1},{7,5},{8,10},{12,14},{10... | collective-permute-start | bytes 307208 | tf_op jit(solution)/shard_map/ppermute | solution.py:470

commit v6 on v5

--- a/solution.py
+++ b/solution.py
@@ -144,8 +144,11 @@
     core = lax.axis_index("core")
     half = heads // 2
 
+    me = lax.axis_index("chip") * spans + lax.axis_index("span")
+
     def head_of(n):
-        chip, span = (n % half) // spans, n % spans
+        place = lax.bitwise_xor(me, n % half)
+        chip, span = lax.div(place, spans), lax.rem(place, spans)
         return (chip * 2 + (1 - core if n < half else core)) * spans + span
 
     copies = []
@@ -252,12 +255,12 @@
         return slice(self.side_at + h * self.patches, self.side_at + (h + 1) * self.patches)
 
 
-def softmax_kernel(lengths_ref, first_ref, own_ref, before_ref, after_ref, out_hbm, done_ref, held,
+def softmax_kernel(lengths_ref, first_ref, own_ref, even_ref, odd_ref, out_hbm, done_ref, held,
                    sems):
     columns, patches = own_ref.shape[0] // 3, own_ref.shape[1]
     heads = columns // HEAD_DIM
     rows = Rows(columns, patches)
-    blocks = (own_ref, before_ref, after_ref)
+    is_even = lax.rem(lax.axis_index("grp"), 2) == 0
     first = first_ref[0, 0]
 
     def image_of(shape, dim, block):
@@ -285,7 +288,11 @@
 
     def kind(block, t, h=None):
         start = t * columns + (0 if h is None else h * HEAD_DIM)
-        return blocks[block][start : start + (columns if h is None else HEAD_DIM)]
+        at = slice(start, start + (columns if h is None else HEAD_DIM))
+        if block == 0:
+            return own_ref[at]
+        before, after = (odd_ref, even_ref) if block == 1 else (even_ref, odd_ref)
+        return jnp.where(is_even, before[at], after[at])
 
     def wide(t, which):
         return jnp.concatenate([kind(b, t).astype(jnp.float32) for b in which], 1).astype(jnp.bfloat16)
@@ -328,7 +335,7 @@
     done_ref[...] = jnp.zeros(done_ref.shape, jnp.float32)
 
 
-def softmax_parts(lengths, first, own, before, after):
+def softmax_parts(lengths, first, own, even, odd):
     columns, patches = own.shape[0] // 3, own.shape[1]
     heads = columns // HEAD_DIM
     rows = Rows(columns, patches)
@@ -351,14 +358,15 @@
             flops=100_000 * work, bytes_accessed=500 * work, transcendentals=9 * work
         ),
         name="softmax_parts",
-    )(lengths.reshape(1, -1), first.reshape(1, 1), own, before, after)
-
-
-def gather_kernel(pieces_ref, _, out_ref):
-    count, row_count, width = pieces_ref.shape
-    total = pieces_ref[0].astype(jnp.float32)
+    )(lengths.reshape(1, -1), first.reshape(1, 1), own, even, odd)
+
+
+def gather_kernel(count, *refs):
+    _, row_count, width = refs[0].shape
+    total = refs[0][0].astype(jnp.float32)
     for p in range(1, count):
-        total = total + pieces_ref[p].astype(jnp.float32)
+        total = total + refs[p][0].astype(jnp.float32)
+    out_ref = refs[-1]
     total = total.astype(jnp.bfloat16)
     columns = width // 4
     patch = iota((row_count, 4 * row_count), 1)
@@ -371,18 +379,19 @@
 
 
 def gathered(pieces, later):
-    _, row_count, width = pieces.shape
+    _, row_count, width = pieces[0].shape
+    size = len(pieces) * row_count * width
     return pl.pallas_call(
-        gather_kernel,
+        functools.partial(gather_kernel, len(pieces)),
         out_shape=jax.ShapeDtypeStruct((width // 4, 4 * row_count), jnp.bfloat16),
-        in_specs=in_vmem(2),
+        in_specs=in_vmem(len(pieces) + 1),
         out_specs=pl.BlockSpec(memory_space=VMEM),
         compiler_params=params(16),
         cost_estimate=pl.CostEstimate(
-            flops=20_000 * pieces.size, bytes_accessed=400 * pieces.size, transcendentals=0
+            flops=20_000 * size, bytes_accessed=400 * size, transcendentals=0
         ),
         name="gather_sum",
-    )(pieces, later)
+    )(*pieces, later)
 
 
 def own_kernel(grad_ref, own_ref, held_ref, query_ref, key_ref, value_ref):
@@ -451,25 +460,27 @@
     )(even, odd, key_part, value_part, held)
 
 
-def from_both_sides(x, axis):
-    size = lax.axis_size(axis)
-    up = [(i, i + 1) for i in range(size - 1)]
-    return (
-        lax.ppermute(x, axis, up),
-        lax.ppermute(x, axis, [(j, i) for i, j in up]),
-    )
-
-
-def from_pairs(x, axis):
-    size = lax.axis_size(axis)
+def from_pairs(x):
+    size = lax.axis_size("grp")
 
     def swapped(first):
-        low = range(first, size - 1, 2)
-        pairs = [(i, i + 1) for i in low] + [(i + 1, i) for i in low]
-        alone = set(range(size)) - {i for i, _ in pairs}
-        return lax.ppermute(x, axis, pairs + [(i, i) for i in sorted(alone)])
+        partner = {}
+        for core in range(2):
+            for i in range(size):
+                j = i + 1 if (i - first) % 2 == 0 else i - 1
+                pair = (core, j) if 0 <= j < size else (1 - core, i)
+                partner[core * size + i] = pair[0] * size + pair[1]
+        return lax.ppermute(x, ("core", "grp"), sorted(partner.items()))
 
     return swapped(0), swapped(1)
+
+
+def exchanged(pieces, axes):
+    count = pieces.shape[0]
+    parts = [pieces[d : d + 1] for d in range(count)]
+    return parts[:1] + [
+        lax.ppermute(parts[d], axes, [(i, i ^ d) for i in range(count)]) for d in range(1, count)
+    ]
 
 
 def on_device(
@@ -486,16 +497,16 @@
     )
     arrived = lax.all_to_all(pieces, ("grp", "span"), split_axis=0, concat_axis=0, tiled=True)
     own = jnp.concatenate([queries.T, key_states.T, value_states.T], 0)
-    before, after = from_both_sides(own, "grp")
+    sides = from_pairs(own)
     first = lax.axis_index("grp") * row_count
     other, shares = up_pieces(arrived, pre_act, w_up, heads, capacity)
+    other, *sides = lax.optimization_barrier((other, *sides))
     other = lax.ppermute(other, "core", [(0, 1), (1, 0)])
     shares = (other.astype(jnp.float32) + shares.astype(jnp.float32)).astype(jnp.bfloat16)
     shares, own = lax.optimization_barrier((shares, own))
-    held, held_done = softmax_parts(lengths, first, own, before, after)
-    shares = lax.all_to_all(shares, ("chip", "span"), split_axis=0, concat_axis=0, tiled=True)
-    grad = gathered(shares, held_done)
-    even, odd = from_pairs(grad, "grp")
+    held, held_done = softmax_parts(lengths, first, own, *sides)
+    grad = gathered(exchanged(shares, ("chip", "span")), held_done)
+    even, odd = from_pairs(grad)
     grad_query, key_part, value_part = own_terms(grad, queries.T, held)
     grad_key, grad_value = side_terms(even, odd, key_part, value_part, held)
     return grad_query.T, grad_key.T, grad_value.T

time: 61.8 us -> 51.6 us (0.83)
  blocking collectives: 16.1 us -> 0 us
  waiting for transfers between devices: 4.31 us -> 9.86 us
  local copies, waits for them, and re-layouts: 0.03 us -> 0.86 us
  other arithmetic: 0.9 us -> 0.15 us
    all_to_all x1 -> x0, blocking collectives: 16.1 us -> none  [on_device(): lax.all_to_all(pieces, ('grp', 'span'), split_axis=0, concat_axis=0, tile...]
    all_to_all x1, waiting for transfers between devices: 0.01 us -> 6.28 us  [on_device(): lax.all_to_all(pieces, ('grp', 'span'), split_axis=0, concat_axis=0, tile...]
    all_to_all x1, starting transfers between devices: 3.5 us -> 7.29 us  [on_device(): lax.all_to_all(pieces, ('grp', 'span'), split_axis=0, concat_axis=0, tile...]
    ppermute x4 -> x7, starting transfers between devices: 11.6 us -> 7.91 us  [the longest x4 4.35 us: swapped(): return lax.ppermute(x, ('core', 'grp'), sorted(partner.items()))]
    ppermute x4 -> x7, waiting for transfers between devices: 4.3 us -> 1.85 us  [the longest x4 1.85 us: swapped(): return lax.ppermute(x, ('core', 'grp'), sorted(partner.items()))]
    ppermute x1, waiting for transfers between devices: 0.01 us -> 1.73 us  [on_device(): other = lax.ppermute(other, 'core', [(0, 1), (1, 0)])]
    unnamed x12, local copies, waits for them, and re-layouts: 0.03 us -> 0.82 us
    convert_element_type x1, other arithmetic: 0.86 us -> 0.1 us  [on_device(): (other.astype(jnp.float32) + shares.astype(jnp.float32)).astype(jnp.bfloa...]
  transfers between devices with their start and end apart: 6 -> 9, of which waited for: 3 -> 3; matrix products, arithmetic and copies ran while one was open for 1% -> 0% of each run, Pallas kernels for 15% -> 31%
where the time goes in v6:
time: 51.6 us; the launch traced here: 51.3 us
  Pallas kernels  24.4 us (47%)
  starting transfers between devices  15.3 us (30%)
  waiting for transfers between devices  9.86 us (19%)
  local copies, waits for them, and re-layouts  0.86 us (2%)
  between operations  0.82 us (2%)
    all_to_all x1, starting transfers between devices, on_device(): lax.all_to_all(pieces, ('grp', 'span'), split_axis=0, concat_axis=0, tile...  7.29 us
    pallas_call x1, Pallas kernels, softmax_parts(): pl.pallas_call(softmax_kernel, out_shape=(jax.ShapeDtypeStruct((rows.tota...  6.79 us
    pallas_call x1, Pallas kernels, down_pieces(): pl.pallas_call(functools.partial(down_kernel, groups, spans, capacity, sl...  6.55 us
    pallas_call x1, Pallas kernels, up_pieces(): pl.pallas_call(functools.partial(up_kernel, heads, capacity), out_shape=[...  6.52 us
    all_to_all x1, waiting for transfers between devices, on_device(): lax.all_to_all(pieces, ('grp', 'span'), split_axis=0, concat_axis=0, tile...  6.28 us
    ppermute x4, starting transfers between devices, swapped(): return lax.ppermute(x, ('core', 'grp'), sorted(partner.items()))  4.35 us
    ppermute x3, starting transfers between devices, exchanged(): lax.ppermute(parts[d], axes, [(i, i ^ d) for i in range(count)])  3.55 us
    pallas_call x1, Pallas kernels, own_terms(): pl.pallas_call(own_kernel, out_shape=(jax.ShapeDtypeStruct(grad.shape, jn...  2.35 us
  transfers between devices with their start and end apart: 9, of which 3 were waited for; matrix products, arithmetic and copies ran while one was open for 0% of the time, Pallas kernels for 31%

profile of v6, /device:TPU:0, one launch (start us, length us, event | category | flops | bytes accessed | tf_op | source)
XLA Modules:
  0.0 51.3 jit_solution(12630748235724959895)
XLA Ops:
  0.6 0.0 copy-start.4
  0.6 0.0 copy-start.5
  0.7 0.0 copy-start.1
  0.7 0.0 copy-start.2
  0.7 6.5 %down_product.1 = bf16[4,2,24,640]{3,2,1,0:T(8,128)(2,1)} custom-call(s32[1,80]{1,0:T(1,128)} %bitcast.16, bf16[80,4096]{1,0:T(8,128)(2,1)} %rows_hbm.1, bf16[1280,4096]{1,0:T(8,128)(2,1)} %weight_ref.2), custom_call_target="tpu_custom_call" | custom-call | tf_op jit(solution)/shard_map/down_product/pallas_call | solution.py:118
  7.2 0.0 copy-start.3
  7.2 7.3 %all-to-all-start = ((bf16[8,24,640]{2,1,0:T(8,128)(2,1)}), bf16[8,24,640]{2,1,0:T(8,128)(2,1)S(1)}, u32[]{:S(2)}, u32[]{:S(2)}) async-start(bf16[8,24,640]{2,1,0:T(8,128)(2,1)} %bitcast.13), calls=%async_computation | async-start | bytes 491520 | tf_op jit(solution)/shard_map/all_to_all | solution.py:498
  14.5 0.0 copy-done.4
  14.6 0.1 collective-permute-start.1
  14.7 3.5 %collective-permute-start = (bf16[480,320]{1,0:T(8,128)(2,1)S(1)}, bf16[480,320]{1,0:T(8,128)(2,1)S(1)}, u32[]{:S(2)}, u32[]{:S(2)}) collective-permute-start(bf16[480,320]{1,0:T(8,128)(2,1)S(1)} %pad_maximum_fusion.own_ref), channel_id=1, source_target_pairs={{0,2},{2,0},{4,6},{6,4},{8,10},{10,8},{12,14},{14,12},{1,3},{3,1},... | collective-permute-start | bytes 921608 | tf_op jit(solution)/shard_map/ppermute | solution.py:473
  18.2 6.3 %all-to-all-done.pieces_ref = bf16[8,24,640]{2,1,0:T(8,128)(2,1)S(1)} async-done(((bf16[8,24,640]{2,1,0:T(8,128)(2,1)}), bf16[8,24,640]{2,1,0:T(8,128)(2,1)S(1)}, u32[]{:S(2)}, u32[]{:S(2)}) %all-to-all-start) | async-done | bytes 245792 | tf_op jit(solution)/shard_map/all_to_all | solution.py:498
  24.4 6.5 %up_product.1 = (bf16[4,80,640]{2,1,0:T(8,128)(2,1)S(1)}, bf16[4,80,640]{2,1,0:T(8,128)(2,1)S(1)}) custom-call(bf16[8,24,640]{2,1,0:T(8,128)(2,1)S(1)} %all-to-all-done.pieces_ref, bf16[80,640]{1,0:T(8,128)(2,1)S(1)} %copy-done.2, bf16[5120,640]{1,0:T(8,128)(2,1)} %weight_ref.3), custom_call_target="tpu_custom_call" | custom-call | flops 2097152000 | bytes 26214400 | tf_op jit(solution)/shard_map/up_product/pallas_call | solution.py:215
  31.0 0.0 collective-permute-done.1.odd_ref
  31.0 0.0 collective-permute-done.even_ref
  31.0 0.1 collective-permute-start.2
  31.1 1.7 %collective-permute-done.2 = bf16[4,80,640]{2,1,0:T(8,128)(2,1)S(1)} collective-permute-done((bf16[4,80,640]{2,1,0:T(8,128)(2,1)S(1)}, bf16[4,80,640]{2,1,0:T(8,128)(2,1)S(1)}, u32[]{:S(2)}, u32[]{:S(2)}) %collective-permute-start.2) | collective-permute-done | bytes 409632 | tf_op jit(solution)/shard_map/ppermute | solution.py:504
  32.8 0.1 add_convert_fusion
  32.9 2.2 %collective-permute-start.5 = (bf16[1,80,640]{2,1,0:T(8,128)(2,1)S(1)}, bf16[1,80,640]{2,1,0:T(8,128)(2,1)S(1)}, u32[]{:S(2)}, u32[]{:S(2)}) collective-permute-start(bf16[1,80,640]{2,1,0:T(8,128)(2,1)S(1)} %get-tuple-element.39), channel_id=1, source_target_pairs={{0,17},{1,16},{16,1},{17,0},{2,19},{3,18},{18,3},{19,2},{4,21},{5,... | collective-permute-start | bytes 307208 | tf_op jit(solution)/shard_map/ppermute | solution.py:482
  35.2 0.5 %collective-permute-start.4 = (bf16[1,80,640]{2,1,0:T(8,128)(2,1)S(1)}, bf16[1,80,640]{2,1,0:T(8,128)(2,1)S(1)}, u32[]{:S(2)}, u32[]{:S(2)}) collective-permute-start(bf16[1,80,640]{2,1,0:T(8,128)(2,1)S(1)} %get-tuple-element.40), channel_id=1, source_target_pairs={{0,16},{1,17},{16,0},{17,1},{2,18},{3,19},{18,2},{19,3},{4,20},{5,... | collective-permute-start | bytes 307208 | tf_op jit(solution)/shard_map/ppermute | solution.py:482
  35.7 0.8 %collective-permute-start.3 = (bf16[1,80,640]{2,1,0:T(8,128)(2,1)S(1)}, bf16[1,80,640]{2,1,0:T(8,128)(2,1)S(1)}, u32[]{:S(2)}, u32[]{:S(2)}) collective-permute-start(bf16[1,80,640]{2,1,0:T(8,128)(2,1)S(1)} %get-tuple-element.41), channel_id=1, source_target_pairs={{0,1},{1,0},{16,17},{17,16},{2,3},{3,2},{18,19},{19,18},{4,5},{5,4... | collective-permute-start | bytes 307208 | tf_op jit(solution)/shard_map/ppermute | solution.py:482
  36.5 6.8 %softmax_parts.1 = (bf16[1920,1024]{1,0:T(8,128)(2,1)}, f32[8,128]{1,0:T(8,128)S(1)}) custom-call(s32[1,12]{1,0:T(1,128)S(1)} %bitcast.12, s32[1,1]{1,0:T(1,128)} %bitcast.6.first_ref, bf16[480,320]{1,0:T(8,128)(2,1)S(1)} %pad_maximum_fusion.own_ref, bf16[480,320]{1,0:T(8,128)(2,1)S(1)} %collective-permute-done.even_ref, ...), custom_call_target="tpu_custom_call" | custom-call | flops 20480000000 | bytes 102400000 | tf_op jit(solution)/shard_map/softmax_parts/pallas_call | solution.py:344
  43.3 0.0 collective-permute-done.5.refs_3_
  43.3 0.0 collective-permute-done.4.refs_2_
  43.3 0.0 collective-permute-done.3.refs_1_
  43.3 0.5 gather_sum.1.grad_ref
  43.8 0.1 collective-permute-start.7
  43.9 0.7 %collective-permute-start.6 = (bf16[160,320]{1,0:T(8,128)(2,1)S(1)}, bf16[160,320]{1,0:T(8,128)(2,1)S(1)}, u32[]{:S(2)}, u32[]{:S(2)}) collective-permute-start(bf16[160,320]{1,0:T(8,128)(2,1)S(1)} %gather_sum.1.grad_ref), channel_id=1, source_target_pairs={{0,2},{2,0},{4,6},{6,4},{8,10},{10,8},{12,14},{14,12},{1,3},{3,1},... | collective-permute-start | bytes 307208 | tf_op jit(solution)/shard_map/ppermute | solution.py:473
  44.7 0.8 %copy-done = bf16[1920,1024]{1,0:T(8,128)(2,1)S(1)} copy-done((bf16[1920,1024]{1,0:T(8,128)(2,1)S(1)}, bf16[1920,1024]{1,0:T(8,128)(2,1)}, u32[]{:S(2)}) %copy-start) | copy-done | bytes 3932184
  45.5 2.4 %own_terms.1 = (bf16[160,320]{1,0:T(8,128)(2,1)}, f32[160,320]{1,0:T(8,128)S(1)}, f32[160,320]{1,0:T(8,128)S(1)}) custom-call(bf16[160,320]{1,0:T(8,128)(2,1)S(1)} %gather_sum.1.grad_ref, bf16[160,320]{1,0:T(8,128)(2,1)S(1)} %bitcast.11, bf16[1920,1024]{1,0:T(8,128)(2,1)S(1)} %copy-done), custom_call_target="tpu_custom_call" | custom-call | tf_op jit(solution)/shard_map/own_terms/pallas_call | solution.py:415
  47.8 0.0 collective-permute-done.7.odd_ref
  47.8 1.8 %collective-permute-done.6.even_ref = bf16[160,320]{1,0:T(8,128)(2,1)S(1)} collective-permute-done((bf16[160,320]{1,0:T(8,128)(2,1)S(1)}, bf16[160,320]{1,0:T(8,128)(2,1)S(1)}, u32[]{:S(2)}, u32[]{:S(2)}) %collective-permute-start.6) | collective-permute-done | bytes 102432 | tf_op jit(solution)/shard_map/ppermute | solution.py:473
  49.6 1.7 %side_terms.1 = (bf16[160,320]{1,0:T(8,128)(2,1)}, bf16[160,320]{1,0:T(8,128)(2,1)}) custom-call(bf16[160,320]{1,0:T(8,128)(2,1)S(1)} %collective-permute-done.6.even_ref, bf16[160,320]{1,0:T(8,128)(2,1)S(1)} %collective-permute-done.7.odd_ref, f32[160,320]{1,0:T(8,128)S(1)} %get-tuple-element.35.key_part_ref, ...), custom_call_target="tpu_custom_call" | custom-call | tf_op jit(solution)/shard_map/side_terms/pallas_call | solution.py:453
  (7 shorter events, 0.1 us)
Async XLA Ops:
  0.6 13.9 %copy-start.4 = (bf16[320,160]{0,1:T(8,128)(2,1)S(1)}, bf16[320,160]{0,1:T(8,128)(2,1)}, u32[]{:S(2)}) copy-start(bf16[320,160]{0,1:T(8,128)(2,1)} %param.16) | copy-start | bytes 307204
  0.6 13.9 %copy-start.5 = (bf16[320,160]{0,1:T(8,128)(2,1)S(1)}, bf16[320,160]{0,1:T(8,128)(2,1)}, u32[]{:S(2)}) copy-start(bf16[320,160]{0,1:T(8,128)(2,1)} %param.15) | copy-start | bytes 307204
  0.7 13.9 %copy-start.1 = (bf16[320,160]{0,1:T(8,128)(2,1)S(1)}, bf16[320,160]{0,1:T(8,128)(2,1)}, u32[]{:S(2)}) copy-start(bf16[320,160]{0,1:T(8,128)(2,1)} %param.14) | copy-start | bytes 307204
  0.7 23.8 %copy-start.2 = (bf16[80,640]{1,0:T(8,128)(2,1)S(1)}, bf16[80,640]{1,0:T(8,128)(2,1)}, u32[]{:S(2)}) copy-start(bf16[80,640]{1,0:T(8,128)(2,1)} %pre_ref.1) | copy-start | bytes 307204
  7.2 29.3 %copy-start.3 = (s32[12]{0:T(128)S(1)}, s32[12]{0:T(128)}, u32[]{:S(2)}) copy-start(s32[12]{0:T(128)} %param.17) | copy-start | bytes 148
  7.2 17.2 %all-to-all-start = ((bf16[8,24,640]{2,1,0:T(8,128)(2,1)}), bf16[8,24,640]{2,1,0:T(8,128)(2,1)S(1)}, u32[]{:S(2)}, u32[]{:S(2)}) async-start(bf16[8,24,640]{2,1,0:T(8,128)(2,1)} %bitcast.13), calls=%async_computation | async-start | bytes 491520 | tf_op jit(solution)/shard_map/all_to_all | solution.py:498
  14.6 16.4 %collective-permute-start.1 = (bf16[480,320]{1,0:T(8,128)(2,1)S(1)}, bf16[480,320]{1,0:T(8,128)(2,1)S(1)}, u32[]{:S(2)}, u32[]{:S(2)}) collective-permute-start(bf16[480,320]{1,0:T(8,128)(2,1)S(1)} %pad_maximum_fusion.own_ref), channel_id=1, source_target_pairs={{0,8},{2,4},{4,2},{6,14},{8,0},{10,12},{12,10},{14,6},{1,9},{3,5},... | collective-permute-start | bytes 921608 | tf_op jit(solution)/shard_map/ppermute | solution.py:473
  14.7 16.3 %collective-permute-start = (bf16[480,320]{1,0:T(8,128)(2,1)S(1)}, bf16[480,320]{1,0:T(8,128)(2,1)S(1)}, u32[]{:S(2)}, u32[]{:S(2)}) collective-permute-start(bf16[480,320]{1,0:T(8,128)(2,1)S(1)} %pad_maximum_fusion.own_ref), channel_id=1, source_target_pairs={{0,2},{2,0},{4,6},{6,4},{8,10},{10,8},{12,14},{14,12},{1,3},{3,1},... | collective-permute-start | bytes 921608 | tf_op jit(solution)/shard_map/ppermute | solution.py:473
  31.0 1.8 %collective-permute-start.2 = (bf16[4,80,640]{2,1,0:T(8,128)(2,1)S(1)}, bf16[4,80,640]{2,1,0:T(8,128)(2,1)S(1)}, u32[]{:S(2)}, u32[]{:S(2)}) collective-permute-start(bf16[4,80,640]{2,1,0:T(8,128)(2,1)S(1)} %get-tuple-element.26), channel_id=1, source_target_pairs={{0,8},{8,0},{1,9},{9,1},{2,10},{10,2},{3,11},{11,3},{4,12},{12,4},... | collective-permute-start | bytes 1228808 | tf_op jit(solution)/shard_map/ppermute | solution.py:504
  32.9 10.4 %collective-permute-start.5 = (bf16[1,80,640]{2,1,0:T(8,128)(2,1)S(1)}, bf16[1,80,640]{2,1,0:T(8,128)(2,1)S(1)}, u32[]{:S(2)}, u32[]{:S(2)}) collective-permute-start(bf16[1,80,640]{2,1,0:T(8,128)(2,1)S(1)} %get-tuple-element.39), channel_id=1, source_target_pairs={{0,17},{1,16},{16,1},{17,0},{2,19},{3,18},{18,3},{19,2},{4,21},{5,... | collective-permute-start | bytes 307208 | tf_op jit(solution)/shard_map/ppermute | solution.py:482
  35.2 8.2 %collective-permute-start.4 = (bf16[1,80,640]{2,1,0:T(8,128)(2,1)S(1)}, bf16[1,80,640]{2,1,0:T(8,128)(2,1)S(1)}, u32[]{:S(2)}, u32[]{:S(2)}) collective-permute-start(bf16[1,80,640]{2,1,0:T(8,128)(2,1)S(1)} %get-tuple-element.40), channel_id=1, source_target_pairs={{0,16},{1,17},{16,0},{17,1},{2,18},{3,19},{18,2},{19,3},{4,20},{5,... | collective-permute-start | bytes 307208 | tf_op jit(solution)/shard_map/ppermute | solution.py:482
  35.7 7.6 %collective-permute-start.3 = (bf16[1,80,640]{2,1,0:T(8,128)(2,1)S(1)}, bf16[1,80,640]{2,1,0:T(8,128)(2,1)S(1)}, u32[]{:S(2)}, u32[]{:S(2)}) collective-permute-start(bf16[1,80,640]{2,1,0:T(8,128)(2,1)S(1)} %get-tuple-element.41), channel_id=1, source_target_pairs={{0,1},{1,0},{16,17},{17,16},{2,3},{3,2},{18,19},{19,18},{4,5},{5,4... | collective-permute-start | bytes 307208 | tf_op jit(solution)/shard_map/ppermute | solution.py:482
  43.3 2.1 %copy-start = (bf16[1920,1024]{1,0:T(8,128)(2,1)S(1)}, bf16[1920,1024]{1,0:T(8,128)(2,1)}, u32[]{:S(2)}) copy-start(bf16[1920,1024]{1,0:T(8,128)(2,1)} %get-tuple-element.33.held_ref) | copy-start | bytes 11796484
  43.8 4.0 %collective-permute-start.7 = (bf16[160,320]{1,0:T(8,128)(2,1)S(1)}, bf16[160,320]{1,0:T(8,128)(2,1)S(1)}, u32[]{:S(2)}, u32[]{:S(2)}) collective-permute-start(bf16[160,320]{1,0:T(8,128)(2,1)S(1)} %gather_sum.1.grad_ref), channel_id=1, source_target_pairs={{0,8},{2,4},{4,2},{6,14},{8,0},{10,12},{12,10},{14,6},{1,9},{3,5},... | collective-permute-start | bytes 307208 | tf_op jit(solution)/shard_map/ppermute | solution.py:473
  43.9 5.7 %collective-permute-start.6 = (bf16[160,320]{1,0:T(8,128)(2,1)S(1)}, bf16[160,320]{1,0:T(8,128)(2,1)S(1)}, u32[]{:S(2)}, u32[]{:S(2)}) collective-permute-start(bf16[160,320]{1,0:T(8,128)(2,1)S(1)} %gather_sum.1.grad_ref), channel_id=1, source_target_pairs={{0,2},{2,0},{4,6},{6,4},{8,10},{10,8},{12,14},{14,12},{1,3},{3,1},... | collective-permute-start | bytes 307208 | tf_op jit(solution)/shard_map/ppermute | solution.py:473

commit v7 on v6

--- a/solution.py
+++ b/solution.py
@@ -49,12 +49,14 @@
     return capacity, -(-(capacity + 1) // 8) * 8
 
 
-def one_product(count, slots, hidden):
-    return count * slots <= hidden
-
-
-def down_kernel(groups, spans, capacity, slots, steps, dest_hbm, rows_hbm, weight_ref, out_hbm,
-                dest_ref, rows_ref, held, total_ref, pieces_ref, sems, out_sems):
+def by_swaps(count, slots, hidden):
+    return count in (2, 4, 8, 16) and count * slots <= hidden
+
+
+def down_kernel(groups, spans, capacity, slots, steps, dest_hbm, rows_hbm, weight_ref, *refs):
+    *outs, dest_ref, rows_ref, held, total_ref, pieces_ref, sems, out_sems = refs
+    count = groups * spans
+    me = lax.axis_index("grp") * spans + lax.axis_index("span")
     row_count = rows_ref.shape[0]
     hidden = weight_ref.shape[0] // spans
     everything = pl.ds(0, weight_ref.shape[0])
@@ -77,34 +79,40 @@
     row_of = group_across[:1] * slots + rank_across
     places = iota((groups * slots, row_count), 0).astype(jnp.float32)
     pick = jnp.where(places == row_of, 1.0, 0.0).astype(jnp.bfloat16)
-    lane = iota((row_count, hidden), 1).astype(jnp.float32)
-    shift = 0.0
-    if one_product(groups * spans, slots, hidden):
-        device = lax.axis_index("grp") * spans + lax.axis_index("span")
-        shift = (device * slots).astype(jnp.float32)
-    at_rank = lane == rank_down + shift
+    width = hidden
+    if by_swaps(count, slots, hidden):
+        width = min(hidden, -(-count * slots // 128) * 128)
+    lane = iota((row_count, width), 1).astype(jnp.float32)
+    rank_in = [jnp.where(group_down[:, :1] == g, rank_down, -1e6) for g in range(groups)]
+
+    def labels(g, s):
+        shift = 0.0
+        if by_swaps(count, slots, hidden):
+            shift = (lax.bitwise_xor(me, g * spans + s) * slots).astype(jnp.float32)
+        hit = lane == rank_in[g] + shift
+        row = jnp.sum(jnp.where(hit, slot_down[:, :1] + 1.0, 0.0), 0, keepdims=True) - 1.0
+        if width < hidden:
+            row = jnp.concatenate([row, jnp.full((1, hidden - width), -1.0, jnp.float32)], 1)
+        return row
+
     label_row = iota((slots, hidden), 0) == capacity
-    labels = []
-    for g in range(groups):
-        hit = at_rank & (group_down[:, :1] == g)
-        labels.append(jnp.sum(jnp.where(hit, slot_down[:, :1] + 1.0, 0.0), 0, keepdims=True) - 1.0)
     copies[1].wait()
     for n, (at, step) in enumerate(steps):
         turned = rows_ref[:, at : at + step].astype(jnp.float32).T.astype(jnp.bfloat16)
         copies[2 + n].wait()
         product = dot(held[:, at : at + step], turned, NN)
         total_ref[...] = product if n == 0 else total_ref[...] + product
-    outgoing = []
     for s in range(spans):
         part = total_ref[s * hidden : (s + 1) * hidden].astype(jnp.bfloat16)
         moved = dot(pick, part, NT)
         for g in range(groups):
-            piece = jnp.where(label_row, labels[g], moved[g * slots : (g + 1) * slots])
-            pieces_ref[s, g] = piece.astype(jnp.bfloat16)
-        copy = pltpu.make_async_copy(pieces_ref.at[s], out_hbm.at[:, s], out_sems.at[s])
-        copy.start()
-        outgoing.append(copy)
-    for copy in outgoing:
+            piece = jnp.where(label_row, labels(g, s), moved[g * slots : (g + 1) * slots])
+            pieces_ref[g * spans + s] = piece.astype(jnp.bfloat16)
+    if by_swaps(count, slots, hidden):
+        pairs = [(pieces_ref.at[pl.ds(lax.bitwise_xor(me, d), 1)], outs[d]) for d in range(count)]
+    else:
+        pairs = [(pieces_ref, outs[0])]
+    for copy in fetched(pairs, out_sems):
         copy.wait()
 
 
@@ -115,30 +123,40 @@
     depth = weight.shape[1]
     edges = [depth * i // 8 for i in (0, 1, 3, 5, 8)]
     steps = [(i, j - i) for i, j in zip(edges, edges[1:])]
+    count = groups * spans
+    parts = count if by_swaps(count, slots, hidden) else 1
     pieces = pl.pallas_call(
         functools.partial(down_kernel, groups, spans, capacity, slots, steps),
-        out_shape=jax.ShapeDtypeStruct((groups, spans, slots, hidden), jnp.bfloat16),
+        out_shape=[jax.ShapeDtypeStruct((count // parts, slots, hidden), jnp.bfloat16)] * parts,
         in_specs=in_hbm(3),
-        out_specs=in_hbm(1)[0],
+        out_specs=in_hbm(parts),
         scratch_shapes=[
             pltpu.VMEM((1, row_count), jnp.int32),
             pltpu.VMEM(rows.shape, jnp.bfloat16),
             pltpu.VMEM(weight.shape, jnp.bfloat16),
             pltpu.VMEM((weight.shape[0], row_count), jnp.float32),
-            pltpu.VMEM((spans, groups, slots, hidden), jnp.bfloat16),
+            pltpu.VMEM((count, slots, hidden), jnp.bfloat16),
             pltpu.SemaphoreType.DMA((2 + len(steps),)),
-            pltpu.SemaphoreType.DMA((spans,)),
+            pltpu.SemaphoreType.DMA((parts,)),
         ],
         compiler_params=params(60),
+        cost_estimate=pl.CostEstimate(
+            flops=200 * row_count * weight.size, bytes_accessed=8 * weight.size, transcendentals=0
+        ),
         name="down_product",
     )(dest.reshape(1, row_count), rows, weight)
-    return pieces.reshape(groups * spans, slots, hidden)
-
-
-def up_kernel(heads, capacity, pieces_ref, pre_ref, weight_ref, send_hbm, keep_hbm, held, out_ref,
-              sems, out_sems):
+    if parts == 1:
+        axes = ("grp", "span")
+        return [lax.all_to_all(pieces[0], axes, split_axis=0, concat_axis=0, tiled=True)]
+    return exchanged(pieces, ("grp", "span"))
+
+
+def up_kernel(heads, capacity, *refs):
+    *pieces_refs, pre_ref, weight_ref, _, send_hbm, keep_hbm, held, out_ref, sems, out_sems = refs
+    pieces_ref = pieces_refs[0]
     row_count, hidden = pre_ref.shape
-    count, slots, _ = pieces_ref.shape
+    slots = pieces_ref.shape[1]
+    count = sum(ref.shape[0] for ref in pieces_refs)
     width = weight_ref.shape[0] // (4 * heads)
     spans = lax.axis_size("span")
     core = lax.axis_index("core")
@@ -163,8 +181,8 @@
             copy.start()
             copies.append(copy)
     label_at = slice(capacity, capacity + 1)
-    if one_product(count, slots, hidden):
-        pieces = [pieces_ref[p].astype(jnp.float32) for p in range(count)]
+    if by_swaps(count, slots, hidden):
+        pieces = [ref[p].astype(jnp.float32) for ref in pieces_refs for p in range(ref.shape[0])]
         labels = functools.reduce(jnp.maximum, [x[label_at, : count * slots] for x in pieces])
         row = iota((row_count, count * slots), 0).astype(jnp.float32)
         put = jnp.where(row == labels, 1.0, 0.0).astype(jnp.bfloat16)
@@ -210,12 +228,12 @@
         copy.wait()
 
 
-def up_pieces(pieces, pre, weight, heads, capacity):
+def up_pieces(pieces, pre, weight, heads, capacity, later):
     width = weight.shape[0] // heads
     return pl.pallas_call(
         functools.partial(up_kernel, heads, capacity),
         out_shape=[jax.ShapeDtypeStruct((heads // 2, pre.shape[0], width), jnp.bfloat16)] * 2,
-        in_specs=in_vmem(2) + in_hbm(1),
+        in_specs=in_vmem(len(pieces) + 1) + in_hbm(1) + in_vmem(1),
         out_specs=in_hbm(2),
         scratch_shapes=[
             pltpu.VMEM((heads, width, weight.shape[1]), jnp.bfloat16),
@@ -228,7 +246,7 @@
             flops=8 * pre.shape[0] * weight.size, bytes_accessed=8 * weight.size, transcendentals=0
         ),
         name="up_product",
-    )(pieces, pre, weight)
+    )(*pieces, pre, weight, later)
 
 
 class Rows:
@@ -476,10 +494,9 @@
 
 
 def exchanged(pieces, axes):
-    count = pieces.shape[0]
-    parts = [pieces[d : d + 1] for d in range(count)]
-    return parts[:1] + [
-        lax.ppermute(parts[d], axes, [(i, i ^ d) for i in range(count)]) for d in range(1, count)
+    count = len(pieces)
+    return [pieces[0]] + [
+        lax.ppermute(pieces[d], axes, [(i, i ^ d) for i in range(count)]) for d in range(1, count)
     ]
 
 
@@ -491,20 +508,15 @@
     heads = lax.axis_size(("chip", "core", "span"))
     row_count = grad_out.shape[0]
     capacity, _ = padded_slots(row_count, groups)
-    pieces = down_pieces(destination, grad_out, w_down, groups, spans)
-    pieces, queries, key_states, value_states = lax.optimization_barrier(
-        (pieces, queries, key_states, value_states)
-    )
-    arrived = lax.all_to_all(pieces, ("grp", "span"), split_axis=0, concat_axis=0, tiled=True)
     own = jnp.concatenate([queries.T, key_states.T, value_states.T], 0)
     sides = from_pairs(own)
+    pieces = down_pieces(destination, grad_out, w_down, groups, spans)
     first = lax.axis_index("grp") * row_count
-    other, shares = up_pieces(arrived, pre_act, w_up, heads, capacity)
-    other, *sides = lax.optimization_barrier((other, *sides))
+    held, held_done = softmax_parts(lengths, first, own, *sides)
+    other, shares = up_pieces(pieces, pre_act, w_up, heads, capacity, held_done)
     other = lax.ppermute(other, "core", [(0, 1), (1, 0)])
     shares = (other.astype(jnp.float32) + shares.astype(jnp.float32)).astype(jnp.bfloat16)
-    shares, own = lax.optimization_barrier((shares, own))
-    held, held_done = softmax_parts(lengths, first, own, *sides)
+    shares = [shares[d : d + 1] for d in range(shares.shape[0])]
     grad = gathered(exchanged(shares, ("chip", "span")), held_done)
     even, odd = from_pairs(grad)
     grad_query, key_part, value_part = own_terms(grad, queries.T, held)

time: 51.6 us -> 55.5 us (1.076)
  starting transfers between devices: 15.3 us -> 20.3 us
  waiting for transfers between devices: 9.86 us -> 7.64 us
  other arithmetic: 0.15 us -> 1.17 us
    ppermute x3 -> x10, starting transfers between devices: 3.55 us -> 16.5 us  [exchanged(): lax.ppermute(pieces[d], axes, [(i, i ^ d) for i in range(count)])]
    all_to_all x1 -> x0, starting transfers between devices: 7.29 us -> none  [on_device(): lax.all_to_all(pieces, ('grp', 'span'), split_axis=0, concat_axis=0, tile...]
    all_to_all x1 -> x0, waiting for transfers between devices: 6.28 us -> none  [on_device(): lax.all_to_all(pieces, ('grp', 'span'), split_axis=0, concat_axis=0, tile...]
    ppermute x3 -> x10, waiting for transfers between devices: 0.01 us -> 4.94 us  [exchanged(): lax.ppermute(pieces[d], axes, [(i, i ^ d) for i in range(count)])]
    concatenate x1, other arithmetic: 0.04 us -> 1.06 us  [on_device(): own = jnp.concatenate([queries.T, key_states.T, value_states.T], 0)]
    ppermute x4, waiting for transfers between devices: 1.85 us -> 0.97 us  [swapped(): return lax.ppermute(x, ('core', 'grp'), sorted(partner.items()))]
    ppermute x4, starting transfers between devices: 4.35 us -> 3.73 us  [swapped(): return lax.ppermute(x, ('core', 'grp'), sorted(partner.items()))]
  transfers between devices with their start and end apart: 9 -> 15, of which waited for: 3 -> 6; matrix products, arithmetic and copies ran while one was open for 0% -> 0% of each run, Pallas kernels for 31% -> 29%
where the time goes in v7:
time: 55.5 us; the launch traced here: 55.4 us
  Pallas kernels  24.5 us (44%)
  starting transfers between devices  20.3 us (37%)
  waiting for transfers between devices  7.64 us (14%)
  other arithmetic  1.17 us (2%)
  local copies, waits for them, and re-layouts  1.05 us (2%)
  between operations  0.75 us (1%)
    ppermute x10, starting transfers between devices, exchanged(): lax.ppermute(pieces[d], axes, [(i, i ^ d) for i in range(count)])  16.5 us
    pallas_call x1, Pallas kernels, softmax_parts(): pl.pallas_call(softmax_kernel, out_shape=(jax.ShapeDtypeStruct((rows.tota...  6.91 us
    pallas_call x1, Pallas kernels, down_pieces(): pl.pallas_call(functools.partial(down_kernel, groups, spans, capacity, sl...  6.58 us
    pallas_call x1, Pallas kernels, up_pieces(): pl.pallas_call(functools.partial(up_kernel, heads, capacity), out_shape=[...  6.52 us
    ppermute x10, waiting for transfers between devices, exchanged(): lax.ppermute(pieces[d], axes, [(i, i ^ d) for i in range(count)])  4.94 us
    ppermute x4, starting transfers between devices, swapped(): return lax.ppermute(x, ('core', 'grp'), sorted(partner.items()))  3.73 us
    pallas_call x1, Pallas kernels, own_terms(): pl.pallas_call(own_kernel, out_shape=(jax.ShapeDtypeStruct(grad.shape, jn...  2.35 us
    ppermute x1, waiting for transfers between devices, on_device(): other = lax.ppermute(other, 'core', [(0, 1), (1, 0)])  1.73 us
  transfers between devices with their start and end apart: 15, of which 6 were waited for; matrix products, arithmetic and copies ran while one was open for 0% of the time, Pallas kernels for 29%

profile of v7, /device:TPU:0, one launch (start us, length us, event | category | flops | bytes accessed | tf_op | source)
XLA Modules:
  0.0 55.4 jit_solution(15073647166096198775)
XLA Ops:
  0.6 1.1 %pad_maximum_fusion.own_ref = bf16[480,320]{1,0:T(8,128)(2,1)S(1)} fusion(bf16[160,320]{1,0:T(8,128)(2,1)} %bitcast.12, bf16[160,320]{1,0:T(8,128)(2,1)} %bitcast.13, bf16[160,320]{1,0:T(8,128)(2,1)} %bitcast.9), kind=kLoop, calls=%fused_computation.1 | loop fusion | flops 921600 | bytes 614400 | tf_op jit(solution)/shard_map/concatenate | solution.py:511
  1.7 3.1 %collective-permute-start.7 = (bf16[480,320]{1,0:T(8,128)(2,1)S(1)}, bf16[480,320]{1,0:T(8,128)(2,1)S(1)}, u32[]{:S(2)}, u32[]{:S(2)}) collective-permute-start(bf16[480,320]{1,0:T(8,128)(2,1)S(1)} %pad_maximum_fusion.own_ref), channel_id=1, source_target_pairs={{0,2},{2,0},{4,6},{6,4},{8,10},{10,8},{12,14},{14,12},{1,3},{3,1},... | collective-permute-start | bytes 921608 | tf_op jit(solution)/shard_map/ppermute | solution.py:491
  4.8 0.0 collective-permute-start.8
  4.8 6.6 %down_product.1 = (bf16[1,24,640]{2,1,0:T(8,128)(2,1)}, bf16[1,24,640]{2,1,0:T(8,128)(2,1)}, bf16[1,24,640]{2,1,0:T(8,128)(2,1)}, bf16[1,24,640]{2,1,0:T(8,128)(...) custom-call(s32[1,80]{1,0:T(1,128)} %bitcast.17, ...), custom_call_target="tpu_custom_call" | custom-call | flops 83886080000 | bytes 41943040 | tf_op jit(solution)/shard_map/down_product/pallas_call | solution.py:128
  11.4 1.6 %collective-permute-start = (bf16[1,24,640]{2,1,0:T(8,128)(2,1)}, bf16[1,24,640]{2,1,0:T(8,128)(2,1)S(1)}, u32[]{:S(2)}, u32[]{:S(2)}) collective-permute-start(bf16[1,24,640]{2,1,0:T(8,128)(2,1)} %get-tuple-element.21), channel_id=1, source_target_pairs={{0,1},{1,0},{2,3},{3,2},{4,5},{5,4},{6,7},{7,6},{8,9},{9,8},{10,11... | collective-permute-start | bytes 92168 | tf_op jit(solution)/shard_map/ppermute | solution.py:499
  13.0 3.1 %collective-permute-start.1 = (bf16[1,24,640]{2,1,0:T(8,128)(2,1)}, bf16[1,24,640]{2,1,0:T(8,128)(2,1)S(1)}, u32[]{:S(2)}, u32[]{:S(2)}) collective-permute-start(bf16[1,24,640]{2,1,0:T(8,128)(2,1)} %get-tuple-element.22), channel_id=1, source_target_pairs={{0,2},{1,3},{2,0},{3,1},{4,6},{5,7},{6,4},{7,5},{8,10},{9,11},{10,... | collective-permute-start | bytes 92168 | tf_op jit(solution)/shard_map/ppermute | solution.py:499
  16.1 0.0 collective-permute-start.2
  16.1 2.0 %collective-permute-start.3 = (bf16[1,24,640]{2,1,0:T(8,128)(2,1)}, bf16[1,24,640]{2,1,0:T(8,128)(2,1)S(1)}, u32[]{:S(2)}, u32[]{:S(2)}) collective-permute-start(bf16[1,24,640]{2,1,0:T(8,128)(2,1)} %get-tuple-element.24), channel_id=1, source_target_pairs={{0,4},{1,5},{2,6},{3,7},{4,0},{5,1},{6,2},{7,3},{8,12},{9,13},{10,... | collective-permute-start | bytes 92168 | tf_op jit(solution)/shard_map/ppermute | solution.py:499
  18.1 0.1 collective-permute-done.1.refs_2_
  18.2 1.7 %collective-permute-start.4 = (bf16[1,24,640]{2,1,0:T(8,128)(2,1)}, bf16[1,24,640]{2,1,0:T(8,128)(2,1)S(1)}, u32[]{:S(2)}, u32[]{:S(2)}) collective-permute-start(bf16[1,24,640]{2,1,0:T(8,128)(2,1)} %get-tuple-element.25), channel_id=1, source_target_pairs={{0,5},{1,4},{2,7},{3,6},{4,1},{5,0},{6,3},{7,2},{8,13},{9,12},{10,... | collective-permute-start | bytes 92168 | tf_op jit(solution)/shard_map/ppermute | solution.py:499
  20.0 2.6 %collective-permute-start.5 = (bf16[1,24,640]{2,1,0:T(8,128)(2,1)}, bf16[1,24,640]{2,1,0:T(8,128)(2,1)S(1)}, u32[]{:S(2)}, u32[]{:S(2)}) collective-permute-start(bf16[1,24,640]{2,1,0:T(8,128)(2,1)} %get-tuple-element.26), channel_id=1, source_target_pairs={{0,6},{1,7},{2,4},{3,5},{4,2},{5,3},{6,0},{7,1},{8,14},{9,15},{10,... | collective-permute-start | bytes 92168 | tf_op jit(solution)/shard_map/ppermute | solution.py:499
  22.5 0.0 collective-permute-done.8.odd_ref
  22.5 1.9 %collective-permute-start.6 = (bf16[1,24,640]{2,1,0:T(8,128)(2,1)}, bf16[1,24,640]{2,1,0:T(8,128)(2,1)S(1)}, u32[]{:S(2)}, u32[]{:S(2)}) collective-permute-start(bf16[1,24,640]{2,1,0:T(8,128)(2,1)} %get-tuple-element.27), channel_id=1, source_target_pairs={{0,7},{1,6},{2,5},{3,4},{4,3},{5,2},{6,1},{7,0},{8,15},{9,14},{10,... | collective-permute-start | bytes 92168 | tf_op jit(solution)/shard_map/ppermute | solution.py:499
  24.4 6.9 %softmax_parts.1 = (bf16[1920,1024]{1,0:T(8,128)(2,1)}, f32[8,128]{1,0:T(8,128)S(1)}) custom-call(s32[1,12]{1,0:T(1,128)S(1)} %bitcast.11, s32[1,1]{1,0:T(1,128)} %bitcast.2.first_ref, bf16[480,320]{1,0:T(8,128)(2,1)S(1)} %pad_maximum_fusion.own_ref, bf16[480,320]{1,0:T(8,128)(2,1)S(1)} %collective-permute-done.7.even_ref, ...), custom_call_target="tpu_custom_call" | custom-call | flops 20480000000 | bytes 102400000 | tf_op jit(solution)/shard_map/softmax_parts/pallas_call | solution.py:362
  31.3 0.0 collective-permute-done.2.refs_3_
  31.4 0.0 collective-permute-done.5.refs_6_
  31.4 6.5 %up_product.1 = (bf16[4,80,640]{2,1,0:T(8,128)(2,1)S(1)}, bf16[4,80,640]{2,1,0:T(8,128)(2,1)S(1)}) custom-call(bf16[1,24,640]{2,1,0:T(8,128)(2,1)S(1)} %copy-done.4, bf16[1,24,640]{2,1,0:T(8,128)(2,1)S(1)} %collective-permute-done.refs_1_, bf16[1,24,640]{2,1,0:T(8,128)(2,1)S(1)} %collective-permute-done.1.refs_2_, ...), custom_call_target="tpu_custom_call" | custom-call | flops 2097152000 | bytes 26214400 | tf_op jit(solution)/shard_map/up_product/pallas_call | solution.py:233
  37.9 0.1 collective-permute-start.9
  38.0 1.7 %collective-permute-done.9 = bf16[4,80,640]{2,1,0:T(8,128)(2,1)S(1)} collective-permute-done((bf16[4,80,640]{2,1,0:T(8,128)(2,1)S(1)}, bf16[4,80,640]{2,1,0:T(8,128)(2,1)S(1)}, u32[]{:S(2)}, u32[]{:S(2)}) %collective-permute-start.9) | collective-permute-done | bytes 409632 | tf_op jit(solution)/shard_map/ppermute | solution.py:517
  39.7 0.1 add_convert_fusion
  39.9 0.9 %collective-permute-start.10 = (bf16[1,80,640]{2,1,0:T(8,128)(2,1)S(1)}, bf16[1,80,640]{2,1,0:T(8,128)(2,1)S(1)}, u32[]{:S(2)}, u32[]{:S(2)}) collective-permute-start(bf16[1,80,640]{2,1,0:T(8,128)(2,1)S(1)} %get-tuple-element.39), channel_id=1, source_target_pairs={{0,1},{1,0},{16,17},{17,16},{2,3},{3,2},{18,19},{19,18},{4,5},{5,4... | collective-permute-start | bytes 307208 | tf_op jit(solution)/shard_map/ppermute | solution.py:499
  40.8 1.5 %collective-permute-start.11 = (bf16[1,80,640]{2,1,0:T(8,128)(2,1)S(1)}, bf16[1,80,640]{2,1,0:T(8,128)(2,1)S(1)}, u32[]{:S(2)}, u32[]{:S(2)}) collective-permute-start(bf16[1,80,640]{2,1,0:T(8,128)(2,1)S(1)} %get-tuple-element.38), channel_id=1, source_target_pairs={{0,16},{1,17},{16,0},{17,1},{2,18},{3,19},{18,2},{19,3},{4,20},{5,... | collective-permute-start | bytes 307208 | tf_op jit(solution)/shard_map/ppermute | solution.py:499
  42.3 1.1 %collective-permute-start.12 = (bf16[1,80,640]{2,1,0:T(8,128)(2,1)S(1)}, bf16[1,80,640]{2,1,0:T(8,128)(2,1)S(1)}, u32[]{:S(2)}, u32[]{:S(2)}) collective-permute-start(bf16[1,80,640]{2,1,0:T(8,128)(2,1)S(1)} %get-tuple-element.37), channel_id=1, source_target_pairs={{0,17},{1,16},{16,1},{17,0},{2,19},{3,18},{18,3},{19,2},{4,21},{5,... | collective-permute-start | bytes 307208 | tf_op jit(solution)/shard_map/ppermute | solution.py:499
  43.5 1.4 %collective-permute-done.10.refs_1_ = bf16[1,80,640]{2,1,0:T(8,128)(2,1)S(1)} collective-permute-done((bf16[1,80,640]{2,1,0:T(8,128)(2,1)S(1)}, bf16[1,80,640]{2,1,0:T(8,128)(2,1)S(1)}, u32[]{:S(2)}, u32[]{:S(2)}) %collective-permute-start.10) | collective-permute-done | bytes 102432 | tf_op jit(solution)/shard_map/ppermute | solution.py:499
  44.9 1.0 %collective-permute-done.11.refs_2_ = bf16[1,80,640]{2,1,0:T(8,128)(2,1)S(1)} collective-permute-done((bf16[1,80,640]{2,1,0:T(8,128)(2,1)S(1)}, bf16[1,80,640]{2,1,0:T(8,128)(2,1)S(1)}, u32[]{:S(2)}, u32[]{:S(2)}) %collective-permute-start.11) | collective-permute-done | bytes 102432 | tf_op jit(solution)/shard_map/ppermute | solution.py:499
  45.9 2.3 %collective-permute-done.12.refs_3_ = bf16[1,80,640]{2,1,0:T(8,128)(2,1)S(1)} collective-permute-done((bf16[1,80,640]{2,1,0:T(8,128)(2,1)S(1)}, bf16[1,80,640]{2,1,0:T(8,128)(2,1)S(1)}, u32[]{:S(2)}, u32[]{:S(2)}) %collective-permute-start.12) | collective-permute-done | bytes 102432 | tf_op jit(solution)/shard_map/ppermute | solution.py:499
  48.3 0.5 gather_sum.1.grad_ref
  48.8 0.6 %collective-permute-start.13 = (bf16[160,320]{1,0:T(8,128)(2,1)S(1)}, bf16[160,320]{1,0:T(8,128)(2,1)S(1)}, u32[]{:S(2)}, u32[]{:S(2)}) collective-permute-start(bf16[160,320]{1,0:T(8,128)(2,1)S(1)} %gather_sum.1.grad_ref), channel_id=1, source_target_pairs={{0,2},{2,0},{4,6},{6,4},{8,10},{10,8},{12,14},{14,12},{1,3},{3,1},... | collective-permute-start | bytes 307208 | tf_op jit(solution)/shard_map/ppermute | solution.py:491
  49.4 1.0 %copy-done = bf16[1920,1024]{1,0:T(8,128)(2,1)S(1)} copy-done((bf16[1920,1024]{1,0:T(8,128)(2,1)S(1)}, bf16[1920,1024]{1,0:T(8,128)(2,1)}, u32[]{:S(2)}) %copy-start) | copy-done | bytes 3932184
  50.4 2.3 %own_terms.1 = (bf16[160,320]{1,0:T(8,128)(2,1)}, f32[160,320]{1,0:T(8,128)S(1)}, f32[160,320]{1,0:T(8,128)S(1)}) custom-call(bf16[160,320]{1,0:T(8,128)(2,1)S(1)} %gather_sum.1.grad_ref, bf16[160,320]{1,0:T(8,128)(2,1)S(1)} %bitcast.10, bf16[1920,1024]{1,0:T(8,128)(2,1)S(1)} %copy-done), custom_call_target="tpu_custom_call" | custom-call | tf_op jit(solution)/shard_map/own_terms/pallas_call | solution.py:433
  52.7 1.0 %collective-permute-done.13.even_ref = bf16[160,320]{1,0:T(8,128)(2,1)S(1)} collective-permute-done((bf16[160,320]{1,0:T(8,128)(2,1)S(1)}, bf16[160,320]{1,0:T(8,128)(2,1)S(1)}, u32[]{:S(2)}, u32[]{:S(2)}) %collective-permute-start.13) | collective-permute-done | bytes 102432 | tf_op jit(solution)/shard_map/ppermute | solution.py:491
  53.7 1.7 %side_terms.1 = (bf16[160,320]{1,0:T(8,128)(2,1)}, bf16[160,320]{1,0:T(8,128)(2,1)}) custom-call(bf16[160,320]{1,0:T(8,128)(2,1)S(1)} %collective-permute-done.13.even_ref, bf16[160,320]{1,0:T(8,128)(2,1)S(1)} %collective-permute-done.14.odd_ref, f32[160,320]{1,0:T(8,128)S(1)} %get-tuple-element.33.key_part_ref, ...), custom_call_target="tpu_custom_call" | custom-call | tf_op jit(solution)/shard_map/side_terms/pallas_call | solution.py:471
  (17 shorter events, 0.1 us)
Async XLA Ops:
  1.7 18.3 %collective-permute-start.7 = (bf16[480,320]{1,0:T(8,128)(2,1)S(1)}, bf16[480,320]{1,0:T(8,128)(2,1)S(1)}, u32[]{:S(2)}, u32[]{:S(2)}) collective-permute-start(bf16[480,320]{1,0:T(8,128)(2,1)S(1)} %pad_maximum_fusion.own_ref), channel_id=1, source_target_pairs={{0,2},{2,0},{4,6},{6,4},{8,10},{10,8},{12,14},{14,12},{1,3},{3,1},... | collective-permute-start | bytes 921608 | tf_op jit(solution)/shard_map/ppermute | solution.py:491
  4.8 17.7 %collective-permute-start.8 = (bf16[480,320]{1,0:T(8,128)(2,1)S(1)}, bf16[480,320]{1,0:T(8,128)(2,1)S(1)}, u32[]{:S(2)}, u32[]{:S(2)}) collective-permute-start(bf16[480,320]{1,0:T(8,128)(2,1)S(1)} %pad_maximum_fusion.own_ref), channel_id=1, source_target_pairs={{0,8},{2,4},{4,2},{6,14},{8,0},{10,12},{12,10},{14,6},{1,9},{3,5},... | collective-permute-start | bytes 921608 | tf_op jit(solution)/shard_map/ppermute | solution.py:491
  4.8 19.6 %copy-start.3 = (s32[12]{0:T(128)S(1)}, s32[12]{0:T(128)}, u32[]{:S(2)}) copy-start(s32[12]{0:T(128)} %param.17) | copy-start | bytes 148
  11.4 4.7 %collective-permute-start = (bf16[1,24,640]{2,1,0:T(8,128)(2,1)}, bf16[1,24,640]{2,1,0:T(8,128)(2,1)S(1)}, u32[]{:S(2)}, u32[]{:S(2)}) collective-permute-start(bf16[1,24,640]{2,1,0:T(8,128)(2,1)} %get-tuple-element.21), channel_id=1, source_target_pairs={{0,1},{1,0},{2,3},{3,2},{4,5},{5,4},{6,7},{7,6},{8,9},{9,8},{10,11... | collective-permute-start | bytes 92168 | tf_op jit(solution)/shard_map/ppermute | solution.py:499
  13.0 5.3 %collective-permute-start.1 = (bf16[1,24,640]{2,1,0:T(8,128)(2,1)}, bf16[1,24,640]{2,1,0:T(8,128)(2,1)S(1)}, u32[]{:S(2)}, u32[]{:S(2)}) collective-permute-start(bf16[1,24,640]{2,1,0:T(8,128)(2,1)} %get-tuple-element.22), channel_id=1, source_target_pairs={{0,2},{1,3},{2,0},{3,1},{4,6},{5,7},{6,4},{7,5},{8,10},{9,11},{10,... | collective-permute-start | bytes 92168 | tf_op jit(solution)/shard_map/ppermute | solution.py:499
  16.1 15.2 %collective-permute-start.2 = (bf16[1,24,640]{2,1,0:T(8,128)(2,1)}, bf16[1,24,640]{2,1,0:T(8,128)(2,1)S(1)}, u32[]{:S(2)}, u32[]{:S(2)}) collective-permute-start(bf16[1,24,640]{2,1,0:T(8,128)(2,1)} %get-tuple-element.23), channel_id=1, source_target_pairs={{0,3},{1,2},{2,1},{3,0},{4,7},{5,6},{6,5},{7,4},{8,11},{9,10},{10,... | collective-permute-start | bytes 92168 | tf_op jit(solution)/shard_map/ppermute | solution.py:499
  16.1 15.2 %collective-permute-start.3 = (bf16[1,24,640]{2,1,0:T(8,128)(2,1)}, bf16[1,24,640]{2,1,0:T(8,128)(2,1)S(1)}, u32[]{:S(2)}, u32[]{:S(2)}) collective-permute-start(bf16[1,24,640]{2,1,0:T(8,128)(2,1)} %get-tuple-element.24), channel_id=1, source_target_pairs={{0,4},{1,5},{2,6},{3,7},{4,0},{5,1},{6,2},{7,3},{8,12},{9,13},{10,... | collective-permute-start | bytes 92168 | tf_op jit(solution)/shard_map/ppermute | solution.py:499
  18.2 13.1 %collective-permute-start.4 = (bf16[1,24,640]{2,1,0:T(8,128)(2,1)}, bf16[1,24,640]{2,1,0:T(8,128)(2,1)S(1)}, u32[]{:S(2)}, u32[]{:S(2)}) collective-permute-start(bf16[1,24,640]{2,1,0:T(8,128)(2,1)} %get-tuple-element.25), channel_id=1, source_target_pairs={{0,5},{1,4},{2,7},{3,6},{4,1},{5,0},{6,3},{7,2},{8,13},{9,12},{10,... | collective-permute-start | bytes 92168 | tf_op jit(solution)/shard_map/ppermute | solution.py:499
  20.0 11.4 %collective-permute-start.5 = (bf16[1,24,640]{2,1,0:T(8,128)(2,1)}, bf16[1,24,640]{2,1,0:T(8,128)(2,1)S(1)}, u32[]{:S(2)}, u32[]{:S(2)}) collective-permute-start(bf16[1,24,640]{2,1,0:T(8,128)(2,1)} %get-tuple-element.26), channel_id=1, source_target_pairs={{0,6},{1,7},{2,4},{3,5},{4,2},{5,3},{6,0},{7,1},{8,14},{9,15},{10,... | collective-permute-start | bytes 92168 | tf_op jit(solution)/shard_map/ppermute | solution.py:499
  22.5 8.8 %collective-permute-start.6 = (bf16[1,24,640]{2,1,0:T(8,128)(2,1)}, bf16[1,24,640]{2,1,0:T(8,128)(2,1)S(1)}, u32[]{:S(2)}, u32[]{:S(2)}) collective-permute-start(bf16[1,24,640]{2,1,0:T(8,128)(2,1)} %get-tuple-element.27), channel_id=1, source_target_pairs={{0,7},{1,6},{2,5},{3,4},{4,3},{5,2},{6,1},{7,0},{8,15},{9,14},{10,... | collective-permute-start | bytes 92168 | tf_op jit(solution)/shard_map/ppermute | solution.py:499
  24.4 7.0 %copy-start.2 = (bf16[80,640]{1,0:T(8,128)(2,1)S(1)}, bf16[80,640]{1,0:T(8,128)(2,1)}, u32[]{:S(2)}) copy-start(bf16[80,640]{1,0:T(8,128)(2,1)} %refs_8_.1) | copy-start | bytes 307204
  24.4 7.0 %copy-start.4 = (bf16[1,24,640]{2,1,0:T(8,128)(2,1)S(1)}, bf16[1,24,640]{2,1,0:T(8,128)(2,1)}, u32[]{:S(2)}) copy-start(bf16[1,24,640]{2,1,0:T(8,128)(2,1)} %get-tuple-element.20.refs_0_) | copy-start | bytes 92164
  37.9 1.8 %collective-permute-start.9 = (bf16[4,80,640]{2,1,0:T(8,128)(2,1)S(1)}, bf16[4,80,640]{2,1,0:T(8,128)(2,1)S(1)}, u32[]{:S(2)}, u32[]{:S(2)}) collective-permute-start(bf16[4,80,640]{2,1,0:T(8,128)(2,1)S(1)} %get-tuple-element.29), channel_id=1, source_target_pairs={{0,8},{8,0},{1,9},{9,1},{2,10},{10,2},{3,11},{11,3},{4,12},{12,4},... | collective-permute-start | bytes 1228808 | tf_op jit(solution)/shard_map/ppermute | solution.py:517
  39.9 5.0 %collective-permute-start.10 = (bf16[1,80,640]{2,1,0:T(8,128)(2,1)S(1)}, bf16[1,80,640]{2,1,0:T(8,128)(2,1)S(1)}, u32[]{:S(2)}, u32[]{:S(2)}) collective-permute-start(bf16[1,80,640]{2,1,0:T(8,128)(2,1)S(1)} %get-tuple-element.39), channel_id=1, source_target_pairs={{0,1},{1,0},{16,17},{17,16},{2,3},{3,2},{18,19},{19,18},{4,5},{5,4... | collective-permute-start | bytes 307208 | tf_op jit(solution)/shard_map/ppermute | solution.py:499
  40.8 5.1 %collective-permute-start.11 = (bf16[1,80,640]{2,1,0:T(8,128)(2,1)S(1)}, bf16[1,80,640]{2,1,0:T(8,128)(2,1)S(1)}, u32[]{:S(2)}, u32[]{:S(2)}) collective-permute-start(bf16[1,80,640]{2,1,0:T(8,128)(2,1)S(1)} %get-tuple-element.38), channel_id=1, source_target_pairs={{0,16},{1,17},{16,0},{17,1},{2,18},{3,19},{18,2},{19,3},{4,20},{5,... | collective-permute-start | bytes 307208 | tf_op jit(solution)/shard_map/ppermute | solution.py:499
  42.3 6.0 %collective-permute-start.12 = (bf16[1,80,640]{2,1,0:T(8,128)(2,1)S(1)}, bf16[1,80,640]{2,1,0:T(8,128)(2,1)S(1)}, u32[]{:S(2)}, u32[]{:S(2)}) collective-permute-start(bf16[1,80,640]{2,1,0:T(8,128)(2,1)S(1)} %get-tuple-element.37), channel_id=1, source_target_pairs={{0,17},{1,16},{16,1},{17,0},{2,19},{3,18},{18,3},{19,2},{4,21},{5,... | collective-permute-start | bytes 307208 | tf_op jit(solution)/shard_map/ppermute | solution.py:499
  48.3 2.1 %copy-start = (bf16[1920,1024]{1,0:T(8,128)(2,1)S(1)}, bf16[1920,1024]{1,0:T(8,128)(2,1)}, u32[]{:S(2)}) copy-start(bf16[1920,1024]{1,0:T(8,128)(2,1)} %get-tuple-element.31.held_ref) | copy-start | bytes 11796484
  48.3 2.1 %copy-start.1 = (bf16[320,160]{0,1:T(8,128)(2,1)S(1)}, bf16[320,160]{0,1:T(8,128)(2,1)}, u32[]{:S(2)}) copy-start(bf16[320,160]{0,1:T(8,128)(2,1)} %param.14) | copy-start | bytes 307204
  48.8 4.9 %collective-permute-start.13 = (bf16[160,320]{1,0:T(8,128)(2,1)S(1)}, bf16[160,320]{1,0:T(8,128)(2,1)S(1)}, u32[]{:S(2)}, u32[]{:S(2)}) collective-permute-start(bf16[160,320]{1,0:T(8,128)(2,1)S(1)} %gather_sum.1.grad_ref), channel_id=1, source_target_pairs={{0,2},{2,0},{4,6},{6,4},{8,10},{10,8},{12,14},{14,12},{1,3},{3,1},... | collective-permute-start | bytes 307208 | tf_op jit(solution)/shard_map/ppermute | solution.py:491
  49.4 4.3 %collective-permute-start.14 = (bf16[160,320]{1,0:T(8,128)(2,1)S(1)}, bf16[160,320]{1,0:T(8,128)(2,1)S(1)}, u32[]{:S(2)}, u32[]{:S(2)}) collective-permute-start(bf16[160,320]{1,0:T(8,128)(2,1)S(1)} %gather_sum.1.grad_ref), channel_id=1, source_target_pairs={{0,8},{2,4},{4,2},{6,14},{8,0},{10,12},{12,10},{14,6},{1,9},{3,5},... | collective-permute-start | bytes 307208 | tf_op jit(solution)/shard_map/ppermute | solution.py:491

commit v8 on v6

--- a/solution.py
+++ b/solution.py
@@ -189,7 +189,7 @@
     def send(h, products):
         for i in range(2):
             part = products[i * width : (i + 1) * width]
-            out_ref[h + i] = part.T.astype(jnp.bfloat16)
+            out_ref[h + i] = part.astype(jnp.bfloat16).T
         out_hbm = send_hbm if h < half else keep_hbm
         copy = pltpu.make_async_copy(
             out_ref.at[pl.ds(h, 2)], out_hbm.at[pl.ds(h % half, 2)], out_sems.at[h // 2]
@@ -255,10 +255,8 @@
         return slice(self.side_at + h * self.patches, self.side_at + (h + 1) * self.patches)
 
 
-def softmax_kernel(lengths_ref, first_ref, own_ref, even_ref, odd_ref, out_hbm, done_ref, held,
-                   sems):
+def softmax_kernel(lengths_ref, first_ref, own_ref, even_ref, odd_ref, held, done_ref):
     columns, patches = own_ref.shape[0] // 3, own_ref.shape[1]
-    heads = columns // HEAD_DIM
     rows = Rows(columns, patches)
     is_even = lax.rem(lax.axis_index("grp"), 2) == 0
     first = first_ref[0, 0]
@@ -276,15 +274,6 @@
 
     down = [image_of((patches, 1), 0, b) for b in (0, -1, 1)]
     across = [image_of((1, patches), 1, b) for b in (0, -1, 1)]
-    all_keys = jnp.concatenate(across, 1)
-    same_own = down[0] == all_keys
-    copies = []
-
-    def send(part, lanes):
-        at = (pl.ds(part.start, part.stop - part.start), pl.ds(0, lanes))
-        copy = pltpu.make_async_copy(held.at[at], out_hbm.at[at], sems.at[len(copies)])
-        copy.start()
-        copies.append(copy)
 
     def kind(block, t, h=None):
         start = t * columns + (0 if h is None else h * HEAD_DIM)
@@ -294,53 +283,41 @@
         before, after = (odd_ref, even_ref) if block == 1 else (even_ref, odd_ref)
         return jnp.where(is_even, before[at], after[at])
 
-    def wide(t, which):
-        return jnp.concatenate([kind(b, t).astype(jnp.float32) for b in which], 1).astype(jnp.bfloat16)
+    def wide(t, which, h=None):
+        parts = [kind(b, t, h).astype(jnp.float32) for b in which]
+        return jnp.concatenate(parts, 1).astype(jnp.bfloat16)
+
+    def softmax(queries, keys, same):
+        scores = jnp.where(same, dot(queries, keys, TN) * SCALE, -jnp.inf)
+        weights = jnp.exp(scores - jnp.max(scores, 1, keepdims=True))
+        return weights * (1.0 / jnp.sum(weights, 1, keepdims=True))
 
     held[rows.kind(rows.values), : 3 * patches] = wide(2, (0, 1, 2))
     held[rows.kind(rows.keys), : 3 * patches] = wide(1, (0, 1, 2))
     held[rows.kind(rows.queries), : 2 * patches] = wide(0, (1, 2))
-    send(rows.kind(rows.values, 2), rows.lanes)
-    send(rows.kind(rows.queries), rows.side_lanes)
-    for h in range(heads):
+    same_own = down[0] == jnp.concatenate(across, 1)
+    same_side = [down[b] == jnp.concatenate([across[0], across[b]], 1) for b in (1, 2)]
+    for h in range(columns // HEAD_DIM):
         keys = held[rows.head(rows.keys, h), : 3 * patches]
-        scores = dot(kind(0, 0, h), keys, TN) * SCALE
-        scores = jnp.where(same_own, scores, -jnp.inf)
-        weights = jnp.exp(scores - jnp.max(scores, 1, keepdims=True))
-        over = 1.0 / jnp.sum(weights, 1, keepdims=True)
-        held[rows.probs(h), : 3 * patches] = (weights * over).astype(jnp.bfloat16)
-        send(rows.probs(h), rows.lanes)
-    for h in range(heads):
-        own_keys = kind(0, 1, h).astype(jnp.float32).T.astype(jnp.bfloat16)
+        probs = softmax(kind(0, 0, h), keys, same_own)
+        held[rows.probs(h), : 3 * patches] = probs.astype(jnp.bfloat16)
         side, attended = [], []
         for b in (1, 2):
-            queries = kind(b, 0, h)
-            keys = kind(b, 1, h).astype(jnp.float32).T.astype(jnp.bfloat16)
-            scores = []
-            for n, k in ((0, own_keys), (b, keys)):
-                scores.append(jnp.where(down[n] == across[b], dot(k, queries, NN) * SCALE, -jnp.inf))
-            top = functools.reduce(jnp.maximum, [jnp.max(x, 0, keepdims=True) for x in scores])
-            weights = [jnp.exp(x - top) for x in scores]
-            over = 1.0 / sum([jnp.sum(w, 0, keepdims=True) for w in weights])
-            probs = [(w * over).astype(jnp.bfloat16) for w in weights]
-            attended.append(dot(kind(0, 2, h), probs[0], NN) + dot(kind(b, 2, h), probs[1], NN))
-            side.append(probs[0].astype(jnp.float32))
+            probs = softmax(kind(b, 0, h), wide(1, (0, b), h), same_side[b - 1])
+            seen = dot(probs.astype(jnp.bfloat16), wide(2, (0, b), h), NT)
+            attended.append(seen.T)
+            side.append(probs[:, :patches].T)
         held[rows.side_probs(h), : 2 * patches] = jnp.concatenate(side, 1).astype(jnp.bfloat16)
-        send(rows.side_probs(h), rows.side_lanes)
         attended = jnp.concatenate(attended, 1).astype(jnp.bfloat16)
         held[rows.head(rows.attended, h), : 2 * patches] = attended
-    send(rows.kind(rows.attended), rows.side_lanes)
-    for copy in copies:
-        copy.wait()
     done_ref[...] = jnp.zeros(done_ref.shape, jnp.float32)
 
 
 def softmax_parts(lengths, first, own, even, odd):
     columns, patches = own.shape[0] // 3, own.shape[1]
-    heads = columns // HEAD_DIM
     rows = Rows(columns, patches)
     smem = pl.BlockSpec(memory_space=pltpu.MemorySpace.SMEM)
-    work = heads * patches * patches
+    work = (columns // HEAD_DIM) * patches * patches
     return pl.pallas_call(
         softmax_kernel,
         out_shape=(
@@ -348,12 +325,8 @@
             jax.ShapeDtypeStruct((8, 128), jnp.float32),
         ),
         in_specs=[smem, smem] + in_vmem(3),
-        out_specs=tuple(in_hbm(1) + in_vmem(1)),
-        scratch_shapes=[
-            pltpu.VMEM((rows.total, rows.lanes), jnp.bfloat16),
-            pltpu.SemaphoreType.DMA((3 + 2 * heads,)),
-        ],
-        compiler_params=params(52),
+        out_specs=tuple(in_vmem(2)),
+        compiler_params=params(32),
         cost_estimate=pl.CostEstimate(
             flops=100_000 * work, bytes_accessed=500 * work, transcendentals=9 * work
         ),

time: 51.6 us -> 50.5 us (0.979)
  Pallas kernels: 24.4 us -> 23.3 us
  local copies, waits for them, and re-layouts: 0.86 us -> 0.06 us
  waiting for transfers between devices: 9.86 us -> 10.6 us
    pallas_call x1, Pallas kernels: 6.79 us -> 5.75 us  [softmax_parts(): pl.pallas_call(softmax_kernel, out_shape=(jax.ShapeDtypeStruct((rows.tota...]
    unnamed x12 -> x10, local copies, waits for them, and re-layouts: 0.82 us -> 0.02 us
    ppermute x4, waiting for transfers between devices: 1.85 us -> 2.63 us  [swapped(): return lax.ppermute(x, ('core', 'grp'), sorted(partner.items()))]
  transfers between devices with their start and end apart: 9 -> 9, of which waited for: 3 -> 3; matrix products, arithmetic and copies ran while one was open for 0% -> 0% of each run, Pallas kernels for 31% -> 29%
where the time goes in v8:
time: 50.5 us; the launch traced here: 50.3 us
  Pallas kernels  23.3 us (46%)
  starting transfers between devices  15.3 us (30%)
  waiting for transfers between devices  10.6 us (21%)
  between operations  0.81 us (2%)
    all_to_all x1, starting transfers between devices, on_device(): lax.all_to_all(pieces, ('grp', 'span'), split_axis=0, concat_axis=0, tile...  7.29 us
    pallas_call x1, Pallas kernels, down_pieces(): pl.pallas_call(functools.partial(down_kernel, groups, spans, capacity, sl...  6.56 us
    pallas_call x1, Pallas kernels, up_pieces(): pl.pallas_call(functools.partial(up_kernel, heads, capacity), out_shape=[...  6.49 us
    all_to_all x1, waiting for transfers between devices, on_device(): lax.all_to_all(pieces, ('grp', 'span'), split_axis=0, concat_axis=0, tile...  6.28 us
    pallas_call x1, Pallas kernels, softmax_parts(): pl.pallas_call(softmax_kernel, out_shape=(jax.ShapeDtypeStruct((rows.tota...  5.75 us
    ppermute x4, starting transfers between devices, swapped(): return lax.ppermute(x, ('core', 'grp'), sorted(partner.items()))  4.37 us
    ppermute x3, starting transfers between devices, exchanged(): lax.ppermute(parts[d], axes, [(i, i ^ d) for i in range(count)])  3.55 us
    ppermute x4, waiting for transfers between devices, swapped(): return lax.ppermute(x, ('core', 'grp'), sorted(partner.items()))  2.63 us
  transfers between devices with their start and end apart: 9, of which 3 were waited for; matrix products, arithmetic and copies ran while one was open for 0% of the time, Pallas kernels for 29%

profile of v8, /device:TPU:0, one launch (start us, length us, event | category | flops | bytes accessed | tf_op | source)
XLA Modules:
  0.0 50.3 jit_solution(8055434207835082196)
XLA Ops:
  0.6 0.0 copy-start.3
  0.6 0.0 copy-start.4
  0.7 0.0 copy-start
  0.7 0.0 copy-start.1
  0.7 6.6 %down_product.1 = bf16[4,2,24,640]{3,2,1,0:T(8,128)(2,1)} custom-call(s32[1,80]{1,0:T(1,128)} %bitcast.16, bf16[80,4096]{1,0:T(8,128)(2,1)} %rows_hbm.1, bf16[1280,4096]{1,0:T(8,128)(2,1)} %weight_ref.2), custom_call_target="tpu_custom_call" | custom-call | tf_op jit(solution)/shard_map/down_product/pallas_call | solution.py:118
  7.2 0.0 copy-start.2
  7.3 7.3 %all-to-all-start = ((bf16[8,24,640]{2,1,0:T(8,128)(2,1)}), bf16[8,24,640]{2,1,0:T(8,128)(2,1)S(1)}, u32[]{:S(2)}, u32[]{:S(2)}) async-start(bf16[8,24,640]{2,1,0:T(8,128)(2,1)} %bitcast.13), calls=%async_computation | async-start | bytes 491520 | tf_op jit(solution)/shard_map/all_to_all | solution.py:471
  14.5 0.0 copy-done.3
  14.6 0.0 copy-done.4
  14.6 0.1 collective-permute-start.1
  14.7 3.5 %collective-permute-start = (bf16[480,320]{1,0:T(8,128)(2,1)S(1)}, bf16[480,320]{1,0:T(8,128)(2,1)S(1)}, u32[]{:S(2)}, u32[]{:S(2)}) collective-permute-start(bf16[480,320]{1,0:T(8,128)(2,1)S(1)} %pad_maximum_fusion.own_ref), channel_id=1, source_target_pairs={{0,2},{2,0},{4,6},{6,4},{8,10},{10,8},{12,14},{14,12},{1,3},{3,1},... | collective-permute-start | bytes 921608 | tf_op jit(solution)/shard_map/ppermute | solution.py:446
  18.2 6.3 %all-to-all-done.pieces_ref = bf16[8,24,640]{2,1,0:T(8,128)(2,1)S(1)} async-done(((bf16[8,24,640]{2,1,0:T(8,128)(2,1)}), bf16[8,24,640]{2,1,0:T(8,128)(2,1)S(1)}, u32[]{:S(2)}, u32[]{:S(2)}) %all-to-all-start) | async-done | bytes 245792 | tf_op jit(solution)/shard_map/all_to_all | solution.py:471
  24.5 6.5 %up_product.1 = (bf16[4,80,640]{2,1,0:T(8,128)(2,1)S(1)}, bf16[4,80,640]{2,1,0:T(8,128)(2,1)S(1)}) custom-call(bf16[8,24,640]{2,1,0:T(8,128)(2,1)S(1)} %all-to-all-done.pieces_ref, bf16[80,640]{1,0:T(8,128)(2,1)S(1)} %copy-done.1, bf16[5120,640]{1,0:T(8,128)(2,1)} %weight_ref.3), custom_call_target="tpu_custom_call" | custom-call | flops 2097152000 | bytes 26214400 | tf_op jit(solution)/shard_map/up_product/pallas_call | solution.py:215
  30.9 0.0 collective-permute-done.1.odd_ref
  31.0 0.0 collective-permute-done.even_ref
  31.0 0.1 collective-permute-start.2
  31.1 1.7 %collective-permute-done.2 = bf16[4,80,640]{2,1,0:T(8,128)(2,1)S(1)} collective-permute-done((bf16[4,80,640]{2,1,0:T(8,128)(2,1)S(1)}, bf16[4,80,640]{2,1,0:T(8,128)(2,1)S(1)}, u32[]{:S(2)}, u32[]{:S(2)}) %collective-permute-start.2) | collective-permute-done | bytes 409632 | tf_op jit(solution)/shard_map/ppermute | solution.py:477
  32.8 0.1 add_convert_fusion
  32.9 2.2 %collective-permute-start.5 = (bf16[1,80,640]{2,1,0:T(8,128)(2,1)S(1)}, bf16[1,80,640]{2,1,0:T(8,128)(2,1)S(1)}, u32[]{:S(2)}, u32[]{:S(2)}) collective-permute-start(bf16[1,80,640]{2,1,0:T(8,128)(2,1)S(1)} %get-tuple-element.39), channel_id=1, source_target_pairs={{0,17},{1,16},{16,1},{17,0},{2,19},{3,18},{18,3},{19,2},{4,21},{5,... | collective-permute-start | bytes 307208 | tf_op jit(solution)/shard_map/ppermute | solution.py:455
  35.1 0.5 %collective-permute-start.4 = (bf16[1,80,640]{2,1,0:T(8,128)(2,1)S(1)}, bf16[1,80,640]{2,1,0:T(8,128)(2,1)S(1)}, u32[]{:S(2)}, u32[]{:S(2)}) collective-permute-start(bf16[1,80,640]{2,1,0:T(8,128)(2,1)S(1)} %get-tuple-element.40), channel_id=1, source_target_pairs={{0,16},{1,17},{16,0},{17,1},{2,18},{3,19},{18,2},{19,3},{4,20},{5,... | collective-permute-start | bytes 307208 | tf_op jit(solution)/shard_map/ppermute | solution.py:455
  35.7 0.8 %collective-permute-start.3 = (bf16[1,80,640]{2,1,0:T(8,128)(2,1)S(1)}, bf16[1,80,640]{2,1,0:T(8,128)(2,1)S(1)}, u32[]{:S(2)}, u32[]{:S(2)}) collective-permute-start(bf16[1,80,640]{2,1,0:T(8,128)(2,1)S(1)} %get-tuple-element.41), channel_id=1, source_target_pairs={{0,1},{1,0},{16,17},{17,16},{2,3},{3,2},{18,19},{19,18},{4,5},{5,4... | collective-permute-start | bytes 307208 | tf_op jit(solution)/shard_map/ppermute | solution.py:455
  36.5 5.7 %softmax_parts.1 = (bf16[1920,1024]{1,0:T(8,128)(2,1)S(1)}, f32[8,128]{1,0:T(8,128)S(1)}) custom-call(s32[1,12]{1,0:T(1,128)S(1)} %bitcast.12, s32[1,1]{1,0:T(1,128)} %bitcast.6.first_ref, bf16[480,320]{1,0:T(8,128)(2,1)S(1)} %pad_maximum_fusion.own_ref, bf16[480,320]{1,0:T(8,128)(2,1)S(1)} %collective-permute-done.even_ref, ...), custom_call_target="tpu_custom_call" | custom-call | flops 20480000000 | bytes 102400000 | tf_op jit(solution)/shard_map/softmax_parts/pallas_call | solution.py:321
  42.2 0.0 collective-permute-done.5.refs_3_
  42.3 0.0 collective-permute-done.4.refs_2_
  42.3 0.0 collective-permute-done.3.refs_1_
  42.3 0.5 gather_sum.1.grad_ref
  42.8 0.1 collective-permute-start.7
  42.8 0.8 %collective-permute-start.6 = (bf16[160,320]{1,0:T(8,128)(2,1)S(1)}, bf16[160,320]{1,0:T(8,128)(2,1)S(1)}, u32[]{:S(2)}, u32[]{:S(2)}) collective-permute-start(bf16[160,320]{1,0:T(8,128)(2,1)S(1)} %gather_sum.1.grad_ref), channel_id=1, source_target_pairs={{0,2},{2,0},{4,6},{6,4},{8,10},{10,8},{12,14},{14,12},{1,3},{3,1},... | collective-permute-start | bytes 307208 | tf_op jit(solution)/shard_map/ppermute | solution.py:446
  43.6 2.4 %own_terms.1 = (bf16[160,320]{1,0:T(8,128)(2,1)}, f32[160,320]{1,0:T(8,128)S(1)}, f32[160,320]{1,0:T(8,128)S(1)}) custom-call(bf16[160,320]{1,0:T(8,128)(2,1)S(1)} %gather_sum.1.grad_ref, bf16[160,320]{1,0:T(8,128)(2,1)S(1)} %bitcast.11, bf16[1920,1024]{1,0:T(8,128)(2,1)S(1)} %get-tuple-element.33.held_ref), custom_call_target="tpu_custom_call" | custom-call | tf_op jit(solution)/shard_map/own_terms/pallas_call | solution.py:388
  46.0 0.0 collective-permute-done.7.odd_ref
  46.0 2.6 %collective-permute-done.6.even_ref = bf16[160,320]{1,0:T(8,128)(2,1)S(1)} collective-permute-done((bf16[160,320]{1,0:T(8,128)(2,1)S(1)}, bf16[160,320]{1,0:T(8,128)(2,1)S(1)}, u32[]{:S(2)}, u32[]{:S(2)}) %collective-permute-start.6) | collective-permute-done | bytes 102432 | tf_op jit(solution)/shard_map/ppermute | solution.py:446
  48.6 1.7 %side_terms.1 = (bf16[160,320]{1,0:T(8,128)(2,1)}, bf16[160,320]{1,0:T(8,128)(2,1)}) custom-call(bf16[160,320]{1,0:T(8,128)(2,1)S(1)} %collective-permute-done.6.even_ref, bf16[160,320]{1,0:T(8,128)(2,1)S(1)} %collective-permute-done.7.odd_ref, f32[160,320]{1,0:T(8,128)S(1)} %get-tuple-element.35.key_part_ref, ...), custom_call_target="tpu_custom_call" | custom-call | tf_op jit(solution)/shard_map/side_terms/pallas_call | solution.py:426
  (5 shorter events, 0.1 us)
Async XLA Ops:
  0.6 13.9 %copy-start.3 = (bf16[320,160]{0,1:T(8,128)(2,1)S(1)}, bf16[320,160]{0,1:T(8,128)(2,1)}, u32[]{:S(2)}) copy-start(bf16[320,160]{0,1:T(8,128)(2,1)} %param.16) | copy-start | bytes 307204
  0.6 13.9 %copy-start.4 = (bf16[320,160]{0,1:T(8,128)(2,1)S(1)}, bf16[320,160]{0,1:T(8,128)(2,1)}, u32[]{:S(2)}) copy-start(bf16[320,160]{0,1:T(8,128)(2,1)} %param.15) | copy-start | bytes 307204
  0.7 13.9 %copy-start = (bf16[320,160]{0,1:T(8,128)(2,1)S(1)}, bf16[320,160]{0,1:T(8,128)(2,1)}, u32[]{:S(2)}) copy-start(bf16[320,160]{0,1:T(8,128)(2,1)} %param.14) | copy-start | bytes 307204
  0.7 23.8 %copy-start.1 = (bf16[80,640]{1,0:T(8,128)(2,1)S(1)}, bf16[80,640]{1,0:T(8,128)(2,1)}, u32[]{:S(2)}) copy-start(bf16[80,640]{1,0:T(8,128)(2,1)} %pre_ref.1) | copy-start | bytes 307204
  7.2 29.2 %copy-start.2 = (s32[12]{0:T(128)S(1)}, s32[12]{0:T(128)}, u32[]{:S(2)}) copy-start(s32[12]{0:T(128)} %param.17) | copy-start | bytes 148
  7.3 17.2 %all-to-all-start = ((bf16[8,24,640]{2,1,0:T(8,128)(2,1)}), bf16[8,24,640]{2,1,0:T(8,128)(2,1)S(1)}, u32[]{:S(2)}, u32[]{:S(2)}) async-start(bf16[8,24,640]{2,1,0:T(8,128)(2,1)} %bitcast.13), calls=%async_computation | async-start | bytes 491520 | tf_op jit(solution)/shard_map/all_to_all | solution.py:471
  14.6 16.3 %collective-permute-start.1 = (bf16[480,320]{1,0:T(8,128)(2,1)S(1)}, bf16[480,320]{1,0:T(8,128)(2,1)S(1)}, u32[]{:S(2)}, u32[]{:S(2)}) collective-permute-start(bf16[480,320]{1,0:T(8,128)(2,1)S(1)} %pad_maximum_fusion.own_ref), channel_id=1, source_target_pairs={{0,8},{2,4},{4,2},{6,14},{8,0},{10,12},{12,10},{14,6},{1,9},{3,5},... | collective-permute-start | bytes 921608 | tf_op jit(solution)/shard_map/ppermute | solution.py:446
  14.7 16.3 %collective-permute-start = (bf16[480,320]{1,0:T(8,128)(2,1)S(1)}, bf16[480,320]{1,0:T(8,128)(2,1)S(1)}, u32[]{:S(2)}, u32[]{:S(2)}) collective-permute-start(bf16[480,320]{1,0:T(8,128)(2,1)S(1)} %pad_maximum_fusion.own_ref), channel_id=1, source_target_pairs={{0,2},{2,0},{4,6},{6,4},{8,10},{10,8},{12,14},{14,12},{1,3},{3,1},... | collective-permute-start | bytes 921608 | tf_op jit(solution)/shard_map/ppermute | solution.py:446
  31.0 1.8 %collective-permute-start.2 = (bf16[4,80,640]{2,1,0:T(8,128)(2,1)S(1)}, bf16[4,80,640]{2,1,0:T(8,128)(2,1)S(1)}, u32[]{:S(2)}, u32[]{:S(2)}) collective-permute-start(bf16[4,80,640]{2,1,0:T(8,128)(2,1)S(1)} %get-tuple-element.26), channel_id=1, source_target_pairs={{0,8},{8,0},{1,9},{9,1},{2,10},{10,2},{3,11},{11,3},{4,12},{12,4},... | collective-permute-start | bytes 1228808 | tf_op jit(solution)/shard_map/ppermute | solution.py:477
  32.9 9.3 %collective-permute-start.5 = (bf16[1,80,640]{2,1,0:T(8,128)(2,1)S(1)}, bf16[1,80,640]{2,1,0:T(8,128)(2,1)S(1)}, u32[]{:S(2)}, u32[]{:S(2)}) collective-permute-start(bf16[1,80,640]{2,1,0:T(8,128)(2,1)S(1)} %get-tuple-element.39), channel_id=1, source_target_pairs={{0,17},{1,16},{16,1},{17,0},{2,19},{3,18},{18,3},{19,2},{4,21},{5,... | collective-permute-start | bytes 307208 | tf_op jit(solution)/shard_map/ppermute | solution.py:455
  35.1 7.1 %collective-permute-start.4 = (bf16[1,80,640]{2,1,0:T(8,128)(2,1)S(1)}, bf16[1,80,640]{2,1,0:T(8,128)(2,1)S(1)}, u32[]{:S(2)}, u32[]{:S(2)}) collective-permute-start(bf16[1,80,640]{2,1,0:T(8,128)(2,1)S(1)} %get-tuple-element.40), channel_id=1, source_target_pairs={{0,16},{1,17},{16,0},{17,1},{2,18},{3,19},{18,2},{19,3},{4,20},{5,... | collective-permute-start | bytes 307208 | tf_op jit(solution)/shard_map/ppermute | solution.py:455
  35.7 6.6 %collective-permute-start.3 = (bf16[1,80,640]{2,1,0:T(8,128)(2,1)S(1)}, bf16[1,80,640]{2,1,0:T(8,128)(2,1)S(1)}, u32[]{:S(2)}, u32[]{:S(2)}) collective-permute-start(bf16[1,80,640]{2,1,0:T(8,128)(2,1)S(1)} %get-tuple-element.41), channel_id=1, source_target_pairs={{0,1},{1,0},{16,17},{17,16},{2,3},{3,2},{18,19},{19,18},{4,5},{5,4... | collective-permute-start | bytes 307208 | tf_op jit(solution)/shard_map/ppermute | solution.py:455
  42.8 3.2 %collective-permute-start.7 = (bf16[160,320]{1,0:T(8,128)(2,1)S(1)}, bf16[160,320]{1,0:T(8,128)(2,1)S(1)}, u32[]{:S(2)}, u32[]{:S(2)}) collective-permute-start(bf16[160,320]{1,0:T(8,128)(2,1)S(1)} %gather_sum.1.grad_ref), channel_id=1, source_target_pairs={{0,8},{2,4},{4,2},{6,14},{8,0},{10,12},{12,10},{14,6},{1,9},{3,5},... | collective-permute-start | bytes 307208 | tf_op jit(solution)/shard_map/ppermute | solution.py:446
  42.8 5.7 %collective-permute-start.6 = (bf16[160,320]{1,0:T(8,128)(2,1)S(1)}, bf16[160,320]{1,0:T(8,128)(2,1)S(1)}, u32[]{:S(2)}, u32[]{:S(2)}) collective-permute-start(bf16[160,320]{1,0:T(8,128)(2,1)S(1)} %gather_sum.1.grad_ref), channel_id=1, source_target_pairs={{0,2},{2,0},{4,6},{6,4},{8,10},{10,8},{12,14},{14,12},{1,3},{3,1},... | collective-permute-start | bytes 307208 | tf_op jit(solution)/shard_map/ppermute | solution.py:446

commit v9 on v8

--- a/solution.py
+++ b/solution.py
@@ -142,26 +142,20 @@
     width = weight_ref.shape[0] // (4 * heads)
     spans = lax.axis_size("span")
     core = lax.axis_index("core")
-    half = heads // 2
-
-    me = lax.axis_index("chip") * spans + lax.axis_index("span")
-
-    def head_of(n):
-        place = lax.bitwise_xor(me, n % half)
-        chip, span = lax.div(place, spans), lax.rem(place, spans)
-        return (chip * 2 + (1 - core if n < half else core)) * spans + span
-
-    copies = []
-    for h in range(heads):
+    chip = lax.axis_index("chip")
+    chips = heads // (2 * spans)
+    block = spans * width
+
+    def first_row(n, j):
+        place = lax.bitwise_xor(chip, n % chips) * 2 + (1 - core if n < chips else core)
+        return pl.multiple_of((j * (heads // spans) + place) * block, block)
+
+    pairs = []
+    for n in range(2 * chips):
         for j in range(4):
-            start = pl.multiple_of((j * heads + head_of(h)) * width, width)
-            copy = pltpu.make_async_copy(
-                weight_ref.at[pl.ds(start, width)],
-                held.at[h, pl.ds(j * width, width)],
-                sems.at[h * 4 + j],
-            )
-            copy.start()
-            copies.append(copy)
+            source = weight_ref.at[pl.ds(first_row(n, j), block)]
+            pairs.append((source, held.at[n, pl.ds(j * block, block)]))
+    copies = fetched(pairs, sems)
     label_at = slice(capacity, capacity + 1)
     if one_product(count, slots, hidden):
         pieces = [pieces_ref[p].astype(jnp.float32) for p in range(count)]
@@ -183,45 +177,47 @@
     cdf = 0.5 * (1.0 + lax.erf(pre * 0.7071067811865476))
     slope = cdf + pre * jnp.exp(-0.5 * pre * pre) * 0.3989422804014327
     grad_pre = (total * slope).T.astype(jnp.bfloat16)
-    width = 4 * width
     outgoing = []
-
-    def send(h, products):
-        for i in range(2):
-            part = products[i * width : (i + 1) * width]
-            out_ref[h + i] = part.astype(jnp.bfloat16).T
-        out_hbm = send_hbm if h < half else keep_hbm
-        copy = pltpu.make_async_copy(
-            out_ref.at[pl.ds(h, 2)], out_hbm.at[pl.ds(h % half, 2)], out_sems.at[h // 2]
-        )
+    span = lax.axis_index("span")
+
+    def send(n, product):
+        for i in range(spans):
+            parts = [product[j * block + i * width : j * block + (i + 1) * width] for j in range(4)]
+            part = jnp.concatenate(parts, 0).astype(jnp.bfloat16).T
+            out_ref[n * spans + lax.bitwise_xor(span, i)] = part
+        out_hbm = send_hbm if n < chips else keep_hbm
+        source, target = pl.ds(n * spans, spans), pl.ds(n % chips * spans, spans)
+        copy = pltpu.make_async_copy(out_ref.at[source], out_hbm.at[target], out_sems.at[n])
         outgoing.append(copy)
-        outgoing[-1].start()
+        copy.start()
 
     waiting = None
-    for h in range(0, heads, 2):
-        for copy in copies[h * 4 : h * 4 + 8]:
+    for n in range(2 * chips):
+        for copy in copies[n * 4 : n * 4 + 4]:
             copy.wait()
-        product = dot(held[h : h + 2].reshape(2 * width, hidden), grad_pre, NN)
+        product = dot(held[n], grad_pre, NN)
         if waiting is not None:
-            send(h - 2, waiting)
+            send(n - 1, waiting)
         waiting = product
-    send(heads - 2, waiting)
+    send(2 * chips - 1, waiting)
     for copy in outgoing:
         copy.wait()
 
 
 def up_pieces(pieces, pre, weight, heads, capacity):
     width = weight.shape[0] // heads
+    spans = lax.axis_size("span")
+    blocks = heads // spans
     return pl.pallas_call(
         functools.partial(up_kernel, heads, capacity),
         out_shape=[jax.ShapeDtypeStruct((heads // 2, pre.shape[0], width), jnp.bfloat16)] * 2,
         in_specs=in_vmem(2) + in_hbm(1),
         out_specs=in_hbm(2),
         scratch_shapes=[
-            pltpu.VMEM((heads, width, weight.shape[1]), jnp.bfloat16),
+            pltpu.VMEM((blocks, spans * width, weight.shape[1]), jnp.bfloat16),
             pltpu.VMEM((heads, pre.shape[0], width), jnp.bfloat16),
-            pltpu.SemaphoreType.DMA((heads * 4,)),
-            pltpu.SemaphoreType.DMA((heads // 2,)),
+            pltpu.SemaphoreType.DMA((blocks * 4,)),
+            pltpu.SemaphoreType.DMA((blocks,)),
         ],
         compiler_params=params(52),
         cost_estimate=pl.CostEstimate(
@@ -334,12 +330,36 @@
     )(lengths.reshape(1, -1), first.reshape(1, 1), own, even, odd)
 
 
+def packed_rows(columns, patches):
+    heads = columns // HEAD_DIM
+    return patches // 128 * columns + (heads + 1) // 2 * HEAD_DIM
+
+
+def packed(x):
+    columns, patches = x.shape
+    whole = patches // 128 * 128
+    parts = [x[:, at : at + 128] for at in range(0, whole, 128)]
+    tails = [x[at : at + HEAD_DIM, whole:] for at in range(0, columns, HEAD_DIM)]
+    tails += [jnp.zeros_like(tails[0])] * (len(tails) % 2)
+    parts += [jnp.concatenate(tails[i : i + 2], 1) for i in range(0, len(tails), 2)]
+    return jnp.concatenate(parts, 0)
+
+
+def unpacked(ref, h, columns, patches):
+    tiles = patches // 128
+    starts = [t * columns + h * HEAD_DIM for t in range(tiles)]
+    parts = [ref[at : at + HEAD_DIM].astype(jnp.float32) for at in starts]
+    at = tiles * columns + h // 2 * HEAD_DIM
+    tail = ref[at : at + HEAD_DIM].astype(jnp.float32)
+    return jnp.concatenate(parts + [tail[:, h % 2 * 64 : h % 2 * 64 + 64]], 1)
+
+
 def gather_kernel(count, *refs):
     _, row_count, width = refs[0].shape
     total = refs[0][0].astype(jnp.float32)
     for p in range(1, count):
         total = total + refs[p][0].astype(jnp.float32)
-    out_ref = refs[-1]
+    out_ref, packed_ref = refs[-2:]
     total = total.astype(jnp.bfloat16)
     columns = width // 4
     patch = iota((row_count, 4 * row_count), 1)
@@ -349,6 +369,7 @@
         put = jnp.where(patch == 4 * token + j, 1.0, 0.0).astype(jnp.bfloat16)
         result = result + dot(total[:, j * columns : (j + 1) * columns], put, TN)
     out_ref[...] = result.astype(jnp.bfloat16)
+    packed_ref[...] = packed(result).astype(jnp.bfloat16)
 
 
 def gathered(pieces, later):
@@ -356,9 +377,12 @@
     size = len(pieces) * row_count * width
     return pl.pallas_call(
         functools.partial(gather_kernel, len(pieces)),
-        out_shape=jax.ShapeDtypeStruct((width // 4, 4 * row_count), jnp.bfloat16),
+        out_shape=(
+            jax.ShapeDtypeStruct((width // 4, 4 * row_count), jnp.bfloat16),
+            jax.ShapeDtypeStruct((packed_rows(width // 4, 4 * row_count), 128), jnp.bfloat16),
+        ),
         in_specs=in_vmem(len(pieces) + 1),
-        out_specs=pl.BlockSpec(memory_space=VMEM),
+        out_specs=tuple(in_vmem(2)),
         compiler_params=params(16),
         cost_estimate=pl.CostEstimate(
             flops=20_000 * size, bytes_accessed=400 * size, transcendentals=0
@@ -400,13 +424,13 @@
 
 
 def side_kernel(even_ref, odd_ref, key_part_ref, value_part_ref, held_ref, key_ref, value_ref):
-    columns, patches = even_ref.shape
+    columns, patches = key_part_ref.shape
     is_even = lax.rem(lax.axis_index("grp"), 2) == 0
     rows = Rows(columns, patches)
     lanes = slice(0, 2 * patches)
     for h in range(columns // HEAD_DIM):
         cols = slice(h * HEAD_DIM, (h + 1) * HEAD_DIM)
-        even, odd = even_ref[cols].astype(jnp.float32), odd_ref[cols].astype(jnp.float32)
+        even, odd = [unpacked(x, h, columns, patches) for x in (even_ref, odd_ref)]
         left, right = jnp.where(is_even, odd, even), jnp.where(is_even, even, odd)
         wide = jnp.concatenate([left, right], 1)
         grad = wide.astype(jnp.bfloat16)
@@ -422,7 +446,7 @@
 
 
 def side_terms(even, odd, key_part, value_part, held):
-    shape = jax.ShapeDtypeStruct(even.shape, jnp.bfloat16)
+    shape = jax.ShapeDtypeStruct(key_part.shape, jnp.bfloat16)
     return pl.pallas_call(
         side_kernel,
         out_shape=(shape, shape),
@@ -478,8 +502,8 @@
     shares = (other.astype(jnp.float32) + shares.astype(jnp.float32)).astype(jnp.bfloat16)
     shares, own = lax.optimization_barrier((shares, own))
     held, held_done = softmax_parts(lengths, first, own, *sides)
-    grad = gathered(exchanged(shares, ("chip", "span")), held_done)
-    even, odd = from_pairs(grad)
+    grad, grad_packed = gathered(exchanged(shares, ("chip", "span")), held_done)
+    even, odd = from_pairs(grad_packed)
     grad_query, key_part, value_part = own_terms(grad, queries.T, held)
     grad_key, grad_value = side_terms(even, odd, key_part, value_part, held)
     return grad_query.T, grad_key.T, grad_value.T

time: 50.5 us -> 49.8 us (0.986)
  waiting for transfers between devices: 10.6 us -> 9.91 us
    ppermute x4, waiting for transfers between devices: 2.63 us -> 1.9 us  [swapped(): return lax.ppermute(x, ('core', 'grp'), sorted(partner.items()))]
where the time goes in v9:
time: 49.8 us; the launch traced here: 49.5 us
  Pallas kernels  23 us (46%)
  starting transfers between devices  15.6 us (31%)
  waiting for transfers between devices  9.91 us (20%)
  between operations  0.81 us (2%)
    all_to_all x1, starting transfers between devices, on_device(): lax.all_to_all(pieces, ('grp', 'span'), split_axis=0, concat_axis=0, tile...  7.29 us
    pallas_call x1, Pallas kernels, down_pieces(): pl.pallas_call(functools.partial(down_kernel, groups, spans, capacity, sl...  6.55 us
    all_to_all x1, waiting for transfers between devices, on_device(): lax.all_to_all(pieces, ('grp', 'span'), split_axis=0, concat_axis=0, tile...  6.28 us
    pallas_call x1, Pallas kernels, up_pieces(): pl.pallas_call(functools.partial(up_kernel, heads, capacity), out_shape=[...  6.21 us
    pallas_call x1, Pallas kernels, softmax_parts(): pl.pallas_call(softmax_kernel, out_shape=(jax.ShapeDtypeStruct((rows.tota...  5.72 us
    ppermute x4, starting transfers between devices, swapped(): return lax.ppermute(x, ('core', 'grp'), sorted(partner.items()))  4.65 us
    ppermute x3, starting transfers between devices, exchanged(): lax.ppermute(parts[d], axes, [(i, i ^ d) for i in range(count)])  3.55 us
    pallas_call x1, Pallas kernels, own_terms(): pl.pallas_call(own_kernel, out_shape=(jax.ShapeDtypeStruct(grad.shape, jn...  2.36 us
  transfers between devices with their start and end apart: 9, of which 3 were waited for; matrix products, arithmetic and copies ran while one was open for 0% of the time, Pallas kernels for 29%

profile of v9, /device:TPU:0, one launch (start us, length us, event | category | flops | bytes accessed | tf_op | source)
XLA Modules:
  0.0 49.5 jit_solution(7216666457505647582)
XLA Ops:
  0.6 0.0 copy-start.3
  0.6 0.0 copy-start.4
  0.7 0.0 copy-start
  0.7 0.0 copy-start.1
  0.7 6.5 %down_product.1 = bf16[4,2,24,640]{3,2,1,0:T(8,128)(2,1)} custom-call(s32[1,80]{1,0:T(1,128)} %bitcast.16, bf16[80,4096]{1,0:T(8,128)(2,1)} %rows_hbm.1, bf16[1280,4096]{1,0:T(8,128)(2,1)} %weight_ref.2), custom_call_target="tpu_custom_call" | custom-call | tf_op jit(solution)/shard_map/down_product/pallas_call | solution.py:118
  7.2 0.0 copy-start.2
  7.2 7.3 %all-to-all-start = ((bf16[8,24,640]{2,1,0:T(8,128)(2,1)}), bf16[8,24,640]{2,1,0:T(8,128)(2,1)S(1)}, u32[]{:S(2)}, u32[]{:S(2)}) async-start(bf16[8,24,640]{2,1,0:T(8,128)(2,1)} %bitcast.13), calls=%async_computation | async-start | bytes 491520 | tf_op jit(solution)/shard_map/all_to_all | solution.py:495
  14.5 0.0 copy-done.3
  14.5 0.0 copy-done.4
  14.6 0.1 collective-permute-start.1
  14.7 3.5 %collective-permute-start = (bf16[480,320]{1,0:T(8,128)(2,1)S(1)}, bf16[480,320]{1,0:T(8,128)(2,1)S(1)}, u32[]{:S(2)}, u32[]{:S(2)}) collective-permute-start(bf16[480,320]{1,0:T(8,128)(2,1)S(1)} %pad_maximum_fusion.own_ref), channel_id=1, source_target_pairs={{0,2},{2,0},{4,6},{6,4},{8,10},{10,8},{12,14},{14,12},{1,3},{3,1},... | collective-permute-start | bytes 921608 | tf_op jit(solution)/shard_map/ppermute | solution.py:470
  18.2 6.3 %all-to-all-done.pieces_ref = bf16[8,24,640]{2,1,0:T(8,128)(2,1)S(1)} async-done(((bf16[8,24,640]{2,1,0:T(8,128)(2,1)}), bf16[8,24,640]{2,1,0:T(8,128)(2,1)S(1)}, u32[]{:S(2)}, u32[]{:S(2)}) %all-to-all-start) | async-done | bytes 245792 | tf_op jit(solution)/shard_map/all_to_all | solution.py:495
  24.4 6.2 %up_product.1 = (bf16[4,80,640]{2,1,0:T(8,128)(2,1)S(1)}, bf16[4,80,640]{2,1,0:T(8,128)(2,1)S(1)}) custom-call(bf16[8,24,640]{2,1,0:T(8,128)(2,1)S(1)} %all-to-all-done.pieces_ref, bf16[80,640]{1,0:T(8,128)(2,1)S(1)} %copy-done.1, bf16[5120,640]{1,0:T(8,128)(2,1)} %weight_ref.3), custom_call_target="tpu_custom_call" | custom-call | flops 2097152000 | bytes 26214400 | tf_op jit(solution)/shard_map/up_product/pallas_call | solution.py:211
  30.7 0.0 collective-permute-done.1.odd_ref
  30.7 0.0 collective-permute-done.even_ref
  30.7 0.1 collective-permute-start.2
  30.8 1.7 %collective-permute-done.2 = bf16[4,80,640]{2,1,0:T(8,128)(2,1)S(1)} collective-permute-done((bf16[4,80,640]{2,1,0:T(8,128)(2,1)S(1)}, bf16[4,80,640]{2,1,0:T(8,128)(2,1)S(1)}, u32[]{:S(2)}, u32[]{:S(2)}) %collective-permute-start.2) | collective-permute-done | bytes 409632 | tf_op jit(solution)/shard_map/ppermute | solution.py:501
  32.5 0.1 add_convert_fusion
  32.6 2.2 %collective-permute-start.5 = (bf16[1,80,640]{2,1,0:T(8,128)(2,1)S(1)}, bf16[1,80,640]{2,1,0:T(8,128)(2,1)S(1)}, u32[]{:S(2)}, u32[]{:S(2)}) collective-permute-start(bf16[1,80,640]{2,1,0:T(8,128)(2,1)S(1)} %get-tuple-element.43), channel_id=1, source_target_pairs={{0,17},{1,16},{16,1},{17,0},{2,19},{3,18},{18,3},{19,2},{4,21},{5,... | collective-permute-start | bytes 307208 | tf_op jit(solution)/shard_map/ppermute | solution.py:479
  34.9 0.5 %collective-permute-start.4 = (bf16[1,80,640]{2,1,0:T(8,128)(2,1)S(1)}, bf16[1,80,640]{2,1,0:T(8,128)(2,1)S(1)}, u32[]{:S(2)}, u32[]{:S(2)}) collective-permute-start(bf16[1,80,640]{2,1,0:T(8,128)(2,1)S(1)} %get-tuple-element.44), channel_id=1, source_target_pairs={{0,16},{1,17},{16,0},{17,1},{2,18},{3,19},{18,2},{19,3},{4,20},{5,... | collective-permute-start | bytes 307208 | tf_op jit(solution)/shard_map/ppermute | solution.py:479
  35.4 0.8 %collective-permute-start.3 = (bf16[1,80,640]{2,1,0:T(8,128)(2,1)S(1)}, bf16[1,80,640]{2,1,0:T(8,128)(2,1)S(1)}, u32[]{:S(2)}, u32[]{:S(2)}) collective-permute-start(bf16[1,80,640]{2,1,0:T(8,128)(2,1)S(1)} %get-tuple-element.45), channel_id=1, source_target_pairs={{0,1},{1,0},{16,17},{17,16},{2,3},{3,2},{18,19},{19,18},{4,5},{5,4... | collective-permute-start | bytes 307208 | tf_op jit(solution)/shard_map/ppermute | solution.py:479
  36.2 5.7 %softmax_parts.1 = (bf16[1920,1024]{1,0:T(8,128)(2,1)S(1)}, f32[8,128]{1,0:T(8,128)S(1)}) custom-call(s32[1,12]{1,0:T(1,128)S(1)} %bitcast.12, s32[1,1]{1,0:T(1,128)} %bitcast.6.first_ref, bf16[480,320]{1,0:T(8,128)(2,1)S(1)} %pad_maximum_fusion.own_ref, bf16[480,320]{1,0:T(8,128)(2,1)S(1)} %collective-permute-done.even_ref, ...), custom_call_target="tpu_custom_call" | custom-call | flops 20480000000 | bytes 102400000 | tf_op jit(solution)/shard_map/softmax_parts/pallas_call | solution.py:317
  41.9 0.0 collective-permute-done.5.refs_3_
  41.9 0.0 collective-permute-done.4.refs_2_
  42.0 0.0 collective-permute-done.3.refs_1_
  42.0 0.5 %gather_sum.1 = (bf16[160,320]{1,0:T(8,128)(2,1)S(1)}, bf16[400,128]{1,0:T(8,128)(2,1)S(1)}) custom-call(bf16[1,80,640]{2,1,0:T(8,128)(2,1)S(1)} %get-tuple-element.46.refs_0_, bf16[1,80,640]{2,1,0:T(8,128)(2,1)S(1)} %collective-permute-done.3.refs_1_, bf16[1,80,640]{2,1,0:T(8,128)(2,1)S(1)} %collective-permute-done.4.refs_2_, ...), custom_call_target="tpu_custom_call" | custom-call | flops 4096000000 | bytes 81920000 | tf_op jit(solution)/shard_map/gather_sum/pallas_call | solution.py:378
  42.5 0.1 collective-permute-start.7
  42.5 1.0 %collective-permute-start.6 = (bf16[400,128]{1,0:T(8,128)(2,1)S(1)}, bf16[400,128]{1,0:T(8,128)(2,1)S(1)}, u32[]{:S(2)}, u32[]{:S(2)}) collective-permute-start(bf16[400,128]{1,0:T(8,128)(2,1)S(1)} %get-tuple-element.38), channel_id=1, source_target_pairs={{0,2},{2,0},{4,6},{6,4},{8,10},{10,8},{12,14},{14,12},{1,3},{3,1},... | collective-permute-start | bytes 307208 | tf_op jit(solution)/shard_map/ppermute | solution.py:470
  43.6 2.4 %own_terms.1 = (bf16[160,320]{1,0:T(8,128)(2,1)}, f32[160,320]{1,0:T(8,128)S(1)}, f32[160,320]{1,0:T(8,128)S(1)}) custom-call(bf16[160,320]{1,0:T(8,128)(2,1)S(1)} %get-tuple-element.35.grad_ref, bf16[160,320]{1,0:T(8,128)(2,1)S(1)} %bitcast.11, bf16[1920,1024]{1,0:T(8,128)(2,1)S(1)} %get-tuple-element.36.held_ref), custom_call_target="tpu_custom_call" | custom-call | tf_op jit(solution)/shard_map/own_terms/pallas_call | solution.py:412
  45.9 0.0 collective-permute-done.7.odd_ref
  46.0 1.9 %collective-permute-done.6.even_ref = bf16[400,128]{1,0:T(8,128)(2,1)S(1)} collective-permute-done((bf16[400,128]{1,0:T(8,128)(2,1)S(1)}, bf16[400,128]{1,0:T(8,128)(2,1)S(1)}, u32[]{:S(2)}, u32[]{:S(2)}) %collective-permute-start.6) | collective-permute-done | bytes 102432 | tf_op jit(solution)/shard_map/ppermute | solution.py:470
  47.8 1.7 %side_terms.1 = (bf16[160,320]{1,0:T(8,128)(2,1)}, bf16[160,320]{1,0:T(8,128)(2,1)}) custom-call(bf16[400,128]{1,0:T(8,128)(2,1)S(1)} %collective-permute-done.6.even_ref, bf16[400,128]{1,0:T(8,128)(2,1)S(1)} %collective-permute-done.7.odd_ref, f32[160,320]{1,0:T(8,128)S(1)} %get-tuple-element.39.key_part_ref, ...), custom_call_target="tpu_custom_call" | custom-call | tf_op jit(solution)/shard_map/side_terms/pallas_call | solution.py:450
  (5 shorter events, 0.1 us)
Async XLA Ops:
  0.6 13.9 %copy-start.3 = (bf16[320,160]{0,1:T(8,128)(2,1)S(1)}, bf16[320,160]{0,1:T(8,128)(2,1)}, u32[]{:S(2)}) copy-start(bf16[320,160]{0,1:T(8,128)(2,1)} %param.16) | copy-start | bytes 307204
  0.6 13.9 %copy-start.4 = (bf16[320,160]{0,1:T(8,128)(2,1)S(1)}, bf16[320,160]{0,1:T(8,128)(2,1)}, u32[]{:S(2)}) copy-start(bf16[320,160]{0,1:T(8,128)(2,1)} %param.15) | copy-start | bytes 307204
  0.7 13.9 %copy-start = (bf16[320,160]{0,1:T(8,128)(2,1)S(1)}, bf16[320,160]{0,1:T(8,128)(2,1)}, u32[]{:S(2)}) copy-start(bf16[320,160]{0,1:T(8,128)(2,1)} %param.14) | copy-start | bytes 307204
  0.7 23.8 %copy-start.1 = (bf16[80,640]{1,0:T(8,128)(2,1)S(1)}, bf16[80,640]{1,0:T(8,128)(2,1)}, u32[]{:S(2)}) copy-start(bf16[80,640]{1,0:T(8,128)(2,1)} %pre_ref.1) | copy-start | bytes 307204
  7.2 29.0 %copy-start.2 = (s32[12]{0:T(128)S(1)}, s32[12]{0:T(128)}, u32[]{:S(2)}) copy-start(s32[12]{0:T(128)} %param.17) | copy-start | bytes 148
  7.2 17.2 %all-to-all-start = ((bf16[8,24,640]{2,1,0:T(8,128)(2,1)}), bf16[8,24,640]{2,1,0:T(8,128)(2,1)S(1)}, u32[]{:S(2)}, u32[]{:S(2)}) async-start(bf16[8,24,640]{2,1,0:T(8,128)(2,1)} %bitcast.13), calls=%async_computation | async-start | bytes 491520 | tf_op jit(solution)/shard_map/all_to_all | solution.py:495
  14.6 16.0 %collective-permute-start.1 = (bf16[480,320]{1,0:T(8,128)(2,1)S(1)}, bf16[480,320]{1,0:T(8,128)(2,1)S(1)}, u32[]{:S(2)}, u32[]{:S(2)}) collective-permute-start(bf16[480,320]{1,0:T(8,128)(2,1)S(1)} %pad_maximum_fusion.own_ref), channel_id=1, source_target_pairs={{0,8},{2,4},{4,2},{6,14},{8,0},{10,12},{12,10},{14,6},{1,9},{3,5},... | collective-permute-start | bytes 921608 | tf_op jit(solution)/shard_map/ppermute | solution.py:470
  14.7 16.0 %collective-permute-start = (bf16[480,320]{1,0:T(8,128)(2,1)S(1)}, bf16[480,320]{1,0:T(8,128)(2,1)S(1)}, u32[]{:S(2)}, u32[]{:S(2)}) collective-permute-start(bf16[480,320]{1,0:T(8,128)(2,1)S(1)} %pad_maximum_fusion.own_ref), channel_id=1, source_target_pairs={{0,2},{2,0},{4,6},{6,4},{8,10},{10,8},{12,14},{14,12},{1,3},{3,1},... | collective-permute-start | bytes 921608 | tf_op jit(solution)/shard_map/ppermute | solution.py:470
  30.7 1.8 %collective-permute-start.2 = (bf16[4,80,640]{2,1,0:T(8,128)(2,1)S(1)}, bf16[4,80,640]{2,1,0:T(8,128)(2,1)S(1)}, u32[]{:S(2)}, u32[]{:S(2)}) collective-permute-start(bf16[4,80,640]{2,1,0:T(8,128)(2,1)S(1)} %get-tuple-element.28), channel_id=1, source_target_pairs={{0,8},{8,0},{1,9},{9,1},{2,10},{10,2},{3,11},{11,3},{4,12},{12,4},... | collective-permute-start | bytes 1228808 | tf_op jit(solution)/shard_map/ppermute | solution.py:501
  32.6 9.3 %collective-permute-start.5 = (bf16[1,80,640]{2,1,0:T(8,128)(2,1)S(1)}, bf16[1,80,640]{2,1,0:T(8,128)(2,1)S(1)}, u32[]{:S(2)}, u32[]{:S(2)}) collective-permute-start(bf16[1,80,640]{2,1,0:T(8,128)(2,1)S(1)} %get-tuple-element.43), channel_id=1, source_target_pairs={{0,17},{1,16},{16,1},{17,0},{2,19},{3,18},{18,3},{19,2},{4,21},{5,... | collective-permute-start | bytes 307208 | tf_op jit(solution)/shard_map/ppermute | solution.py:479
  34.9 7.1 %collective-permute-start.4 = (bf16[1,80,640]{2,1,0:T(8,128)(2,1)S(1)}, bf16[1,80,640]{2,1,0:T(8,128)(2,1)S(1)}, u32[]{:S(2)}, u32[]{:S(2)}) collective-permute-start(bf16[1,80,640]{2,1,0:T(8,128)(2,1)S(1)} %get-tuple-element.44), channel_id=1, source_target_pairs={{0,16},{1,17},{16,0},{17,1},{2,18},{3,19},{18,2},{19,3},{4,20},{5,... | collective-permute-start | bytes 307208 | tf_op jit(solution)/shard_map/ppermute | solution.py:479
  35.4 6.6 %collective-permute-start.3 = (bf16[1,80,640]{2,1,0:T(8,128)(2,1)S(1)}, bf16[1,80,640]{2,1,0:T(8,128)(2,1)S(1)}, u32[]{:S(2)}, u32[]{:S(2)}) collective-permute-start(bf16[1,80,640]{2,1,0:T(8,128)(2,1)S(1)} %get-tuple-element.45), channel_id=1, source_target_pairs={{0,1},{1,0},{16,17},{17,16},{2,3},{3,2},{18,19},{19,18},{4,5},{5,4... | collective-permute-start | bytes 307208 | tf_op jit(solution)/shard_map/ppermute | solution.py:479
  42.5 3.5 %collective-permute-start.7 = (bf16[400,128]{1,0:T(8,128)(2,1)S(1)}, bf16[400,128]{1,0:T(8,128)(2,1)S(1)}, u32[]{:S(2)}, u32[]{:S(2)}) collective-permute-start(bf16[400,128]{1,0:T(8,128)(2,1)S(1)} %get-tuple-element.38), channel_id=1, source_target_pairs={{0,8},{2,4},{4,2},{6,14},{8,0},{10,12},{12,10},{14,6},{1,9},{3,5},... | collective-permute-start | bytes 307208 | tf_op jit(solution)/shard_map/ppermute | solution.py:470
  42.5 5.3 %collective-permute-start.6 = (bf16[400,128]{1,0:T(8,128)(2,1)S(1)}, bf16[400,128]{1,0:T(8,128)(2,1)S(1)}, u32[]{:S(2)}, u32[]{:S(2)}) collective-permute-start(bf16[400,128]{1,0:T(8,128)(2,1)S(1)} %get-tuple-element.38), channel_id=1, source_target_pairs={{0,2},{2,0},{4,6},{6,4},{8,10},{10,8},{12,14},{14,12},{1,3},{3,1},... | collective-permute-start | bytes 307208 | tf_op jit(solution)/shard_map/ppermute | solution.py:470

commit v10 on v9

--- a/solution.py
+++ b/solution.py
@@ -139,22 +139,17 @@
               sems, out_sems):
     row_count, hidden = pre_ref.shape
     count, slots, _ = pieces_ref.shape
-    width = weight_ref.shape[0] // (4 * heads)
+    width = weight_ref.shape[2] // lax.axis_size("span")
     spans = lax.axis_size("span")
     core = lax.axis_index("core")
     chip = lax.axis_index("chip")
     chips = heads // (2 * spans)
     block = spans * width
 
-    def first_row(n, j):
-        place = lax.bitwise_xor(chip, n % chips) * 2 + (1 - core if n < chips else core)
-        return pl.multiple_of((j * (heads // spans) + place) * block, block)
-
     pairs = []
     for n in range(2 * chips):
-        for j in range(4):
-            source = weight_ref.at[pl.ds(first_row(n, j), block)]
-            pairs.append((source, held.at[n, pl.ds(j * block, block)]))
+        place = lax.bitwise_xor(chip, n % chips) * 2 + (1 - core if n < chips else core)
+        pairs.append((weight_ref.at[:, place], held.at[n]))
     copies = fetched(pairs, sems)
     label_at = slice(capacity, capacity + 1)
     if one_product(count, slots, hidden):
@@ -193,9 +188,8 @@
 
     waiting = None
     for n in range(2 * chips):
-        for copy in copies[n * 4 : n * 4 + 4]:
-            copy.wait()
-        product = dot(held[n], grad_pre, NN)
+        copies[n].wait()
+        product = dot(held[n].reshape(4 * block, hidden), grad_pre, NN)
         if waiting is not None:
             send(n - 1, waiting)
         waiting = product
@@ -214,9 +208,9 @@
         in_specs=in_vmem(2) + in_hbm(1),
         out_specs=in_hbm(2),
         scratch_shapes=[
-            pltpu.VMEM((blocks, spans * width, weight.shape[1]), jnp.bfloat16),
+            pltpu.VMEM((blocks, 4, spans * width // 4, weight.shape[1]), jnp.bfloat16),
             pltpu.VMEM((heads, pre.shape[0], width), jnp.bfloat16),
-            pltpu.SemaphoreType.DMA((blocks * 4,)),
+            pltpu.SemaphoreType.DMA((blocks,)),
             pltpu.SemaphoreType.DMA((blocks,)),
         ],
         compiler_params=params(52),
@@ -224,37 +218,41 @@
             flops=8 * pre.shape[0] * weight.size, bytes_accessed=8 * weight.size, transcendentals=0
         ),
         name="up_product",
-    )(pieces, pre, weight)
+    )(pieces, pre, weight.reshape(4, blocks, -1, weight.shape[1]))
 
 
 class Rows:
     def __init__(self, columns, patches):
         heads = columns // HEAD_DIM
         self.lanes = -(-3 * patches // 128) * 128
-        self.side_lanes = -(-2 * patches // 128) * 128
         self.columns, self.patches = columns, patches
-        self.values, self.keys, self.queries, self.attended = [i * columns for i in range(4)]
-        self.probs_at = 4 * columns
-        self.side_at = self.probs_at + heads * patches
-        self.total = self.side_at + heads * patches
+        self.values, self.keys, self.probs_at = 0, columns, 2 * columns
+        self.total = 2 * columns + heads * patches
 
     def head(self, start, h):
         return slice(start + h * HEAD_DIM, start + (h + 1) * HEAD_DIM)
 
-    def kind(self, start, count=1):
-        return slice(start, start + count * self.columns)
+    def kind(self, start):
+        return slice(start, start + self.columns)
 
     def probs(self, h):
         return slice(self.probs_at + h * self.patches, self.probs_at + (h + 1) * self.patches)
 
-    def side_probs(self, h):
-        return slice(self.side_at + h * self.patches, self.side_at + (h + 1) * self.patches)
-
-
-def softmax_kernel(lengths_ref, first_ref, own_ref, even_ref, odd_ref, held, done_ref):
+    def side(self, i):
+        start = i * self.total
+        return start, start + self.columns
+
+    def side_probs(self, i, h):
+        start = i * self.total + self.probs_at + h * self.patches
+        return slice(start, start + self.patches)
+
+
+def softmax_kernel(lengths_ref, first_ref, own_ref, odd_ref, even_ref, held, side_ref, done_ref):
     columns, patches = own_ref.shape[0] // 3, own_ref.shape[1]
     rows = Rows(columns, patches)
-    is_even = lax.rem(lax.axis_index("grp"), 2) == 0
+    heads = columns // HEAD_DIM
+    step_even = 1 - 2 * lax.rem(lax.axis_index("grp"), 2)
+    offsets = (0, -step_even, step_even)
     first = first_ref[0, 0]
 
     def image_of(shape, dim, block):
@@ -268,48 +266,44 @@
         start = (jnp.where(token < 0, -1, 0), jnp.int32(0))
         return lax.fori_loop(0, lengths_ref.shape[1], step, start)[0]
 
-    down = [image_of((patches, 1), 0, b) for b in (0, -1, 1)]
-    across = [image_of((1, patches), 1, b) for b in (0, -1, 1)]
-
-    def kind(block, t, h=None):
-        start = t * columns + (0 if h is None else h * HEAD_DIM)
-        at = slice(start, start + (columns if h is None else HEAD_DIM))
+    down = [image_of((patches, 1), 0, b) for b in offsets]
+    across = [image_of((1, patches), 1, b) for b in offsets]
+
+    def kind(block, t, h):
         if block == 0:
-            return own_ref[at]
-        before, after = (odd_ref, even_ref) if block == 1 else (even_ref, odd_ref)
-        return jnp.where(is_even, before[at], after[at])
-
-    def wide(t, which, h=None):
-        parts = [kind(b, t, h).astype(jnp.float32) for b in which]
-        return jnp.concatenate(parts, 1).astype(jnp.bfloat16)
+            start = t * columns + h * HEAD_DIM
+            return own_ref[start : start + HEAD_DIM].astype(jnp.float32)
+        return unpacked((odd_ref, even_ref)[block - 1], t * heads + h, 3 * columns, patches)
+
+    def wide(t, which, h):
+        return jnp.concatenate([kind(b, t, h) for b in which], 1).astype(jnp.bfloat16)
 
     def softmax(queries, keys, same):
         scores = jnp.where(same, dot(queries, keys, TN) * SCALE, -jnp.inf)
         weights = jnp.exp(scores - jnp.max(scores, 1, keepdims=True))
         return weights * (1.0 / jnp.sum(weights, 1, keepdims=True))
 
-    held[rows.kind(rows.values), : 3 * patches] = wide(2, (0, 1, 2))
-    held[rows.kind(rows.keys), : 3 * patches] = wide(1, (0, 1, 2))
-    held[rows.kind(rows.queries), : 2 * patches] = wide(0, (1, 2))
+    for h in range(heads):
+        held[rows.head(rows.values, h), : 3 * patches] = wide(2, (0, 1, 2), h)
+        held[rows.head(rows.keys, h), : 3 * patches] = wide(1, (0, 1, 2), h)
     same_own = down[0] == jnp.concatenate(across, 1)
     same_side = [down[b] == jnp.concatenate([across[0], across[b]], 1) for b in (1, 2)]
-    for h in range(columns // HEAD_DIM):
+    for h in range(heads):
         keys = held[rows.head(rows.keys, h), : 3 * patches]
-        probs = softmax(kind(0, 0, h), keys, same_own)
+        probs = softmax(kind(0, 0, h).astype(jnp.bfloat16), keys, same_own)
         held[rows.probs(h), : 3 * patches] = probs.astype(jnp.bfloat16)
-        side, attended = [], []
-        for b in (1, 2):
-            probs = softmax(kind(b, 0, h), wide(1, (0, b), h), same_side[b - 1])
+        for i, b in enumerate((1, 2)):
+            queries_at, attended_at = rows.side(i)
+            queries = kind(b, 0, h).astype(jnp.bfloat16)
+            probs = softmax(queries, wide(1, (0, b), h), same_side[i])
             seen = dot(probs.astype(jnp.bfloat16), wide(2, (0, b), h), NT)
-            attended.append(seen.T)
-            side.append(probs[:, :patches].T)
-        held[rows.side_probs(h), : 2 * patches] = jnp.concatenate(side, 1).astype(jnp.bfloat16)
-        attended = jnp.concatenate(attended, 1).astype(jnp.bfloat16)
-        held[rows.head(rows.attended, h), : 2 * patches] = attended
+            side_ref[rows.head(queries_at, h)] = queries
+            side_ref[rows.head(attended_at, h)] = seen.T.astype(jnp.bfloat16)
+            side_ref[rows.side_probs(i, h)] = probs[:, :patches].T.astype(jnp.bfloat16)
     done_ref[...] = jnp.zeros(done_ref.shape, jnp.float32)
 
 
-def softmax_parts(lengths, first, own, even, odd):
+def softmax_parts(lengths, first, own, odd, even):
     columns, patches = own.shape[0] // 3, own.shape[1]
     rows = Rows(columns, patches)
     smem = pl.BlockSpec(memory_space=pltpu.MemorySpace.SMEM)
@@ -318,16 +312,17 @@
         softmax_kernel,
         out_shape=(
             jax.ShapeDtypeStruct((rows.total, rows.lanes), jnp.bfloat16),
+            jax.ShapeDtypeStruct((2 * rows.total, patches), jnp.bfloat16),
             jax.ShapeDtypeStruct((8, 128), jnp.float32),
         ),
         in_specs=[smem, smem] + in_vmem(3),
-        out_specs=tuple(in_vmem(2)),
+        out_specs=tuple(in_vmem(3)),
         compiler_params=params(32),
         cost_estimate=pl.CostEstimate(
             flops=100_000 * work, bytes_accessed=500 * work, transcendentals=9 * work
         ),
         name="softmax_parts",
-    )(lengths.reshape(1, -1), first.reshape(1, 1), own, even, odd)
+    )(lengths.reshape(1, -1), first.reshape(1, 1), own, odd, even)
 
 
 def packed_rows(columns, patches):
@@ -423,38 +418,37 @@
     )(grad, own, held)
 
 
-def side_kernel(even_ref, odd_ref, key_part_ref, value_part_ref, held_ref, key_ref, value_ref):
+def side_kernel(i, grad_ref, key_part_ref, value_part_ref, held_ref, side_ref, key_ref, value_ref):
     columns, patches = key_part_ref.shape
-    is_even = lax.rem(lax.axis_index("grp"), 2) == 0
     rows = Rows(columns, patches)
-    lanes = slice(0, 2 * patches)
+    queries_at, attended_at = rows.side(i)
     for h in range(columns // HEAD_DIM):
         cols = slice(h * HEAD_DIM, (h + 1) * HEAD_DIM)
-        even, odd = [unpacked(x, h, columns, patches) for x in (even_ref, odd_ref)]
-        left, right = jnp.where(is_even, odd, even), jnp.where(is_even, even, odd)
-        wide = jnp.concatenate([left, right], 1)
+        wide = unpacked(grad_ref, h, columns, patches)
         grad = wide.astype(jnp.bfloat16)
         slope = dot(held_ref[rows.head(rows.values, h), :patches], grad, TN)
-        attended = held_ref[rows.head(rows.attended, h), lanes].astype(jnp.float32)
+        attended = side_ref[rows.head(attended_at, h)].astype(jnp.float32)
         delta = jnp.sum(wide * attended, 0, keepdims=True)
-        probs = held_ref[rows.side_probs(h), lanes]
+        probs = side_ref[rows.side_probs(i, h)]
         value = dot(probs, grad, NT)
         scores = (probs.astype(jnp.float32) * (slope - delta)).astype(jnp.bfloat16)
-        key = dot(scores, held_ref[rows.head(rows.queries, h), lanes], NT)
-        key_ref[cols] = ((key_part_ref[cols] + key.T) * SCALE).astype(jnp.bfloat16)
-        value_ref[cols] = (value_part_ref[cols] + value.T).astype(jnp.bfloat16)
-
-
-def side_terms(even, odd, key_part, value_part, held):
-    shape = jax.ShapeDtypeStruct(key_part.shape, jnp.bfloat16)
+        key = dot(scores, side_ref[rows.head(queries_at, h)], NT)
+        key = key_part_ref[cols] + key.T
+        key_ref[cols] = (key * SCALE if i == 1 else key).astype(key_ref.dtype)
+        value_ref[cols] = (value_part_ref[cols] + value.T).astype(value_ref.dtype)
+
+
+def side_terms(i, grad, key_part, value_part, held, side):
+    kind = jnp.bfloat16 if i == 1 else jnp.float32
+    shape = jax.ShapeDtypeStruct(key_part.shape, kind)
     return pl.pallas_call(
-        side_kernel,
+        functools.partial(side_kernel, i),
         out_shape=(shape, shape),
         in_specs=in_vmem(5),
         out_specs=tuple(in_vmem(2)),
         compiler_params=params(24),
         name="side_terms",
-    )(even, odd, key_part, value_part, held)
+    )(grad, key_part, value_part, held, side)
 
 
 def from_pairs(x):
@@ -473,10 +467,9 @@
 
 
 def exchanged(pieces, axes):
-    count = pieces.shape[0]
-    parts = [pieces[d : d + 1] for d in range(count)]
-    return parts[:1] + [
-        lax.ppermute(parts[d], axes, [(i, i ^ d) for i in range(count)]) for d in range(1, count)
+    count = len(pieces)
+    return pieces[:1] + [
+        lax.ppermute(pieces[d], axes, [(i, i ^ d) for i in range(count)]) for d in range(1, count)
     ]
 
 
@@ -494,18 +487,20 @@
     )
     arrived = lax.all_to_all(pieces, ("grp", "span"), split_axis=0, concat_axis=0, tiled=True)
     own = jnp.concatenate([queries.T, key_states.T, value_states.T], 0)
-    sides = from_pairs(own)
+    even, odd = from_pairs(packed(own))
     first = lax.axis_index("grp") * row_count
     other, shares = up_pieces(arrived, pre_act, w_up, heads, capacity)
-    other, *sides = lax.optimization_barrier((other, *sides))
+    other, odd, even = lax.optimization_barrier((other, odd, even))
     other = lax.ppermute(other, "core", [(0, 1), (1, 0)])
     shares = (other.astype(jnp.float32) + shares.astype(jnp.float32)).astype(jnp.bfloat16)
     shares, own = lax.optimization_barrier((shares, own))
-    held, held_done = softmax_parts(lengths, first, own, *sides)
+    held, side, held_done = softmax_parts(lengths, first, own, odd, even)
+    shares = [shares[d : d + 1] for d in range(shares.shape[0])]
     grad, grad_packed = gathered(exchanged(shares, ("chip", "span")), held_done)
     even, odd = from_pairs(grad_packed)
     grad_query, key_part, value_part = own_terms(grad, queries.T, held)
-    grad_key, grad_value = side_terms(even, odd, key_part, value_part, held)
+    parts = side_terms(0, odd, key_part, value_part, held, side)
+    grad_key, grad_value = side_terms(1, even, *parts, held, side)
     return grad_query.T, grad_key.T, grad_value.T
 
 

time: 49.8 us -> 49.1 us (0.986)
  starting transfers between devices: 15.6 us -> 13.5 us
  waiting for transfers between devices: 9.91 us -> 10.9 us
    ppermute x4, starting transfers between devices: 4.65 us -> 2.58 us  [swapped(): return lax.ppermute(x, ('core', 'grp'), sorted(partner.items()))]
    all_to_all x1, waiting for transfers between devices: 6.28 us -> 7.32 us  [on_device(): lax.all_to_all(pieces, ('grp', 'span'), split_axis=0, concat_axis=0, tile...]
    pallas_call x1 -> x2, Pallas kernels: 1.7 us -> 2.09 us  [side_terms(): pl.pallas_call(functools.partial(side_kernel, i), out_shape=(shape, shape...]
  transfers between devices with their start and end apart: 9 -> 9, of which waited for: 3 -> 3; matrix products, arithmetic and copies ran while one was open for 0% -> 1% of each run, Pallas kernels for 29% -> 30%
where the time goes in v10:
time: 49.1 us; the launch traced here: 48.9 us
  Pallas kernels  23.2 us (47%)
  starting transfers between devices  13.5 us (27%)
  waiting for transfers between devices  10.9 us (22%)
  between operations  0.85 us (2%)
    all_to_all x1, waiting for transfers between devices, on_device(): lax.all_to_all(pieces, ('grp', 'span'), split_axis=0, concat_axis=0, tile...  7.32 us
    all_to_all x1, starting transfers between devices, on_device(): lax.all_to_all(pieces, ('grp', 'span'), split_axis=0, concat_axis=0, tile...  7.29 us
    pallas_call x1, Pallas kernels, down_pieces(): pl.pallas_call(functools.partial(down_kernel, groups, spans, capacity, sl...  6.58 us
    pallas_call x1, Pallas kernels, up_pieces(): pl.pallas_call(functools.partial(up_kernel, heads, capacity), out_shape=[...  6.14 us
    pallas_call x1, Pallas kernels, softmax_parts(): pl.pallas_call(softmax_kernel, out_shape=(jax.ShapeDtypeStruct((rows.tota...  5.53 us
    ppermute x3, starting transfers between devices, exchanged(): lax.ppermute(pieces[d], axes, [(i, i ^ d) for i in range(count)])  3.55 us
    ppermute x4, starting transfers between devices, swapped(): return lax.ppermute(x, ('core', 'grp'), sorted(partner.items()))  2.58 us
    pallas_call x1, Pallas kernels, own_terms(): pl.pallas_call(own_kernel, out_shape=(jax.ShapeDtypeStruct(grad.shape, jn...  2.36 us
  transfers between devices with their start and end apart: 9, of which 3 were waited for; matrix products, arithmetic and copies ran while one was open for 1% of the time, Pallas kernels for 30%

profile of v10, /device:TPU:0, one launch (start us, length us, event | category | flops | bytes accessed | tf_op | source)
XLA Modules:
  0.0 48.9 jit_solution(11152248365595499137)
XLA Ops:
  0.7 6.6 %down_product.1 = bf16[4,2,24,640]{3,2,1,0:T(8,128)(2,1)} custom-call(s32[1,80]{1,0:T(1,128)} %bitcast.20, bf16[80,4096]{1,0:T(8,128)(2,1)} %rows_hbm.1, bf16[1280,4096]{1,0:T(8,128)(2,1)} %weight_ref.1), custom_call_target="tpu_custom_call" | custom-call | tf_op jit(solution)/shard_map/down_product/pallas_call | solution.py:118
  7.3 0.0 copy-start.2
  7.3 7.3 %all-to-all-start = ((bf16[8,24,640]{2,1,0:T(8,128)(2,1)}), bf16[8,24,640]{2,1,0:T(8,128)(2,1)S(1)}, u32[]{:S(2)}, u32[]{:S(2)}) async-start(bf16[8,24,640]{2,1,0:T(8,128)(2,1)} %bitcast.15), calls=%async_computation | async-start | bytes 491520 | tf_op jit(solution)/shard_map/all_to_all | solution.py:488
  14.6 0.0 copy-done.3
  14.7 0.1 maximum_dynamic-update-slice_fusion.2
  14.8 0.1 maximum_dynamic-update-slice_fusion.1
  14.9 0.1 maximum_dynamic-update-slice_fusion
  15.0 2.1 %collective-permute-start.1 = (bf16[1200,128]{1,0:T(8,128)(2,1)S(1)}, bf16[1200,128]{1,0:T(8,128)(2,1)S(1)}, u32[]{:S(2)}, u32[]{:S(2)}) collective-permute-start(bf16[1200,128]{1,0:T(8,128)(2,1)S(1)} %maximum_dynamic-update-slice_fusion), channel_id=1, source_target_pairs={{0,2},{2,0},{4,6},{6,4},{8,10},{10,8},{12,14},{14,12},{1,3},{3,1},... | collective-permute-start | bytes 921608 | tf_op jit(solution)/shard_map/ppermute | solution.py:464
  17.1 0.0 collective-permute-start
  17.1 7.3 %all-to-all-done.pieces_ref = bf16[8,24,640]{2,1,0:T(8,128)(2,1)S(1)} async-done(((bf16[8,24,640]{2,1,0:T(8,128)(2,1)}), bf16[8,24,640]{2,1,0:T(8,128)(2,1)S(1)}, u32[]{:S(2)}, u32[]{:S(2)}) %all-to-all-start) | async-done | bytes 245792 | tf_op jit(solution)/shard_map/all_to_all | solution.py:488
  24.4 6.1 %up_product.1 = (bf16[4,80,640]{2,1,0:T(8,128)(2,1)S(1)}, bf16[4,80,640]{2,1,0:T(8,128)(2,1)S(1)}) custom-call(bf16[8,24,640]{2,1,0:T(8,128)(2,1)S(1)} %all-to-all-done.pieces_ref, bf16[80,640]{1,0:T(8,128)(2,1)S(1)} %copy-done.1, bf16[4,4,320,640]{3,2,1,0:T(8,128)(2,1)} %bitcast.21), custom_call_target="tpu_custom_call" | custom-call | flops 2097152000 | bytes 26214400 | tf_op jit(solution)/shard_map/up_product/pallas_call | solution.py:205
  30.6 0.0 collective-permute-done.1.even_ref
  30.6 0.0 collective-permute-done.odd_ref
  30.6 0.1 collective-permute-start.2
  30.7 1.7 %collective-permute-done.2 = bf16[4,80,640]{2,1,0:T(8,128)(2,1)S(1)} collective-permute-done((bf16[4,80,640]{2,1,0:T(8,128)(2,1)S(1)}, bf16[4,80,640]{2,1,0:T(8,128)(2,1)S(1)}, u32[]{:S(2)}, u32[]{:S(2)}) %collective-permute-start.2) | collective-permute-done | bytes 409632 | tf_op jit(solution)/shard_map/ppermute | solution.py:494
  32.4 0.1 add_convert_fusion
  32.5 2.3 %collective-permute-start.5 = (bf16[1,80,640]{2,1,0:T(8,128)(2,1)S(1)}, bf16[1,80,640]{2,1,0:T(8,128)(2,1)S(1)}, u32[]{:S(2)}, u32[]{:S(2)}) collective-permute-start(bf16[1,80,640]{2,1,0:T(8,128)(2,1)S(1)} %get-tuple-element.49), channel_id=1, source_target_pairs={{0,17},{1,16},{16,1},{17,0},{2,19},{3,18},{18,3},{19,2},{4,21},{5,... | collective-permute-start | bytes 307208 | tf_op jit(solution)/shard_map/ppermute | solution.py:472
  34.8 0.5 %collective-permute-start.4 = (bf16[1,80,640]{2,1,0:T(8,128)(2,1)S(1)}, bf16[1,80,640]{2,1,0:T(8,128)(2,1)S(1)}, u32[]{:S(2)}, u32[]{:S(2)}) collective-permute-start(bf16[1,80,640]{2,1,0:T(8,128)(2,1)S(1)} %get-tuple-element.50), channel_id=1, source_target_pairs={{0,16},{1,17},{16,0},{17,1},{2,18},{3,19},{18,2},{19,3},{4,20},{5,... | collective-permute-start | bytes 307208 | tf_op jit(solution)/shard_map/ppermute | solution.py:472
  35.3 0.7 %collective-permute-start.3 = (bf16[1,80,640]{2,1,0:T(8,128)(2,1)S(1)}, bf16[1,80,640]{2,1,0:T(8,128)(2,1)S(1)}, u32[]{:S(2)}, u32[]{:S(2)}) collective-permute-start(bf16[1,80,640]{2,1,0:T(8,128)(2,1)S(1)} %get-tuple-element.51), channel_id=1, source_target_pairs={{0,1},{1,0},{16,17},{17,16},{2,3},{3,2},{18,19},{19,18},{4,5},{5,4... | collective-permute-start | bytes 307208 | tf_op jit(solution)/shard_map/ppermute | solution.py:472
  36.1 0.0 copy-done.2
  36.1 5.5 %softmax_parts.1 = (bf16[960,1024]{1,0:T(8,128)(2,1)S(1)}, bf16[1920,320]{1,0:T(8,128)(2,1)S(1)}, f32[8,128]{1,0:T(8,128)S(1)}) custom-call(s32[1,12]{1,0:T(1,128)S(1)} %bitcast.14, s32[1,1]{1,0:T(1,128)} %bitcast.7.first_ref, bf16[480,320]{1,0:T(8,128)(2,1)S(1)} %pad_maximum_fusion.own_ref, bf16[1200,128]{1,0:T(8,128)(2,1)S(1)} %collective-permute-done.odd_ref, ...), custom_call_target="tpu_custom_call" | custom-call | flops 20480000000 | bytes 102400000 | tf_op jit(solution)/shard_map/softmax_parts/pallas_call | solution.py:311
  41.6 0.0 collective-permute-done.5.refs_3_
  41.6 0.0 collective-permute-done.4.refs_2_
  41.7 0.0 collective-permute-done.3.refs_1_
  41.7 0.5 %gather_sum.1 = (bf16[160,320]{1,0:T(8,128)(2,1)S(1)}, bf16[400,128]{1,0:T(8,128)(2,1)S(1)}) custom-call(bf16[1,80,640]{2,1,0:T(8,128)(2,1)S(1)} %get-tuple-element.52.refs_0_, bf16[1,80,640]{2,1,0:T(8,128)(2,1)S(1)} %collective-permute-done.3.refs_1_, bf16[1,80,640]{2,1,0:T(8,128)(2,1)S(1)} %collective-permute-done.4.refs_2_, ...), custom_call_target="tpu_custom_call" | custom-call | flops 4096000000 | bytes 81920000 | tf_op jit(solution)/shard_map/gather_sum/pallas_call | solution.py:373
  42.2 0.1 collective-permute-start.7
  42.2 0.4 collective-permute-start.6
  42.7 2.4 %own_terms.1 = (bf16[160,320]{1,0:T(8,128)(2,1)}, f32[160,320]{1,0:T(8,128)S(1)}, f32[160,320]{1,0:T(8,128)S(1)}) custom-call(bf16[160,320]{1,0:T(8,128)(2,1)S(1)} %get-tuple-element.38.grad_ref, bf16[160,320]{1,0:T(8,128)(2,1)S(1)} %bitcast.13, bf16[960,1024]{1,0:T(8,128)(2,1)S(1)} %get-tuple-element.39.held_ref), custom_call_target="tpu_custom_call" | custom-call | tf_op jit(solution)/shard_map/own_terms/pallas_call | solution.py:407
  45.0 0.0 collective-permute-done.7.grad_ref
  45.0 0.7 %side_terms.2 = (f32[160,320]{1,0:T(8,128)S(1)}, f32[160,320]{1,0:T(8,128)S(1)}) custom-call(bf16[400,128]{1,0:T(8,128)(2,1)S(1)} %collective-permute-done.7.grad_ref, f32[160,320]{1,0:T(8,128)S(1)} %get-tuple-element.42.key_part_ref, f32[160,320]{1,0:T(8,128)S(1)} %get-tuple-element.43.value_part_ref, bf16[960,1024]{1,0:T(8,128)(2,1)S(1)} %get-tuple-element.39.held_ref, ...), custom_call_target="tpu_custom_call" | custom-call | tf_op jit(solution)/shard_map/side_terms/pallas_call | solution.py:444
  45.7 1.8 %collective-permute-done.6.grad_ref = bf16[400,128]{1,0:T(8,128)(2,1)S(1)} collective-permute-done((bf16[400,128]{1,0:T(8,128)(2,1)S(1)}, bf16[400,128]{1,0:T(8,128)(2,1)S(1)}, u32[]{:S(2)}, u32[]{:S(2)}) %collective-permute-start.6) | collective-permute-done | bytes 102432 | tf_op jit(solution)/shard_map/ppermute | solution.py:464
  47.5 1.4 %side_terms.3 = (bf16[160,320]{1,0:T(8,128)(2,1)}, bf16[160,320]{1,0:T(8,128)(2,1)}) custom-call(bf16[400,128]{1,0:T(8,128)(2,1)S(1)} %collective-permute-done.6.grad_ref, f32[160,320]{1,0:T(8,128)S(1)} %get-tuple-element.45.key_part_ref, f32[160,320]{1,0:T(8,128)S(1)} %get-tuple-element.46.value_part_ref, bf16[960,1024]{1,0:T(8,128)(2,1)S(1)} %get-tuple-element.39.held_ref, ...), custom_call_target="tpu_custom_call" | custom-call | tf_op jit(solution)/shard_map/side_terms/pallas_call | solution.py:444
  (14 shorter events, 0.1 us)
Async XLA Ops:
  0.6 14.0 %copy-start.4 = (bf16[320,160]{0,1:T(8,128)(2,1)S(1)}, bf16[320,160]{0,1:T(8,128)(2,1)}, u32[]{:S(2)}) copy-start(bf16[320,160]{0,1:T(8,128)(2,1)} %param.16) | copy-start | bytes 307204
  0.6 13.9 %copy-start.3 = (bf16[320,160]{0,1:T(8,128)(2,1)S(1)}, bf16[320,160]{0,1:T(8,128)(2,1)}, u32[]{:S(2)}) copy-start(bf16[320,160]{0,1:T(8,128)(2,1)} %param.15) | copy-start | bytes 307204
  0.7 13.9 %copy-start = (bf16[320,160]{0,1:T(8,128)(2,1)S(1)}, bf16[320,160]{0,1:T(8,128)(2,1)}, u32[]{:S(2)}) copy-start(bf16[320,160]{0,1:T(8,128)(2,1)} %param.14) | copy-start | bytes 307204
  0.7 23.7 %copy-start.1 = (bf16[80,640]{1,0:T(8,128)(2,1)S(1)}, bf16[80,640]{1,0:T(8,128)(2,1)}, u32[]{:S(2)}) copy-start(bf16[80,640]{1,0:T(8,128)(2,1)} %pre_ref.1) | copy-start | bytes 307204
  7.3 28.8 %copy-start.2 = (s32[12]{0:T(128)S(1)}, s32[12]{0:T(128)}, u32[]{:S(2)}) copy-start(s32[12]{0:T(128)} %param.17) | copy-start | bytes 148
  7.3 17.1 %all-to-all-start = ((bf16[8,24,640]{2,1,0:T(8,128)(2,1)}), bf16[8,24,640]{2,1,0:T(8,128)(2,1)S(1)}, u32[]{:S(2)}, u32[]{:S(2)}) async-start(bf16[8,24,640]{2,1,0:T(8,128)(2,1)} %bitcast.15), calls=%async_computation | async-start | bytes 491520 | tf_op jit(solution)/shard_map/all_to_all | solution.py:488
  15.0 15.6 %collective-permute-start.1 = (bf16[1200,128]{1,0:T(8,128)(2,1)S(1)}, bf16[1200,128]{1,0:T(8,128)(2,1)S(1)}, u32[]{:S(2)}, u32[]{:S(2)}) collective-permute-start(bf16[1200,128]{1,0:T(8,128)(2,1)S(1)} %maximum_dynamic-update-slice_fusion), channel_id=1, source_target_pairs={{0,2},{2,0},{4,6},{6,4},{8,10},{10,8},{12,14},{14,12},{1,3},{3,1},... | collective-permute-start | bytes 921608 | tf_op jit(solution)/shard_map/ppermute | solution.py:464
  17.1 13.5 %collective-permute-start = (bf16[1200,128]{1,0:T(8,128)(2,1)S(1)}, bf16[1200,128]{1,0:T(8,128)(2,1)S(1)}, u32[]{:S(2)}, u32[]{:S(2)}) collective-permute-start(bf16[1200,128]{1,0:T(8,128)(2,1)S(1)} %maximum_dynamic-update-slice_fusion), channel_id=1, source_target_pairs={{0,8},{2,4},{4,2},{6,14},{8,0},{10,12},{12,10},{14,6},{1,9},{3,5},... | collective-permute-start | bytes 921608 | tf_op jit(solution)/shard_map/ppermute | solution.py:464
  30.6 1.8 %collective-permute-start.2 = (bf16[4,80,640]{2,1,0:T(8,128)(2,1)S(1)}, bf16[4,80,640]{2,1,0:T(8,128)(2,1)S(1)}, u32[]{:S(2)}, u32[]{:S(2)}) collective-permute-start(bf16[4,80,640]{2,1,0:T(8,128)(2,1)S(1)} %get-tuple-element.31), channel_id=1, source_target_pairs={{0,8},{8,0},{1,9},{9,1},{2,10},{10,2},{3,11},{11,3},{4,12},{12,4},... | collective-permute-start | bytes 1228808 | tf_op jit(solution)/shard_map/ppermute | solution.py:494
  32.5 9.1 %collective-permute-start.5 = (bf16[1,80,640]{2,1,0:T(8,128)(2,1)S(1)}, bf16[1,80,640]{2,1,0:T(8,128)(2,1)S(1)}, u32[]{:S(2)}, u32[]{:S(2)}) collective-permute-start(bf16[1,80,640]{2,1,0:T(8,128)(2,1)S(1)} %get-tuple-element.49), channel_id=1, source_target_pairs={{0,17},{1,16},{16,1},{17,0},{2,19},{3,18},{18,3},{19,2},{4,21},{5,... | collective-permute-start | bytes 307208 | tf_op jit(solution)/shard_map/ppermute | solution.py:472
  34.8 6.8 %collective-permute-start.4 = (bf16[1,80,640]{2,1,0:T(8,128)(2,1)S(1)}, bf16[1,80,640]{2,1,0:T(8,128)(2,1)S(1)}, u32[]{:S(2)}, u32[]{:S(2)}) collective-permute-start(bf16[1,80,640]{2,1,0:T(8,128)(2,1)S(1)} %get-tuple-element.50), channel_id=1, source_target_pairs={{0,16},{1,17},{16,0},{17,1},{2,18},{3,19},{18,2},{19,3},{4,20},{5,... | collective-permute-start | bytes 307208 | tf_op jit(solution)/shard_map/ppermute | solution.py:472
  35.3 6.3 %collective-permute-start.3 = (bf16[1,80,640]{2,1,0:T(8,128)(2,1)S(1)}, bf16[1,80,640]{2,1,0:T(8,128)(2,1)S(1)}, u32[]{:S(2)}, u32[]{:S(2)}) collective-permute-start(bf16[1,80,640]{2,1,0:T(8,128)(2,1)S(1)} %get-tuple-element.51), channel_id=1, source_target_pairs={{0,1},{1,0},{16,17},{17,16},{2,3},{3,2},{18,19},{19,18},{4,5},{5,4... | collective-permute-start | bytes 307208 | tf_op jit(solution)/shard_map/ppermute | solution.py:472
  42.2 2.9 %collective-permute-start.7 = (bf16[400,128]{1,0:T(8,128)(2,1)S(1)}, bf16[400,128]{1,0:T(8,128)(2,1)S(1)}, u32[]{:S(2)}, u32[]{:S(2)}) collective-permute-start(bf16[400,128]{1,0:T(8,128)(2,1)S(1)} %get-tuple-element.41), channel_id=1, source_target_pairs={{0,8},{2,4},{4,2},{6,14},{8,0},{10,12},{12,10},{14,6},{1,9},{3,5},... | collective-permute-start | bytes 307208 | tf_op jit(solution)/shard_map/ppermute | solution.py:464
  42.2 5.3 %collective-permute-start.6 = (bf16[400,128]{1,0:T(8,128)(2,1)S(1)}, bf16[400,128]{1,0:T(8,128)(2,1)S(1)}, u32[]{:S(2)}, u32[]{:S(2)}) collective-permute-start(bf16[400,128]{1,0:T(8,128)(2,1)S(1)} %get-tuple-element.41), channel_id=1, source_target_pairs={{0,2},{2,0},{4,6},{6,4},{8,10},{10,8},{12,14},{14,12},{1,3},{3,1},... | collective-permute-start | bytes 307208 | tf_op jit(solution)/shard_map/ppermute | solution.py:464

commit v11 on v10

--- a/solution.py
+++ b/solution.py
@@ -49,12 +49,13 @@
     return capacity, -(-(capacity + 1) // 8) * 8
 
 
-def one_product(count, slots, hidden):
-    return count * slots <= hidden
-
-
-def down_kernel(groups, spans, capacity, slots, steps, dest_hbm, rows_hbm, weight_ref, out_hbm,
-                dest_ref, rows_ref, held, total_ref, pieces_ref, sems, out_sems):
+def by_swaps(groups, spans, slots, hidden):
+    return spans == 2 and groups in (2, 4, 8) and groups * slots <= hidden
+
+
+def down_kernel(groups, spans, capacity, slots, steps, dest_hbm, rows_hbm, weight_ref, *refs):
+    *outs, dest_ref, rows_ref, held, total_ref, pieces_ref, sems, out_sems = refs
+    me, span = lax.axis_index("grp"), lax.axis_index("span")
     row_count = rows_ref.shape[0]
     hidden = weight_ref.shape[0] // spans
     everything = pl.ds(0, weight_ref.shape[0])
@@ -77,34 +78,36 @@
     row_of = group_across[:1] * slots + rank_across
     places = iota((groups * slots, row_count), 0).astype(jnp.float32)
     pick = jnp.where(places == row_of, 1.0, 0.0).astype(jnp.bfloat16)
+    swaps = by_swaps(groups, spans, slots, hidden)
     lane = iota((row_count, hidden), 1).astype(jnp.float32)
-    shift = 0.0
-    if one_product(groups * spans, slots, hidden):
-        device = lax.axis_index("grp") * spans + lax.axis_index("span")
-        shift = (device * slots).astype(jnp.float32)
-    at_rank = lane == rank_down + shift
-    label_row = iota((slots, hidden), 0) == capacity
     labels = []
     for g in range(groups):
-        hit = at_rank & (group_down[:, :1] == g)
+        shift = (lax.bitwise_xor(me, g) * slots).astype(jnp.float32) if swaps else 0.0
+        hit = (lane == rank_down + shift) & (group_down[:, :1] == g)
         labels.append(jnp.sum(jnp.where(hit, slot_down[:, :1] + 1.0, 0.0), 0, keepdims=True) - 1.0)
+    label_row = iota((slots, hidden), 0) == capacity
     copies[1].wait()
     for n, (at, step) in enumerate(steps):
         turned = rows_ref[:, at : at + step].astype(jnp.float32).T.astype(jnp.bfloat16)
         copies[2 + n].wait()
         product = dot(held[:, at : at + step], turned, NN)
         total_ref[...] = product if n == 0 else total_ref[...] + product
-    outgoing = []
     for s in range(spans):
         part = total_ref[s * hidden : (s + 1) * hidden].astype(jnp.bfloat16)
         moved = dot(pick, part, NT)
+        said = jnp.where(span == s, 1.0, 0.0) if swaps else 1.0
         for g in range(groups):
-            piece = jnp.where(label_row, labels[g], moved[g * slots : (g + 1) * slots])
+            piece = jnp.where(label_row, labels[g] * said, moved[g * slots : (g + 1) * slots])
             pieces_ref[s, g] = piece.astype(jnp.bfloat16)
-        copy = pltpu.make_async_copy(pieces_ref.at[s], out_hbm.at[:, s], out_sems.at[s])
-        copy.start()
-        outgoing.append(copy)
-    for copy in outgoing:
+    if swaps:
+        pairs = [
+            (pieces_ref.at[s, lax.bitwise_xor(me, d)], out.at[d])
+            for out, s in zip(outs, (1 - span, span))
+            for d in range(groups)
+        ]
+    else:
+        pairs = [(pieces_ref.at[s], outs[0].at[:, s]) for s in range(spans)]
+    for copy in fetched(pairs, out_sems):
         copy.wait()
 
 
@@ -115,11 +118,14 @@
     depth = weight.shape[1]
     edges = [depth * i // 8 for i in (0, 1, 3, 5, 8)]
     steps = [(i, j - i) for i, j in zip(edges, edges[1:])]
+    swaps = by_swaps(groups, spans, slots, hidden)
+    shape = (groups, spans, slots, hidden)
+    shapes = [shape[:1] + shape[2:]] * 2 if swaps else [shape]
     pieces = pl.pallas_call(
         functools.partial(down_kernel, groups, spans, capacity, slots, steps),
-        out_shape=jax.ShapeDtypeStruct((groups, spans, slots, hidden), jnp.bfloat16),
+        out_shape=[jax.ShapeDtypeStruct(x, jnp.bfloat16) for x in shapes],
         in_specs=in_hbm(3),
-        out_specs=in_hbm(1)[0],
+        out_specs=in_hbm(len(shapes)),
         scratch_shapes=[
             pltpu.VMEM((1, row_count), jnp.int32),
             pltpu.VMEM(rows.shape, jnp.bfloat16),
@@ -127,16 +133,19 @@
             pltpu.VMEM((weight.shape[0], row_count), jnp.float32),
             pltpu.VMEM((spans, groups, slots, hidden), jnp.bfloat16),
             pltpu.SemaphoreType.DMA((2 + len(steps),)),
-            pltpu.SemaphoreType.DMA((spans,)),
+            pltpu.SemaphoreType.DMA((2 * groups if swaps else spans,)),
         ],
         compiler_params=params(60),
         name="down_product",
     )(dest.reshape(1, row_count), rows, weight)
-    return pieces.reshape(groups * spans, slots, hidden)
-
-
-def up_kernel(heads, capacity, pieces_ref, pre_ref, weight_ref, send_hbm, keep_hbm, held, out_ref,
-              sems, out_sems):
+    if swaps:
+        return pieces
+    return [pieces[0].reshape(groups * spans, slots, hidden)]
+
+
+def up_kernel(heads, capacity, swaps, *refs):
+    *pieces_refs, pre_ref, weight_ref, send_hbm, keep_hbm, held, out_ref, sems, out_sems = refs
+    pieces_ref = pieces_refs[0]
     row_count, hidden = pre_ref.shape
     count, slots, _ = pieces_ref.shape
     width = weight_ref.shape[2] // lax.axis_size("span")
@@ -152,8 +161,9 @@
         pairs.append((weight_ref.at[:, place], held.at[n]))
     copies = fetched(pairs, sems)
     label_at = slice(capacity, capacity + 1)
-    if one_product(count, slots, hidden):
-        pieces = [pieces_ref[p].astype(jnp.float32) for p in range(count)]
+    if swaps:
+        count = len(pieces_refs)
+        pieces = [ref[0].astype(jnp.float32) for ref in pieces_refs]
         labels = functools.reduce(jnp.maximum, [x[label_at, : count * slots] for x in pieces])
         row = iota((row_count, count * slots), 0).astype(jnp.float32)
         put = jnp.where(row == labels, 1.0, 0.0).astype(jnp.bfloat16)
@@ -203,9 +213,9 @@
     spans = lax.axis_size("span")
     blocks = heads // spans
     return pl.pallas_call(
-        functools.partial(up_kernel, heads, capacity),
+        functools.partial(up_kernel, heads, capacity, len(pieces) > 1),
         out_shape=[jax.ShapeDtypeStruct((heads // 2, pre.shape[0], width), jnp.bfloat16)] * 2,
-        in_specs=in_vmem(2) + in_hbm(1),
+        in_specs=in_vmem(len(pieces) + 1) + in_hbm(1),
         out_specs=in_hbm(2),
         scratch_shapes=[
             pltpu.VMEM((blocks, 4, spans * width // 4, weight.shape[1]), jnp.bfloat16),
@@ -218,7 +228,7 @@
             flops=8 * pre.shape[0] * weight.size, bytes_accessed=8 * weight.size, transcendentals=0
         ),
         name="up_product",
-    )(pieces, pre, weight.reshape(4, blocks, -1, weight.shape[1]))
+    )(*pieces, pre, weight.reshape(4, blocks, -1, weight.shape[1]))
 
 
 class Rows:
@@ -466,6 +476,12 @@
     return swapped(0), swapped(1)
 
 
+def summed(other, mine, axis):
+    other = lax.ppermute(other, axis, [(0, 1), (1, 0)])
+    total = (other.astype(jnp.float32) + mine.astype(jnp.float32)).astype(jnp.bfloat16)
+    return [total[d : d + 1] for d in range(total.shape[0])]
+
+
 def exchanged(pieces, axes):
     count = len(pieces)
     return pieces[:1] + [
@@ -485,7 +501,11 @@
     pieces, queries, key_states, value_states = lax.optimization_barrier(
         (pieces, queries, key_states, value_states)
     )
-    arrived = lax.all_to_all(pieces, ("grp", "span"), split_axis=0, concat_axis=0, tiled=True)
+    if len(pieces) > 1:
+        arrived = exchanged(summed(*pieces, "span"), "grp")
+    else:
+        axes = ("grp", "span")
+        arrived = [lax.all_to_all(pieces[0], axes, split_axis=0, concat_axis=0, tiled=True)]
     own = jnp.concatenate([queries.T, key_states.T, value_states.T], 0)
     even, odd = from_pairs(packed(own))
     first = lax.axis_index("grp") * row_count

time: 49.1 us -> 49.2 us (level)
  waiting for transfers between devices: 10.9 us -> 8.43 us
  starting transfers between devices: 13.5 us -> 14.9 us
  other arithmetic: 0.41 us -> 1.36 us
    all_to_all x1 -> x0, waiting for transfers between devices: 7.32 us -> none  [on_device(): lax.all_to_all(pieces, ('grp', 'span'), split_axis=0, concat_axis=0, tile...]
    all_to_all x1 -> x0, starting transfers between devices: 7.29 us -> none  [on_device(): lax.all_to_all(pieces, ('grp', 'span'), split_axis=0, concat_axis=0, tile...]
    ppermute x3 -> x6, waiting for transfers between devices: 0.01 us -> 4.98 us  [exchanged(): lax.ppermute(pieces[d], axes, [(i, i ^ d) for i in range(count)])]
    ppermute x3 -> x6, starting transfers between devices: 3.55 us -> 8.09 us  [exchanged(): lax.ppermute(pieces[d], axes, [(i, i ^ d) for i in range(count)])]
    ppermute x0 -> x1, starting transfers between devices: none -> 3.03 us  [summed(): other = lax.ppermute(other, axis, [(0, 1), (1, 0)])]
    ppermute x4, waiting for transfers between devices: 1.8 us -> 0.26 us  [swapped(): return lax.ppermute(x, ('core', 'grp'), sorted(partner.items()))]
    ppermute x0 -> x1, waiting for transfers between devices: none -> 1.47 us  [summed(): other = lax.ppermute(other, axis, [(0, 1), (1, 0)])]
    ppermute x4, starting transfers between devices: 2.58 us -> 3.68 us  [swapped(): return lax.ppermute(x, ('core', 'grp'), sorted(partner.items()))]
  transfers between devices with their start and end apart: 9 -> 12, of which waited for: 3 -> 5; matrix products, arithmetic and copies ran while one was open for 1% -> 3% of each run, Pallas kernels for 30% -> 30%
where the time goes in v11:
time: 49.2 us; the launch traced here: 49.1 us
  Pallas kernels  23.5 us (48%)
  starting transfers between devices  14.9 us (30%)
  waiting for transfers between devices  8.43 us (17%)
  other arithmetic  1.36 us (3%)
  between operations  0.85 us (2%)
    ppermute x6, starting transfers between devices, exchanged(): lax.ppermute(pieces[d], axes, [(i, i ^ d) for i in range(count)])  8.09 us
    pallas_call x1, Pallas kernels, down_pieces(): pl.pallas_call(functools.partial(down_kernel, groups, spans, capacity, sl...  6.66 us
    pallas_call x1, Pallas kernels, up_pieces(): pl.pallas_call(functools.partial(up_kernel, heads, capacity, len(pieces)...  6.31 us
    pallas_call x1, Pallas kernels, softmax_parts(): pl.pallas_call(softmax_kernel, out_shape=(jax.ShapeDtypeStruct((rows.tota...  5.54 us
    ppermute x6, waiting for transfers between devices, exchanged(): lax.ppermute(pieces[d], axes, [(i, i ^ d) for i in range(count)])  4.98 us
    ppermute x4, starting transfers between devices, swapped(): return lax.ppermute(x, ('core', 'grp'), sorted(partner.items()))  3.68 us
    ppermute x1, starting transfers between devices, summed(): other = lax.ppermute(other, axis, [(0, 1), (1, 0)])  3.03 us
    pallas_call x1, Pallas kernels, own_terms(): pl.pallas_call(own_kernel, out_shape=(jax.ShapeDtypeStruct(grad.shape, jn...  2.36 us
  transfers between devices with their start and end apart: 12, of which 5 were waited for; matrix products, arithmetic and copies ran while one was open for 3% of the time, Pallas kernels for 30%

profile of v11, /device:TPU:0, one launch (start us, length us, event | category | flops | bytes accessed | tf_op | source)
XLA Modules:
  0.0 49.1 jit_solution(6563739652332515449)
XLA Ops:
  0.7 6.7 %down_product.1 = (bf16[4,24,640]{2,1,0:T(8,128)(2,1)}, bf16[4,24,640]{2,1,0:T(8,128)(2,1)}) custom-call(s32[1,80]{1,0:T(1,128)} %bitcast.18, bf16[80,4096]{1,0:T(8,128)(2,1)} %rows_hbm.1, bf16[1280,4096]{1,0:T(8,128)(2,1)} %weight_ref.1), custom_call_target="tpu_custom_call" | custom-call | tf_op jit(solution)/shard_map/down_product/pallas_call | solution.py:124
  7.3 0.0 copy-start.2
  7.4 3.0 %collective-permute-start = (bf16[4,24,640]{2,1,0:T(8,128)(2,1)}, bf16[4,24,640]{2,1,0:T(8,128)(2,1)S(1)}, u32[]{:S(2)}, u32[]{:S(2)}) collective-permute-start(bf16[4,24,640]{2,1,0:T(8,128)(2,1)} %get-tuple-element.31), channel_id=1, source_target_pairs={{0,1},{1,0},{2,3},{3,2},{4,5},{5,4},{6,7},{7,6},{8,9},{9,8},{10,11... | collective-permute-start | bytes 368648 | tf_op jit(solution)/shard_map/ppermute | solution.py:480
  10.5 0.1 maximum_dynamic-update-slice_fusion.2
  10.6 0.1 maximum_dynamic-update-slice_fusion.1
  10.7 0.1 maximum_dynamic-update-slice_fusion
  10.8 1.6 %collective-permute-start.5 = (bf16[1200,128]{1,0:T(8,128)(2,1)S(1)}, bf16[1200,128]{1,0:T(8,128)(2,1)S(1)}, u32[]{:S(2)}, u32[]{:S(2)}) collective-permute-start(bf16[1200,128]{1,0:T(8,128)(2,1)S(1)} %maximum_dynamic-update-slice_fusion), channel_id=1, source_target_pairs={{0,2},{2,0},{4,6},{6,4},{8,10},{10,8},{12,14},{14,12},{1,3},{3,1},... | collective-permute-start | bytes 921608 | tf_op jit(solution)/shard_map/ppermute | solution.py:474
  12.5 1.5 %collective-permute-done = bf16[4,24,640]{2,1,0:T(8,128)(2,1)S(1)} collective-permute-done((bf16[4,24,640]{2,1,0:T(8,128)(2,1)}, bf16[4,24,640]{2,1,0:T(8,128)(2,1)S(1)}, u32[]{:S(2)}, u32[]{:S(2)}) %collective-permute-start) | collective-permute-done | bytes 122912 | tf_op jit(solution)/shard_map/ppermute | solution.py:480
  13.9 0.9 %add_convert_fusion.1 = bf16[4,24,640]{2,1,0:T(8,128)(2,1)S(1)} fusion(bf16[4,24,640]{2,1,0:T(8,128)(2,1)} %get-tuple-element.32, bf16[4,24,640]{2,1,0:T(8,128)(2,1)S(1)} %collective-permute-done), kind=kLoop, calls=%fused_computation.2 | loop fusion | flops 245760 | bytes 368640 | tf_op jit(solution)/shard_map/convert_element_type | solution.py:481
  14.9 3.9 %collective-permute-start.3 = (bf16[1,24,640]{2,1,0:T(8,128)(2,1)S(1)}, bf16[1,24,640]{2,1,0:T(8,128)(2,1)S(1)}, u32[]{:S(2)}, u32[]{:S(2)}) collective-permute-start(bf16[1,24,640]{2,1,0:T(8,128)(2,1)S(1)} %get-tuple-element.65), channel_id=1, source_target_pairs={{0,6},{2,4},{4,2},{6,0},{1,7},{3,5},{5,3},{7,1},{8,14},{10,12},{12... | collective-permute-start | bytes 92168 | tf_op jit(solution)/shard_map/ppermute | solution.py:488
  18.8 0.6 %collective-permute-start.1 = (bf16[1,24,640]{2,1,0:T(8,128)(2,1)S(1)}, bf16[1,24,640]{2,1,0:T(8,128)(2,1)S(1)}, u32[]{:S(2)}, u32[]{:S(2)}) collective-permute-start(bf16[1,24,640]{2,1,0:T(8,128)(2,1)S(1)} %get-tuple-element.67), channel_id=1, source_target_pairs={{0,2},{2,0},{4,6},{6,4},{1,3},{3,1},{5,7},{7,5},{8,10},{10,8},{12,... | collective-permute-start | bytes 92168 | tf_op jit(solution)/shard_map/ppermute | solution.py:488
  19.4 3.6 %collective-permute-done.3.refs_3_ = bf16[1,24,640]{2,1,0:T(8,128)(2,1)S(1)} collective-permute-done((bf16[1,24,640]{2,1,0:T(8,128)(2,1)S(1)}, bf16[1,24,640]{2,1,0:T(8,128)(2,1)S(1)}, u32[]{:S(2)}, u32[]{:S(2)}) %collective-permute-start.3) | collective-permute-done | bytes 30752 | tf_op jit(solution)/shard_map/ppermute | solution.py:488
  23.0 1.3 %collective-permute-done.2.refs_2_ = bf16[1,24,640]{2,1,0:T(8,128)(2,1)S(1)} collective-permute-done((bf16[1,24,640]{2,1,0:T(8,128)(2,1)S(1)}, bf16[1,24,640]{2,1,0:T(8,128)(2,1)S(1)}, u32[]{:S(2)}, u32[]{:S(2)}) %collective-permute-start.2) | collective-permute-done | bytes 30752 | tf_op jit(solution)/shard_map/ppermute | solution.py:488
  24.4 6.3 %up_product.1 = (bf16[4,80,640]{2,1,0:T(8,128)(2,1)S(1)}, bf16[4,80,640]{2,1,0:T(8,128)(2,1)S(1)}) custom-call(bf16[1,24,640]{2,1,0:T(8,128)(2,1)S(1)} %get-tuple-element.68.refs_0_, bf16[1,24,640]{2,1,0:T(8,128)(2,1)S(1)} %collective-permute-done.1.refs_1_, bf16[1,24,640]{2,1,0:T(8,128)(2,1)S(1)} %collective-permute-done.2.refs_2_, ...), custom_call_target="tpu_custom_call" | custom-call | flops 2097152000 | bytes 26214400 | tf_op jit(solution)/shard_map/up_product/pallas_call | solution.py:215
  30.7 0.0 collective-permute-done.5.even_ref
  30.7 0.0 collective-permute-done.4.odd_ref
  30.7 0.1 collective-permute-start.6
  30.8 1.7 %collective-permute-done.6 = bf16[4,80,640]{2,1,0:T(8,128)(2,1)S(1)} collective-permute-done((bf16[4,80,640]{2,1,0:T(8,128)(2,1)S(1)}, bf16[4,80,640]{2,1,0:T(8,128)(2,1)S(1)}, u32[]{:S(2)}, u32[]{:S(2)}) %collective-permute-start.6) | collective-permute-done | bytes 409632 | tf_op jit(solution)/shard_map/ppermute | solution.py:514
  32.5 0.1 add_convert_fusion
  32.7 1.7 %collective-permute-start.9 = (bf16[1,80,640]{2,1,0:T(8,128)(2,1)S(1)}, bf16[1,80,640]{2,1,0:T(8,128)(2,1)S(1)}, u32[]{:S(2)}, u32[]{:S(2)}) collective-permute-start(bf16[1,80,640]{2,1,0:T(8,128)(2,1)S(1)} %get-tuple-element.55), channel_id=1, source_target_pairs={{0,17},{1,16},{16,1},{17,0},{2,19},{3,18},{18,3},{19,2},{4,21},{5,... | collective-permute-start | bytes 307208 | tf_op jit(solution)/shard_map/ppermute | solution.py:488
  34.4 0.5 %collective-permute-start.8 = (bf16[1,80,640]{2,1,0:T(8,128)(2,1)S(1)}, bf16[1,80,640]{2,1,0:T(8,128)(2,1)S(1)}, u32[]{:S(2)}, u32[]{:S(2)}) collective-permute-start(bf16[1,80,640]{2,1,0:T(8,128)(2,1)S(1)} %get-tuple-element.56), channel_id=1, source_target_pairs={{0,16},{1,17},{16,0},{17,1},{2,18},{3,19},{18,2},{19,3},{4,20},{5,... | collective-permute-start | bytes 307208 | tf_op jit(solution)/shard_map/ppermute | solution.py:488
  34.9 1.3 %collective-permute-start.7 = (bf16[1,80,640]{2,1,0:T(8,128)(2,1)S(1)}, bf16[1,80,640]{2,1,0:T(8,128)(2,1)S(1)}, u32[]{:S(2)}, u32[]{:S(2)}) collective-permute-start(bf16[1,80,640]{2,1,0:T(8,128)(2,1)S(1)} %get-tuple-element.57), channel_id=1, source_target_pairs={{0,1},{1,0},{16,17},{17,16},{2,3},{3,2},{18,19},{19,18},{4,5},{5,4... | collective-permute-start | bytes 307208 | tf_op jit(solution)/shard_map/ppermute | solution.py:488
  36.3 5.5 %softmax_parts.1 = (bf16[960,1024]{1,0:T(8,128)(2,1)S(1)}, bf16[1920,320]{1,0:T(8,128)(2,1)S(1)}, f32[8,128]{1,0:T(8,128)S(1)}) custom-call(s32[1,12]{1,0:T(1,128)S(1)} %bitcast.13, s32[1,1]{1,0:T(1,128)} %bitcast.6.first_ref, bf16[480,320]{1,0:T(8,128)(2,1)S(1)} %pad_maximum_fusion.own_ref, bf16[1200,128]{1,0:T(8,128)(2,1)S(1)} %collective-permute-done.4.odd_ref, ...), custom_call_target="tpu_custom_call" | custom-call | flops 20480000000 | bytes 102400000 | tf_op jit(solution)/shard_map/softmax_parts/pallas_call | solution.py:321
  41.8 0.0 collective-permute-done.8.refs_2_
  41.8 0.0 collective-permute-done.7.refs_1_
  41.8 0.5 %gather_sum.1 = (bf16[160,320]{1,0:T(8,128)(2,1)S(1)}, bf16[400,128]{1,0:T(8,128)(2,1)S(1)}) custom-call(bf16[1,80,640]{2,1,0:T(8,128)(2,1)S(1)} %get-tuple-element.58.refs_0_, bf16[1,80,640]{2,1,0:T(8,128)(2,1)S(1)} %collective-permute-done.7.refs_1_, bf16[1,80,640]{2,1,0:T(8,128)(2,1)S(1)} %collective-permute-done.8.refs_2_, ...), custom_call_target="tpu_custom_call" | custom-call | flops 4096000000 | bytes 81920000 | tf_op jit(solution)/shard_map/gather_sum/pallas_call | solution.py:383
  42.3 0.1 collective-permute-start.11
  42.4 2.0 %collective-permute-start.10 = (bf16[400,128]{1,0:T(8,128)(2,1)S(1)}, bf16[400,128]{1,0:T(8,128)(2,1)S(1)}, u32[]{:S(2)}, u32[]{:S(2)}) collective-permute-start(bf16[400,128]{1,0:T(8,128)(2,1)S(1)} %get-tuple-element.47), channel_id=1, source_target_pairs={{0,2},{2,0},{4,6},{6,4},{8,10},{10,8},{12,14},{14,12},{1,3},{3,1},... | collective-permute-start | bytes 307208 | tf_op jit(solution)/shard_map/ppermute | solution.py:474
  44.4 2.4 %own_terms.1 = (bf16[160,320]{1,0:T(8,128)(2,1)}, f32[160,320]{1,0:T(8,128)S(1)}, f32[160,320]{1,0:T(8,128)S(1)}) custom-call(bf16[160,320]{1,0:T(8,128)(2,1)S(1)} %get-tuple-element.44.grad_ref, bf16[160,320]{1,0:T(8,128)(2,1)S(1)} %bitcast.12, bf16[960,1024]{1,0:T(8,128)(2,1)S(1)} %get-tuple-element.45.held_ref), custom_call_target="tpu_custom_call" | custom-call | tf_op jit(solution)/shard_map/own_terms/pallas_call | solution.py:417
  46.7 0.7 %side_terms.2 = (f32[160,320]{1,0:T(8,128)S(1)}, f32[160,320]{1,0:T(8,128)S(1)}) custom-call(bf16[400,128]{1,0:T(8,128)(2,1)S(1)} %collective-permute-done.11.grad_ref, f32[160,320]{1,0:T(8,128)S(1)} %get-tuple-element.48.key_part_ref, f32[160,320]{1,0:T(8,128)S(1)} %get-tuple-element.49.value_part_ref, bf16[960,1024]{1,0:T(8,128)(2,1)S(1)} %get-tuple-element.45.held_ref, ...), custom_call_target="tpu_custom_call" | custom-call | tf_op jit(solution)/shard_map/side_terms/pallas_call | solution.py:454
  47.4 0.3 collective-permute-done.10.grad_ref
  47.7 1.4 %side_terms.3 = (bf16[160,320]{1,0:T(8,128)(2,1)}, bf16[160,320]{1,0:T(8,128)(2,1)}) custom-call(bf16[400,128]{1,0:T(8,128)(2,1)S(1)} %collective-permute-done.10.grad_ref, f32[160,320]{1,0:T(8,128)S(1)} %get-tuple-element.51.key_part_ref, f32[160,320]{1,0:T(8,128)S(1)} %get-tuple-element.52.value_part_ref, ...), custom_call_target="tpu_custom_call" | custom-call | tf_op jit(solution)/shard_map/side_terms/pallas_call | solution.py:454
  (22 shorter events, 0.2 us)
Async XLA Ops:
  0.6 9.8 %copy-start.3 = (bf16[320,160]{0,1:T(8,128)(2,1)S(1)}, bf16[320,160]{0,1:T(8,128)(2,1)}, u32[]{:S(2)}) copy-start(bf16[320,160]{0,1:T(8,128)(2,1)} %param.16) | copy-start | bytes 307204
  0.6 9.8 %copy-start.4 = (bf16[320,160]{0,1:T(8,128)(2,1)S(1)}, bf16[320,160]{0,1:T(8,128)(2,1)}, u32[]{:S(2)}) copy-start(bf16[320,160]{0,1:T(8,128)(2,1)} %param.15) | copy-start | bytes 307204
  0.7 9.7 %copy-start = (bf16[320,160]{0,1:T(8,128)(2,1)S(1)}, bf16[320,160]{0,1:T(8,128)(2,1)}, u32[]{:S(2)}) copy-start(bf16[320,160]{0,1:T(8,128)(2,1)} %param.14) | copy-start | bytes 307204
  0.7 23.7 %copy-start.1 = (bf16[80,640]{1,0:T(8,128)(2,1)S(1)}, bf16[80,640]{1,0:T(8,128)(2,1)}, u32[]{:S(2)}) copy-start(bf16[80,640]{1,0:T(8,128)(2,1)} %refs_4_.1) | copy-start | bytes 307204
  7.3 28.9 %copy-start.2 = (s32[12]{0:T(128)S(1)}, s32[12]{0:T(128)}, u32[]{:S(2)}) copy-start(s32[12]{0:T(128)} %param.17) | copy-start | bytes 148
  7.4 6.6 %collective-permute-start = (bf16[4,24,640]{2,1,0:T(8,128)(2,1)}, bf16[4,24,640]{2,1,0:T(8,128)(2,1)S(1)}, u32[]{:S(2)}, u32[]{:S(2)}) collective-permute-start(bf16[4,24,640]{2,1,0:T(8,128)(2,1)} %get-tuple-element.31), channel_id=1, source_target_pairs={{0,1},{1,0},{2,3},{3,2},{4,5},{5,4},{6,7},{7,6},{8,9},{9,8},{10,11... | collective-permute-start | bytes 368648 | tf_op jit(solution)/shard_map/ppermute | solution.py:480
  10.8 19.9 %collective-permute-start.5 = (bf16[1200,128]{1,0:T(8,128)(2,1)S(1)}, bf16[1200,128]{1,0:T(8,128)(2,1)S(1)}, u32[]{:S(2)}, u32[]{:S(2)}) collective-permute-start(bf16[1200,128]{1,0:T(8,128)(2,1)S(1)} %maximum_dynamic-update-slice_fusion), channel_id=1, source_target_pairs={{0,2},{2,0},{4,6},{6,4},{8,10},{10,8},{12,14},{14,12},{1,3},{3,1},... | collective-permute-start | bytes 921608 | tf_op jit(solution)/shard_map/ppermute | solution.py:474
  12.4 18.3 %collective-permute-start.4 = (bf16[1200,128]{1,0:T(8,128)(2,1)S(1)}, bf16[1200,128]{1,0:T(8,128)(2,1)S(1)}, u32[]{:S(2)}, u32[]{:S(2)}) collective-permute-start(bf16[1200,128]{1,0:T(8,128)(2,1)S(1)} %maximum_dynamic-update-slice_fusion), channel_id=1, source_target_pairs={{0,8},{2,4},{4,2},{6,14},{8,0},{10,12},{12,10},{14,6},{1,9},{3,5},... | collective-permute-start | bytes 921608 | tf_op jit(solution)/shard_map/ppermute | solution.py:474
  14.9 8.2 %collective-permute-start.3 = (bf16[1,24,640]{2,1,0:T(8,128)(2,1)S(1)}, bf16[1,24,640]{2,1,0:T(8,128)(2,1)S(1)}, u32[]{:S(2)}, u32[]{:S(2)}) collective-permute-start(bf16[1,24,640]{2,1,0:T(8,128)(2,1)S(1)} %get-tuple-element.65), channel_id=1, source_target_pairs={{0,6},{2,4},{4,2},{6,0},{1,7},{3,5},{5,3},{7,1},{8,14},{10,12},{12... | collective-permute-start | bytes 92168 | tf_op jit(solution)/shard_map/ppermute | solution.py:488
  18.8 5.6 %collective-permute-start.2 = (bf16[1,24,640]{2,1,0:T(8,128)(2,1)S(1)}, bf16[1,24,640]{2,1,0:T(8,128)(2,1)S(1)}, u32[]{:S(2)}, u32[]{:S(2)}) collective-permute-start(bf16[1,24,640]{2,1,0:T(8,128)(2,1)S(1)} %get-tuple-element.66), channel_id=1, source_target_pairs={{0,4},{2,6},{4,0},{6,2},{1,5},{3,7},{5,1},{7,3},{8,12},{10,14},{12... | collective-permute-start | bytes 92168 | tf_op jit(solution)/shard_map/ppermute | solution.py:488
  18.8 5.6 %collective-permute-start.1 = (bf16[1,24,640]{2,1,0:T(8,128)(2,1)S(1)}, bf16[1,24,640]{2,1,0:T(8,128)(2,1)S(1)}, u32[]{:S(2)}, u32[]{:S(2)}) collective-permute-start(bf16[1,24,640]{2,1,0:T(8,128)(2,1)S(1)} %get-tuple-element.67), channel_id=1, source_target_pairs={{0,2},{2,0},{4,6},{6,4},{1,3},{3,1},{5,7},{7,5},{8,10},{10,8},{12,... | collective-permute-start | bytes 92168 | tf_op jit(solution)/shard_map/ppermute | solution.py:488
  30.7 1.8 %collective-permute-start.6 = (bf16[4,80,640]{2,1,0:T(8,128)(2,1)S(1)}, bf16[4,80,640]{2,1,0:T(8,128)(2,1)S(1)}, u32[]{:S(2)}, u32[]{:S(2)}) collective-permute-start(bf16[4,80,640]{2,1,0:T(8,128)(2,1)S(1)} %get-tuple-element.37), channel_id=1, source_target_pairs={{0,8},{8,0},{1,9},{9,1},{2,10},{10,2},{3,11},{11,3},{4,12},{12,4},... | collective-permute-start | bytes 1228808 | tf_op jit(solution)/shard_map/ppermute | solution.py:514
  32.7 9.1 %collective-permute-start.9 = (bf16[1,80,640]{2,1,0:T(8,128)(2,1)S(1)}, bf16[1,80,640]{2,1,0:T(8,128)(2,1)S(1)}, u32[]{:S(2)}, u32[]{:S(2)}) collective-permute-start(bf16[1,80,640]{2,1,0:T(8,128)(2,1)S(1)} %get-tuple-element.55), channel_id=1, source_target_pairs={{0,17},{1,16},{16,1},{17,0},{2,19},{3,18},{18,3},{19,2},{4,21},{5,... | collective-permute-start | bytes 307208 | tf_op jit(solution)/shard_map/ppermute | solution.py:488
  34.4 7.4 %collective-permute-start.8 = (bf16[1,80,640]{2,1,0:T(8,128)(2,1)S(1)}, bf16[1,80,640]{2,1,0:T(8,128)(2,1)S(1)}, u32[]{:S(2)}, u32[]{:S(2)}) collective-permute-start(bf16[1,80,640]{2,1,0:T(8,128)(2,1)S(1)} %get-tuple-element.56), channel_id=1, source_target_pairs={{0,16},{1,17},{16,0},{17,1},{2,18},{3,19},{18,2},{19,3},{4,20},{5,... | collective-permute-start | bytes 307208 | tf_op jit(solution)/shard_map/ppermute | solution.py:488
  34.9 6.9 %collective-permute-start.7 = (bf16[1,80,640]{2,1,0:T(8,128)(2,1)S(1)}, bf16[1,80,640]{2,1,0:T(8,128)(2,1)S(1)}, u32[]{:S(2)}, u32[]{:S(2)}) collective-permute-start(bf16[1,80,640]{2,1,0:T(8,128)(2,1)S(1)} %get-tuple-element.57), channel_id=1, source_target_pairs={{0,1},{1,0},{16,17},{17,16},{2,3},{3,2},{18,19},{19,18},{4,5},{5,4... | collective-permute-start | bytes 307208 | tf_op jit(solution)/shard_map/ppermute | solution.py:488
  42.3 4.4 %collective-permute-start.11 = (bf16[400,128]{1,0:T(8,128)(2,1)S(1)}, bf16[400,128]{1,0:T(8,128)(2,1)S(1)}, u32[]{:S(2)}, u32[]{:S(2)}) collective-permute-start(bf16[400,128]{1,0:T(8,128)(2,1)S(1)} %get-tuple-element.47), channel_id=1, source_target_pairs={{0,8},{2,4},{4,2},{6,14},{8,0},{10,12},{12,10},{14,6},{1,9},{3,5},... | collective-permute-start | bytes 307208 | tf_op jit(solution)/shard_map/ppermute | solution.py:474
  42.4 5.3 %collective-permute-start.10 = (bf16[400,128]{1,0:T(8,128)(2,1)S(1)}, bf16[400,128]{1,0:T(8,128)(2,1)S(1)}, u32[]{:S(2)}, u32[]{:S(2)}) collective-permute-start(bf16[400,128]{1,0:T(8,128)(2,1)S(1)} %get-tuple-element.47), channel_id=1, source_target_pairs={{0,2},{2,0},{4,6},{6,4},{8,10},{10,8},{12,14},{14,12},{1,3},{3,1},... | collective-permute-start | bytes 307208 | tf_op jit(solution)/shard_map/ppermute | solution.py:474

commit v12 on v11

--- a/solution.py
+++ b/solution.py
@@ -498,11 +498,13 @@
     row_count = grad_out.shape[0]
     capacity, _ = padded_slots(row_count, groups)
     pieces = down_pieces(destination, grad_out, w_down, groups, spans)
+    if len(pieces) > 1:
+        pieces = summed(*pieces, "span")
     pieces, queries, key_states, value_states = lax.optimization_barrier(
         (pieces, queries, key_states, value_states)
     )
     if len(pieces) > 1:
-        arrived = exchanged(summed(*pieces, "span"), "grp")
+        arrived = exchanged(pieces, "grp")
     else:
         axes = ("grp", "span")
         arrived = [lax.all_to_all(pieces[0], axes, split_axis=0, concat_axis=0, tiled=True)]

time: 49.2 us -> 53.4 us (1.085)
  waiting for transfers between devices: 8.43 us -> 10.8 us
  starting transfers between devices: 14.9 us -> 16.7 us
    ppermute x1, waiting for transfers between devices: 1.47 us -> 3.53 us  [summed(): other = lax.ppermute(other, axis, [(0, 1), (1, 0)])]
    ppermute x6, starting transfers between devices: 8.09 us -> 9.07 us  [exchanged(): lax.ppermute(pieces[d], axes, [(i, i ^ d) for i in range(count)])]
    ppermute x4, starting transfers between devices: 3.68 us -> 4.55 us  [swapped(): return lax.ppermute(x, ('core', 'grp'), sorted(partner.items()))]
  transfers between devices with their start and end apart: 12 -> 12, of which waited for: 5 -> 4; matrix products, arithmetic and copies ran while one was open for 3% -> 0% of each run, Pallas kernels for 30% -> 28%
where the time goes in v12:
time: 53.4 us; the launch traced here: 53.3 us
  Pallas kernels  23.5 us (44%)
  starting transfers between devices  16.7 us (31%)
  waiting for transfers between devices  10.8 us (20%)
  other arithmetic  1.36 us (3%)
  between operations  0.87 us (2%)
    ppermute x6, starting transfers between devices, exchanged(): lax.ppermute(pieces[d], axes, [(i, i ^ d) for i in range(count)])  9.07 us
    pallas_call x1, Pallas kernels, down_pieces(): pl.pallas_call(functools.partial(down_kernel, groups, spans, capacity, sl...  6.66 us
    pallas_call x1, Pallas kernels, up_pieces(): pl.pallas_call(functools.partial(up_kernel, heads, capacity, len(pieces)...  6.31 us
    pallas_call x1, Pallas kernels, softmax_parts(): pl.pallas_call(softmax_kernel, out_shape=(jax.ShapeDtypeStruct((rows.tota...  5.54 us
    ppermute x6, waiting for transfers between devices, exchanged(): lax.ppermute(pieces[d], axes, [(i, i ^ d) for i in range(count)])  5.5 us
    ppermute x4, starting transfers between devices, swapped(): return lax.ppermute(x, ('core', 'grp'), sorted(partner.items()))  4.55 us
    ppermute x1, waiting for transfers between devices, summed(): other = lax.ppermute(other, axis, [(0, 1), (1, 0)])  3.53 us
    ppermute x1, starting transfers between devices, summed(): other = lax.ppermute(other, axis, [(0, 1), (1, 0)])  3.03 us
  transfers between devices with their start and end apart: 12, of which 4 were waited for; matrix products, arithmetic and copies ran while one was open for 0% of the time, Pallas kernels for 28%

profile of v12, /device:TPU:0, one launch (start us, length us, event | category | flops | bytes accessed | tf_op | source)
XLA Modules:
  0.0 53.3 jit_solution(2274249872689070588)
XLA Ops:
  0.7 6.7 %down_product.1 = (bf16[4,24,640]{2,1,0:T(8,128)(2,1)}, bf16[4,24,640]{2,1,0:T(8,128)(2,1)}) custom-call(s32[1,80]{1,0:T(1,128)} %bitcast.18, bf16[80,4096]{1,0:T(8,128)(2,1)} %rows_hbm.1, bf16[1280,4096]{1,0:T(8,128)(2,1)} %weight_ref.1), custom_call_target="tpu_custom_call" | custom-call | tf_op jit(solution)/shard_map/down_product/pallas_call | solution.py:124
  7.3 0.0 copy-start.2
  7.4 3.0 %collective-permute-start = (bf16[4,24,640]{2,1,0:T(8,128)(2,1)}, bf16[4,24,640]{2,1,0:T(8,128)(2,1)S(1)}, u32[]{:S(2)}, u32[]{:S(2)}) collective-permute-start(bf16[4,24,640]{2,1,0:T(8,128)(2,1)} %get-tuple-element.31), channel_id=1, source_target_pairs={{0,1},{1,0},{2,3},{3,2},{4,5},{5,4},{6,7},{7,6},{8,9},{9,8},{10,11... | collective-permute-start | bytes 368648 | tf_op jit(solution)/shard_map/ppermute | solution.py:480
  10.4 3.5 %collective-permute-done = bf16[4,24,640]{2,1,0:T(8,128)(2,1)S(1)} collective-permute-done((bf16[4,24,640]{2,1,0:T(8,128)(2,1)}, bf16[4,24,640]{2,1,0:T(8,128)(2,1)S(1)}, u32[]{:S(2)}, u32[]{:S(2)}) %collective-permute-start) | collective-permute-done | bytes 122912 | tf_op jit(solution)/shard_map/ppermute | solution.py:480
  13.9 0.9 %add_convert_fusion.1 = bf16[4,24,640]{2,1,0:T(8,128)(2,1)S(1)} fusion(bf16[4,24,640]{2,1,0:T(8,128)(2,1)} %get-tuple-element.32, bf16[4,24,640]{2,1,0:T(8,128)(2,1)S(1)} %collective-permute-done), kind=kLoop, calls=%fused_computation.2 | loop fusion | flops 245760 | bytes 368640 | tf_op jit(solution)/shard_map/convert_element_type | solution.py:481
  15.0 0.1 maximum_dynamic-update-slice_fusion.2
  15.1 0.1 maximum_dynamic-update-slice_fusion.1
  15.2 0.1 maximum_dynamic-update-slice_fusion
  15.3 1.9 %collective-permute-start.5 = (bf16[1200,128]{1,0:T(8,128)(2,1)S(1)}, bf16[1200,128]{1,0:T(8,128)(2,1)S(1)}, u32[]{:S(2)}, u32[]{:S(2)}) collective-permute-start(bf16[1200,128]{1,0:T(8,128)(2,1)S(1)} %maximum_dynamic-update-slice_fusion), channel_id=1, source_target_pairs={{0,2},{2,0},{4,6},{6,4},{8,10},{10,8},{12,14},{14,12},{1,3},{3,1},... | collective-permute-start | bytes 921608 | tf_op jit(solution)/shard_map/ppermute | solution.py:474
  17.2 0.0 collective-permute-start.4
  17.2 3.2 %collective-permute-start.1 = (bf16[1,24,640]{2,1,0:T(8,128)(2,1)S(1)}, bf16[1,24,640]{2,1,0:T(8,128)(2,1)S(1)}, u32[]{:S(2)}, u32[]{:S(2)}) collective-permute-start(bf16[1,24,640]{2,1,0:T(8,128)(2,1)S(1)} %get-tuple-element.34), channel_id=1, source_target_pairs={{0,2},{2,0},{4,6},{6,4},{1,3},{3,1},{5,7},{7,5},{8,10},{10,8},{12,... | collective-permute-start | bytes 92168 | tf_op jit(solution)/shard_map/ppermute | solution.py:488
  20.3 0.0 collective-permute-start.2
  20.3 2.4 %collective-permute-start.3 = (bf16[1,24,640]{2,1,0:T(8,128)(2,1)S(1)}, bf16[1,24,640]{2,1,0:T(8,128)(2,1)S(1)}, u32[]{:S(2)}, u32[]{:S(2)}) collective-permute-start(bf16[1,24,640]{2,1,0:T(8,128)(2,1)S(1)} %get-tuple-element.36), channel_id=1, source_target_pairs={{0,6},{2,4},{4,2},{6,0},{1,7},{3,5},{5,3},{7,1},{8,14},{10,12},{12... | collective-permute-start | bytes 92168 | tf_op jit(solution)/shard_map/ppermute | solution.py:488
  22.7 2.1 %collective-permute-done.1.refs_1_ = bf16[1,24,640]{2,1,0:T(8,128)(2,1)S(1)} collective-permute-done((bf16[1,24,640]{2,1,0:T(8,128)(2,1)S(1)}, bf16[1,24,640]{2,1,0:T(8,128)(2,1)S(1)}, u32[]{:S(2)}, u32[]{:S(2)}) %collective-permute-start.1) | collective-permute-done | bytes 30752 | tf_op jit(solution)/shard_map/ppermute | solution.py:488
  24.8 3.4 %collective-permute-done.2.refs_2_ = bf16[1,24,640]{2,1,0:T(8,128)(2,1)S(1)} collective-permute-done((bf16[1,24,640]{2,1,0:T(8,128)(2,1)S(1)}, bf16[1,24,640]{2,1,0:T(8,128)(2,1)S(1)}, u32[]{:S(2)}, u32[]{:S(2)}) %collective-permute-start.2) | collective-permute-done | bytes 30752 | tf_op jit(solution)/shard_map/ppermute | solution.py:488
  28.2 0.0 collective-permute-done.3.refs_3_
  28.2 6.3 %up_product.1 = (bf16[4,80,640]{2,1,0:T(8,128)(2,1)S(1)}, bf16[4,80,640]{2,1,0:T(8,128)(2,1)S(1)}) custom-call(bf16[1,24,640]{2,1,0:T(8,128)(2,1)S(1)} %get-tuple-element.33.refs_0_, bf16[1,24,640]{2,1,0:T(8,128)(2,1)S(1)} %collective-permute-done.1.refs_1_, bf16[1,24,640]{2,1,0:T(8,128)(2,1)S(1)} %collective-permute-done.2.refs_2_, ...), custom_call_target="tpu_custom_call" | custom-call | flops 2097152000 | bytes 26214400 | tf_op jit(solution)/shard_map/up_product/pallas_call | solution.py:215
  34.5 0.1 collective-permute-start.6
  34.6 1.7 %collective-permute-done.6 = bf16[4,80,640]{2,1,0:T(8,128)(2,1)S(1)} collective-permute-done((bf16[4,80,640]{2,1,0:T(8,128)(2,1)S(1)}, bf16[4,80,640]{2,1,0:T(8,128)(2,1)S(1)}, u32[]{:S(2)}, u32[]{:S(2)}) %collective-permute-start.6) | collective-permute-done | bytes 409632 | tf_op jit(solution)/shard_map/ppermute | solution.py:516
  36.4 0.1 add_convert_fusion
  36.5 2.5 %collective-permute-start.9 = (bf16[1,80,640]{2,1,0:T(8,128)(2,1)S(1)}, bf16[1,80,640]{2,1,0:T(8,128)(2,1)S(1)}, u32[]{:S(2)}, u32[]{:S(2)}) collective-permute-start(bf16[1,80,640]{2,1,0:T(8,128)(2,1)S(1)} %get-tuple-element.59), channel_id=1, source_target_pairs={{0,17},{1,16},{16,1},{17,0},{2,19},{3,18},{18,3},{19,2},{4,21},{5,... | collective-permute-start | bytes 307208 | tf_op jit(solution)/shard_map/ppermute | solution.py:488
  39.0 0.5 %collective-permute-start.8 = (bf16[1,80,640]{2,1,0:T(8,128)(2,1)S(1)}, bf16[1,80,640]{2,1,0:T(8,128)(2,1)S(1)}, u32[]{:S(2)}, u32[]{:S(2)}) collective-permute-start(bf16[1,80,640]{2,1,0:T(8,128)(2,1)S(1)} %get-tuple-element.60), channel_id=1, source_target_pairs={{0,16},{1,17},{16,0},{17,1},{2,18},{3,19},{18,2},{19,3},{4,20},{5,... | collective-permute-start | bytes 307208 | tf_op jit(solution)/shard_map/ppermute | solution.py:488
  39.6 0.5 collective-permute-start.7
  40.1 5.5 %softmax_parts.1 = (bf16[960,1024]{1,0:T(8,128)(2,1)S(1)}, bf16[1920,320]{1,0:T(8,128)(2,1)S(1)}, f32[8,128]{1,0:T(8,128)S(1)}) custom-call(s32[1,12]{1,0:T(1,128)S(1)} %bitcast.13, s32[1,1]{1,0:T(1,128)} %bitcast.6.first_ref, bf16[480,320]{1,0:T(8,128)(2,1)S(1)} %pad_maximum_fusion.own_ref, bf16[1200,128]{1,0:T(8,128)(2,1)S(1)} %collective-permute-done.4.odd_ref, ...), custom_call_target="tpu_custom_call" | custom-call | flops 20480000000 | bytes 102400000 | tf_op jit(solution)/shard_map/softmax_parts/pallas_call | solution.py:321
  45.6 0.0 collective-permute-done.9.refs_3_
  45.6 0.5 gather_sum.1
  46.1 0.1 collective-permute-start.11
  46.2 2.6 %collective-permute-start.10 = (bf16[400,128]{1,0:T(8,128)(2,1)S(1)}, bf16[400,128]{1,0:T(8,128)(2,1)S(1)}, u32[]{:S(2)}, u32[]{:S(2)}) collective-permute-start(bf16[400,128]{1,0:T(8,128)(2,1)S(1)} %get-tuple-element.51), channel_id=1, source_target_pairs={{0,2},{2,0},{4,6},{6,4},{8,10},{10,8},{12,14},{14,12},{1,3},{3,1},... | collective-permute-start | bytes 307208 | tf_op jit(solution)/shard_map/ppermute | solution.py:474
  48.8 2.4 %own_terms.1 = (bf16[160,320]{1,0:T(8,128)(2,1)}, f32[160,320]{1,0:T(8,128)S(1)}, f32[160,320]{1,0:T(8,128)S(1)}) custom-call(bf16[160,320]{1,0:T(8,128)(2,1)S(1)} %get-tuple-element.48.grad_ref, bf16[160,320]{1,0:T(8,128)(2,1)S(1)} %bitcast.12, bf16[960,1024]{1,0:T(8,128)(2,1)S(1)} %get-tuple-element.49.held_ref), custom_call_target="tpu_custom_call" | custom-call | tf_op jit(solution)/shard_map/own_terms/pallas_call | solution.py:417
  51.2 0.0 collective-permute-done.11.grad_ref
  51.2 0.7 %side_terms.2 = (f32[160,320]{1,0:T(8,128)S(1)}, f32[160,320]{1,0:T(8,128)S(1)}) custom-call(bf16[400,128]{1,0:T(8,128)(2,1)S(1)} %collective-permute-done.11.grad_ref, f32[160,320]{1,0:T(8,128)S(1)} %get-tuple-element.52.key_part_ref, f32[160,320]{1,0:T(8,128)S(1)} %get-tuple-element.53.value_part_ref, bf16[960,1024]{1,0:T(8,128)(2,1)S(1)} %get-tuple-element.49.held_ref, ...), custom_call_target="tpu_custom_call" | custom-call | tf_op jit(solution)/shard_map/side_terms/pallas_call | solution.py:454
  51.9 1.4 %side_terms.3 = (bf16[160,320]{1,0:T(8,128)(2,1)}, bf16[160,320]{1,0:T(8,128)(2,1)}) custom-call(bf16[400,128]{1,0:T(8,128)(2,1)S(1)} %collective-permute-done.10.grad_ref, f32[160,320]{1,0:T(8,128)S(1)} %get-tuple-element.55.key_part_ref, f32[160,320]{1,0:T(8,128)S(1)} %get-tuple-element.56.value_part_ref, ...), custom_call_target="tpu_custom_call" | custom-call | tf_op jit(solution)/shard_map/side_terms/pallas_call | solution.py:454
  (22 shorter events, 0.2 us)
Async XLA Ops:
  0.6 14.3 %copy-start.3 = (bf16[320,160]{0,1:T(8,128)(2,1)S(1)}, bf16[320,160]{0,1:T(8,128)(2,1)}, u32[]{:S(2)}) copy-start(bf16[320,160]{0,1:T(8,128)(2,1)} %param.16) | copy-start | bytes 307204
  0.6 14.3 %copy-start.4 = (bf16[320,160]{0,1:T(8,128)(2,1)S(1)}, bf16[320,160]{0,1:T(8,128)(2,1)}, u32[]{:S(2)}) copy-start(bf16[320,160]{0,1:T(8,128)(2,1)} %param.15) | copy-start | bytes 307204
  0.7 14.2 %copy-start = (bf16[320,160]{0,1:T(8,128)(2,1)S(1)}, bf16[320,160]{0,1:T(8,128)(2,1)}, u32[]{:S(2)}) copy-start(bf16[320,160]{0,1:T(8,128)(2,1)} %param.14) | copy-start | bytes 307204
  0.7 27.5 %copy-start.1 = (bf16[80,640]{1,0:T(8,128)(2,1)S(1)}, bf16[80,640]{1,0:T(8,128)(2,1)}, u32[]{:S(2)}) copy-start(bf16[80,640]{1,0:T(8,128)(2,1)} %refs_4_.1) | copy-start | bytes 307204
  7.3 32.7 %copy-start.2 = (s32[12]{0:T(128)S(1)}, s32[12]{0:T(128)}, u32[]{:S(2)}) copy-start(s32[12]{0:T(128)} %param.17) | copy-start | bytes 148
  7.4 6.6 %collective-permute-start = (bf16[4,24,640]{2,1,0:T(8,128)(2,1)}, bf16[4,24,640]{2,1,0:T(8,128)(2,1)S(1)}, u32[]{:S(2)}, u32[]{:S(2)}) collective-permute-start(bf16[4,24,640]{2,1,0:T(8,128)(2,1)} %get-tuple-element.31), channel_id=1, source_target_pairs={{0,1},{1,0},{2,3},{3,2},{4,5},{5,4},{6,7},{7,6},{8,9},{9,8},{10,11... | collective-permute-start | bytes 368648 | tf_op jit(solution)/shard_map/ppermute | solution.py:480
  15.3 19.2 %collective-permute-start.5 = (bf16[1200,128]{1,0:T(8,128)(2,1)S(1)}, bf16[1200,128]{1,0:T(8,128)(2,1)S(1)}, u32[]{:S(2)}, u32[]{:S(2)}) collective-permute-start(bf16[1200,128]{1,0:T(8,128)(2,1)S(1)} %maximum_dynamic-update-slice_fusion), channel_id=1, source_target_pairs={{0,2},{2,0},{4,6},{6,4},{8,10},{10,8},{12,14},{14,12},{1,3},{3,1},... | collective-permute-start | bytes 921608 | tf_op jit(solution)/shard_map/ppermute | solution.py:474
  17.2 17.3 %collective-permute-start.4 = (bf16[1200,128]{1,0:T(8,128)(2,1)S(1)}, bf16[1200,128]{1,0:T(8,128)(2,1)S(1)}, u32[]{:S(2)}, u32[]{:S(2)}) collective-permute-start(bf16[1200,128]{1,0:T(8,128)(2,1)S(1)} %maximum_dynamic-update-slice_fusion), channel_id=1, source_target_pairs={{0,8},{2,4},{4,2},{6,14},{8,0},{10,12},{12,10},{14,6},{1,9},{3,5},... | collective-permute-start | bytes 921608 | tf_op jit(solution)/shard_map/ppermute | solution.py:474
  17.2 7.6 %collective-permute-start.1 = (bf16[1,24,640]{2,1,0:T(8,128)(2,1)S(1)}, bf16[1,24,640]{2,1,0:T(8,128)(2,1)S(1)}, u32[]{:S(2)}, u32[]{:S(2)}) collective-permute-start(bf16[1,24,640]{2,1,0:T(8,128)(2,1)S(1)} %get-tuple-element.34), channel_id=1, source_target_pairs={{0,2},{2,0},{4,6},{6,4},{1,3},{3,1},{5,7},{7,5},{8,10},{10,8},{12,... | collective-permute-start | bytes 92168 | tf_op jit(solution)/shard_map/ppermute | solution.py:488
  20.3 7.9 %collective-permute-start.2 = (bf16[1,24,640]{2,1,0:T(8,128)(2,1)S(1)}, bf16[1,24,640]{2,1,0:T(8,128)(2,1)S(1)}, u32[]{:S(2)}, u32[]{:S(2)}) collective-permute-start(bf16[1,24,640]{2,1,0:T(8,128)(2,1)S(1)} %get-tuple-element.35), channel_id=1, source_target_pairs={{0,4},{2,6},{4,0},{6,2},{1,5},{3,7},{5,1},{7,3},{8,12},{10,14},{12... | collective-permute-start | bytes 92168 | tf_op jit(solution)/shard_map/ppermute | solution.py:488
  20.3 7.9 %collective-permute-start.3 = (bf16[1,24,640]{2,1,0:T(8,128)(2,1)S(1)}, bf16[1,24,640]{2,1,0:T(8,128)(2,1)S(1)}, u32[]{:S(2)}, u32[]{:S(2)}) collective-permute-start(bf16[1,24,640]{2,1,0:T(8,128)(2,1)S(1)} %get-tuple-element.36), channel_id=1, source_target_pairs={{0,6},{2,4},{4,2},{6,0},{1,7},{3,5},{5,3},{7,1},{8,14},{10,12},{12... | collective-permute-start | bytes 92168 | tf_op jit(solution)/shard_map/ppermute | solution.py:488
  34.5 1.8 %collective-permute-start.6 = (bf16[4,80,640]{2,1,0:T(8,128)(2,1)S(1)}, bf16[4,80,640]{2,1,0:T(8,128)(2,1)S(1)}, u32[]{:S(2)}, u32[]{:S(2)}) collective-permute-start(bf16[4,80,640]{2,1,0:T(8,128)(2,1)S(1)} %get-tuple-element.41), channel_id=1, source_target_pairs={{0,8},{8,0},{1,9},{9,1},{2,10},{10,2},{3,11},{11,3},{4,12},{12,4},... | collective-permute-start | bytes 1228808 | tf_op jit(solution)/shard_map/ppermute | solution.py:516
  36.5 9.1 %collective-permute-start.9 = (bf16[1,80,640]{2,1,0:T(8,128)(2,1)S(1)}, bf16[1,80,640]{2,1,0:T(8,128)(2,1)S(1)}, u32[]{:S(2)}, u32[]{:S(2)}) collective-permute-start(bf16[1,80,640]{2,1,0:T(8,128)(2,1)S(1)} %get-tuple-element.59), channel_id=1, source_target_pairs={{0,17},{1,16},{16,1},{17,0},{2,19},{3,18},{18,3},{19,2},{4,21},{5,... | collective-permute-start | bytes 307208 | tf_op jit(solution)/shard_map/ppermute | solution.py:488
  39.0 6.6 %collective-permute-start.8 = (bf16[1,80,640]{2,1,0:T(8,128)(2,1)S(1)}, bf16[1,80,640]{2,1,0:T(8,128)(2,1)S(1)}, u32[]{:S(2)}, u32[]{:S(2)}) collective-permute-start(bf16[1,80,640]{2,1,0:T(8,128)(2,1)S(1)} %get-tuple-element.60), channel_id=1, source_target_pairs={{0,16},{1,17},{16,0},{17,1},{2,18},{3,19},{18,2},{19,3},{4,20},{5,... | collective-permute-start | bytes 307208 | tf_op jit(solution)/shard_map/ppermute | solution.py:488
  39.6 6.1 %collective-permute-start.7 = (bf16[1,80,640]{2,1,0:T(8,128)(2,1)S(1)}, bf16[1,80,640]{2,1,0:T(8,128)(2,1)S(1)}, u32[]{:S(2)}, u32[]{:S(2)}) collective-permute-start(bf16[1,80,640]{2,1,0:T(8,128)(2,1)S(1)} %get-tuple-element.61), channel_id=1, source_target_pairs={{0,1},{1,0},{16,17},{17,16},{2,3},{3,2},{18,19},{19,18},{4,5},{5,4... | collective-permute-start | bytes 307208 | tf_op jit(solution)/shard_map/ppermute | solution.py:488
  46.1 5.1 %collective-permute-start.11 = (bf16[400,128]{1,0:T(8,128)(2,1)S(1)}, bf16[400,128]{1,0:T(8,128)(2,1)S(1)}, u32[]{:S(2)}, u32[]{:S(2)}) collective-permute-start(bf16[400,128]{1,0:T(8,128)(2,1)S(1)} %get-tuple-element.51), channel_id=1, source_target_pairs={{0,8},{2,4},{4,2},{6,14},{8,0},{10,12},{12,10},{14,6},{1,9},{3,5},... | collective-permute-start | bytes 307208 | tf_op jit(solution)/shard_map/ppermute | solution.py:474
  46.2 5.7 %collective-permute-start.10 = (bf16[400,128]{1,0:T(8,128)(2,1)S(1)}, bf16[400,128]{1,0:T(8,128)(2,1)S(1)}, u32[]{:S(2)}, u32[]{:S(2)}) collective-permute-start(bf16[400,128]{1,0:T(8,128)(2,1)S(1)} %get-tuple-element.51), channel_id=1, source_target_pairs={{0,2},{2,0},{4,6},{6,4},{8,10},{10,8},{12,14},{14,12},{1,3},{3,1},... | collective-permute-start | bytes 307208 | tf_op jit(solution)/shard_map/ppermute | solution.py:474

commit v13 on v10

--- a/solution.py
+++ b/solution.py
@@ -266,6 +266,13 @@
         start = (jnp.where(token < 0, -1, 0), jnp.int32(0))
         return lax.fori_loop(0, lengths_ref.shape[1], step, start)[0]
 
+    def near(start, i, h):
+        part = held[rows.head(start, h), :]
+        if i == 0:
+            return part[:, : 2 * patches]
+        parts = [part[:, :patches], part[:, 2 * patches : 3 * patches]]
+        return jnp.concatenate([x.astype(jnp.float32) for x in parts], 1).astype(jnp.bfloat16)
+
     down = [image_of((patches, 1), 0, b) for b in offsets]
     across = [image_of((1, patches), 1, b) for b in offsets]
 
@@ -295,8 +302,8 @@
         for i, b in enumerate((1, 2)):
             queries_at, attended_at = rows.side(i)
             queries = kind(b, 0, h).astype(jnp.bfloat16)
-            probs = softmax(queries, wide(1, (0, b), h), same_side[i])
-            seen = dot(probs.astype(jnp.bfloat16), wide(2, (0, b), h), NT)
+            probs = softmax(queries, near(rows.keys, i, h), same_side[i])
+            seen = dot(probs.astype(jnp.bfloat16), near(rows.values, i, h), NT)
             side_ref[rows.head(queries_at, h)] = queries
             side_ref[rows.head(attended_at, h)] = seen.T.astype(jnp.bfloat16)
             side_ref[rows.side_probs(i, h)] = probs[:, :patches].T.astype(jnp.bfloat16)

time: 49.1 us -> 49 us (level)
  no operation moved by 1% of the time
where the time goes in v13:
time: 49 us; the launch traced here: 48.8 us
  Pallas kernels  23 us (47%)
  starting transfers between devices  13.5 us (28%)
  waiting for transfers between devices  10.9 us (22%)
  between operations  0.85 us (2%)
    all_to_all x1, waiting for transfers between devices, on_device(): lax.all_to_all(pieces, ('grp', 'span'), split_axis=0, concat_axis=0, tile...  7.32 us
    all_to_all x1, starting transfers between devices, on_device(): lax.all_to_all(pieces, ('grp', 'span'), split_axis=0, concat_axis=0, tile...  7.29 us
    pallas_call x1, Pallas kernels, down_pieces(): pl.pallas_call(functools.partial(down_kernel, groups, spans, capacity, sl...  6.58 us
    pallas_call x1, Pallas kernels, up_pieces(): pl.pallas_call(functools.partial(up_kernel, heads, capacity), out_shape=[...  6.14 us
    pallas_call x1, Pallas kernels, softmax_parts(): pl.pallas_call(softmax_kernel, out_shape=(jax.ShapeDtypeStruct((rows.tota...  5.37 us
    ppermute x3, starting transfers between devices, exchanged(): lax.ppermute(pieces[d], axes, [(i, i ^ d) for i in range(count)])  3.55 us
    ppermute x4, starting transfers between devices, swapped(): return lax.ppermute(x, ('core', 'grp'), sorted(partner.items()))  2.58 us
    pallas_call x1, Pallas kernels, own_terms(): pl.pallas_call(own_kernel, out_shape=(jax.ShapeDtypeStruct(grad.shape, jn...  2.36 us
  transfers between devices with their start and end apart: 9, of which 3 were waited for; matrix products, arithmetic and copies ran while one was open for 1% of the time, Pallas kernels for 30%

profile of v13, /device:TPU:0, one launch (start us, length us, event | category | flops | bytes accessed | tf_op | source)
XLA Modules:
  0.0 48.8 jit_solution(6756864169510306809)
XLA Ops:
  0.6 0.0 copy-start.4
  0.6 0.0 copy-start.3
  0.7 6.6 %down_product.1 = bf16[4,2,24,640]{3,2,1,0:T(8,128)(2,1)} custom-call(s32[1,80]{1,0:T(1,128)} %bitcast.20, bf16[80,4096]{1,0:T(8,128)(2,1)} %rows_hbm.1, bf16[1280,4096]{1,0:T(8,128)(2,1)} %weight_ref.1), custom_call_target="tpu_custom_call" | custom-call | tf_op jit(solution)/shard_map/down_product/pallas_call | solution.py:118
  7.3 0.0 copy-start.2
  7.3 7.3 %all-to-all-start = ((bf16[8,24,640]{2,1,0:T(8,128)(2,1)}), bf16[8,24,640]{2,1,0:T(8,128)(2,1)S(1)}, u32[]{:S(2)}, u32[]{:S(2)}) async-start(bf16[8,24,640]{2,1,0:T(8,128)(2,1)} %bitcast.15), calls=%async_computation | async-start | bytes 491520 | tf_op jit(solution)/shard_map/all_to_all | solution.py:495
  14.7 0.1 maximum_dynamic-update-slice_fusion.2
  14.8 0.1 maximum_dynamic-update-slice_fusion.1
  14.9 0.1 maximum_dynamic-update-slice_fusion
  15.0 2.1 %collective-permute-start.1 = (bf16[1200,128]{1,0:T(8,128)(2,1)S(1)}, bf16[1200,128]{1,0:T(8,128)(2,1)S(1)}, u32[]{:S(2)}, u32[]{:S(2)}) collective-permute-start(bf16[1200,128]{1,0:T(8,128)(2,1)S(1)} %maximum_dynamic-update-slice_fusion), channel_id=1, source_target_pairs={{0,2},{2,0},{4,6},{6,4},{8,10},{10,8},{12,14},{14,12},{1,3},{3,1},... | collective-permute-start | bytes 921608 | tf_op jit(solution)/shard_map/ppermute | solution.py:471
  17.1 0.0 collective-permute-start
  17.1 7.3 %all-to-all-done.pieces_ref = bf16[8,24,640]{2,1,0:T(8,128)(2,1)S(1)} async-done(((bf16[8,24,640]{2,1,0:T(8,128)(2,1)}), bf16[8,24,640]{2,1,0:T(8,128)(2,1)S(1)}, u32[]{:S(2)}, u32[]{:S(2)}) %all-to-all-start) | async-done | bytes 245792 | tf_op jit(solution)/shard_map/all_to_all | solution.py:495
  24.4 6.1 %up_product.1 = (bf16[4,80,640]{2,1,0:T(8,128)(2,1)S(1)}, bf16[4,80,640]{2,1,0:T(8,128)(2,1)S(1)}) custom-call(bf16[8,24,640]{2,1,0:T(8,128)(2,1)S(1)} %all-to-all-done.pieces_ref, bf16[80,640]{1,0:T(8,128)(2,1)S(1)} %copy-done.1, bf16[4,4,320,640]{3,2,1,0:T(8,128)(2,1)} %bitcast.21), custom_call_target="tpu_custom_call" | custom-call | flops 2097152000 | bytes 26214400 | tf_op jit(solution)/shard_map/up_product/pallas_call | solution.py:205
  30.6 0.0 collective-permute-done.1.even_ref
  30.6 0.0 collective-permute-done.odd_ref
  30.6 0.1 collective-permute-start.2
  30.7 1.7 %collective-permute-done.2 = bf16[4,80,640]{2,1,0:T(8,128)(2,1)S(1)} collective-permute-done((bf16[4,80,640]{2,1,0:T(8,128)(2,1)S(1)}, bf16[4,80,640]{2,1,0:T(8,128)(2,1)S(1)}, u32[]{:S(2)}, u32[]{:S(2)}) %collective-permute-start.2) | collective-permute-done | bytes 409632 | tf_op jit(solution)/shard_map/ppermute | solution.py:501
  32.4 0.1 add_convert_fusion
  32.5 2.3 %collective-permute-start.5 = (bf16[1,80,640]{2,1,0:T(8,128)(2,1)S(1)}, bf16[1,80,640]{2,1,0:T(8,128)(2,1)S(1)}, u32[]{:S(2)}, u32[]{:S(2)}) collective-permute-start(bf16[1,80,640]{2,1,0:T(8,128)(2,1)S(1)} %get-tuple-element.49), channel_id=1, source_target_pairs={{0,17},{1,16},{16,1},{17,0},{2,19},{3,18},{18,3},{19,2},{4,21},{5,... | collective-permute-start | bytes 307208 | tf_op jit(solution)/shard_map/ppermute | solution.py:479
  34.8 0.5 %collective-permute-start.4 = (bf16[1,80,640]{2,1,0:T(8,128)(2,1)S(1)}, bf16[1,80,640]{2,1,0:T(8,128)(2,1)S(1)}, u32[]{:S(2)}, u32[]{:S(2)}) collective-permute-start(bf16[1,80,640]{2,1,0:T(8,128)(2,1)S(1)} %get-tuple-element.50), channel_id=1, source_target_pairs={{0,16},{1,17},{16,0},{17,1},{2,18},{3,19},{18,2},{19,3},{4,20},{5,... | collective-permute-start | bytes 307208 | tf_op jit(solution)/shard_map/ppermute | solution.py:479
  35.3 0.7 %collective-permute-start.3 = (bf16[1,80,640]{2,1,0:T(8,128)(2,1)S(1)}, bf16[1,80,640]{2,1,0:T(8,128)(2,1)S(1)}, u32[]{:S(2)}, u32[]{:S(2)}) collective-permute-start(bf16[1,80,640]{2,1,0:T(8,128)(2,1)S(1)} %get-tuple-element.51), channel_id=1, source_target_pairs={{0,1},{1,0},{16,17},{17,16},{2,3},{3,2},{18,19},{19,18},{4,5},{5,4... | collective-permute-start | bytes 307208 | tf_op jit(solution)/shard_map/ppermute | solution.py:479
  36.1 5.4 %softmax_parts.1 = (bf16[960,1024]{1,0:T(8,128)(2,1)S(1)}, bf16[1920,320]{1,0:T(8,128)(2,1)S(1)}, f32[8,128]{1,0:T(8,128)S(1)}) custom-call(s32[1,12]{1,0:T(1,128)S(1)} %bitcast.14, s32[1,1]{1,0:T(1,128)} %bitcast.7.first_ref, bf16[480,320]{1,0:T(8,128)(2,1)S(1)} %pad_maximum_fusion.own_ref, bf16[1200,128]{1,0:T(8,128)(2,1)S(1)} %collective-permute-done.odd_ref, ...), custom_call_target="tpu_custom_call" | custom-call | flops 20480000000 | bytes 102400000 | tf_op jit(solution)/shard_map/softmax_parts/pallas_call | solution.py:318
  41.5 0.0 collective-permute-done.5.refs_3_
  41.5 0.0 collective-permute-done.4.refs_2_
  41.5 0.0 collective-permute-done.3.refs_1_
  41.5 0.5 %gather_sum.1 = (bf16[160,320]{1,0:T(8,128)(2,1)S(1)}, bf16[400,128]{1,0:T(8,128)(2,1)S(1)}) custom-call(bf16[1,80,640]{2,1,0:T(8,128)(2,1)S(1)} %get-tuple-element.52.refs_0_, bf16[1,80,640]{2,1,0:T(8,128)(2,1)S(1)} %collective-permute-done.3.refs_1_, bf16[1,80,640]{2,1,0:T(8,128)(2,1)S(1)} %collective-permute-done.4.refs_2_, ...), custom_call_target="tpu_custom_call" | custom-call | flops 4096000000 | bytes 81920000 | tf_op jit(solution)/shard_map/gather_sum/pallas_call | solution.py:380
  42.0 0.1 collective-permute-start.7
  42.1 0.4 collective-permute-start.6
  42.5 2.4 %own_terms.1 = (bf16[160,320]{1,0:T(8,128)(2,1)}, f32[160,320]{1,0:T(8,128)S(1)}, f32[160,320]{1,0:T(8,128)S(1)}) custom-call(bf16[160,320]{1,0:T(8,128)(2,1)S(1)} %get-tuple-element.38.grad_ref, bf16[160,320]{1,0:T(8,128)(2,1)S(1)} %bitcast.13, bf16[960,1024]{1,0:T(8,128)(2,1)S(1)} %get-tuple-element.39.held_ref), custom_call_target="tpu_custom_call" | custom-call | tf_op jit(solution)/shard_map/own_terms/pallas_call | solution.py:414
  44.9 0.0 collective-permute-done.7.grad_ref
  44.9 0.7 %side_terms.2 = (f32[160,320]{1,0:T(8,128)S(1)}, f32[160,320]{1,0:T(8,128)S(1)}) custom-call(bf16[400,128]{1,0:T(8,128)(2,1)S(1)} %collective-permute-done.7.grad_ref, f32[160,320]{1,0:T(8,128)S(1)} %get-tuple-element.42.key_part_ref, f32[160,320]{1,0:T(8,128)S(1)} %get-tuple-element.43.value_part_ref, bf16[960,1024]{1,0:T(8,128)(2,1)S(1)} %get-tuple-element.39.held_ref, ...), custom_call_target="tpu_custom_call" | custom-call | tf_op jit(solution)/shard_map/side_terms/pallas_call | solution.py:451
  45.6 1.8 %collective-permute-done.6.grad_ref = bf16[400,128]{1,0:T(8,128)(2,1)S(1)} collective-permute-done((bf16[400,128]{1,0:T(8,128)(2,1)S(1)}, bf16[400,128]{1,0:T(8,128)(2,1)S(1)}, u32[]{:S(2)}, u32[]{:S(2)}) %collective-permute-start.6) | collective-permute-done | bytes 102432 | tf_op jit(solution)/shard_map/ppermute | solution.py:471
  47.4 1.4 %side_terms.3 = (bf16[160,320]{1,0:T(8,128)(2,1)}, bf16[160,320]{1,0:T(8,128)(2,1)}) custom-call(bf16[400,128]{1,0:T(8,128)(2,1)S(1)} %collective-permute-done.6.grad_ref, f32[160,320]{1,0:T(8,128)S(1)} %get-tuple-element.45.key_part_ref, f32[160,320]{1,0:T(8,128)S(1)} %get-tuple-element.46.value_part_ref, bf16[960,1024]{1,0:T(8,128)(2,1)S(1)} %get-tuple-element.39.held_ref, ...), custom_call_target="tpu_custom_call" | custom-call | tf_op jit(solution)/shard_map/side_terms/pallas_call | solution.py:451
  (14 shorter events, 0.1 us)
Async XLA Ops:
  0.6 14.0 %copy-start.4 = (bf16[320,160]{0,1:T(8,128)(2,1)S(1)}, bf16[320,160]{0,1:T(8,128)(2,1)}, u32[]{:S(2)}) copy-start(bf16[320,160]{0,1:T(8,128)(2,1)} %param.16) | copy-start | bytes 307204
  0.6 13.9 %copy-start.3 = (bf16[320,160]{0,1:T(8,128)(2,1)S(1)}, bf16[320,160]{0,1:T(8,128)(2,1)}, u32[]{:S(2)}) copy-start(bf16[320,160]{0,1:T(8,128)(2,1)} %param.15) | copy-start | bytes 307204
  0.7 13.9 %copy-start = (bf16[320,160]{0,1:T(8,128)(2,1)S(1)}, bf16[320,160]{0,1:T(8,128)(2,1)}, u32[]{:S(2)}) copy-start(bf16[320,160]{0,1:T(8,128)(2,1)} %param.14) | copy-start | bytes 307204
  0.7 23.7 %copy-start.1 = (bf16[80,640]{1,0:T(8,128)(2,1)S(1)}, bf16[80,640]{1,0:T(8,128)(2,1)}, u32[]{:S(2)}) copy-start(bf16[80,640]{1,0:T(8,128)(2,1)} %pre_ref.1) | copy-start | bytes 307204
  7.3 28.8 %copy-start.2 = (s32[12]{0:T(128)S(1)}, s32[12]{0:T(128)}, u32[]{:S(2)}) copy-start(s32[12]{0:T(128)} %param.17) | copy-start | bytes 148
  7.3 17.1 %all-to-all-start = ((bf16[8,24,640]{2,1,0:T(8,128)(2,1)}), bf16[8,24,640]{2,1,0:T(8,128)(2,1)S(1)}, u32[]{:S(2)}, u32[]{:S(2)}) async-start(bf16[8,24,640]{2,1,0:T(8,128)(2,1)} %bitcast.15), calls=%async_computation | async-start | bytes 491520 | tf_op jit(solution)/shard_map/all_to_all | solution.py:495
  15.0 15.6 %collective-permute-start.1 = (bf16[1200,128]{1,0:T(8,128)(2,1)S(1)}, bf16[1200,128]{1,0:T(8,128)(2,1)S(1)}, u32[]{:S(2)}, u32[]{:S(2)}) collective-permute-start(bf16[1200,128]{1,0:T(8,128)(2,1)S(1)} %maximum_dynamic-update-slice_fusion), channel_id=1, source_target_pairs={{0,2},{2,0},{4,6},{6,4},{8,10},{10,8},{12,14},{14,12},{1,3},{3,1},... | collective-permute-start | bytes 921608 | tf_op jit(solution)/shard_map/ppermute | solution.py:471
  17.1 13.5 %collective-permute-start = (bf16[1200,128]{1,0:T(8,128)(2,1)S(1)}, bf16[1200,128]{1,0:T(8,128)(2,1)S(1)}, u32[]{:S(2)}, u32[]{:S(2)}) collective-permute-start(bf16[1200,128]{1,0:T(8,128)(2,1)S(1)} %maximum_dynamic-update-slice_fusion), channel_id=1, source_target_pairs={{0,8},{2,4},{4,2},{6,14},{8,0},{10,12},{12,10},{14,6},{1,9},{3,5},... | collective-permute-start | bytes 921608 | tf_op jit(solution)/shard_map/ppermute | solution.py:471
  30.6 1.8 %collective-permute-start.2 = (bf16[4,80,640]{2,1,0:T(8,128)(2,1)S(1)}, bf16[4,80,640]{2,1,0:T(8,128)(2,1)S(1)}, u32[]{:S(2)}, u32[]{:S(2)}) collective-permute-start(bf16[4,80,640]{2,1,0:T(8,128)(2,1)S(1)} %get-tuple-element.31), channel_id=1, source_target_pairs={{0,8},{8,0},{1,9},{9,1},{2,10},{10,2},{3,11},{11,3},{4,12},{12,4},... | collective-permute-start | bytes 1228808 | tf_op jit(solution)/shard_map/ppermute | solution.py:501
  32.5 8.9 %collective-permute-start.5 = (bf16[1,80,640]{2,1,0:T(8,128)(2,1)S(1)}, bf16[1,80,640]{2,1,0:T(8,128)(2,1)S(1)}, u32[]{:S(2)}, u32[]{:S(2)}) collective-permute-start(bf16[1,80,640]{2,1,0:T(8,128)(2,1)S(1)} %get-tuple-element.49), channel_id=1, source_target_pairs={{0,17},{1,16},{16,1},{17,0},{2,19},{3,18},{18,3},{19,2},{4,21},{5,... | collective-permute-start | bytes 307208 | tf_op jit(solution)/shard_map/ppermute | solution.py:479
  34.8 6.7 %collective-permute-start.4 = (bf16[1,80,640]{2,1,0:T(8,128)(2,1)S(1)}, bf16[1,80,640]{2,1,0:T(8,128)(2,1)S(1)}, u32[]{:S(2)}, u32[]{:S(2)}) collective-permute-start(bf16[1,80,640]{2,1,0:T(8,128)(2,1)S(1)} %get-tuple-element.50), channel_id=1, source_target_pairs={{0,16},{1,17},{16,0},{17,1},{2,18},{3,19},{18,2},{19,3},{4,20},{5,... | collective-permute-start | bytes 307208 | tf_op jit(solution)/shard_map/ppermute | solution.py:479
  35.3 6.1 %collective-permute-start.3 = (bf16[1,80,640]{2,1,0:T(8,128)(2,1)S(1)}, bf16[1,80,640]{2,1,0:T(8,128)(2,1)S(1)}, u32[]{:S(2)}, u32[]{:S(2)}) collective-permute-start(bf16[1,80,640]{2,1,0:T(8,128)(2,1)S(1)} %get-tuple-element.51), channel_id=1, source_target_pairs={{0,1},{1,0},{16,17},{17,16},{2,3},{3,2},{18,19},{19,18},{4,5},{5,4... | collective-permute-start | bytes 307208 | tf_op jit(solution)/shard_map/ppermute | solution.py:479
  42.0 2.9 %collective-permute-start.7 = (bf16[400,128]{1,0:T(8,128)(2,1)S(1)}, bf16[400,128]{1,0:T(8,128)(2,1)S(1)}, u32[]{:S(2)}, u32[]{:S(2)}) collective-permute-start(bf16[400,128]{1,0:T(8,128)(2,1)S(1)} %get-tuple-element.41), channel_id=1, source_target_pairs={{0,8},{2,4},{4,2},{6,14},{8,0},{10,12},{12,10},{14,6},{1,9},{3,5},... | collective-permute-start | bytes 307208 | tf_op jit(solution)/shard_map/ppermute | solution.py:471
  42.1 5.3 %collective-permute-start.6 = (bf16[400,128]{1,0:T(8,128)(2,1)S(1)}, bf16[400,128]{1,0:T(8,128)(2,1)S(1)}, u32[]{:S(2)}, u32[]{:S(2)}) collective-permute-start(bf16[400,128]{1,0:T(8,128)(2,1)S(1)} %get-tuple-element.41), channel_id=1, source_target_pairs={{0,2},{2,0},{4,6},{6,4},{8,10},{10,8},{12,14},{14,12},{1,3},{3,1},... | collective-permute-start | bytes 307208 | tf_op jit(solution)/shard_map/ppermute | solution.py:471

commit v14 on v13

--- a/solution.py
+++ b/solution.py
@@ -273,8 +273,8 @@
         parts = [part[:, :patches], part[:, 2 * patches : 3 * patches]]
         return jnp.concatenate([x.astype(jnp.float32) for x in parts], 1).astype(jnp.bfloat16)
 
-    down = [image_of((patches, 1), 0, b) for b in offsets]
-    across = [image_of((1, patches), 1, b) for b in offsets]
+    across = [image_of((1, patches), 1, b).astype(jnp.float32) for b in offsets]
+    down = [jnp.broadcast_to(x, (128, patches)).T[:, :1] for x in across]
 
     def kind(block, t, h):
         if block == 0:

time: 49 us -> 48.4 us (0.988)
  Pallas kernels: 23 us -> 22.4 us
    pallas_call x1, Pallas kernels: 5.37 us -> 4.78 us  [softmax_parts(): pl.pallas_call(softmax_kernel, out_shape=(jax.ShapeDtypeStruct((rows.tota...]
  transfers between devices with their start and end apart: 9 -> 9, of which waited for: 3 -> 3; matrix products, arithmetic and copies ran while one was open for 1% -> 1% of each run, Pallas kernels for 30% -> 29%
where the time goes in v14:
time: 48.4 us; the launch traced here: 48.2 us
  Pallas kernels  22.4 us (46%)
  starting transfers between devices  13.5 us (28%)
  waiting for transfers between devices  10.9 us (23%)
  between operations  0.85 us (2%)
    all_to_all x1, waiting for transfers between devices, on_device(): lax.all_to_all(pieces, ('grp', 'span'), split_axis=0, concat_axis=0, tile...  7.32 us
    all_to_all x1, starting transfers between devices, on_device(): lax.all_to_all(pieces, ('grp', 'span'), split_axis=0, concat_axis=0, tile...  7.29 us
    pallas_call x1, Pallas kernels, down_pieces(): pl.pallas_call(functools.partial(down_kernel, groups, spans, capacity, sl...  6.58 us
    pallas_call x1, Pallas kernels, up_pieces(): pl.pallas_call(functools.partial(up_kernel, heads, capacity), out_shape=[...  6.14 us
    pallas_call x1, Pallas kernels, softmax_parts(): pl.pallas_call(softmax_kernel, out_shape=(jax.ShapeDtypeStruct((rows.tota...  4.78 us
    ppermute x3, starting transfers between devices, exchanged(): lax.ppermute(pieces[d], axes, [(i, i ^ d) for i in range(count)])  3.55 us
    ppermute x4, starting transfers between devices, swapped(): return lax.ppermute(x, ('core', 'grp'), sorted(partner.items()))  2.58 us
    pallas_call x1, Pallas kernels, own_terms(): pl.pallas_call(own_kernel, out_shape=(jax.ShapeDtypeStruct(grad.shape, jn...  2.36 us
  transfers between devices with their start and end apart: 9, of which 3 were waited for; matrix products, arithmetic and copies ran while one was open for 1% of the time, Pallas kernels for 29%

profile of v14, /device:TPU:0, one launch (start us, length us, event | category | flops | bytes accessed | tf_op | source)
XLA Modules:
  0.0 48.2 jit_solution(15095321168115953625)
XLA Ops:
  0.6 0.0 copy-start.4
  0.6 0.0 copy-start.3
  0.7 6.6 %down_product.1 = bf16[4,2,24,640]{3,2,1,0:T(8,128)(2,1)} custom-call(s32[1,80]{1,0:T(1,128)} %bitcast.20, bf16[80,4096]{1,0:T(8,128)(2,1)} %rows_hbm.1, bf16[1280,4096]{1,0:T(8,128)(2,1)} %weight_ref.1), custom_call_target="tpu_custom_call" | custom-call | tf_op jit(solution)/shard_map/down_product/pallas_call | solution.py:118
  7.3 0.0 copy-start.2
  7.3 7.3 %all-to-all-start = ((bf16[8,24,640]{2,1,0:T(8,128)(2,1)}), bf16[8,24,640]{2,1,0:T(8,128)(2,1)S(1)}, u32[]{:S(2)}, u32[]{:S(2)}) async-start(bf16[8,24,640]{2,1,0:T(8,128)(2,1)} %bitcast.15), calls=%async_computation | async-start | bytes 491520 | tf_op jit(solution)/shard_map/all_to_all | solution.py:495
  14.7 0.1 maximum_dynamic-update-slice_fusion.2
  14.8 0.1 maximum_dynamic-update-slice_fusion.1
  14.9 0.1 maximum_dynamic-update-slice_fusion
  15.0 2.1 %collective-permute-start.1 = (bf16[1200,128]{1,0:T(8,128)(2,1)S(1)}, bf16[1200,128]{1,0:T(8,128)(2,1)S(1)}, u32[]{:S(2)}, u32[]{:S(2)}) collective-permute-start(bf16[1200,128]{1,0:T(8,128)(2,1)S(1)} %maximum_dynamic-update-slice_fusion), channel_id=1, source_target_pairs={{0,2},{2,0},{4,6},{6,4},{8,10},{10,8},{12,14},{14,12},{1,3},{3,1},... | collective-permute-start | bytes 921608 | tf_op jit(solution)/shard_map/ppermute | solution.py:471
  17.1 0.0 collective-permute-start
  17.1 7.3 %all-to-all-done.pieces_ref = bf16[8,24,640]{2,1,0:T(8,128)(2,1)S(1)} async-done(((bf16[8,24,640]{2,1,0:T(8,128)(2,1)}), bf16[8,24,640]{2,1,0:T(8,128)(2,1)S(1)}, u32[]{:S(2)}, u32[]{:S(2)}) %all-to-all-start) | async-done | bytes 245792 | tf_op jit(solution)/shard_map/all_to_all | solution.py:495
  24.4 6.1 %up_product.1 = (bf16[4,80,640]{2,1,0:T(8,128)(2,1)S(1)}, bf16[4,80,640]{2,1,0:T(8,128)(2,1)S(1)}) custom-call(bf16[8,24,640]{2,1,0:T(8,128)(2,1)S(1)} %all-to-all-done.pieces_ref, bf16[80,640]{1,0:T(8,128)(2,1)S(1)} %copy-done.1, bf16[4,4,320,640]{3,2,1,0:T(8,128)(2,1)} %bitcast.21), custom_call_target="tpu_custom_call" | custom-call | flops 2097152000 | bytes 26214400 | tf_op jit(solution)/shard_map/up_product/pallas_call | solution.py:205
  30.6 0.0 collective-permute-done.1.even_ref
  30.6 0.0 collective-permute-done.odd_ref
  30.6 0.1 collective-permute-start.2
  30.7 1.7 %collective-permute-done.2 = bf16[4,80,640]{2,1,0:T(8,128)(2,1)S(1)} collective-permute-done((bf16[4,80,640]{2,1,0:T(8,128)(2,1)S(1)}, bf16[4,80,640]{2,1,0:T(8,128)(2,1)S(1)}, u32[]{:S(2)}, u32[]{:S(2)}) %collective-permute-start.2) | collective-permute-done | bytes 409632 | tf_op jit(solution)/shard_map/ppermute | solution.py:501
  32.4 0.1 add_convert_fusion
  32.5 2.3 %collective-permute-start.5 = (bf16[1,80,640]{2,1,0:T(8,128)(2,1)S(1)}, bf16[1,80,640]{2,1,0:T(8,128)(2,1)S(1)}, u32[]{:S(2)}, u32[]{:S(2)}) collective-permute-start(bf16[1,80,640]{2,1,0:T(8,128)(2,1)S(1)} %get-tuple-element.49), channel_id=1, source_target_pairs={{0,17},{1,16},{16,1},{17,0},{2,19},{3,18},{18,3},{19,2},{4,21},{5,... | collective-permute-start | bytes 307208 | tf_op jit(solution)/shard_map/ppermute | solution.py:479
  34.8 0.5 %collective-permute-start.4 = (bf16[1,80,640]{2,1,0:T(8,128)(2,1)S(1)}, bf16[1,80,640]{2,1,0:T(8,128)(2,1)S(1)}, u32[]{:S(2)}, u32[]{:S(2)}) collective-permute-start(bf16[1,80,640]{2,1,0:T(8,128)(2,1)S(1)} %get-tuple-element.50), channel_id=1, source_target_pairs={{0,16},{1,17},{16,0},{17,1},{2,18},{3,19},{18,2},{19,3},{4,20},{5,... | collective-permute-start | bytes 307208 | tf_op jit(solution)/shard_map/ppermute | solution.py:479
  35.3 0.7 %collective-permute-start.3 = (bf16[1,80,640]{2,1,0:T(8,128)(2,1)S(1)}, bf16[1,80,640]{2,1,0:T(8,128)(2,1)S(1)}, u32[]{:S(2)}, u32[]{:S(2)}) collective-permute-start(bf16[1,80,640]{2,1,0:T(8,128)(2,1)S(1)} %get-tuple-element.51), channel_id=1, source_target_pairs={{0,1},{1,0},{16,17},{17,16},{2,3},{3,2},{18,19},{19,18},{4,5},{5,4... | collective-permute-start | bytes 307208 | tf_op jit(solution)/shard_map/ppermute | solution.py:479
  36.1 4.8 %softmax_parts.1 = (bf16[960,1024]{1,0:T(8,128)(2,1)S(1)}, bf16[1920,320]{1,0:T(8,128)(2,1)S(1)}, f32[8,128]{1,0:T(8,128)S(1)}) custom-call(s32[1,12]{1,0:T(1,128)S(1)} %bitcast.14, s32[1,1]{1,0:T(1,128)} %bitcast.7.first_ref, bf16[480,320]{1,0:T(8,128)(2,1)S(1)} %pad_maximum_fusion.own_ref, bf16[1200,128]{1,0:T(8,128)(2,1)S(1)} %collective-permute-done.odd_ref, ...), custom_call_target="tpu_custom_call" | custom-call | flops 20480000000 | bytes 102400000 | tf_op jit(solution)/shard_map/softmax_parts/pallas_call | solution.py:318
  40.9 0.0 collective-permute-done.5.refs_3_
  40.9 0.0 collective-permute-done.4.refs_2_
  40.9 0.0 collective-permute-done.3.refs_1_
  40.9 0.5 %gather_sum.1 = (bf16[160,320]{1,0:T(8,128)(2,1)S(1)}, bf16[400,128]{1,0:T(8,128)(2,1)S(1)}) custom-call(bf16[1,80,640]{2,1,0:T(8,128)(2,1)S(1)} %get-tuple-element.52.refs_0_, bf16[1,80,640]{2,1,0:T(8,128)(2,1)S(1)} %collective-permute-done.3.refs_1_, bf16[1,80,640]{2,1,0:T(8,128)(2,1)S(1)} %collective-permute-done.4.refs_2_, ...), custom_call_target="tpu_custom_call" | custom-call | flops 4096000000 | bytes 81920000 | tf_op jit(solution)/shard_map/gather_sum/pallas_call | solution.py:380
  41.4 0.1 collective-permute-start.7
  41.5 0.4 collective-permute-start.6
  41.9 2.4 %own_terms.1 = (bf16[160,320]{1,0:T(8,128)(2,1)}, f32[160,320]{1,0:T(8,128)S(1)}, f32[160,320]{1,0:T(8,128)S(1)}) custom-call(bf16[160,320]{1,0:T(8,128)(2,1)S(1)} %get-tuple-element.38.grad_ref, bf16[160,320]{1,0:T(8,128)(2,1)S(1)} %bitcast.13, bf16[960,1024]{1,0:T(8,128)(2,1)S(1)} %get-tuple-element.39.held_ref), custom_call_target="tpu_custom_call" | custom-call | tf_op jit(solution)/shard_map/own_terms/pallas_call | solution.py:414
  44.3 0.0 collective-permute-done.7.grad_ref
  44.3 0.7 %side_terms.2 = (f32[160,320]{1,0:T(8,128)S(1)}, f32[160,320]{1,0:T(8,128)S(1)}) custom-call(bf16[400,128]{1,0:T(8,128)(2,1)S(1)} %collective-permute-done.7.grad_ref, f32[160,320]{1,0:T(8,128)S(1)} %get-tuple-element.42.key_part_ref, f32[160,320]{1,0:T(8,128)S(1)} %get-tuple-element.43.value_part_ref, bf16[960,1024]{1,0:T(8,128)(2,1)S(1)} %get-tuple-element.39.held_ref, ...), custom_call_target="tpu_custom_call" | custom-call | tf_op jit(solution)/shard_map/side_terms/pallas_call | solution.py:451
  45.0 1.8 %collective-permute-done.6.grad_ref = bf16[400,128]{1,0:T(8,128)(2,1)S(1)} collective-permute-done((bf16[400,128]{1,0:T(8,128)(2,1)S(1)}, bf16[400,128]{1,0:T(8,128)(2,1)S(1)}, u32[]{:S(2)}, u32[]{:S(2)}) %collective-permute-start.6) | collective-permute-done | bytes 102432 | tf_op jit(solution)/shard_map/ppermute | solution.py:471
  46.8 1.4 %side_terms.3 = (bf16[160,320]{1,0:T(8,128)(2,1)}, bf16[160,320]{1,0:T(8,128)(2,1)}) custom-call(bf16[400,128]{1,0:T(8,128)(2,1)S(1)} %collective-permute-done.6.grad_ref, f32[160,320]{1,0:T(8,128)S(1)} %get-tuple-element.45.key_part_ref, f32[160,320]{1,0:T(8,128)S(1)} %get-tuple-element.46.value_part_ref, bf16[960,1024]{1,0:T(8,128)(2,1)S(1)} %get-tuple-element.39.held_ref, ...), custom_call_target="tpu_custom_call" | custom-call | tf_op jit(solution)/shard_map/side_terms/pallas_call | solution.py:451
  (14 shorter events, 0.1 us)
Async XLA Ops:
  0.6 14.0 %copy-start.4 = (bf16[320,160]{0,1:T(8,128)(2,1)S(1)}, bf16[320,160]{0,1:T(8,128)(2,1)}, u32[]{:S(2)}) copy-start(bf16[320,160]{0,1:T(8,128)(2,1)} %param.16) | copy-start | bytes 307204
  0.6 13.9 %copy-start.3 = (bf16[320,160]{0,1:T(8,128)(2,1)S(1)}, bf16[320,160]{0,1:T(8,128)(2,1)}, u32[]{:S(2)}) copy-start(bf16[320,160]{0,1:T(8,128)(2,1)} %param.15) | copy-start | bytes 307204
  0.7 13.9 %copy-start = (bf16[320,160]{0,1:T(8,128)(2,1)S(1)}, bf16[320,160]{0,1:T(8,128)(2,1)}, u32[]{:S(2)}) copy-start(bf16[320,160]{0,1:T(8,128)(2,1)} %param.14) | copy-start | bytes 307204
  0.7 23.7 %copy-start.1 = (bf16[80,640]{1,0:T(8,128)(2,1)S(1)}, bf16[80,640]{1,0:T(8,128)(2,1)}, u32[]{:S(2)}) copy-start(bf16[80,640]{1,0:T(8,128)(2,1)} %pre_ref.1) | copy-start | bytes 307204
  7.3 28.8 %copy-start.2 = (s32[12]{0:T(128)S(1)}, s32[12]{0:T(128)}, u32[]{:S(2)}) copy-start(s32[12]{0:T(128)} %param.17) | copy-start | bytes 148
  7.3 17.1 %all-to-all-start = ((bf16[8,24,640]{2,1,0:T(8,128)(2,1)}), bf16[8,24,640]{2,1,0:T(8,128)(2,1)S(1)}, u32[]{:S(2)}, u32[]{:S(2)}) async-start(bf16[8,24,640]{2,1,0:T(8,128)(2,1)} %bitcast.15), calls=%async_computation | async-start | bytes 491520 | tf_op jit(solution)/shard_map/all_to_all | solution.py:495
  15.0 15.6 %collective-permute-start.1 = (bf16[1200,128]{1,0:T(8,128)(2,1)S(1)}, bf16[1200,128]{1,0:T(8,128)(2,1)S(1)}, u32[]{:S(2)}, u32[]{:S(2)}) collective-permute-start(bf16[1200,128]{1,0:T(8,128)(2,1)S(1)} %maximum_dynamic-update-slice_fusion), channel_id=1, source_target_pairs={{0,2},{2,0},{4,6},{6,4},{8,10},{10,8},{12,14},{14,12},{1,3},{3,1},... | collective-permute-start | bytes 921608 | tf_op jit(solution)/shard_map/ppermute | solution.py:471
  17.1 13.5 %collective-permute-start = (bf16[1200,128]{1,0:T(8,128)(2,1)S(1)}, bf16[1200,128]{1,0:T(8,128)(2,1)S(1)}, u32[]{:S(2)}, u32[]{:S(2)}) collective-permute-start(bf16[1200,128]{1,0:T(8,128)(2,1)S(1)} %maximum_dynamic-update-slice_fusion), channel_id=1, source_target_pairs={{0,8},{2,4},{4,2},{6,14},{8,0},{10,12},{12,10},{14,6},{1,9},{3,5},... | collective-permute-start | bytes 921608 | tf_op jit(solution)/shard_map/ppermute | solution.py:471
  30.6 1.8 %collective-permute-start.2 = (bf16[4,80,640]{2,1,0:T(8,128)(2,1)S(1)}, bf16[4,80,640]{2,1,0:T(8,128)(2,1)S(1)}, u32[]{:S(2)}, u32[]{:S(2)}) collective-permute-start(bf16[4,80,640]{2,1,0:T(8,128)(2,1)S(1)} %get-tuple-element.31), channel_id=1, source_target_pairs={{0,8},{8,0},{1,9},{9,1},{2,10},{10,2},{3,11},{11,3},{4,12},{12,4},... | collective-permute-start | bytes 1228808 | tf_op jit(solution)/shard_map/ppermute | solution.py:501
  32.5 8.3 %collective-permute-start.5 = (bf16[1,80,640]{2,1,0:T(8,128)(2,1)S(1)}, bf16[1,80,640]{2,1,0:T(8,128)(2,1)S(1)}, u32[]{:S(2)}, u32[]{:S(2)}) collective-permute-start(bf16[1,80,640]{2,1,0:T(8,128)(2,1)S(1)} %get-tuple-element.49), channel_id=1, source_target_pairs={{0,17},{1,16},{16,1},{17,0},{2,19},{3,18},{18,3},{19,2},{4,21},{5,... | collective-permute-start | bytes 307208 | tf_op jit(solution)/shard_map/ppermute | solution.py:479
  34.8 6.1 %collective-permute-start.4 = (bf16[1,80,640]{2,1,0:T(8,128)(2,1)S(1)}, bf16[1,80,640]{2,1,0:T(8,128)(2,1)S(1)}, u32[]{:S(2)}, u32[]{:S(2)}) collective-permute-start(bf16[1,80,640]{2,1,0:T(8,128)(2,1)S(1)} %get-tuple-element.50), channel_id=1, source_target_pairs={{0,16},{1,17},{16,0},{17,1},{2,18},{3,19},{18,2},{19,3},{4,20},{5,... | collective-permute-start | bytes 307208 | tf_op jit(solution)/shard_map/ppermute | solution.py:479
  35.3 5.6 %collective-permute-start.3 = (bf16[1,80,640]{2,1,0:T(8,128)(2,1)S(1)}, bf16[1,80,640]{2,1,0:T(8,128)(2,1)S(1)}, u32[]{:S(2)}, u32[]{:S(2)}) collective-permute-start(bf16[1,80,640]{2,1,0:T(8,128)(2,1)S(1)} %get-tuple-element.51), channel_id=1, source_target_pairs={{0,1},{1,0},{16,17},{17,16},{2,3},{3,2},{18,19},{19,18},{4,5},{5,4... | collective-permute-start | bytes 307208 | tf_op jit(solution)/shard_map/ppermute | solution.py:479
  41.4 2.9 %collective-permute-start.7 = (bf16[400,128]{1,0:T(8,128)(2,1)S(1)}, bf16[400,128]{1,0:T(8,128)(2,1)S(1)}, u32[]{:S(2)}, u32[]{:S(2)}) collective-permute-start(bf16[400,128]{1,0:T(8,128)(2,1)S(1)} %get-tuple-element.41), channel_id=1, source_target_pairs={{0,8},{2,4},{4,2},{6,14},{8,0},{10,12},{12,10},{14,6},{1,9},{3,5},... | collective-permute-start | bytes 307208 | tf_op jit(solution)/shard_map/ppermute | solution.py:471
  41.5 5.3 %collective-permute-start.6 = (bf16[400,128]{1,0:T(8,128)(2,1)S(1)}, bf16[400,128]{1,0:T(8,128)(2,1)S(1)}, u32[]{:S(2)}, u32[]{:S(2)}) collective-permute-start(bf16[400,128]{1,0:T(8,128)(2,1)S(1)} %get-tuple-element.41), channel_id=1, source_target_pairs={{0,2},{2,0},{4,6},{6,4},{8,10},{10,8},{12,14},{14,12},{1,3},{3,1},... | collective-permute-start | bytes 307208 | tf_op jit(solution)/shard_map/ppermute | solution.py:471

commit v15 on v14

--- a/solution.py
+++ b/solution.py
@@ -425,34 +425,53 @@
     )(grad, own, held)
 
 
-def side_kernel(i, grad_ref, key_part_ref, value_part_ref, held_ref, side_ref, key_ref, value_ref):
+def side_kernel(i, grad_ref, key_part_ref, value_part_ref, held_ref, side_ref, *refs):
     columns, patches = key_part_ref.shape
     rows = Rows(columns, patches)
     queries_at, attended_at = rows.side(i)
+    key_ref, value_ref = refs[:2]
+    outgoing = []
+    if i == 1:
+        key_hbm, value_hbm, key_ref, value_ref, sems = refs
+
+    def send(ref, out, h):
+        if i == 1:
+            at = pl.ds(h * HEAD_DIM, HEAD_DIM)
+            copy = pltpu.make_async_copy(ref.at[at], out.at[at], sems.at[len(outgoing)])
+            copy.start()
+            outgoing.append(copy)
+
     for h in range(columns // HEAD_DIM):
         cols = slice(h * HEAD_DIM, (h + 1) * HEAD_DIM)
         wide = unpacked(grad_ref, h, columns, patches)
         grad = wide.astype(jnp.bfloat16)
+        probs = side_ref[rows.side_probs(i, h)]
+        value = dot(probs, grad, NT)
+        value_ref[cols] = (value_part_ref[cols] + value.T).astype(value_ref.dtype)
+        send(value_ref, refs[1], h)
         slope = dot(held_ref[rows.head(rows.values, h), :patches], grad, TN)
         attended = side_ref[rows.head(attended_at, h)].astype(jnp.float32)
         delta = jnp.sum(wide * attended, 0, keepdims=True)
-        probs = side_ref[rows.side_probs(i, h)]
-        value = dot(probs, grad, NT)
         scores = (probs.astype(jnp.float32) * (slope - delta)).astype(jnp.bfloat16)
         key = dot(scores, side_ref[rows.head(queries_at, h)], NT)
         key = key_part_ref[cols] + key.T
         key_ref[cols] = (key * SCALE if i == 1 else key).astype(key_ref.dtype)
-        value_ref[cols] = (value_part_ref[cols] + value.T).astype(value_ref.dtype)
+        send(key_ref, refs[0], h)
+    for copy in outgoing:
+        copy.wait()
 
 
 def side_terms(i, grad, key_part, value_part, held, side):
     kind = jnp.bfloat16 if i == 1 else jnp.float32
     shape = jax.ShapeDtypeStruct(key_part.shape, kind)
+    count = 2 * (key_part.shape[0] // HEAD_DIM)
+    scratch = [pltpu.VMEM(key_part.shape, kind)] * 2 + [pltpu.SemaphoreType.DMA((count,))]
     return pl.pallas_call(
         functools.partial(side_kernel, i),
         out_shape=(shape, shape),
         in_specs=in_vmem(5),
-        out_specs=tuple(in_vmem(2)),
+        out_specs=tuple(in_hbm(2) if i == 1 else in_vmem(2)),
+        scratch_shapes=scratch if i == 1 else [],
         compiler_params=params(24),
         name="side_terms",
     )(grad, key_part, value_part, held, side)

time: 48.4 us -> 48.6 us (level)
  no operation moved by 1% of the time
where the time goes in v15:
time: 48.6 us; the launch traced here: 48.4 us
  Pallas kernels  22.5 us (46%)
  starting transfers between devices  13.5 us (28%)
  waiting for transfers between devices  10.8 us (22%)
  between operations  1.01 us (2%)
    all_to_all x1, waiting for transfers between devices, on_device(): lax.all_to_all(pieces, ('grp', 'span'), split_axis=0, concat_axis=0, tile...  7.32 us
    all_to_all x1, starting transfers between devices, on_device(): lax.all_to_all(pieces, ('grp', 'span'), split_axis=0, concat_axis=0, tile...  7.29 us
    pallas_call x1, Pallas kernels, down_pieces(): pl.pallas_call(functools.partial(down_kernel, groups, spans, capacity, sl...  6.58 us
    pallas_call x1, Pallas kernels, up_pieces(): pl.pallas_call(functools.partial(up_kernel, heads, capacity), out_shape=[...  6.14 us
    pallas_call x1, Pallas kernels, softmax_parts(): pl.pallas_call(softmax_kernel, out_shape=(jax.ShapeDtypeStruct((rows.tota...  4.78 us
    ppermute x3, starting transfers between devices, exchanged(): lax.ppermute(pieces[d], axes, [(i, i ^ d) for i in range(count)])  3.55 us
    ppermute x4, starting transfers between devices, swapped(): return lax.ppermute(x, ('core', 'grp'), sorted(partner.items()))  2.58 us
    pallas_call x1, Pallas kernels, own_terms(): pl.pallas_call(own_kernel, out_shape=(jax.ShapeDtypeStruct(grad.shape, jn...  2.36 us
  transfers between devices with their start and end apart: 9, of which 3 were waited for; matrix products, arithmetic and copies ran while one was open for 1% of the time, Pallas kernels for 29%

profile of v15, /device:TPU:0, one launch (start us, length us, event | category | flops | bytes accessed | tf_op | source)
XLA Modules:
  0.0 48.4 jit_solution(1020414723851673980)
XLA Ops:
  0.6 0.0 copy-start.4
  0.6 0.0 copy-start.3
  0.7 6.6 %down_product.1 = bf16[4,2,24,640]{3,2,1,0:T(8,128)(2,1)} custom-call(s32[1,80]{1,0:T(1,128)} %bitcast.20, bf16[80,4096]{1,0:T(8,128)(2,1)} %rows_hbm.1, bf16[1280,4096]{1,0:T(8,128)(2,1)} %weight_ref.1), custom_call_target="tpu_custom_call" | custom-call | tf_op jit(solution)/shard_map/down_product/pallas_call | solution.py:118
  7.3 0.0 copy-start.2
  7.3 7.3 %all-to-all-start = ((bf16[8,24,640]{2,1,0:T(8,128)(2,1)}), bf16[8,24,640]{2,1,0:T(8,128)(2,1)S(1)}, u32[]{:S(2)}, u32[]{:S(2)}) async-start(bf16[8,24,640]{2,1,0:T(8,128)(2,1)} %bitcast.15), calls=%async_computation | async-start | bytes 491520 | tf_op jit(solution)/shard_map/all_to_all | solution.py:514
  14.7 0.1 maximum_dynamic-update-slice_fusion.2
  14.8 0.1 maximum_dynamic-update-slice_fusion.1
  14.9 0.1 maximum_dynamic-update-slice_fusion
  15.0 2.1 %collective-permute-start.1 = (bf16[1200,128]{1,0:T(8,128)(2,1)S(1)}, bf16[1200,128]{1,0:T(8,128)(2,1)S(1)}, u32[]{:S(2)}, u32[]{:S(2)}) collective-permute-start(bf16[1200,128]{1,0:T(8,128)(2,1)S(1)} %maximum_dynamic-update-slice_fusion), channel_id=1, source_target_pairs={{0,2},{2,0},{4,6},{6,4},{8,10},{10,8},{12,14},{14,12},{1,3},{3,1},... | collective-permute-start | bytes 921608 | tf_op jit(solution)/shard_map/ppermute | solution.py:490
  17.1 0.0 collective-permute-start
  17.1 7.3 %all-to-all-done.pieces_ref = bf16[8,24,640]{2,1,0:T(8,128)(2,1)S(1)} async-done(((bf16[8,24,640]{2,1,0:T(8,128)(2,1)}), bf16[8,24,640]{2,1,0:T(8,128)(2,1)S(1)}, u32[]{:S(2)}, u32[]{:S(2)}) %all-to-all-start) | async-done | bytes 245792 | tf_op jit(solution)/shard_map/all_to_all | solution.py:514
  24.4 6.1 %up_product.1 = (bf16[4,80,640]{2,1,0:T(8,128)(2,1)S(1)}, bf16[4,80,640]{2,1,0:T(8,128)(2,1)S(1)}) custom-call(bf16[8,24,640]{2,1,0:T(8,128)(2,1)S(1)} %all-to-all-done.pieces_ref, bf16[80,640]{1,0:T(8,128)(2,1)S(1)} %copy-done.1, bf16[4,4,320,640]{3,2,1,0:T(8,128)(2,1)} %bitcast.21), custom_call_target="tpu_custom_call" | custom-call | flops 2097152000 | bytes 26214400 | tf_op jit(solution)/shard_map/up_product/pallas_call | solution.py:205
  30.6 0.0 collective-permute-done.1.even_ref
  30.6 0.0 collective-permute-done.odd_ref
  30.6 0.1 collective-permute-start.2
  30.7 1.7 %collective-permute-done.2 = bf16[4,80,640]{2,1,0:T(8,128)(2,1)S(1)} collective-permute-done((bf16[4,80,640]{2,1,0:T(8,128)(2,1)S(1)}, bf16[4,80,640]{2,1,0:T(8,128)(2,1)S(1)}, u32[]{:S(2)}, u32[]{:S(2)}) %collective-permute-start.2) | collective-permute-done | bytes 409632 | tf_op jit(solution)/shard_map/ppermute | solution.py:520
  32.4 0.1 add_convert_fusion
  32.5 2.3 %collective-permute-start.5 = (bf16[1,80,640]{2,1,0:T(8,128)(2,1)S(1)}, bf16[1,80,640]{2,1,0:T(8,128)(2,1)S(1)}, u32[]{:S(2)}, u32[]{:S(2)}) collective-permute-start(bf16[1,80,640]{2,1,0:T(8,128)(2,1)S(1)} %get-tuple-element.49), channel_id=1, source_target_pairs={{0,17},{1,16},{16,1},{17,0},{2,19},{3,18},{18,3},{19,2},{4,21},{5,... | collective-permute-start | bytes 307208 | tf_op jit(solution)/shard_map/ppermute | solution.py:498
  34.8 0.5 %collective-permute-start.4 = (bf16[1,80,640]{2,1,0:T(8,128)(2,1)S(1)}, bf16[1,80,640]{2,1,0:T(8,128)(2,1)S(1)}, u32[]{:S(2)}, u32[]{:S(2)}) collective-permute-start(bf16[1,80,640]{2,1,0:T(8,128)(2,1)S(1)} %get-tuple-element.50), channel_id=1, source_target_pairs={{0,16},{1,17},{16,0},{17,1},{2,18},{3,19},{18,2},{19,3},{4,20},{5,... | collective-permute-start | bytes 307208 | tf_op jit(solution)/shard_map/ppermute | solution.py:498
  35.3 0.7 %collective-permute-start.3 = (bf16[1,80,640]{2,1,0:T(8,128)(2,1)S(1)}, bf16[1,80,640]{2,1,0:T(8,128)(2,1)S(1)}, u32[]{:S(2)}, u32[]{:S(2)}) collective-permute-start(bf16[1,80,640]{2,1,0:T(8,128)(2,1)S(1)} %get-tuple-element.51), channel_id=1, source_target_pairs={{0,1},{1,0},{16,17},{17,16},{2,3},{3,2},{18,19},{19,18},{4,5},{5,4... | collective-permute-start | bytes 307208 | tf_op jit(solution)/shard_map/ppermute | solution.py:498
  36.1 4.8 %softmax_parts.1 = (bf16[960,1024]{1,0:T(8,128)(2,1)S(1)}, bf16[1920,320]{1,0:T(8,128)(2,1)S(1)}, f32[8,128]{1,0:T(8,128)S(1)}) custom-call(s32[1,12]{1,0:T(1,128)S(1)} %bitcast.14, s32[1,1]{1,0:T(1,128)} %bitcast.7.first_ref, bf16[480,320]{1,0:T(8,128)(2,1)S(1)} %pad_maximum_fusion.own_ref, bf16[1200,128]{1,0:T(8,128)(2,1)S(1)} %collective-permute-done.odd_ref, ...), custom_call_target="tpu_custom_call" | custom-call | flops 20480000000 | bytes 102400000 | tf_op jit(solution)/shard_map/softmax_parts/pallas_call | solution.py:318
  40.9 0.0 collective-permute-done.5.refs_3_
  40.9 0.0 collective-permute-done.4.refs_2_
  40.9 0.0 collective-permute-done.3.refs_1_
  40.9 0.5 %gather_sum.1 = (bf16[160,320]{1,0:T(8,128)(2,1)S(1)}, bf16[400,128]{1,0:T(8,128)(2,1)S(1)}) custom-call(bf16[1,80,640]{2,1,0:T(8,128)(2,1)S(1)} %get-tuple-element.52.refs_0_, bf16[1,80,640]{2,1,0:T(8,128)(2,1)S(1)} %collective-permute-done.3.refs_1_, bf16[1,80,640]{2,1,0:T(8,128)(2,1)S(1)} %collective-permute-done.4.refs_2_, ...), custom_call_target="tpu_custom_call" | custom-call | flops 4096000000 | bytes 81920000 | tf_op jit(solution)/shard_map/gather_sum/pallas_call | solution.py:380
  41.4 0.1 collective-permute-start.7
  41.5 0.4 collective-permute-start.6
  41.9 2.4 %own_terms.1 = (bf16[160,320]{1,0:T(8,128)(2,1)}, f32[160,320]{1,0:T(8,128)S(1)}, f32[160,320]{1,0:T(8,128)S(1)}) custom-call(bf16[160,320]{1,0:T(8,128)(2,1)S(1)} %get-tuple-element.38.grad_ref, bf16[160,320]{1,0:T(8,128)(2,1)S(1)} %bitcast.13, bf16[960,1024]{1,0:T(8,128)(2,1)S(1)} %get-tuple-element.39.held_ref), custom_call_target="tpu_custom_call" | custom-call | tf_op jit(solution)/shard_map/own_terms/pallas_call | solution.py:414
  44.3 0.0 collective-permute-done.7.grad_ref
  44.3 0.7 %side_terms.2 = (f32[160,320]{1,0:T(8,128)S(1)}, f32[160,320]{1,0:T(8,128)S(1)}) custom-call(bf16[400,128]{1,0:T(8,128)(2,1)S(1)} %collective-permute-done.7.grad_ref, f32[160,320]{1,0:T(8,128)S(1)} %get-tuple-element.42.key_part_ref, f32[160,320]{1,0:T(8,128)S(1)} %get-tuple-element.43.value_part_ref, bf16[960,1024]{1,0:T(8,128)(2,1)S(1)} %get-tuple-element.39.held_ref, ...), custom_call_target="tpu_custom_call" | custom-call | tf_op jit(solution)/shard_map/side_terms/pallas_call | solution.py:469
  45.0 1.8 %collective-permute-done.6.grad_ref = bf16[400,128]{1,0:T(8,128)(2,1)S(1)} collective-permute-done((bf16[400,128]{1,0:T(8,128)(2,1)S(1)}, bf16[400,128]{1,0:T(8,128)(2,1)S(1)}, u32[]{:S(2)}, u32[]{:S(2)}) %collective-permute-start.6) | collective-permute-done | bytes 102432 | tf_op jit(solution)/shard_map/ppermute | solution.py:490
  46.8 1.4 %side_terms.3 = (bf16[160,320]{1,0:T(8,128)(2,1)}, bf16[160,320]{1,0:T(8,128)(2,1)}) custom-call(bf16[400,128]{1,0:T(8,128)(2,1)S(1)} %collective-permute-done.6.grad_ref, f32[160,320]{1,0:T(8,128)S(1)} %get-tuple-element.45.key_part_ref, f32[160,320]{1,0:T(8,128)S(1)} %get-tuple-element.46.value_part_ref, bf16[960,1024]{1,0:T(8,128)(2,1)S(1)} %get-tuple-element.39.held_ref, ...), custom_call_target="tpu_custom_call" | custom-call | tf_op jit(solution)/shard_map/side_terms/pallas_call | solution.py:469
  (14 shorter events, 0.1 us)
Async XLA Ops:
  0.6 14.0 %copy-start.4 = (bf16[320,160]{0,1:T(8,128)(2,1)S(1)}, bf16[320,160]{0,1:T(8,128)(2,1)}, u32[]{:S(2)}) copy-start(bf16[320,160]{0,1:T(8,128)(2,1)} %param.16) | copy-start | bytes 307204
  0.6 13.9 %copy-start.3 = (bf16[320,160]{0,1:T(8,128)(2,1)S(1)}, bf16[320,160]{0,1:T(8,128)(2,1)}, u32[]{:S(2)}) copy-start(bf16[320,160]{0,1:T(8,128)(2,1)} %param.15) | copy-start | bytes 307204
  0.7 13.9 %copy-start = (bf16[320,160]{0,1:T(8,128)(2,1)S(1)}, bf16[320,160]{0,1:T(8,128)(2,1)}, u32[]{:S(2)}) copy-start(bf16[320,160]{0,1:T(8,128)(2,1)} %param.14) | copy-start | bytes 307204
  0.7 23.7 %copy-start.1 = (bf16[80,640]{1,0:T(8,128)(2,1)S(1)}, bf16[80,640]{1,0:T(8,128)(2,1)}, u32[]{:S(2)}) copy-start(bf16[80,640]{1,0:T(8,128)(2,1)} %pre_ref.1) | copy-start | bytes 307204
  7.3 28.8 %copy-start.2 = (s32[12]{0:T(128)S(1)}, s32[12]{0:T(128)}, u32[]{:S(2)}) copy-start(s32[12]{0:T(128)} %param.17) | copy-start | bytes 148
  7.3 17.1 %all-to-all-start = ((bf16[8,24,640]{2,1,0:T(8,128)(2,1)}), bf16[8,24,640]{2,1,0:T(8,128)(2,1)S(1)}, u32[]{:S(2)}, u32[]{:S(2)}) async-start(bf16[8,24,640]{2,1,0:T(8,128)(2,1)} %bitcast.15), calls=%async_computation | async-start | bytes 491520 | tf_op jit(solution)/shard_map/all_to_all | solution.py:514
  15.0 15.6 %collective-permute-start.1 = (bf16[1200,128]{1,0:T(8,128)(2,1)S(1)}, bf16[1200,128]{1,0:T(8,128)(2,1)S(1)}, u32[]{:S(2)}, u32[]{:S(2)}) collective-permute-start(bf16[1200,128]{1,0:T(8,128)(2,1)S(1)} %maximum_dynamic-update-slice_fusion), channel_id=1, source_target_pairs={{0,2},{2,0},{4,6},{6,4},{8,10},{10,8},{12,14},{14,12},{1,3},{3,1},... | collective-permute-start | bytes 921608 | tf_op jit(solution)/shard_map/ppermute | solution.py:490
  17.1 13.5 %collective-permute-start = (bf16[1200,128]{1,0:T(8,128)(2,1)S(1)}, bf16[1200,128]{1,0:T(8,128)(2,1)S(1)}, u32[]{:S(2)}, u32[]{:S(2)}) collective-permute-start(bf16[1200,128]{1,0:T(8,128)(2,1)S(1)} %maximum_dynamic-update-slice_fusion), channel_id=1, source_target_pairs={{0,8},{2,4},{4,2},{6,14},{8,0},{10,12},{12,10},{14,6},{1,9},{3,5},... | collective-permute-start | bytes 921608 | tf_op jit(solution)/shard_map/ppermute | solution.py:490
  30.6 1.8 %collective-permute-start.2 = (bf16[4,80,640]{2,1,0:T(8,128)(2,1)S(1)}, bf16[4,80,640]{2,1,0:T(8,128)(2,1)S(1)}, u32[]{:S(2)}, u32[]{:S(2)}) collective-permute-start(bf16[4,80,640]{2,1,0:T(8,128)(2,1)S(1)} %get-tuple-element.31), channel_id=1, source_target_pairs={{0,8},{8,0},{1,9},{9,1},{2,10},{10,2},{3,11},{11,3},{4,12},{12,4},... | collective-permute-start | bytes 1228808 | tf_op jit(solution)/shard_map/ppermute | solution.py:520
  32.5 8.3 %collective-permute-start.5 = (bf16[1,80,640]{2,1,0:T(8,128)(2,1)S(1)}, bf16[1,80,640]{2,1,0:T(8,128)(2,1)S(1)}, u32[]{:S(2)}, u32[]{:S(2)}) collective-permute-start(bf16[1,80,640]{2,1,0:T(8,128)(2,1)S(1)} %get-tuple-element.49), channel_id=1, source_target_pairs={{0,17},{1,16},{16,1},{17,0},{2,19},{3,18},{18,3},{19,2},{4,21},{5,... | collective-permute-start | bytes 307208 | tf_op jit(solution)/shard_map/ppermute | solution.py:498
  34.8 6.1 %collective-permute-start.4 = (bf16[1,80,640]{2,1,0:T(8,128)(2,1)S(1)}, bf16[1,80,640]{2,1,0:T(8,128)(2,1)S(1)}, u32[]{:S(2)}, u32[]{:S(2)}) collective-permute-start(bf16[1,80,640]{2,1,0:T(8,128)(2,1)S(1)} %get-tuple-element.50), channel_id=1, source_target_pairs={{0,16},{1,17},{16,0},{17,1},{2,18},{3,19},{18,2},{19,3},{4,20},{5,... | collective-permute-start | bytes 307208 | tf_op jit(solution)/shard_map/ppermute | solution.py:498
  35.3 5.6 %collective-permute-start.3 = (bf16[1,80,640]{2,1,0:T(8,128)(2,1)S(1)}, bf16[1,80,640]{2,1,0:T(8,128)(2,1)S(1)}, u32[]{:S(2)}, u32[]{:S(2)}) collective-permute-start(bf16[1,80,640]{2,1,0:T(8,128)(2,1)S(1)} %get-tuple-element.51), channel_id=1, source_target_pairs={{0,1},{1,0},{16,17},{17,16},{2,3},{3,2},{18,19},{19,18},{4,5},{5,4... | collective-permute-start | bytes 307208 | tf_op jit(solution)/shard_map/ppermute | solution.py:498
  41.4 2.9 %collective-permute-start.7 = (bf16[400,128]{1,0:T(8,128)(2,1)S(1)}, bf16[400,128]{1,0:T(8,128)(2,1)S(1)}, u32[]{:S(2)}, u32[]{:S(2)}) collective-permute-start(bf16[400,128]{1,0:T(8,128)(2,1)S(1)} %get-tuple-element.41), channel_id=1, source_target_pairs={{0,8},{2,4},{4,2},{6,14},{8,0},{10,12},{12,10},{14,6},{1,9},{3,5},... | collective-permute-start | bytes 307208 | tf_op jit(solution)/shard_map/ppermute | solution.py:490
  41.5 5.3 %collective-permute-start.6 = (bf16[400,128]{1,0:T(8,128)(2,1)S(1)}, bf16[400,128]{1,0:T(8,128)(2,1)S(1)}, u32[]{:S(2)}, u32[]{:S(2)}) collective-permute-start(bf16[400,128]{1,0:T(8,128)(2,1)S(1)} %get-tuple-element.41), channel_id=1, source_target_pairs={{0,2},{2,0},{4,6},{6,4},{8,10},{10,8},{12,14},{14,12},{1,3},{3,1},... | collective-permute-start | bytes 307208 | tf_op jit(solution)/shard_map/ppermute | solution.py:490

commit v16 on v14

--- a/solution.py
+++ b/solution.py
@@ -113,7 +113,7 @@
     capacity, slots = padded_slots(row_count, groups)
     hidden = weight.shape[0] // spans
     depth = weight.shape[1]
-    edges = [depth * i // 8 for i in (0, 1, 3, 5, 8)]
+    edges = [depth * i // 16 for i in (0, 2, 5, 10, 16)]
     steps = [(i, j - i) for i, j in zip(edges, edges[1:])]
     pieces = pl.pallas_call(
         functools.partial(down_kernel, groups, spans, capacity, slots, steps),

time: 48.4 us -> 48.4 us (level)
  no operation moved by 1% of the time
where the time goes in v16:
time: 48.4 us; the launch traced here: 48.2 us
  Pallas kernels  22.4 us (46%)
  starting transfers between devices  13.5 us (28%)
  waiting for transfers between devices  10.9 us (23%)
  between operations  0.85 us (2%)
    all_to_all x1, waiting for transfers between devices, on_device(): lax.all_to_all(pieces, ('grp', 'span'), split_axis=0, concat_axis=0, tile...  7.32 us
    all_to_all x1, starting transfers between devices, on_device(): lax.all_to_all(pieces, ('grp', 'span'), split_axis=0, concat_axis=0, tile...  7.29 us
    pallas_call x1, Pallas kernels, down_pieces(): pl.pallas_call(functools.partial(down_kernel, groups, spans, capacity, sl...  6.58 us
    pallas_call x1, Pallas kernels, up_pieces(): pl.pallas_call(functools.partial(up_kernel, heads, capacity), out_shape=[...  6.14 us
    pallas_call x1, Pallas kernels, softmax_parts(): pl.pallas_call(softmax_kernel, out_shape=(jax.ShapeDtypeStruct((rows.tota...  4.78 us
    ppermute x3, starting transfers between devices, exchanged(): lax.ppermute(pieces[d], axes, [(i, i ^ d) for i in range(count)])  3.55 us
    ppermute x4, starting transfers between devices, swapped(): return lax.ppermute(x, ('core', 'grp'), sorted(partner.items()))  2.58 us
    pallas_call x1, Pallas kernels, own_terms(): pl.pallas_call(own_kernel, out_shape=(jax.ShapeDtypeStruct(grad.shape, jn...  2.36 us
  transfers between devices with their start and end apart: 9, of which 3 were waited for; matrix products, arithmetic and copies ran while one was open for 1% of the time, Pallas kernels for 29%

profile of v16, /device:TPU:0, one launch (start us, length us, event | category | flops | bytes accessed | tf_op | source)
XLA Modules:
  0.0 48.2 jit_solution(17282031214481021615)
XLA Ops:
  0.6 0.0 copy-start.4
  0.6 0.0 copy-start.3
  0.7 6.6 %down_product.1 = bf16[4,2,24,640]{3,2,1,0:T(8,128)(2,1)} custom-call(s32[1,80]{1,0:T(1,128)} %bitcast.20, bf16[80,4096]{1,0:T(8,128)(2,1)} %rows_hbm.1, bf16[1280,4096]{1,0:T(8,128)(2,1)} %weight_ref.1), custom_call_target="tpu_custom_call" | custom-call | tf_op jit(solution)/shard_map/down_product/pallas_call | solution.py:118
  7.3 0.0 copy-start.2
  7.3 7.3 %all-to-all-start = ((bf16[8,24,640]{2,1,0:T(8,128)(2,1)}), bf16[8,24,640]{2,1,0:T(8,128)(2,1)S(1)}, u32[]{:S(2)}, u32[]{:S(2)}) async-start(bf16[8,24,640]{2,1,0:T(8,128)(2,1)} %bitcast.15), calls=%async_computation | async-start | bytes 491520 | tf_op jit(solution)/shard_map/all_to_all | solution.py:495
  14.7 0.1 maximum_dynamic-update-slice_fusion.2
  14.8 0.1 maximum_dynamic-update-slice_fusion.1
  14.9 0.1 maximum_dynamic-update-slice_fusion
  15.0 2.1 %collective-permute-start.1 = (bf16[1200,128]{1,0:T(8,128)(2,1)S(1)}, bf16[1200,128]{1,0:T(8,128)(2,1)S(1)}, u32[]{:S(2)}, u32[]{:S(2)}) collective-permute-start(bf16[1200,128]{1,0:T(8,128)(2,1)S(1)} %maximum_dynamic-update-slice_fusion), channel_id=1, source_target_pairs={{0,2},{2,0},{4,6},{6,4},{8,10},{10,8},{12,14},{14,12},{1,3},{3,1},... | collective-permute-start | bytes 921608 | tf_op jit(solution)/shard_map/ppermute | solution.py:471
  17.1 0.0 collective-permute-start
  17.1 7.3 %all-to-all-done.pieces_ref = bf16[8,24,640]{2,1,0:T(8,128)(2,1)S(1)} async-done(((bf16[8,24,640]{2,1,0:T(8,128)(2,1)}), bf16[8,24,640]{2,1,0:T(8,128)(2,1)S(1)}, u32[]{:S(2)}, u32[]{:S(2)}) %all-to-all-start) | async-done | bytes 245792 | tf_op jit(solution)/shard_map/all_to_all | solution.py:495
  24.4 6.1 %up_product.1 = (bf16[4,80,640]{2,1,0:T(8,128)(2,1)S(1)}, bf16[4,80,640]{2,1,0:T(8,128)(2,1)S(1)}) custom-call(bf16[8,24,640]{2,1,0:T(8,128)(2,1)S(1)} %all-to-all-done.pieces_ref, bf16[80,640]{1,0:T(8,128)(2,1)S(1)} %copy-done.1, bf16[4,4,320,640]{3,2,1,0:T(8,128)(2,1)} %bitcast.21), custom_call_target="tpu_custom_call" | custom-call | flops 2097152000 | bytes 26214400 | tf_op jit(solution)/shard_map/up_product/pallas_call | solution.py:205
  30.6 0.0 collective-permute-done.1.even_ref
  30.6 0.0 collective-permute-done.odd_ref
  30.6 0.1 collective-permute-start.2
  30.7 1.7 %collective-permute-done.2 = bf16[4,80,640]{2,1,0:T(8,128)(2,1)S(1)} collective-permute-done((bf16[4,80,640]{2,1,0:T(8,128)(2,1)S(1)}, bf16[4,80,640]{2,1,0:T(8,128)(2,1)S(1)}, u32[]{:S(2)}, u32[]{:S(2)}) %collective-permute-start.2) | collective-permute-done | bytes 409632 | tf_op jit(solution)/shard_map/ppermute | solution.py:501
  32.4 0.1 add_convert_fusion
  32.5 2.3 %collective-permute-start.5 = (bf16[1,80,640]{2,1,0:T(8,128)(2,1)S(1)}, bf16[1,80,640]{2,1,0:T(8,128)(2,1)S(1)}, u32[]{:S(2)}, u32[]{:S(2)}) collective-permute-start(bf16[1,80,640]{2,1,0:T(8,128)(2,1)S(1)} %get-tuple-element.49), channel_id=1, source_target_pairs={{0,17},{1,16},{16,1},{17,0},{2,19},{3,18},{18,3},{19,2},{4,21},{5,... | collective-permute-start | bytes 307208 | tf_op jit(solution)/shard_map/ppermute | solution.py:479
  34.8 0.5 %collective-permute-start.4 = (bf16[1,80,640]{2,1,0:T(8,128)(2,1)S(1)}, bf16[1,80,640]{2,1,0:T(8,128)(2,1)S(1)}, u32[]{:S(2)}, u32[]{:S(2)}) collective-permute-start(bf16[1,80,640]{2,1,0:T(8,128)(2,1)S(1)} %get-tuple-element.50), channel_id=1, source_target_pairs={{0,16},{1,17},{16,0},{17,1},{2,18},{3,19},{18,2},{19,3},{4,20},{5,... | collective-permute-start | bytes 307208 | tf_op jit(solution)/shard_map/ppermute | solution.py:479
  35.3 0.7 %collective-permute-start.3 = (bf16[1,80,640]{2,1,0:T(8,128)(2,1)S(1)}, bf16[1,80,640]{2,1,0:T(8,128)(2,1)S(1)}, u32[]{:S(2)}, u32[]{:S(2)}) collective-permute-start(bf16[1,80,640]{2,1,0:T(8,128)(2,1)S(1)} %get-tuple-element.51), channel_id=1, source_target_pairs={{0,1},{1,0},{16,17},{17,16},{2,3},{3,2},{18,19},{19,18},{4,5},{5,4... | collective-permute-start | bytes 307208 | tf_op jit(solution)/shard_map/ppermute | solution.py:479
  36.1 4.8 %softmax_parts.1 = (bf16[960,1024]{1,0:T(8,128)(2,1)S(1)}, bf16[1920,320]{1,0:T(8,128)(2,1)S(1)}, f32[8,128]{1,0:T(8,128)S(1)}) custom-call(s32[1,12]{1,0:T(1,128)S(1)} %bitcast.14, s32[1,1]{1,0:T(1,128)} %bitcast.7.first_ref, bf16[480,320]{1,0:T(8,128)(2,1)S(1)} %pad_maximum_fusion.own_ref, bf16[1200,128]{1,0:T(8,128)(2,1)S(1)} %collective-permute-done.odd_ref, ...), custom_call_target="tpu_custom_call" | custom-call | flops 20480000000 | bytes 102400000 | tf_op jit(solution)/shard_map/softmax_parts/pallas_call | solution.py:318
  40.9 0.0 collective-permute-done.5.refs_3_
  40.9 0.0 collective-permute-done.4.refs_2_
  40.9 0.0 collective-permute-done.3.refs_1_
  40.9 0.5 %gather_sum.1 = (bf16[160,320]{1,0:T(8,128)(2,1)S(1)}, bf16[400,128]{1,0:T(8,128)(2,1)S(1)}) custom-call(bf16[1,80,640]{2,1,0:T(8,128)(2,1)S(1)} %get-tuple-element.52.refs_0_, bf16[1,80,640]{2,1,0:T(8,128)(2,1)S(1)} %collective-permute-done.3.refs_1_, bf16[1,80,640]{2,1,0:T(8,128)(2,1)S(1)} %collective-permute-done.4.refs_2_, ...), custom_call_target="tpu_custom_call" | custom-call | flops 4096000000 | bytes 81920000 | tf_op jit(solution)/shard_map/gather_sum/pallas_call | solution.py:380
  41.4 0.1 collective-permute-start.7
  41.5 0.4 collective-permute-start.6
  41.9 2.4 %own_terms.1 = (bf16[160,320]{1,0:T(8,128)(2,1)}, f32[160,320]{1,0:T(8,128)S(1)}, f32[160,320]{1,0:T(8,128)S(1)}) custom-call(bf16[160,320]{1,0:T(8,128)(2,1)S(1)} %get-tuple-element.38.grad_ref, bf16[160,320]{1,0:T(8,128)(2,1)S(1)} %bitcast.13, bf16[960,1024]{1,0:T(8,128)(2,1)S(1)} %get-tuple-element.39.held_ref), custom_call_target="tpu_custom_call" | custom-call | tf_op jit(solution)/shard_map/own_terms/pallas_call | solution.py:414
  44.3 0.0 collective-permute-done.7.grad_ref
  44.3 0.7 %side_terms.2 = (f32[160,320]{1,0:T(8,128)S(1)}, f32[160,320]{1,0:T(8,128)S(1)}) custom-call(bf16[400,128]{1,0:T(8,128)(2,1)S(1)} %collective-permute-done.7.grad_ref, f32[160,320]{1,0:T(8,128)S(1)} %get-tuple-element.42.key_part_ref, f32[160,320]{1,0:T(8,128)S(1)} %get-tuple-element.43.value_part_ref, bf16[960,1024]{1,0:T(8,128)(2,1)S(1)} %get-tuple-element.39.held_ref, ...), custom_call_target="tpu_custom_call" | custom-call | tf_op jit(solution)/shard_map/side_terms/pallas_call | solution.py:451
  45.0 1.8 %collective-permute-done.6.grad_ref = bf16[400,128]{1,0:T(8,128)(2,1)S(1)} collective-permute-done((bf16[400,128]{1,0:T(8,128)(2,1)S(1)}, bf16[400,128]{1,0:T(8,128)(2,1)S(1)}, u32[]{:S(2)}, u32[]{:S(2)}) %collective-permute-start.6) | collective-permute-done | bytes 102432 | tf_op jit(solution)/shard_map/ppermute | solution.py:471
  46.8 1.4 %side_terms.3 = (bf16[160,320]{1,0:T(8,128)(2,1)}, bf16[160,320]{1,0:T(8,128)(2,1)}) custom-call(bf16[400,128]{1,0:T(8,128)(2,1)S(1)} %collective-permute-done.6.grad_ref, f32[160,320]{1,0:T(8,128)S(1)} %get-tuple-element.45.key_part_ref, f32[160,320]{1,0:T(8,128)S(1)} %get-tuple-element.46.value_part_ref, bf16[960,1024]{1,0:T(8,128)(2,1)S(1)} %get-tuple-element.39.held_ref, ...), custom_call_target="tpu_custom_call" | custom-call | tf_op jit(solution)/shard_map/side_terms/pallas_call | solution.py:451
  (14 shorter events, 0.1 us)
Async XLA Ops:
  0.6 14.0 %copy-start.4 = (bf16[320,160]{0,1:T(8,128)(2,1)S(1)}, bf16[320,160]{0,1:T(8,128)(2,1)}, u32[]{:S(2)}) copy-start(bf16[320,160]{0,1:T(8,128)(2,1)} %param.16) | copy-start | bytes 307204
  0.6 13.9 %copy-start.3 = (bf16[320,160]{0,1:T(8,128)(2,1)S(1)}, bf16[320,160]{0,1:T(8,128)(2,1)}, u32[]{:S(2)}) copy-start(bf16[320,160]{0,1:T(8,128)(2,1)} %param.15) | copy-start | bytes 307204
  0.7 13.9 %copy-start = (bf16[320,160]{0,1:T(8,128)(2,1)S(1)}, bf16[320,160]{0,1:T(8,128)(2,1)}, u32[]{:S(2)}) copy-start(bf16[320,160]{0,1:T(8,128)(2,1)} %param.14) | copy-start | bytes 307204
  0.7 23.7 %copy-start.1 = (bf16[80,640]{1,0:T(8,128)(2,1)S(1)}, bf16[80,640]{1,0:T(8,128)(2,1)}, u32[]{:S(2)}) copy-start(bf16[80,640]{1,0:T(8,128)(2,1)} %pre_ref.1) | copy-start | bytes 307204
  7.3 28.8 %copy-start.2 = (s32[12]{0:T(128)S(1)}, s32[12]{0:T(128)}, u32[]{:S(2)}) copy-start(s32[12]{0:T(128)} %param.17) | copy-start | bytes 148
  7.3 17.1 %all-to-all-start = ((bf16[8,24,640]{2,1,0:T(8,128)(2,1)}), bf16[8,24,640]{2,1,0:T(8,128)(2,1)S(1)}, u32[]{:S(2)}, u32[]{:S(2)}) async-start(bf16[8,24,640]{2,1,0:T(8,128)(2,1)} %bitcast.15), calls=%async_computation | async-start | bytes 491520 | tf_op jit(solution)/shard_map/all_to_all | solution.py:495
  15.0 15.6 %collective-permute-start.1 = (bf16[1200,128]{1,0:T(8,128)(2,1)S(1)}, bf16[1200,128]{1,0:T(8,128)(2,1)S(1)}, u32[]{:S(2)}, u32[]{:S(2)}) collective-permute-start(bf16[1200,128]{1,0:T(8,128)(2,1)S(1)} %maximum_dynamic-update-slice_fusion), channel_id=1, source_target_pairs={{0,2},{2,0},{4,6},{6,4},{8,10},{10,8},{12,14},{14,12},{1,3},{3,1},... | collective-permute-start | bytes 921608 | tf_op jit(solution)/shard_map/ppermute | solution.py:471
  17.1 13.5 %collective-permute-start = (bf16[1200,128]{1,0:T(8,128)(2,1)S(1)}, bf16[1200,128]{1,0:T(8,128)(2,1)S(1)}, u32[]{:S(2)}, u32[]{:S(2)}) collective-permute-start(bf16[1200,128]{1,0:T(8,128)(2,1)S(1)} %maximum_dynamic-update-slice_fusion), channel_id=1, source_target_pairs={{0,8},{2,4},{4,2},{6,14},{8,0},{10,12},{12,10},{14,6},{1,9},{3,5},... | collective-permute-start | bytes 921608 | tf_op jit(solution)/shard_map/ppermute | solution.py:471
  30.6 1.8 %collective-permute-start.2 = (bf16[4,80,640]{2,1,0:T(8,128)(2,1)S(1)}, bf16[4,80,640]{2,1,0:T(8,128)(2,1)S(1)}, u32[]{:S(2)}, u32[]{:S(2)}) collective-permute-start(bf16[4,80,640]{2,1,0:T(8,128)(2,1)S(1)} %get-tuple-element.31), channel_id=1, source_target_pairs={{0,8},{8,0},{1,9},{9,1},{2,10},{10,2},{3,11},{11,3},{4,12},{12,4},... | collective-permute-start | bytes 1228808 | tf_op jit(solution)/shard_map/ppermute | solution.py:501
  32.5 8.3 %collective-permute-start.5 = (bf16[1,80,640]{2,1,0:T(8,128)(2,1)S(1)}, bf16[1,80,640]{2,1,0:T(8,128)(2,1)S(1)}, u32[]{:S(2)}, u32[]{:S(2)}) collective-permute-start(bf16[1,80,640]{2,1,0:T(8,128)(2,1)S(1)} %get-tuple-element.49), channel_id=1, source_target_pairs={{0,17},{1,16},{16,1},{17,0},{2,19},{3,18},{18,3},{19,2},{4,21},{5,... | collective-permute-start | bytes 307208 | tf_op jit(solution)/shard_map/ppermute | solution.py:479
  34.8 6.1 %collective-permute-start.4 = (bf16[1,80,640]{2,1,0:T(8,128)(2,1)S(1)}, bf16[1,80,640]{2,1,0:T(8,128)(2,1)S(1)}, u32[]{:S(2)}, u32[]{:S(2)}) collective-permute-start(bf16[1,80,640]{2,1,0:T(8,128)(2,1)S(1)} %get-tuple-element.50), channel_id=1, source_target_pairs={{0,16},{1,17},{16,0},{17,1},{2,18},{3,19},{18,2},{19,3},{4,20},{5,... | collective-permute-start | bytes 307208 | tf_op jit(solution)/shard_map/ppermute | solution.py:479
  35.3 5.6 %collective-permute-start.3 = (bf16[1,80,640]{2,1,0:T(8,128)(2,1)S(1)}, bf16[1,80,640]{2,1,0:T(8,128)(2,1)S(1)}, u32[]{:S(2)}, u32[]{:S(2)}) collective-permute-start(bf16[1,80,640]{2,1,0:T(8,128)(2,1)S(1)} %get-tuple-element.51), channel_id=1, source_target_pairs={{0,1},{1,0},{16,17},{17,16},{2,3},{3,2},{18,19},{19,18},{4,5},{5,4... | collective-permute-start | bytes 307208 | tf_op jit(solution)/shard_map/ppermute | solution.py:479
  41.4 2.9 %collective-permute-start.7 = (bf16[400,128]{1,0:T(8,128)(2,1)S(1)}, bf16[400,128]{1,0:T(8,128)(2,1)S(1)}, u32[]{:S(2)}, u32[]{:S(2)}) collective-permute-start(bf16[400,128]{1,0:T(8,128)(2,1)S(1)} %get-tuple-element.41), channel_id=1, source_target_pairs={{0,8},{2,4},{4,2},{6,14},{8,0},{10,12},{12,10},{14,6},{1,9},{3,5},... | collective-permute-start | bytes 307208 | tf_op jit(solution)/shard_map/ppermute | solution.py:471
  41.5 5.3 %collective-permute-start.6 = (bf16[400,128]{1,0:T(8,128)(2,1)S(1)}, bf16[400,128]{1,0:T(8,128)(2,1)S(1)}, u32[]{:S(2)}, u32[]{:S(2)}) collective-permute-start(bf16[400,128]{1,0:T(8,128)(2,1)S(1)} %get-tuple-element.41), channel_id=1, source_target_pairs={{0,2},{2,0},{4,6},{6,4},{8,10},{10,8},{12,14},{14,12},{1,3},{3,1},... | collective-permute-start | bytes 307208 | tf_op jit(solution)/shard_map/ppermute | solution.py:471

commit v17 on v16

--- a/solution.py
+++ b/solution.py
@@ -113,7 +113,7 @@
     capacity, slots = padded_slots(row_count, groups)
     hidden = weight.shape[0] // spans
     depth = weight.shape[1]
-    edges = [depth * i // 16 for i in (0, 2, 5, 10, 16)]
+    edges = [depth * i // 16 for i in (0, 1, 4, 9, 16)]
     steps = [(i, j - i) for i, j in zip(edges, edges[1:])]
     pieces = pl.pallas_call(
         functools.partial(down_kernel, groups, spans, capacity, slots, steps),

time: 48.4 us -> 48.6 us (level)
  no operation moved by 1% of the time
where the time goes in v17:
time: 48.6 us; the launch traced here: 48.4 us
  Pallas kernels  22.7 us (47%)
  starting transfers between devices  13.5 us (28%)
  waiting for transfers between devices  10.9 us (22%)
  between operations  0.85 us (2%)
    all_to_all x1, waiting for transfers between devices, on_device(): lax.all_to_all(pieces, ('grp', 'span'), split_axis=0, concat_axis=0, tile...  7.32 us
    all_to_all x1, starting transfers between devices, on_device(): lax.all_to_all(pieces, ('grp', 'span'), split_axis=0, concat_axis=0, tile...  7.29 us
    pallas_call x1, Pallas kernels, down_pieces(): pl.pallas_call(functools.partial(down_kernel, groups, spans, capacity, sl...  6.83 us
    pallas_call x1, Pallas kernels, up_pieces(): pl.pallas_call(functools.partial(up_kernel, heads, capacity), out_shape=[...  6.14 us
    pallas_call x1, Pallas kernels, softmax_parts(): pl.pallas_call(softmax_kernel, out_shape=(jax.ShapeDtypeStruct((rows.tota...  4.78 us
    ppermute x3, starting transfers between devices, exchanged(): lax.ppermute(pieces[d], axes, [(i, i ^ d) for i in range(count)])  3.55 us
    ppermute x4, starting transfers between devices, swapped(): return lax.ppermute(x, ('core', 'grp'), sorted(partner.items()))  2.58 us
    pallas_call x1, Pallas kernels, own_terms(): pl.pallas_call(own_kernel, out_shape=(jax.ShapeDtypeStruct(grad.shape, jn...  2.36 us
  transfers between devices with their start and end apart: 9, of which 3 were waited for; matrix products, arithmetic and copies ran while one was open for 1% of the time, Pallas kernels for 29%

profile of v17, /device:TPU:0, one launch (start us, length us, event | category | flops | bytes accessed | tf_op | source)
XLA Modules:
  0.0 48.4 jit_solution(2672225128721583431)
XLA Ops:
  0.6 0.0 copy-start.4
  0.7 6.8 %down_product.1 = bf16[4,2,24,640]{3,2,1,0:T(8,128)(2,1)} custom-call(s32[1,80]{1,0:T(1,128)} %bitcast.20, bf16[80,4096]{1,0:T(8,128)(2,1)} %rows_hbm.1, bf16[1280,4096]{1,0:T(8,128)(2,1)} %weight_ref.1), custom_call_target="tpu_custom_call" | custom-call | tf_op jit(solution)/shard_map/down_product/pallas_call | solution.py:118
  7.5 0.0 copy-start.2
  7.5 7.3 %all-to-all-start = ((bf16[8,24,640]{2,1,0:T(8,128)(2,1)}), bf16[8,24,640]{2,1,0:T(8,128)(2,1)S(1)}, u32[]{:S(2)}, u32[]{:S(2)}) async-start(bf16[8,24,640]{2,1,0:T(8,128)(2,1)} %bitcast.15), calls=%async_computation | async-start | bytes 491520 | tf_op jit(solution)/shard_map/all_to_all | solution.py:495
  15.0 0.1 maximum_dynamic-update-slice_fusion.2
  15.1 0.1 maximum_dynamic-update-slice_fusion.1
  15.2 0.1 maximum_dynamic-update-slice_fusion
  15.2 2.1 %collective-permute-start.1 = (bf16[1200,128]{1,0:T(8,128)(2,1)S(1)}, bf16[1200,128]{1,0:T(8,128)(2,1)S(1)}, u32[]{:S(2)}, u32[]{:S(2)}) collective-permute-start(bf16[1200,128]{1,0:T(8,128)(2,1)S(1)} %maximum_dynamic-update-slice_fusion), channel_id=1, source_target_pairs={{0,2},{2,0},{4,6},{6,4},{8,10},{10,8},{12,14},{14,12},{1,3},{3,1},... | collective-permute-start | bytes 921608 | tf_op jit(solution)/shard_map/ppermute | solution.py:471
  17.3 0.0 collective-permute-start
  17.3 7.3 %all-to-all-done.pieces_ref = bf16[8,24,640]{2,1,0:T(8,128)(2,1)S(1)} async-done(((bf16[8,24,640]{2,1,0:T(8,128)(2,1)}), bf16[8,24,640]{2,1,0:T(8,128)(2,1)S(1)}, u32[]{:S(2)}, u32[]{:S(2)}) %all-to-all-start) | async-done | bytes 245792 | tf_op jit(solution)/shard_map/all_to_all | solution.py:495
  24.6 0.0 copy-done.1
  24.7 6.1 %up_product.1 = (bf16[4,80,640]{2,1,0:T(8,128)(2,1)S(1)}, bf16[4,80,640]{2,1,0:T(8,128)(2,1)S(1)}) custom-call(bf16[8,24,640]{2,1,0:T(8,128)(2,1)S(1)} %all-to-all-done.pieces_ref, bf16[80,640]{1,0:T(8,128)(2,1)S(1)} %copy-done.1, bf16[4,4,320,640]{3,2,1,0:T(8,128)(2,1)} %bitcast.21), custom_call_target="tpu_custom_call" | custom-call | flops 2097152000 | bytes 26214400 | tf_op jit(solution)/shard_map/up_product/pallas_call | solution.py:205
  30.8 0.0 collective-permute-done.1.even_ref
  30.8 0.0 collective-permute-done.odd_ref
  30.8 0.1 collective-permute-start.2
  30.9 1.7 %collective-permute-done.2 = bf16[4,80,640]{2,1,0:T(8,128)(2,1)S(1)} collective-permute-done((bf16[4,80,640]{2,1,0:T(8,128)(2,1)S(1)}, bf16[4,80,640]{2,1,0:T(8,128)(2,1)S(1)}, u32[]{:S(2)}, u32[]{:S(2)}) %collective-permute-start.2) | collective-permute-done | bytes 409632 | tf_op jit(solution)/shard_map/ppermute | solution.py:501
  32.6 0.1 add_convert_fusion
  32.8 2.3 %collective-permute-start.5 = (bf16[1,80,640]{2,1,0:T(8,128)(2,1)S(1)}, bf16[1,80,640]{2,1,0:T(8,128)(2,1)S(1)}, u32[]{:S(2)}, u32[]{:S(2)}) collective-permute-start(bf16[1,80,640]{2,1,0:T(8,128)(2,1)S(1)} %get-tuple-element.49), channel_id=1, source_target_pairs={{0,17},{1,16},{16,1},{17,0},{2,19},{3,18},{18,3},{19,2},{4,21},{5,... | collective-permute-start | bytes 307208 | tf_op jit(solution)/shard_map/ppermute | solution.py:479
  35.1 0.5 %collective-permute-start.4 = (bf16[1,80,640]{2,1,0:T(8,128)(2,1)S(1)}, bf16[1,80,640]{2,1,0:T(8,128)(2,1)S(1)}, u32[]{:S(2)}, u32[]{:S(2)}) collective-permute-start(bf16[1,80,640]{2,1,0:T(8,128)(2,1)S(1)} %get-tuple-element.50), channel_id=1, source_target_pairs={{0,16},{1,17},{16,0},{17,1},{2,18},{3,19},{18,2},{19,3},{4,20},{5,... | collective-permute-start | bytes 307208 | tf_op jit(solution)/shard_map/ppermute | solution.py:479
  35.6 0.7 %collective-permute-start.3 = (bf16[1,80,640]{2,1,0:T(8,128)(2,1)S(1)}, bf16[1,80,640]{2,1,0:T(8,128)(2,1)S(1)}, u32[]{:S(2)}, u32[]{:S(2)}) collective-permute-start(bf16[1,80,640]{2,1,0:T(8,128)(2,1)S(1)} %get-tuple-element.51), channel_id=1, source_target_pairs={{0,1},{1,0},{16,17},{17,16},{2,3},{3,2},{18,19},{19,18},{4,5},{5,4... | collective-permute-start | bytes 307208 | tf_op jit(solution)/shard_map/ppermute | solution.py:479
  36.3 4.8 %softmax_parts.1 = (bf16[960,1024]{1,0:T(8,128)(2,1)S(1)}, bf16[1920,320]{1,0:T(8,128)(2,1)S(1)}, f32[8,128]{1,0:T(8,128)S(1)}) custom-call(s32[1,12]{1,0:T(1,128)S(1)} %bitcast.14, s32[1,1]{1,0:T(1,128)} %bitcast.7.first_ref, bf16[480,320]{1,0:T(8,128)(2,1)S(1)} %pad_maximum_fusion.own_ref, bf16[1200,128]{1,0:T(8,128)(2,1)S(1)} %collective-permute-done.odd_ref, ...), custom_call_target="tpu_custom_call" | custom-call | flops 20480000000 | bytes 102400000 | tf_op jit(solution)/shard_map/softmax_parts/pallas_call | solution.py:318
  41.1 0.0 collective-permute-done.5.refs_3_
  41.1 0.0 collective-permute-done.4.refs_2_
  41.2 0.0 collective-permute-done.3.refs_1_
  41.2 0.5 %gather_sum.1 = (bf16[160,320]{1,0:T(8,128)(2,1)S(1)}, bf16[400,128]{1,0:T(8,128)(2,1)S(1)}) custom-call(bf16[1,80,640]{2,1,0:T(8,128)(2,1)S(1)} %get-tuple-element.52.refs_0_, bf16[1,80,640]{2,1,0:T(8,128)(2,1)S(1)} %collective-permute-done.3.refs_1_, bf16[1,80,640]{2,1,0:T(8,128)(2,1)S(1)} %collective-permute-done.4.refs_2_, ...), custom_call_target="tpu_custom_call" | custom-call | flops 4096000000 | bytes 81920000 | tf_op jit(solution)/shard_map/gather_sum/pallas_call | solution.py:380
  41.7 0.1 collective-permute-start.7
  41.7 0.4 collective-permute-start.6
  42.2 2.4 %own_terms.1 = (bf16[160,320]{1,0:T(8,128)(2,1)}, f32[160,320]{1,0:T(8,128)S(1)}, f32[160,320]{1,0:T(8,128)S(1)}) custom-call(bf16[160,320]{1,0:T(8,128)(2,1)S(1)} %get-tuple-element.38.grad_ref, bf16[160,320]{1,0:T(8,128)(2,1)S(1)} %bitcast.13, bf16[960,1024]{1,0:T(8,128)(2,1)S(1)} %get-tuple-element.39.held_ref), custom_call_target="tpu_custom_call" | custom-call | tf_op jit(solution)/shard_map/own_terms/pallas_call | solution.py:414
  44.5 0.0 collective-permute-done.7.grad_ref
  44.5 0.7 %side_terms.2 = (f32[160,320]{1,0:T(8,128)S(1)}, f32[160,320]{1,0:T(8,128)S(1)}) custom-call(bf16[400,128]{1,0:T(8,128)(2,1)S(1)} %collective-permute-done.7.grad_ref, f32[160,320]{1,0:T(8,128)S(1)} %get-tuple-element.42.key_part_ref, f32[160,320]{1,0:T(8,128)S(1)} %get-tuple-element.43.value_part_ref, bf16[960,1024]{1,0:T(8,128)(2,1)S(1)} %get-tuple-element.39.held_ref, ...), custom_call_target="tpu_custom_call" | custom-call | tf_op jit(solution)/shard_map/side_terms/pallas_call | solution.py:451
  45.2 1.8 %collective-permute-done.6.grad_ref = bf16[400,128]{1,0:T(8,128)(2,1)S(1)} collective-permute-done((bf16[400,128]{1,0:T(8,128)(2,1)S(1)}, bf16[400,128]{1,0:T(8,128)(2,1)S(1)}, u32[]{:S(2)}, u32[]{:S(2)}) %collective-permute-start.6) | collective-permute-done | bytes 102432 | tf_op jit(solution)/shard_map/ppermute | solution.py:471
  47.0 1.4 %side_terms.3 = (bf16[160,320]{1,0:T(8,128)(2,1)}, bf16[160,320]{1,0:T(8,128)(2,1)}) custom-call(bf16[400,128]{1,0:T(8,128)(2,1)S(1)} %collective-permute-done.6.grad_ref, f32[160,320]{1,0:T(8,128)S(1)} %get-tuple-element.45.key_part_ref, f32[160,320]{1,0:T(8,128)S(1)} %get-tuple-element.46.value_part_ref, bf16[960,1024]{1,0:T(8,128)(2,1)S(1)} %get-tuple-element.39.held_ref, ...), custom_call_target="tpu_custom_call" | custom-call | tf_op jit(solution)/shard_map/side_terms/pallas_call | solution.py:451
  (14 shorter events, 0.1 us)
Async XLA Ops:
  0.6 14.2 %copy-start.4 = (bf16[320,160]{0,1:T(8,128)(2,1)S(1)}, bf16[320,160]{0,1:T(8,128)(2,1)}, u32[]{:S(2)}) copy-start(bf16[320,160]{0,1:T(8,128)(2,1)} %param.16) | copy-start | bytes 307204
  0.6 14.2 %copy-start.3 = (bf16[320,160]{0,1:T(8,128)(2,1)S(1)}, bf16[320,160]{0,1:T(8,128)(2,1)}, u32[]{:S(2)}) copy-start(bf16[320,160]{0,1:T(8,128)(2,1)} %param.15) | copy-start | bytes 307204
  0.7 14.2 %copy-start = (bf16[320,160]{0,1:T(8,128)(2,1)S(1)}, bf16[320,160]{0,1:T(8,128)(2,1)}, u32[]{:S(2)}) copy-start(bf16[320,160]{0,1:T(8,128)(2,1)} %param.14) | copy-start | bytes 307204
  0.7 24.0 %copy-start.1 = (bf16[80,640]{1,0:T(8,128)(2,1)S(1)}, bf16[80,640]{1,0:T(8,128)(2,1)}, u32[]{:S(2)}) copy-start(bf16[80,640]{1,0:T(8,128)(2,1)} %pre_ref.1) | copy-start | bytes 307204
  7.5 28.8 %copy-start.2 = (s32[12]{0:T(128)S(1)}, s32[12]{0:T(128)}, u32[]{:S(2)}) copy-start(s32[12]{0:T(128)} %param.17) | copy-start | bytes 148
  7.5 17.1 %all-to-all-start = ((bf16[8,24,640]{2,1,0:T(8,128)(2,1)}), bf16[8,24,640]{2,1,0:T(8,128)(2,1)S(1)}, u32[]{:S(2)}, u32[]{:S(2)}) async-start(bf16[8,24,640]{2,1,0:T(8,128)(2,1)} %bitcast.15), calls=%async_computation | async-start | bytes 491520 | tf_op jit(solution)/shard_map/all_to_all | solution.py:495
  15.2 15.6 %collective-permute-start.1 = (bf16[1200,128]{1,0:T(8,128)(2,1)S(1)}, bf16[1200,128]{1,0:T(8,128)(2,1)S(1)}, u32[]{:S(2)}, u32[]{:S(2)}) collective-permute-start(bf16[1200,128]{1,0:T(8,128)(2,1)S(1)} %maximum_dynamic-update-slice_fusion), channel_id=1, source_target_pairs={{0,2},{2,0},{4,6},{6,4},{8,10},{10,8},{12,14},{14,12},{1,3},{3,1},... | collective-permute-start | bytes 921608 | tf_op jit(solution)/shard_map/ppermute | solution.py:471
  17.3 13.5 %collective-permute-start = (bf16[1200,128]{1,0:T(8,128)(2,1)S(1)}, bf16[1200,128]{1,0:T(8,128)(2,1)S(1)}, u32[]{:S(2)}, u32[]{:S(2)}) collective-permute-start(bf16[1200,128]{1,0:T(8,128)(2,1)S(1)} %maximum_dynamic-update-slice_fusion), channel_id=1, source_target_pairs={{0,8},{2,4},{4,2},{6,14},{8,0},{10,12},{12,10},{14,6},{1,9},{3,5},... | collective-permute-start | bytes 921608 | tf_op jit(solution)/shard_map/ppermute | solution.py:471
  30.8 1.8 %collective-permute-start.2 = (bf16[4,80,640]{2,1,0:T(8,128)(2,1)S(1)}, bf16[4,80,640]{2,1,0:T(8,128)(2,1)S(1)}, u32[]{:S(2)}, u32[]{:S(2)}) collective-permute-start(bf16[4,80,640]{2,1,0:T(8,128)(2,1)S(1)} %get-tuple-element.31), channel_id=1, source_target_pairs={{0,8},{8,0},{1,9},{9,1},{2,10},{10,2},{3,11},{11,3},{4,12},{12,4},... | collective-permute-start | bytes 1228808 | tf_op jit(solution)/shard_map/ppermute | solution.py:501
  32.8 8.3 %collective-permute-start.5 = (bf16[1,80,640]{2,1,0:T(8,128)(2,1)S(1)}, bf16[1,80,640]{2,1,0:T(8,128)(2,1)S(1)}, u32[]{:S(2)}, u32[]{:S(2)}) collective-permute-start(bf16[1,80,640]{2,1,0:T(8,128)(2,1)S(1)} %get-tuple-element.49), channel_id=1, source_target_pairs={{0,17},{1,16},{16,1},{17,0},{2,19},{3,18},{18,3},{19,2},{4,21},{5,... | collective-permute-start | bytes 307208 | tf_op jit(solution)/shard_map/ppermute | solution.py:479
  35.1 6.1 %collective-permute-start.4 = (bf16[1,80,640]{2,1,0:T(8,128)(2,1)S(1)}, bf16[1,80,640]{2,1,0:T(8,128)(2,1)S(1)}, u32[]{:S(2)}, u32[]{:S(2)}) collective-permute-start(bf16[1,80,640]{2,1,0:T(8,128)(2,1)S(1)} %get-tuple-element.50), channel_id=1, source_target_pairs={{0,16},{1,17},{16,0},{17,1},{2,18},{3,19},{18,2},{19,3},{4,20},{5,... | collective-permute-start | bytes 307208 | tf_op jit(solution)/shard_map/ppermute | solution.py:479
  35.6 5.6 %collective-permute-start.3 = (bf16[1,80,640]{2,1,0:T(8,128)(2,1)S(1)}, bf16[1,80,640]{2,1,0:T(8,128)(2,1)S(1)}, u32[]{:S(2)}, u32[]{:S(2)}) collective-permute-start(bf16[1,80,640]{2,1,0:T(8,128)(2,1)S(1)} %get-tuple-element.51), channel_id=1, source_target_pairs={{0,1},{1,0},{16,17},{17,16},{2,3},{3,2},{18,19},{19,18},{4,5},{5,4... | collective-permute-start | bytes 307208 | tf_op jit(solution)/shard_map/ppermute | solution.py:479
  41.7 2.9 %collective-permute-start.7 = (bf16[400,128]{1,0:T(8,128)(2,1)S(1)}, bf16[400,128]{1,0:T(8,128)(2,1)S(1)}, u32[]{:S(2)}, u32[]{:S(2)}) collective-permute-start(bf16[400,128]{1,0:T(8,128)(2,1)S(1)} %get-tuple-element.41), channel_id=1, source_target_pairs={{0,8},{2,4},{4,2},{6,14},{8,0},{10,12},{12,10},{14,6},{1,9},{3,5},... | collective-permute-start | bytes 307208 | tf_op jit(solution)/shard_map/ppermute | solution.py:471
  41.7 5.3 %collective-permute-start.6 = (bf16[400,128]{1,0:T(8,128)(2,1)S(1)}, bf16[400,128]{1,0:T(8,128)(2,1)S(1)}, u32[]{:S(2)}, u32[]{:S(2)}) collective-permute-start(bf16[400,128]{1,0:T(8,128)(2,1)S(1)} %get-tuple-element.41), channel_id=1, source_target_pairs={{0,2},{2,0},{4,6},{6,4},{8,10},{10,8},{12,14},{14,12},{1,3},{3,1},... | collective-permute-start | bytes 307208 | tf_op jit(solution)/shard_map/ppermute | solution.py:471
